TPU v7x, 32 devices: a whole 2x2x4 slice. The times are simulated.
32 devices in a mesh: dp: 8 (over z, y), blk: 4 (over x, core).
Axes of the slice: x: 2, y: 2, z: 4, core: 2. Of those that a mesh axis runs over, the one named last changes fastest.
Arguments:
- patches: bfloat16 [5632, 768], P(('dp', 'blk')), may hold values from -6 to 6
- special: bfloat16 [160, 768], P('dp'), may hold values from -6 to 6
- image_ids: int32 [5632], P('dp'), may hold values from 0 to 2, as said below
- w_qkv: bfloat16 [768, 2304], P(('dp', 'blk')), may hold values from -0.21875 to 0.21875
- w_out: bfloat16 [768, 768], P(('dp', 'blk')), may hold values from -2.5 to 2.5
- w_up: bfloat16 [768, 3072], P(('dp', 'blk')), may hold values from -0.21875 to 0.21875
- w_down: bfloat16 [3072, 768], P(('dp', 'blk')), may hold values from -0.109375 to 0.109375
- gains: bfloat16 [4, 768], P(None, ('dp', 'blk')), may hold values from 0.5 to 1.5
- cot_patches: bfloat16 [5632, 768], P(('dp', 'blk')), may hold values from -6 to 6
- cot_special: bfloat16 [160, 768], P('dp'), may hold values from -6 to 6
Outputs:
- out_patches: bfloat16 [5632, 768], P(('dp', 'blk'))
- out_special: bfloat16 [160, 768], P('dp')
- grad_patches: float32 [5632, 768], P(('dp', 'blk'))
- grad_special: float32 [160, 768], P('dp')
- grad_qkv: float32 [768, 2304], P(('dp', 'blk'))
- grad_out: float32 [768, 768], P(('dp', 'blk'))
- grad_up: float32 [768, 3072], P(('dp', 'blk'))
- grad_down: float32 [3072, 768], P(('dp', 'blk'))
- grad_gains: float32 [4, 768], P(None, ('dp', 'blk'))
Inputs may be any that keep to these rules, and one draw needn't show every extreme that they name: `image_ids`: along a group's slots in band order the ids never fall. A group holds either one 518px image of 348 slots followed by padding, or 2 224px images of 176 slots each followed by padding (possibly none); image places without slots have only their special rows. Some group of every draw holds a 518px image.
All inputs are finite; a program needn't handle non-finite values.
Results may differ from a plain program's by a relative error of at most 0.015.
Values may be sent and summed in bfloat16 or wider, within the bound.
No kernel may reach another device: no remote copies, remote signals or barrier semaphores. Data moves between devices by JAX's collectives and lax.ppermute only.
A program may use at most 192 MiB of HBM per device.

v0:
```python
import jax
import jax.numpy as jnp
from jax import lax
from jax.sharding import PartitionSpec as P

HEAD_DIM = 64
SPECIAL = 5
MICRO = 2
TOK_MB = 88


SCORE_SCALE = 0.125
MASKED = -1e30
EPSILON = 1e-06


def merged(shard, axis, combine):
    everything = jax.tree.map(
        lambda part, kind: lax.all_gather(part.astype(kind), axis),
        shard,
        (jnp.bfloat16, jnp.bfloat16, jnp.bfloat16),
    )

    def take(k):
        return jax.tree.map(lambda part, own: part[k].astype(own.dtype), everything, shard)

    return lax.fori_loop(
        1, lax.axis_size(axis), lambda k, so_far: combine(so_far, take(k)), take(0)
    )


def from_behind(shard, axis, by):
    peers = lax.axis_size(axis)
    return lax.ppermute(shard, axis, [(i, (i + by) % peers) for i in range(peers)])


def norm_rows(values, gain_row):
    centre = values - jnp.mean(values, -1, keepdims=True)
    spread = jnp.mean(centre * centre, -1, keepdims=True)
    return centre * lax.rsqrt(spread + EPSILON) * gain_row


def split_heads(matrix):
    return matrix.reshape(matrix.shape[0], -1, HEAD_DIM)


def widen(per_head):
    return jnp.repeat(per_head.T, HEAD_DIM, axis=1)


def empty_state(length, head_count, feature_width):
    return (
        jnp.full((head_count, length), MASKED, jnp.float32),
        jnp.zeros((head_count, length), jnp.float32),
        jnp.zeros((length, feature_width), jnp.float32),
    )


def online(carried, queries, query_ids, key_rows, value_rows, key_ids):
    top_score, totals, accumulated = carried
    same_image = (query_ids[:, None] == key_ids[None, :])[None]
    scores = (
        jnp.einsum(
            "qhd,khd->hqk",
            split_heads(queries),
            split_heads(key_rows),
            preferred_element_type=jnp.float32,
        )
        * SCORE_SCALE
    )
    scores = jnp.where(same_image, scores, MASKED)
    new_top = jnp.maximum(top_score, jnp.max(scores, -1))
    weights = jnp.where(same_image, jnp.exp(scores - new_top[..., None]), 0.0)
    factor = jnp.exp(top_score - new_top)
    totals = totals * factor + jnp.sum(weights, -1)
    mixture = jnp.einsum(
        "hqk,khd->qhd",
        weights.astype(jnp.bfloat16),
        split_heads(value_rows),
        preferred_element_type=jnp.float32,
    )
    accumulated = accumulated * widen(factor) + mixture.reshape(accumulated.shape)
    return (new_top, totals, accumulated)


def combine(former, latter):
    highest = jnp.maximum(former[0], latter[0])
    scale_former = jnp.exp(former[0] - highest)
    scale_latter = jnp.exp(latter[0] - highest)
    return (
        highest,
        former[1] * scale_former + latter[1] * scale_latter,
        former[2] * widen(scale_former) + latter[2] * widen(scale_latter),
    )


def finish(carried):
    top_score, totals, accumulated = carried
    return (accumulated / widen(totals), top_score + jnp.log(totals))


def block_grads(queries, grad_attn, log_total, row_delta, query_ids, key_rows, value_rows, key_ids):
    same_image = (query_ids[:, None] == key_ids[None, :])[None]
    q_heads = split_heads(queries)
    g_heads = split_heads(grad_attn)
    scores = (
        jnp.einsum(
            "qhd,khd->hqk", q_heads, split_heads(key_rows), preferred_element_type=jnp.float32
        )
        * SCORE_SCALE
    )
    probabilities = jnp.where(same_image, jnp.exp(scores - log_total[..., None]), 0.0)
    grad_prob = jnp.einsum(
        "qhd,khd->hqk", g_heads, split_heads(value_rows), preferred_element_type=jnp.float32
    )
    dscore = (probabilities * (grad_prob - row_delta[..., None])).astype(jnp.bfloat16)
    grad_query = (
        jnp.einsum(
            "hqk,khd->qhd", dscore, split_heads(key_rows), preferred_element_type=jnp.float32
        ).reshape(queries.shape[0], -1)
        * SCORE_SCALE
    )
    grad_key = (
        jnp.einsum("hqk,qhd->khd", dscore, q_heads, preferred_element_type=jnp.float32).reshape(
            key_rows.shape[0], -1
        )
        * SCORE_SCALE
    )
    grad_value = jnp.einsum(
        "hqk,qhd->khd",
        probabilities.astype(jnp.bfloat16),
        g_heads,
        preferred_element_type=jnp.float32,
    ).reshape(key_rows.shape[0], -1)
    return (grad_query, grad_key, grad_value)


def fetch_weights(w_qkv, w_out, w_up, w_down, gains):
    return (
        lax.all_gather(w_qkv, ("dp", "blk"), axis=0, tiled=True),
        lax.all_gather(w_out, ("dp", "blk"), axis=0, tiled=True),
        lax.all_gather(w_up, ("dp", "blk"), axis=0, tiled=True),
        lax.all_gather(w_down, ("dp", "blk"), axis=0, tiled=True),
        lax.all_gather(gains, ("dp", "blk"), axis=1, tiled=True),
    )


def reduce_grads(grad_terms):
    g_qkv, g_out, g_up, g_down, g_gains = grad_terms
    return (
        lax.psum_scatter(g_qkv, ("dp", "blk"), scatter_dimension=0, tiled=True),
        lax.psum_scatter(g_out, ("dp", "blk"), scatter_dimension=0, tiled=True),
        lax.psum_scatter(g_up, ("dp", "blk"), scatter_dimension=0, tiled=True),
        lax.psum_scatter(g_down, ("dp", "blk"), scatter_dimension=0, tiled=True),
        lax.psum_scatter(g_gains, ("dp", "blk"), scatter_dimension=1, tiled=True),
    )


def contract_rows(left_rows, right_rows):
    return jnp.einsum("ra,rb->ab", left_rows, right_rows, preferred_element_type=jnp.float32)


def row_delta_of(grad_attn, attended):
    product = grad_attn.astype(jnp.float32) * attended
    return product.reshape(product.shape[0], -1, HEAD_DIM).sum(-1).T


def on_device(
    patches, special, image_ids, w_qkv, w_out, w_up, w_down, gains, cot_patches, cot_special
):
    cycle_size = lax.axis_size("blk")
    cycle_index = lax.axis_index("blk")
    width = w_out.shape[1]
    head_count = width // HEAD_DIM
    tok_rows = TOK_MB
    spec_rows = special.shape[0] // MICRO
    ids_group = image_ids.reshape(cycle_size, MICRO, tok_rows)
    spec_ids = jnp.arange(spec_rows, dtype=jnp.int32) // SPECIAL
    row_weight = jnp.concatenate(
        [jnp.ones((tok_rows,), jnp.float32), jnp.full((spec_rows,), 1.0 / cycle_size, jnp.float32)]
    )
    row_weight_low = row_weight.astype(jnp.bfloat16)[:, None]
    summed_terms = None
    shard_terms = None
    out_parts = []
    spec_parts = []
    grad_parts = []
    grad_spec_parts = []
    for micro_index in range(MICRO):
        full_weights = fetch_weights(w_qkv, w_out, w_up, w_down, gains)
        qkv_full, out_full, up_full, down_full, gains_full = full_weights
        gain_rows = gains_full.astype(jnp.float32)
        tokens = jnp.concatenate(
            [
                patches[micro_index * tok_rows : (micro_index + 1) * tok_rows],
                special[micro_index * spec_rows : (micro_index + 1) * spec_rows],
            ],
            0,
        ).astype(jnp.float32)
        ids_flat = ids_group[:, micro_index].reshape(-1)
        patch_ids = lax.dynamic_slice_in_dim(ids_flat, cycle_index * tok_rows, tok_rows)
        normed = norm_rows(tokens, gain_rows[0]).astype(jnp.bfloat16)
        projected = jnp.dot(normed, qkv_full, preferred_element_type=jnp.float32).astype(
            jnp.bfloat16
        )
        patch_q = projected[:tok_rows, :width]
        patch_k = projected[:tok_rows, width : 2 * width]
        patch_v = projected[:tok_rows, 2 * width :]
        spec_q = projected[tok_rows:, :width]
        spec_k = projected[tok_rows:, width : 2 * width]
        spec_v = projected[tok_rows:, 2 * width :]
        start_state = online(
            empty_state(tok_rows, head_count, width), patch_q, patch_ids, spec_k, spec_v, spec_ids
        )
        partial_value = start_state
        key_rows = lax.all_gather(patch_k, "blk", axis=0, tiled=True)
        value_rows = lax.all_gather(patch_v, "blk", axis=0, tiled=True)
        length = key_rows.shape[0]
        key_ids = ids_flat
        blocks = length // tok_rows

        def visit_block(running, block_item):
            return (
                online(running, patch_q, patch_ids, block_item[0], block_item[1], block_item[2]),
                None,
            )

        partial_value, unused = lax.scan(
            visit_block,
            partial_value,
            (
                key_rows.reshape(blocks, tok_rows, -1),
                value_rows.reshape(blocks, tok_rows, -1),
                key_ids.reshape(blocks, tok_rows),
            ),
        )
        spec_top, spec_total, spec_accum = online(
            empty_state(spec_rows, head_count, width), spec_q, spec_ids, patch_k, patch_v, patch_ids
        )
        spec_state = merged((spec_top, spec_total, spec_accum), "blk", combine)
        spec_state = online(spec_state, spec_q, spec_ids, spec_k, spec_v, spec_ids)
        patch_attn, patch_lse = finish(partial_value)
        spec_attn, spec_lse = finish(spec_state)
        attended = jnp.concatenate([patch_attn, spec_attn], 0)
        attended_low = attended.astype(jnp.bfloat16)
        branch = jnp.dot(attended_low, out_full, preferred_element_type=jnp.float32)
        middle = tokens + gain_rows[1] * branch
        normed_mlp = norm_rows(middle, gain_rows[2]).astype(jnp.bfloat16)
        hidden = jnp.dot(normed_mlp, up_full, preferred_element_type=jnp.float32)
        active = jax.nn.gelu(hidden, approximate=False).astype(jnp.bfloat16)
        mlp_out = jnp.dot(active, down_full, preferred_element_type=jnp.float32)
        final = middle + gain_rows[3] * mlp_out
        out_parts.append(final[:tok_rows].astype(jnp.bfloat16))
        spec_parts.append(final[tok_rows:].astype(jnp.bfloat16))
        upstream = jnp.concatenate(
            [
                cot_patches[micro_index * tok_rows : (micro_index + 1) * tok_rows],
                cot_special[micro_index * spec_rows : (micro_index + 1) * spec_rows],
            ],
            0,
        ).astype(jnp.float32)
        grad_mlp = (gain_rows[3] * upstream).astype(jnp.bfloat16)
        g_down = contract_rows(active, grad_mlp * row_weight_low)
        grad_active = jnp.einsum(
            "rd,fd->rf", grad_mlp, down_full, preferred_element_type=jnp.float32
        )
        unused_value, gelu_pull = jax.vjp(
            lambda pre_act: jax.nn.gelu(pre_act, approximate=False), hidden
        )
        grad_hidden = gelu_pull(grad_active)[0].astype(jnp.bfloat16)
        g_up = contract_rows(normed_mlp, grad_hidden * row_weight_low)
        grad_normed_mlp = jnp.einsum(
            "rf,df->rd", grad_hidden, up_full, preferred_element_type=jnp.float32
        )
        unused_value, norm_pull_mlp = jax.vjp(
            lambda rows_in: norm_rows(rows_in, gain_rows[2]), middle
        )
        grad_middle = upstream + norm_pull_mlp(grad_normed_mlp)[0]
        g_ln2 = jnp.sum(row_weight[:, None] * grad_normed_mlp * norm_rows(middle, 1.0), 0)
        g_ls2 = jnp.sum(row_weight[:, None] * upstream * mlp_out, 0)
        g_ls1 = jnp.sum(row_weight[:, None] * grad_middle * branch, 0)
        grad_branch = (gain_rows[1] * grad_middle).astype(jnp.bfloat16)
        g_out = contract_rows(attended_low, grad_branch * row_weight_low)
        grad_attended = jnp.einsum(
            "re,de->rd", grad_branch, out_full, preferred_element_type=jnp.float32
        ).astype(jnp.bfloat16)
        all_delta = row_delta_of(grad_attended, attended)
        patch_delta = all_delta[:, :tok_rows]
        spec_delta = all_delta[:, tok_rows:]
        patch_grad_attn = grad_attended[:tok_rows]
        spec_grad_attn = grad_attended[tok_rows:]
        grad_pq_first, grad_sk_part, grad_sv_part = block_grads(
            patch_q, patch_grad_attn, patch_lse, patch_delta, patch_ids, spec_k, spec_v, spec_ids
        )
        grad_sq_part, grad_pk_local, grad_pv_local = block_grads(
            spec_q, spec_grad_attn, spec_lse, spec_delta, spec_ids, patch_k, patch_v, patch_ids
        )
        sum_sq, sum_sk, sum_sv = (
            lax.psum(grad_sq_part.astype(jnp.bfloat16), "blk").astype(jnp.float32),
            lax.psum(grad_sk_part.astype(jnp.bfloat16), "blk").astype(jnp.float32),
            lax.psum(grad_sv_part.astype(jnp.bfloat16), "blk").astype(jnp.float32),
        )
        grad_sq_own, grad_sk_own, grad_sv_own = block_grads(
            spec_q, spec_grad_attn, spec_lse, spec_delta, spec_ids, spec_k, spec_v, spec_ids
        )

        def cycle_step(hop_index, carried):
            keys_now, values_now, grad_keys, grad_values, grad_queries = carried
            source = (cycle_index - hop_index) % cycle_size
            key_ids = lax.dynamic_slice_in_dim(ids_flat, source * tok_rows, tok_rows)
            term_q, term_k, term_v = block_grads(
                patch_q,
                patch_grad_attn,
                patch_lse,
                patch_delta,
                patch_ids,
                keys_now,
                values_now,
                key_ids,
            )
            keys_now, values_now = from_behind((keys_now, values_now), "blk", 1)
            grad_keys, grad_values = (
                from_behind((grad_keys + term_k).astype(jnp.bfloat16), "blk", 1).astype(
                    jnp.float32
                ),
                from_behind((grad_values + term_v).astype(jnp.bfloat16), "blk", 1).astype(
                    jnp.float32
                ),
            )
            return (keys_now, values_now, grad_keys, grad_values, grad_queries + term_q)

        zero_rows = jnp.zeros((tok_rows, width), jnp.float32)
        unused_keys, unused_values, grad_pk, grad_pv, grad_pq = lax.fori_loop(
            0, cycle_size, cycle_step, (patch_k, patch_v, zero_rows, zero_rows, grad_pq_first)
        )
        grad_pk = grad_pk + grad_pk_local
        grad_pv = grad_pv + grad_pv_local
        grad_patch_qkv = jnp.concatenate([grad_pq, grad_pk, grad_pv], 1)
        grad_spec_qkv = jnp.concatenate(
            [sum_sq + grad_sq_own, sum_sk + grad_sk_own, sum_sv + grad_sv_own], 1
        )
        grad_projected = jnp.concatenate([grad_patch_qkv, grad_spec_qkv], 0).astype(jnp.bfloat16)
        g_qkv = contract_rows(normed, grad_projected * row_weight_low)
        grad_normed = jnp.einsum(
            "re,de->rd", grad_projected, qkv_full, preferred_element_type=jnp.float32
        )
        unused_value, norm_pull_attn = jax.vjp(
            lambda rows_in: norm_rows(rows_in, gain_rows[0]), tokens
        )
        grad_tokens = grad_middle + norm_pull_attn(grad_normed)[0]
        g_ln1 = jnp.sum(row_weight[:, None] * grad_normed * norm_rows(tokens, 1.0), 0)
        grad_parts.append(grad_tokens[:tok_rows])
        grad_spec_parts.append(grad_tokens[tok_rows:])
        grad_terms = (g_qkv, g_out, g_up, g_down, jnp.stack([g_ln1, g_ls1, g_ln2, g_ls2], 0))
        summed_terms = (
            grad_terms
            if summed_terms is None
            else tuple((held + extra for held, extra in zip(summed_terms, grad_terms)))
        )
    shard_terms = reduce_grads(summed_terms)
    return (
        jnp.concatenate(out_parts, 0),
        jnp.concatenate(spec_parts, 0),
        jnp.concatenate(grad_parts, 0),
        jnp.concatenate(grad_spec_parts, 0),
        shard_terms[0],
        shard_terms[1],
        shard_terms[2],
        shard_terms[3],
        shard_terms[4],
    )


def solution(mesh):
    placed = (
        P(("dp", "blk"), None),
        P("dp", None),
        P("dp"),
        P(("dp", "blk"), None),
        P(("dp", "blk"), None),
        P(("dp", "blk"), None),
        P(("dp", "blk"), None),
        P(None, ("dp", "blk")),
        P(("dp", "blk"), None),
        P("dp", None),
    )
    return jax.shard_map(
        on_device,
        mesh=mesh,
        in_specs=placed,
        out_specs=(
            P(("dp", "blk"), None),
            P("dp", None),
            P(("dp", "blk"), None),
            P("dp", None),
            P(("dp", "blk"), None),
            P(("dp", "blk"), None),
            P(("dp", "blk"), None),
            P(("dp", "blk"), None),
            P(None, ("dp", "blk")),
        ),
        check_vma=False,
    )
```

profile of v0, /device:TPU:0, one launch (start us, length us, event | category | flops | bytes accessed | tf_op | source)
XLA Modules:
  0.0 990.3 jit_solution(7570600167616403072)
XLA Ops:
  15.9 43.3 %all-gather.4 = bf16[32,24,4]{1,2,0:T(4,128)(2,1)S(1)} all-gather(bf16[1,24,4]{1,2,0:T(4,128)(2,1)S(1)} %bitcast.524), channel_id=1, replica_groups=mesh['dp'=8,'blk'=4] {'dp','blk'}, dimensions={0}, use_global_device_ids=true | all-gather | bytes 6336 | tf_op jit(solution)/shard_map/all_gather | solution.py:144
  61.7 12.2 %all-gather.14.cloned.1.call-done = bf16[768,2304]{1,0:T(8,128)(2,1)} async-done(((bf16[24,2304]{1,0:T(8,128)(2,1)}), bf16[768,2304]{1,0:T(8,128)(2,1)}) %all-gather.14.cloned.1.call-update) | async-done | bytes 3538960 | tf_op jit(solution)/shard_map/all_gather | solution.py:140
  73.9 2.7 convolution_convert_fusion.1
  76.7 7.7 all_gather.58
  85.3 7.8 all_gather.59
  96.5 2.7 convolution_convert_fusion
  100.5 7.4 all_gather.66
  108.0 7.8 all_gather.67
  118.1 11.9 %while.114 = (s32[]{:T(128)}, f32[12,88]{1,0:T(8,128)S(1)}, f32[12,88]{1,0:T(8,128)S(1)}, f32[88,768]{0,1:T(8,128)S(1)}, s32[88]{0:T(128)S(1)}, /*index=5*/s32[4...) while((s32[]{:T(128)}, f32[12,88]{1,0:T(8,128)S(1)}, ...), condition=%wide.region_7.8_spmd, body=%wide.region_4.7_spmd.sunk | while | flops 24772000 | bytes 3794725 | solution.py:228
  133.4 5.3 all_gather.62
  138.7 5.2 all-gather.6
  143.9 5.2 all-gather.5
  149.1 1.9 while.115
  156.5 11.8 %while.116 = (s32[]{:T(128)}, f32[12,88]{1,0:T(8,128)S(1)}, f32[12,88]{1,0:T(8,128)S(1)}, f32[88,768]{0,1:T(8,128)S(1)}, s32[88]{0:T(128)S(1)}, /*index=5*/s32[4...) while((s32[]{:T(128)}, f32[12,88]{1,0:T(8,128)S(1)}, ...), condition=%wide.region_23.24_spmd, body=%wide.region_20.23_spmd.sunk | while | flops 24772000 | bytes 3783405 | solution.py:228
  172.9 5.2 all-gather.8
  178.1 5.2 all-gather.7
  183.3 5.5 all_gather.70
  198.7 2.2 fusion.311
  203.6 4.5 fusion.305
  208.1 4.4 multiply_convert_fusion.1
  212.6 48.5 %all-gather.20.cloned.1.call-done = bf16[3072,768]{1,0:T(8,128)(2,1)} async-done(((bf16[96,768]{1,0:T(8,128)(2,1)}), bf16[3072,768]{1,0:T(8,128)(2,1)}) %all-gather.20.cloned.1.call-update) | async-done | bytes 4718608 | tf_op jit(solution)/shard_map/all_gather | solution.py:143
  261.1 6.7 add_convert_fusion
  270.4 4.4 add_convert_fusion.1
  274.9 2.4 multiply_reduce_fusion.2
  281.5 1.9 copy.451
  292.4 2.1 convert_multiply_fusion.8
  321.9 2.0 convolution_add_fusion.3
  323.9 59.0 %while.118 = (s32[]{:T(128)}, bf16[88,768]{0,1:T(8,128)(2,1)}, bf16[88,768]{0,1:T(8,128)(2,1)}, f32[88,768]{0,1:T(8,128)S(1)}, f32[88,768]{0,1:T(8,128)}, /*inde...) while((s32[]{:T(128)}, bf16[88,768]{0,1:T(8,128)(2,1)}, ...), condition=%wide.region_36.37_spmd.clone, body=%wide.region_35.36_spmd.clone.sunk | while | flops 60875600 | bytes 10214175 | solution.py:333
  331.8 3.4 collective-permute-done.2
  347.0 2.6 collective-permute-done.2
  361.4 3.4 collective-permute-done.2
  376.5 2.6 collective-permute-done.2
  386.5 50.3 %while.119 = (s32[]{:T(128)}, bf16[88,768]{0,1:T(8,128)(2,1)S(1)}, bf16[88,768]{0,1:T(8,128)(2,1)S(1)}, f32[88,768]{0,1:T(8,128)S(1)}, f32[88,768]{0,1:T(8,128)S...) while((s32[]{:T(128)}, bf16[88,768]{0,1:T(8,128)(2,1)S(1)}, ...), condition=%wide.region_46.47_spmd.clone, body=%wide.region_45.46_spmd.clone.sunk | while | flops 60875600 | bytes 9132803 | solution.py:333
  392.1 3.9 collective-permute-done.6
  404.7 3.9 collective-permute-done.6
  417.3 3.9 collective-permute-done.6
  429.9 3.9 collective-permute-done.6
  441.4 28.1 %all-reduce.4.cloned.1.call-done = (bf16[10,768]{1,0:T(8,128)(2,1)}, bf16[10,768]{1,0:T(8,128)(2,1)}, bf16[10,768]{1,0:T(8,128)(2,1)}, bf16[10,768]{1,0:T(8,128)...) async-done(((bf16[10,768]{1,0:T(8,128)(2,1)}, bf16[10,768]{1,0:T(8,128)(2,1)}, bf16[10,768]{1,0:T(8,128)(2,1)}, bf16[10,768]{1,0:T(8,128)(2,1)}, ...) | async-done | bytes 92176 | tf_op jit(solution)/shard_map/psum | solution.py:301
  475.4 4.2 convolution_add_fusion
  482.4 5.2 convolution_add_fusion.2
  490.3 6.5 convolution_add_fusion.1
  496.9 3.4 fusion.323
  500.4 5.7 multiply_reduce_fusion.1
  511.8 40.7 %all-reduce = f32[4,768]{1,0:T(4,128)S(1)} all-reduce(f32[4,768]{1,0:T(4,128)S(1)} %maximum_add_fusion), channel_id=10, replica_groups=mesh['dp'=8,'blk'=4] {'dp','blk'}, use_global_device_ids=true, to_apply=%region_64.65.clone | all-reduce | flops 3072 | bytes 24576
  554.7 21.2 %reduce-scatter.8.cloned.1.call-done = f32[24,768]{1,0:T(8,128)} async-done(((f32[768,768]{1,0:T(8,128)}), f32[24,768]{1,0:T(8,128)}) %reduce-scatter.8.cloned.1.call-update) | async-done | bytes 73744 | tf_op jit(solution)/shard_map/reduce_scatter | solution.py:152
  575.8 124.4 %reduce-scatter.6.cloned.1.call-done = f32[24,2304]{1,0:T(8,128)} async-done(((f32[768,2304]{1,0:T(8,128)}), f32[24,2304]{1,0:T(8,128)}) %reduce-scatter.6.cloned.1.call-update) | async-done | bytes 221200 | tf_op jit(solution)/shard_map/reduce_scatter | solution.py:151
  700.3 142.3 %reduce-scatter.10.cloned.1.call-done = f32[24,3072]{1,0:T(8,128)} async-done(((f32[768,3072]{1,0:T(8,128)}), f32[24,3072]{1,0:T(8,128)}) %reduce-scatter.10.cloned.1.call-update) | async-done | bytes 294928 | tf_op jit(solution)/shard_map/reduce_scatter | solution.py:153
  842.6 141.0 %reduce-scatter.12.cloned.1.call-done = f32[96,768]{1,0:T(8,128)} async-done(((f32[3072,768]{1,0:T(8,128)}), f32[96,768]{1,0:T(8,128)}) %reduce-scatter.12.cloned.1.call-update) | async-done | bytes 294928 | tf_op jit(solution)/shard_map/reduce_scatter | solution.py:154
  (1037 shorter events, 220.8 us)
Async XLA Ops:
  7.2 66.7 %all-gather.14.cloned.1.call-start = ((), (), s32[]{:S(2)}) async-start(), calls=%async_computation.4 | async-start | bytes 3649536 | tf_op jit(solution)/shard_map/all_gather | solution.py:140
  7.9 189.0 %all-gather.16.cloned.1.call-start = ((), (), s32[]{:S(2)}) async-start(), calls=%async_computation.5 | async-start | bytes 1216512 | tf_op jit(solution)/shard_map/all_gather | solution.py:141
  8.7 194.9 %all-gather.18.cloned.1.call-start = ((), (), s32[]{:S(2)}) async-start(), calls=%async_computation.6 | async-start | bytes 4866048 | tf_op jit(solution)/shard_map/all_gather | solution.py:142
  9.4 251.7 %all-gather.20.cloned.1.call-start = ((), (), s32[]{:S(2)}) async-start(), calls=%async_computation.7 | async-start | bytes 4866048 | tf_op jit(solution)/shard_map/all_gather | solution.py:143
  10.0 459.5 %all-reduce.4.cloned.1.call-start = ((), (), s32[]{:S(2)}) async-start(), calls=%async_computation.12 | async-start | bytes 294912 | tf_op jit(solution)/shard_map/psum | solution.py:301
  11.8 105.7 %copy-start.135 = (pred[88,10]{0,1:T(8,128)(4,1)}, pred[88,10]{0,1:T(8,128)(4,1)S(1)}, u32[]{:S(2)}) copy-start(pred[88,10]{0,1:T(8,128)(4,1)S(1)} %get-tuple-element.1638) | copy-start | bytes 2644
  11.8 144.1 %copy-start.133 = (pred[88,10]{0,1:T(8,128)(4,1)}, pred[88,10]{0,1:T(8,128)(4,1)S(1)}, u32[]{:S(2)}) copy-start(pred[88,10]{0,1:T(8,128)(4,1)S(1)} %get-tuple-element.1639) | copy-start | bytes 2644
  12.5 119.5 %copy-start.156 = (pred[10,88]{1,0:T(8,128)(4,1)}, pred[10,88]{1,0:T(8,128)(4,1)S(1)}, u32[]{:S(2)}) copy-start(pred[10,88]{1,0:T(8,128)(4,1)S(1)} %get-tuple-element.1640) | copy-start | bytes 2644
  14.2 82.3 %copy-start.14 = (bf16[88,768]{1,0:T(8,128)(2,1)}, bf16[88,768]{1,0:T(8,128)(2,1)S(1)}, u32[]{:S(2)}) copy-start(bf16[88,768]{1,0:T(8,128)(2,1)S(1)} %get-tuple-element.1606) | copy-start | bytes 405508
  200.9 76.4 %copy-start.5 = (f32[98,768]{1,0:T(8,128)}, f32[98,768]{1,0:T(8,128)S(1)}, u32[]{:S(2)}) copy-start(f32[98,768]{1,0:T(8,128)S(1)} %get-tuple-element.1633) | copy-start | bytes 903172
  201.0 76.4 %copy-start.177 = (f32[98]{0:T(128)}, f32[98]{0:T(128)S(1)}, u32[]{:S(2)}) copy-start(f32[98]{0:T(128)S(1)} %broadcast_multiply_fusion.2) | copy-start | bytes 1180
  201.9 75.5 %copy-start.175 = (f32[98]{0:T(128)}, f32[98]{0:T(128)S(1)}, u32[]{:S(2)}) copy-start(f32[98]{0:T(128)S(1)} %broadcast_multiply_fusion) | copy-start | bytes 1180
  324.8 14.2 %collective-permute-start = (bf16[88,768]{0,1:T(8,128)(2,1)S(1)}, bf16[88,768]{0,1:T(8,128)(2,1)}, u32[]{:S(2)}, u32[]{:S(2)}) collective-permute-start(bf16[88,768]{0,1:T(8,128)(2,1)S(1)} %copy.700), channel_id=1, source_target_pairs={{0,1},{1,2},{2,3},{3,0},{4,5},{5,6},{6,7},{7,4},{8,9},{9,10},{10,1... | collective-permute-start | bytes 405512 | tf_op jit(solution)/shard_map/while/body/eval_jaxpr/ppermute | solution.py:34
  326.0 13.0 %collective-permute-start.1 = (bf16[88,768]{0,1:T(8,128)(2,1)S(1)}, bf16[88,768]{0,1:T(8,128)(2,1)}, u32[]{:S(2)}, u32[]{:S(2)}) collective-permute-start(bf16[88,768]{0,1:T(8,128)(2,1)S(1)} %copy.701), channel_id=1, source_target_pairs={{0,1},{1,2},{2,3},{3,0},{4,5},{5,6},{6,7},{7,4},{8,9},{9,10},{10,1... | collective-permute-start | bytes 405512 | tf_op jit(solution)/shard_map/while/body/eval_jaxpr/ppermute | solution.py:34
  329.8 5.4 collective-permute-start.2
  331.0 6.3 collective-permute-start.3
  340.0 13.4 %collective-permute-start = (bf16[88,768]{0,1:T(8,128)(2,1)S(1)}, bf16[88,768]{0,1:T(8,128)(2,1)}, u32[]{:S(2)}, u32[]{:S(2)}) collective-permute-start(bf16[88,768]{0,1:T(8,128)(2,1)S(1)} %copy.700), channel_id=1, source_target_pairs={{0,1},{1,2},{2,3},{3,0},{4,5},{5,6},{6,7},{7,4},{8,9},{9,10},{10,1... | collective-permute-start | bytes 405512 | tf_op jit(solution)/shard_map/while/body/eval_jaxpr/ppermute | solution.py:34
  340.9 12.5 %collective-permute-start.1 = (bf16[88,768]{0,1:T(8,128)(2,1)S(1)}, bf16[88,768]{0,1:T(8,128)(2,1)}, u32[]{:S(2)}, u32[]{:S(2)}) collective-permute-start(bf16[88,768]{0,1:T(8,128)(2,1)S(1)} %copy.701), channel_id=1, source_target_pairs={{0,1},{1,2},{2,3},{3,0},{4,5},{5,6},{6,7},{7,4},{8,9},{9,10},{10,1... | collective-permute-start | bytes 405512 | tf_op jit(solution)/shard_map/while/body/eval_jaxpr/ppermute | solution.py:34
  344.2 5.4 collective-permute-start.2
  345.1 6.6 collective-permute-start.3
  354.3 14.2 %collective-permute-start = (bf16[88,768]{0,1:T(8,128)(2,1)S(1)}, bf16[88,768]{0,1:T(8,128)(2,1)}, u32[]{:S(2)}, u32[]{:S(2)}) collective-permute-start(bf16[88,768]{0,1:T(8,128)(2,1)S(1)} %copy.700), channel_id=1, source_target_pairs={{0,1},{1,2},{2,3},{3,0},{4,5},{5,6},{6,7},{7,4},{8,9},{9,10},{10,1... | collective-permute-start | bytes 405512 | tf_op jit(solution)/shard_map/while/body/eval_jaxpr/ppermute | solution.py:34
  355.3 13.3 %collective-permute-start.1 = (bf16[88,768]{0,1:T(8,128)(2,1)S(1)}, bf16[88,768]{0,1:T(8,128)(2,1)}, u32[]{:S(2)}, u32[]{:S(2)}) collective-permute-start(bf16[88,768]{0,1:T(8,128)(2,1)S(1)} %copy.701), channel_id=1, source_target_pairs={{0,1},{1,2},{2,3},{3,0},{4,5},{5,6},{6,7},{7,4},{8,9},{9,10},{10,1... | collective-permute-start | bytes 405512 | tf_op jit(solution)/shard_map/while/body/eval_jaxpr/ppermute | solution.py:34
  359.3 5.4 collective-permute-start.2
  360.3 6.6 collective-permute-start.3
  369.5 13.4 %collective-permute-start = (bf16[88,768]{0,1:T(8,128)(2,1)S(1)}, bf16[88,768]{0,1:T(8,128)(2,1)}, u32[]{:S(2)}, u32[]{:S(2)}) collective-permute-start(bf16[88,768]{0,1:T(8,128)(2,1)S(1)} %copy.700), channel_id=1, source_target_pairs={{0,1},{1,2},{2,3},{3,0},{4,5},{5,6},{6,7},{7,4},{8,9},{9,10},{10,1... | collective-permute-start | bytes 405512 | tf_op jit(solution)/shard_map/while/body/eval_jaxpr/ppermute | solution.py:34
  370.4 12.5 %collective-permute-start.1 = (bf16[88,768]{0,1:T(8,128)(2,1)S(1)}, bf16[88,768]{0,1:T(8,128)(2,1)}, u32[]{:S(2)}, u32[]{:S(2)}) collective-permute-start(bf16[88,768]{0,1:T(8,128)(2,1)S(1)} %copy.701), channel_id=1, source_target_pairs={{0,1},{1,2},{2,3},{3,0},{4,5},{5,6},{6,7},{7,4},{8,9},{9,10},{10,1... | collective-permute-start | bytes 405512 | tf_op jit(solution)/shard_map/while/body/eval_jaxpr/ppermute | solution.py:34
  373.7 5.4 collective-permute-start.2
  374.6 6.6 collective-permute-start.3
  386.6 12.5 %collective-permute-start.4 = (bf16[88,768]{0,1:T(8,128)(2,1)S(1)}, bf16[88,768]{0,1:T(8,128)(2,1)S(1)}, u32[]{:S(2)}, u32[]{:S(2)}) collective-permute-start(bf16[88,768]{0,1:T(8,128)(2,1)S(1)} %copy.682), channel_id=1, source_target_pairs={{0,1},{1,2},{2,3},{3,0},{4,5},{5,6},{6,7},{7,4},{8,9},{9,10},{10,1... | collective-permute-start | bytes 405512 | tf_op jit(solution)/shard_map/while/body/eval_jaxpr/ppermute | solution.py:34
  386.6 12.5 %collective-permute-start.5 = (bf16[88,768]{0,1:T(8,128)(2,1)S(1)}, bf16[88,768]{0,1:T(8,128)(2,1)S(1)}, u32[]{:S(2)}, u32[]{:S(2)}) collective-permute-start(bf16[88,768]{0,1:T(8,128)(2,1)S(1)} %copy.683), channel_id=1, source_target_pairs={{0,1},{1,2},{2,3},{3,0},{4,5},{5,6},{6,7},{7,4},{8,9},{9,10},{10,1... | collective-permute-start | bytes 405512 | tf_op jit(solution)/shard_map/while/body/eval_jaxpr/ppermute | solution.py:34
  390.1 6.0 collective-permute-start.6
  391.1 7.0 collective-permute-start.7
  399.1 12.5 %collective-permute-start.4 = (bf16[88,768]{0,1:T(8,128)(2,1)S(1)}, bf16[88,768]{0,1:T(8,128)(2,1)S(1)}, u32[]{:S(2)}, u32[]{:S(2)}) collective-permute-start(bf16[88,768]{0,1:T(8,128)(2,1)S(1)} %copy.682), channel_id=1, source_target_pairs={{0,1},{1,2},{2,3},{3,0},{4,5},{5,6},{6,7},{7,4},{8,9},{9,10},{10,1... | collective-permute-start | bytes 405512 | tf_op jit(solution)/shard_map/while/body/eval_jaxpr/ppermute | solution.py:34
  399.2 12.5 %collective-permute-start.5 = (bf16[88,768]{0,1:T(8,128)(2,1)S(1)}, bf16[88,768]{0,1:T(8,128)(2,1)S(1)}, u32[]{:S(2)}, u32[]{:S(2)}) collective-permute-start(bf16[88,768]{0,1:T(8,128)(2,1)S(1)} %copy.683), channel_id=1, source_target_pairs={{0,1},{1,2},{2,3},{3,0},{4,5},{5,6},{6,7},{7,4},{8,9},{9,10},{10,1... | collective-permute-start | bytes 405512 | tf_op jit(solution)/shard_map/while/body/eval_jaxpr/ppermute | solution.py:34
  402.6 6.0 collective-permute-start.6
  403.7 7.0 collective-permute-start.7
  411.7 12.5 %collective-permute-start.4 = (bf16[88,768]{0,1:T(8,128)(2,1)S(1)}, bf16[88,768]{0,1:T(8,128)(2,1)S(1)}, u32[]{:S(2)}, u32[]{:S(2)}) collective-permute-start(bf16[88,768]{0,1:T(8,128)(2,1)S(1)} %copy.682), channel_id=1, source_target_pairs={{0,1},{1,2},{2,3},{3,0},{4,5},{5,6},{6,7},{7,4},{8,9},{9,10},{10,1... | collective-permute-start | bytes 405512 | tf_op jit(solution)/shard_map/while/body/eval_jaxpr/ppermute | solution.py:34
  411.8 12.5 %collective-permute-start.5 = (bf16[88,768]{0,1:T(8,128)(2,1)S(1)}, bf16[88,768]{0,1:T(8,128)(2,1)S(1)}, u32[]{:S(2)}, u32[]{:S(2)}) collective-permute-start(bf16[88,768]{0,1:T(8,128)(2,1)S(1)} %copy.683), channel_id=1, source_target_pairs={{0,1},{1,2},{2,3},{3,0},{4,5},{5,6},{6,7},{7,4},{8,9},{9,10},{10,1... | collective-permute-start | bytes 405512 | tf_op jit(solution)/shard_map/while/body/eval_jaxpr/ppermute | solution.py:34
  415.2 6.0 collective-permute-start.6
  416.3 7.0 collective-permute-start.7
  424.3 12.5 %collective-permute-start.4 = (bf16[88,768]{0,1:T(8,128)(2,1)S(1)}, bf16[88,768]{0,1:T(8,128)(2,1)S(1)}, u32[]{:S(2)}, u32[]{:S(2)}) collective-permute-start(bf16[88,768]{0,1:T(8,128)(2,1)S(1)} %copy.682), channel_id=1, source_target_pairs={{0,1},{1,2},{2,3},{3,0},{4,5},{5,6},{6,7},{7,4},{8,9},{9,10},{10,1... | collective-permute-start | bytes 405512 | tf_op jit(solution)/shard_map/while/body/eval_jaxpr/ppermute | solution.py:34
  424.4 12.5 %collective-permute-start.5 = (bf16[88,768]{0,1:T(8,128)(2,1)S(1)}, bf16[88,768]{0,1:T(8,128)(2,1)S(1)}, u32[]{:S(2)}, u32[]{:S(2)}) collective-permute-start(bf16[88,768]{0,1:T(8,128)(2,1)S(1)} %copy.683), channel_id=1, source_target_pairs={{0,1},{1,2},{2,3},{3,0},{4,5},{5,6},{6,7},{7,4},{8,9},{9,10},{10,1... | collective-permute-start | bytes 405512 | tf_op jit(solution)/shard_map/while/body/eval_jaxpr/ppermute | solution.py:34
  427.8 6.0 collective-permute-start.6
  428.9 7.0 collective-permute-start.7
  439.2 136.7 %reduce-scatter.8.cloned.1.call-start = ((), (), s32[]{:S(2)}) async-start(), calls=%async_computation.9 | async-start | bytes 2433024 | tf_op jit(solution)/shard_map/reduce_scatter | solution.py:152
  440.4 259.9 %reduce-scatter.6.cloned.1.call-start = ((), (), s32[]{:S(2)}) async-start(), calls=%async_computation.8 | async-start | bytes 7299072 | tf_op jit(solution)/shard_map/reduce_scatter | solution.py:151
  479.8 362.8 %reduce-scatter.10.cloned.1.call-start = ((), (), s32[]{:S(2)}) async-start(), calls=%async_computation.10 | async-start | bytes 9732096 | tf_op jit(solution)/shard_map/reduce_scatter | solution.py:153
  487.7 495.9 %reduce-scatter.12.cloned.1.call-start = ((), (), s32[]{:S(2)}) async-start(), calls=%async_computation.11 | async-start | bytes 9732096 | tf_op jit(solution)/shard_map/reduce_scatter | solution.py:154
  (213 other events, 1929.9 us)
Sparse Core Ops, SparseCore 0:
  10.9 62.9 all-gather.13
  76.8 53.4 all-gather.15
  133.2 62.8 all-gather.17
  198.9 62.1 all-gather.19
  439.3 30.1 all-reduce.3
  476.1 99.7 reduce-scatter.7
  582.1 118.1 reduce-scatter.5
  707.8 134.8 reduce-scatter.9
  849.1 134.4 reduce-scatter.11
where the time goes:
time: 1000 us; the launch traced here: 990 us
  waiting for transfers between devices  557 us (56%)
  blocking collectives  146 us (15%)
  matrix products  113 us (11%)
  local copies, waits for them, and re-layouts  77 us (8%)
  other arithmetic  59.3 us (6%)
  starting transfers between devices  19.1 us (2%)
  between operations  17.1 us (2%)
    reduce_scatter x1, waiting for transfers between devices, reduce_grads(): lax.psum_scatter(g_up, ('dp', 'blk'), scatter_dimension=0, tiled=True)  142 us
    reduce_scatter x1, waiting for transfers between devices, reduce_grads(): lax.psum_scatter(g_down, ('dp', 'blk'), scatter_dimension=0, tiled=True)  141 us
    reduce_scatter x1, waiting for transfers between devices, reduce_grads(): lax.psum_scatter(g_qkv, ('dp', 'blk'), scatter_dimension=0, tiled=True)  124 us
    all_gather x1, waiting for transfers between devices, fetch_weights(): lax.all_gather(w_down, ('dp', 'blk'), axis=0, tiled=True)  48.5 us
    all_gather x1, blocking collectives, fetch_weights(): lax.all_gather(gains, ('dp', 'blk'), axis=1, tiled=True)  43.3 us
    unnamed x1, blocking collectives  40.7 us
    ppermute x32, waiting for transfers between devices, from_behind(): lax.ppermute(shard, axis, [(i, (i + by) % peers) for i in range(peers)])  36.8 us
    all_gather x6, blocking collectives, merged(): lax.all_gather(part.astype(kind), axis)  31.6 us
  transfers between devices with their start and end apart: 41, of which 23 were waited for; matrix products, arithmetic and copies ran while one was open for 17% of the time, Pallas kernels for 0%

commit v1 on v0

--- a/solution.py
+++ b/solution.py
@@ -1,6 +1,8 @@
 import jax
 import jax.numpy as jnp
 from jax import lax
+from jax.experimental import pallas as pl
+from jax.experimental.pallas import tpu as pltpu
 from jax.sharding import PartitionSpec as P
 
 HEAD_DIM = 64
@@ -8,10 +10,12 @@
 MICRO = 2
 TOK_MB = 88
 
-
 SCORE_SCALE = 0.125
 MASKED = -1e30
 EPSILON = 1e-06
+
+BF16 = jnp.bfloat16
+F32 = jnp.float32
 
 
 def merged(shard, axis, combine):
@@ -371,6 +375,663 @@
     )
 
 
+PAD_ID = 99
+
+
+def mm(a, b):
+    return jnp.dot(a, b, preferred_element_type=F32)
+
+
+def mm_nt(a, b):
+    return lax.dot_general(a, b, (((1,), (1,)), ((), ())), preferred_element_type=F32)
+
+
+def mm_tn(a, b):
+    return lax.dot_general(a, b, (((0,), (0,)), ((), ())), preferred_element_type=F32)
+
+
+def here():
+    place = lax.axis_index("blk")
+    group = lax.axis_index("dp")
+    return place, place // 2, place % 2, group // 2, group % 2
+
+
+def chunk_index(slot, z, y):
+    hops, crossed = slot % 4, slot // 4
+    source_z = lax.rem(z + 4 - hops, 4)
+    source_y = y if not crossed else 1 - y
+    return source_z * 2 + source_y
+
+
+def loop_rows(count, block, body):
+    def step(i, carry):
+        body(pl.ds(pl.multiple_of(i * block, block), block))
+        return carry
+
+    lax.fori_loop(0, count // block, step, 0)
+
+
+def call(kernel, outs, ins, scratch=(), flops=0, limit=48):
+    moved = sum(o.size * o.dtype.itemsize for o in outs) + sum(i.size * i.dtype.itemsize for i in ins)
+    return pl.pallas_call(
+        kernel,
+        out_shape=tuple(outs),
+        in_specs=[pl.BlockSpec(memory_space=pltpu.VMEM)] * len(ins),
+        out_specs=tuple(pl.BlockSpec(memory_space=pltpu.VMEM) for _ in outs),
+        scratch_shapes=list(scratch),
+        compiler_params=pltpu.CompilerParams(vmem_limit_bytes=limit * 2**20),
+        cost_estimate=pl.CostEstimate(flops=flops, bytes_accessed=moved, transcendentals=0),
+        name=kernel.__name__,
+    )(*ins)
+
+
+def sds(*shape, dtype=BF16):
+    return jax.ShapeDtypeStruct(shape, dtype)
+
+
+def pick_pieces(w_qkv, w_up, gains, patches, cots, own, near, far, rows, held):
+    place = here()[0]
+    held[...] = jnp.zeros_like(held)
+    up = w_up[...].astype(F32)
+    qkv = w_qkv[...].astype(F32)
+    gain = gains[...].astype(F32)
+    for b in range(4):
+        for d in range(8):
+            held[b, 0:24, d * 96 : d * 96 + 96] = up[:, d * 384 + b * 96 : d * 384 + b * 96 + 96]
+        for part in range(3):
+            held[b, 24:48, part * 192 : part * 192 + 192] = qkv[
+                :, part * 768 + b * 192 : part * 768 + b * 192 + 192
+            ]
+        held[b, 24:28, 576:600] = gain
+    own[...] = held[place].astype(BF16)
+    near[...] = held[place ^ 1].astype(BF16)
+    far[0:48, :] = held[place ^ 2].astype(BF16)
+    far[48:96, :] = held[place ^ 3].astype(BF16)
+    rows[0:176, :] = patches[...]
+    rows[176:352, :] = cots[...]
+
+
+def join_pieces(own, near, far, near_far, w_out, pack, up_chunk, pack_f, up_f):
+    place = here()[0]
+    pieces = (
+        own[...].astype(F32),
+        near[...].astype(F32),
+        far[0:48, :].astype(F32),
+        near_far[48:96, :].astype(F32),
+    )
+    for k, piece in enumerate(pieces):
+        source = place ^ k
+        at = pl.ds(pl.multiple_of(source * 24, 8), 24)
+        up_f[at, :] = piece[0:24]
+        pack_f[at, 0:576] = piece[24:48, 0:576]
+        pack_f[pl.ds(pl.multiple_of(96 + source * 8, 8), 8), 0:576] = jnp.zeros((8, 576), F32)
+        pack_f[pl.ds(pl.multiple_of(96 + source * 8, 8), 8), 576:768] = piece[24:32, 576:768]
+    out = w_out[...].astype(F32)
+    for i in range(4):
+        pack_f[i * 24 : i * 24 + 24, 576:768] = out[:, i * 192 : i * 192 + 192]
+    pack[...] = pack_f[...].astype(BF16)
+    up_chunk[...] = up_f[...].astype(BF16)
+
+
+def open_pack(*refs):
+    chunks, (w_qkv, w_out, gain_rows, out_f, gain_f) = refs[:8], refs[8:]
+    _, _, _, z, y = here()
+    for slot, chunk in enumerate(chunks):
+        d = chunk_index(slot, z, y)
+        w_qkv[pl.ds(pl.multiple_of(d * 96, 96), 96), :] = chunk[0:96, 0:576]
+        tail = chunk[0:128, 576:768].astype(F32)
+        for i in range(4):
+            out_f[pl.ds(pl.multiple_of(d * 24, 8), 24), i * 192 : i * 192 + 192] = tail[
+                i * 24 : i * 24 + 24
+            ]
+        gain_f[d] = tail[96:128, :]
+    w_out[...] = out_f[...].astype(BF16)
+    gain_rows[...] = jnp.zeros_like(gain_rows)
+    for d in range(8):
+        for b in range(4):
+            at = (d * 4 + b) * 24
+            gain_rows[0:4, at : at + 24] = gain_f[d, b * 8 : b * 8 + 4, 0:24]
+
+
+def normalise(rows):
+    centre = rows - jnp.mean(rows, -1, keepdims=True)
+    spread = jnp.mean(centre * centre, -1, keepdims=True)
+    scale = lax.rsqrt(spread + EPSILON)
+    return centre * scale, scale
+
+
+def place_rows(scratch, blocks, tail, first):
+    place = here()[0]
+    for k, block in enumerate(blocks):
+        rows = block[first : first + 176, :].astype(F32)
+        source = place ^ k
+        for m in range(MICRO):
+            scratch[pl.ds(pl.multiple_of(m * 368 + source * 88, 8), 88), :] = rows[m * 88 : m * 88 + 88]
+    rows = tail[...].astype(F32)
+    for m in range(MICRO):
+        scratch[m * 368 + 352 : m * 368 + 368, :] = rows[m * 16 : m * 16 + 16]
+
+
+def attend(
+    rows_0, rows_1, rows_2, rows_3, tail, cot_tail, ids_col, ids_row, w_qkv, gain_rows,
+    tokens, cots, normed, projected, probs, attended, rows_f,
+):
+    place_rows(rows_f, (rows_0, rows_1, rows_2, rows_3), cot_tail, 176)
+    cots[...] = rows_f[...].astype(BF16)
+    place_rows(rows_f, (rows_0, rows_1, rows_2, rows_3), tail, 0)
+    gain = gain_rows[0:1, :]
+
+    def norm_block(at):
+        rows = rows_f[at, :]
+        tokens[at, :] = rows.astype(BF16)
+        normed[at, :] = (normalise(rows)[0] * gain).astype(BF16)
+
+    loop_rows(736, 16, norm_block)
+    for m in range(MICRO):
+        at = slice(m * 368, m * 368 + 368)
+        qkv = mm(normed[at, :], w_qkv[...]).astype(BF16)
+        projected[at, :] = qkv
+        same = ids_col[at, :] == ids_row[m : m + 1, :]
+        heads = []
+        for h in range(3):
+            q = qkv[:, h * 64 : h * 64 + 64]
+            k = qkv[:, 192 + h * 64 : 192 + h * 64 + 64]
+            v = qkv[:, 384 + h * 64 : 384 + h * 64 + 64]
+            scores = jnp.where(same, mm_nt(q, k) * SCORE_SCALE, MASKED)
+            weights = jnp.exp(scores - jnp.max(scores, -1, keepdims=True))
+            weights = weights * (1.0 / jnp.sum(weights, -1, keepdims=True))
+            weights = weights.astype(BF16)
+            probs[m * 3 + h] = weights
+            heads.append(mm(weights, v))
+        attended[at, :] = jnp.concatenate(heads, -1).astype(BF16)
+
+
+def order_out(out_0, out_1, out_2, out_3, ordered, mine, out_f):
+    place = here()[0]
+    for k, part in enumerate((out_0, out_1, out_2, out_3)):
+        source = place ^ k
+        rows = part[...].astype(F32)
+        for d in range(8):
+            at = pl.multiple_of((d * 4 + source) * 24, 8)
+            out_f[pl.ds(at, 24), :] = rows[d * 24 : d * 24 + 24]
+    ordered[...] = out_f[...].astype(BF16)
+    mine[...] = out_f[pl.ds(pl.multiple_of(place * 192, 8), 192), :].astype(BF16)
+
+
+def raise_rows(*refs):
+    heads, (w_out, tokens, gain_rows), chunks = refs[0:4], refs[4:7], refs[7:15]
+    branch, middle, normed, active, slope, w_up, up_f = refs[15:]
+    place, _, _, z, y = here()
+    for slot, chunk in enumerate(chunks):
+        d = chunk_index(slot, z, y)
+        w_up[pl.ds(pl.multiple_of(d * 96, 96), 96), :] = chunk[...]
+    for m in range(MICRO):
+        at = slice(m * 368, m * 368 + 368)
+        total = None
+        for k, part in enumerate(heads):
+            source = place ^ k
+            rows = w_out[pl.ds(pl.multiple_of(source * 192, 16), 192), :]
+            term = mm(part[at, :], rows)
+            total = term if total is None else total + term
+        up_f[at, :] = total
+    gain_s, gain_n = gain_rows[1:2, :], gain_rows[2:3, :]
+
+    def norm_block(at):
+        a = up_f[at, :]
+        branch[at, :] = a.astype(BF16)
+        rows = tokens[at, :].astype(F32) + gain_s * a
+        middle[at, :] = rows
+        normed[at, :] = (normalise(rows)[0] * gain_n).astype(BF16)
+
+    loop_rows(736, 16, norm_block)
+    for m in range(MICRO):
+        at = slice(m * 368, m * 368 + 368)
+        up_f[at, :] = mm(normed[at, :], w_up[...])
+
+    def gelu_block(at):
+        u = up_f[at, :]
+        half = 0.5 + 0.5 * lax.erf(u * 0.7071067811865476)
+        active[at, :] = (u * half).astype(BF16)
+        slope[at, :] = half + u * (0.3989422804014327 * jnp.exp(-0.5 * u * u))
+
+    loop_rows(736, 16, gelu_block)
+
+
+def lower_rows(*refs):
+    (active, slope, cots, gain_rows, w_up), chunks = refs[:5], refs[5:13]
+    w_down, grad_mlp, grad_hidden, away, kept, work = refs[13:]
+    _, _, core, z, y = here()
+    for slot, chunk in enumerate(chunks):
+        d = chunk_index(slot, z, y)
+        w_down[pl.ds(pl.multiple_of(d * 96, 96), 96), :] = chunk[...]
+    gain = gain_rows[3:4, :]
+
+    def scale_block(at):
+        grad_mlp[at, :] = (gain * cots[at, :].astype(F32)).astype(BF16)
+
+    loop_rows(736, 16, scale_block)
+    for m in range(MICRO):
+        at = slice(m * 368, m * 368 + 368)
+        grad = mm_nt(grad_mlp[at, :], w_down[...])
+        grad_hidden[at, :] = (slope[at, :] * grad).astype(BF16)
+        work[m] = mm_nt(grad_hidden[at, :], w_up[...])
+    away[...] = work[1 - core].astype(BF16)
+    kept[...] = work[core]
+
+
+def split_rows(pieces, place, away, kept):
+    away[0:208, :] = pieces[place ^ 1].astype(BF16)
+    away[208:416, :] = pieces[place ^ 3].astype(BF16)
+    kept[0:208, :] = pieces[place]
+    kept[208:416, :] = pieces[place ^ 2]
+
+
+def cut_rows(rows_f, pieces):
+    for b in range(4):
+        for m in range(MICRO):
+            pieces[b, m * 104 : m * 104 + 88, :] = rows_f[m * 368 + b * 88 : m * 368 + b * 88 + 88, :]
+            pieces[b, m * 104 + 88 : m * 104 + 104, :] = rows_f[m * 368 + 352 : m * 368 + 368, :]
+
+
+def halve(grad_f, y, away, kept, rows):
+    for zz in range(4):
+        other = pl.ds(pl.multiple_of((zz * 2 + 1 - y) * rows, 8), rows)
+        ours = pl.ds(pl.multiple_of((zz * 2 + y) * rows, 8), rows)
+        away[zz] = grad_f[other, :].astype(BF16)
+        kept[zz] = grad_f[ours, :]
+
+
+def mlp_grads(
+    active, normed, grad_mlp, grad_hidden, w_down, cots,
+    down_away, down_kept, up_away, up_kept, rows_away, rows_kept, scale_grad, work, pieces,
+):
+    place, _, _, _, y = here()
+    work[0:768, :] = mm_tn(active[...], grad_mlp[...])
+    halve(work, y, down_away, down_kept, 96)
+    work[0:768, :] = mm_tn(normed[...], grad_hidden[...])
+    halve(work, y, up_away, up_kept, 96)
+    for m in range(MICRO):
+        at = slice(m * 368, m * 368 + 368)
+        work[at, :] = mm(active[at, :], w_down[...])
+    scale_grad[...] = jnp.zeros_like(scale_grad)
+
+    def sum_block(at):
+        scale_grad[...] += (cots[at, :].astype(F32) * work[at, :]).reshape(2, 8, 768).sum(0)
+
+    loop_rows(736, 16, sum_block)
+    cut_rows(work, pieces)
+    split_rows(pieces, place, rows_away, rows_kept)
+
+
+def add_rows(kept, came, total):
+    total[...] = (kept[...] + came[...].astype(F32)).astype(BF16)
+
+
+def add_pair(here_rows, came, total):
+    total[...] = (here_rows[...].astype(F32) + came[...].astype(F32)).astype(BF16)
+
+
+def attend_back(
+    sum_own, sum_near, middle, cots, branch, tokens, gain_rows, w_mine, w_qkv, projected, probs,
+    head_0, head_1, head_2, head_3, normed, targets, scale_grad_mlp,
+    grad_rows, away, kept, rows_away, rows_kept,
+    work, grad_branch, grad_heads, grad_qkv, grad_mid, extra, pieces, scale_grad,
+):
+    place, _, core, _, y = here()
+    for m in range(MICRO):
+        at = slice(m * 368, m * 368 + 368)
+
+        @pl.when(core == m)
+        def _():
+            work[at, :] = sum_own[...].astype(F32)
+
+        @pl.when(core != m)
+        def _():
+            work[at, :] = sum_near[...].astype(F32)
+
+    scale_grad[...] = jnp.zeros_like(scale_grad)
+    gain_s, gain_n = gain_rows[1:2, :], gain_rows[2:3, :]
+
+    def norm_block(at):
+        unit, scale = normalise(middle[at, :])
+        grad = work[at, :]
+        pulled = grad * gain_n
+        pulled = pulled - jnp.mean(pulled, -1, keepdims=True) - unit * jnp.mean(
+            pulled * unit, -1, keepdims=True
+        )
+        through = cots[at, :].astype(F32) + scale * pulled
+        grad_mid[at, :] = through
+        grad_branch[at, :] = (gain_s * through).astype(BF16)
+        scale_grad[1] += (through * branch[at, :].astype(F32)).reshape(2, 8, 768).sum(0)
+        scale_grad[2] += (grad * unit).reshape(2, 8, 768).sum(0)
+
+    loop_rows(736, 16, norm_block)
+    for m in range(MICRO):
+        for part, first in ((0, place * 88), (88, 352)):
+            rows = 88 if part == 0 else 16
+            grad_rows[m * 104 + part : m * 104 + part + rows, :] = grad_mid[
+                pl.ds(pl.multiple_of(m * 368 + first, 8), rows), :
+            ]
+    for m in range(MICRO):
+        at = slice(m * 368, m * 368 + 368)
+        grad_heads[at, :] = mm_nt(grad_branch[at, :], w_mine[...]).astype(BF16)
+        qkv = projected[at, :]
+        g_heads = grad_heads[at, :]
+        grads = [[], [], []]
+        for h in range(3):
+            q = qkv[:, h * 64 : h * 64 + 64]
+            k = qkv[:, 192 + h * 64 : 192 + h * 64 + 64]
+            v = qkv[:, 384 + h * 64 : 384 + h * 64 + 64]
+            g = g_heads[:, h * 64 : h * 64 + 64]
+            weights = probs[m * 3 + h]
+            grad_prob = mm_nt(g, v)
+            wide = weights.astype(F32)
+            moved = wide * grad_prob
+            delta = jnp.sum(moved, -1, keepdims=True)
+            grad_score = (moved - wide * delta).astype(BF16)
+            grads[0].append(mm(grad_score, k) * SCORE_SCALE)
+            grads[1].append(mm_tn(grad_score, q) * SCORE_SCALE)
+            grads[2].append(mm_tn(weights, g))
+        grad_qkv[at, :] = jnp.concatenate(grads[0] + grads[1] + grads[2], -1).astype(BF16)
+    for m in range(MICRO):
+        at = slice(m * 368, m * 368 + 368)
+        work[at, :] = mm_nt(grad_qkv[at, :], w_qkv[...])
+
+    def sum_block(at):
+        unit, _ = normalise(tokens[at, :].astype(F32))
+        scale_grad[0] += (work[at, :] * unit).reshape(2, 8, 768).sum(0)
+
+    loop_rows(736, 16, sum_block)
+    cut_rows(work, pieces)
+    split_rows(pieces, place, rows_away, rows_kept)
+    grad_mid[0:768, 0:576] = mm_tn(normed[...], grad_qkv[...])
+    chosen = None
+    for k, part in enumerate((head_0, head_1, head_2, head_3)):
+        source = place ^ k
+        index = lax.broadcasted_iota(jnp.int32, (192, 192), 0) + source * 192
+        pick = jnp.where(index == targets[...], 1.0, 0.0).astype(BF16)
+        term = mm(part[...], pick)
+        chosen = term if chosen is None else chosen + term
+    extra[...] = mm_tn(chosen.astype(BF16), grad_branch[...])
+    rows = [
+        jnp.sum(scale_grad[0], 0, keepdims=True),
+        0.25 * jnp.sum(scale_grad[1], 0, keepdims=True),
+        0.25 * jnp.sum(scale_grad[2], 0, keepdims=True),
+        jnp.sum(scale_grad_mlp[...], 0, keepdims=True),
+    ]
+    for d in range(8):
+        base = d * 112
+        work[base : base + 96, 0:576] = grad_mid[d * 96 : d * 96 + 96, 0:576]
+        for i in range(4):
+            work[base + i * 24 : base + i * 24 + 24, 576:768] = extra[
+                d * 24 : d * 24 + 24, i * 192 : i * 192 + 192
+            ]
+        work[base + 96 : base + 112, :] = jnp.zeros((16, 768), F32)
+        for i in range(4):
+            work[base + 96 + i : base + 97 + i, 0:96] = rows[i][:, d * 96 : d * 96 + 96]
+    halve(work, y, away, kept, 112)
+
+
+def sum_y(kept, came, own, send_1, send_2, send_3):
+    _, _, _, z, _ = here()
+    own[...] = kept[z] + came[z].astype(F32)
+    for k, send in ((1, send_1), (2, send_2), (3, send_3)):
+        there = lax.rem(z + k, 4)
+        send[...] = (kept[there] + came[there].astype(F32)).astype(BF16)
+
+
+def sum_z(own, came_1, came_2, came_3, total):
+    total[...] = (
+        own[...]
+        + came_1[...].astype(F32)
+        + came_2[...].astype(F32)
+        + came_3[...].astype(F32)
+    )
+
+
+def add_pieces(kept_m, came_m, kept_h, came_h, stay, go):
+    for i, (kept, came) in enumerate(((kept_m, came_m), (kept_h, came_h))):
+        stay[i * 208 : i * 208 + 208, :] = kept[0:208, :] + came[0:208, :].astype(F32)
+        go[i * 208 : i * 208 + 208, :] = (kept[208:416, :] + came[208:416, :].astype(F32)).astype(BF16)
+
+
+def finish_rows(
+    stay, came, middle, grad_rows, patches, tail, gain_rows,
+    out_patches, out_special, grad_patches, grad_special,
+):
+    place = here()[0]
+    own = patches[...].astype(F32)
+    rest = tail[...].astype(F32)
+    outs, out_tails = [], []
+    for m in range(MICRO):
+        for part, first in ((0, place * 88), (88, 352)):
+            count = 88 if part == 0 else 16
+            at = slice(m * 104 + part, m * 104 + part + count)
+            far_at = slice(208 + m * 104 + part, 208 + m * 104 + part + count)
+            mid = middle[pl.ds(pl.multiple_of(m * 368 + first, 8), count), :]
+            final = mid + gain_rows[3:4, :] * (stay[at, :] + came[at, :].astype(F32))
+            (outs if part == 0 else out_tails).append(final)
+            rows = own[m * 88 : m * 88 + 88] if part == 0 else rest[m * 16 : m * 16 + 16]
+            unit, scale = normalise(rows)
+            pulled = gain_rows[0:1, :] * (stay[far_at, :] + came[far_at, :].astype(F32))
+            pulled = pulled - jnp.mean(pulled, -1, keepdims=True) - unit * jnp.mean(
+                pulled * unit, -1, keepdims=True
+            )
+            grad = grad_rows[at, :] + scale * pulled
+            if part == 0:
+                grad_patches[m * 88 : m * 88 + 88, :] = grad
+            else:
+                grad_special[m * 10 : m * 10 + 10, :] = grad[0:10]
+    out_patches[...] = jnp.concatenate(outs, 0).astype(BF16)
+    out_special[...] = jnp.concatenate([part[0:10] for part in out_tails], 0).astype(BF16)
+
+
+def pick_grads(up, pack, own, near, far, grad_out, held):
+    place = here()[0]
+    for b in range(4):
+        held[b, 0:24, :] = up[b * 24 : b * 24 + 24, :]
+        held[b, 24:48, 0:576] = pack[b * 24 : b * 24 + 24, 0:576]
+        held[b, 24:48, 576:768] = jnp.zeros((24, 192), F32)
+        held[b, 24:28, 576:600] = pack[96:100, b * 24 : b * 24 + 24]
+        grad_out[:, b * 192 : b * 192 + 192] = pack[b * 24 : b * 24 + 24, 576:768]
+    own[...] = held[place]
+    near[...] = held[place ^ 1].astype(BF16)
+    far[0:48, :] = held[place ^ 2].astype(BF16)
+    far[48:96, :] = held[place ^ 3].astype(BF16)
+
+
+def join_grads(own, near, far, near_far, grad_qkv, grad_up, grad_gains, held):
+    place = here()[0]
+    held[place] = own[...]
+    held[place ^ 1] = near[...].astype(F32)
+    held[place ^ 2] = far[0:48, :].astype(F32)
+    held[place ^ 3] = near_far[48:96, :].astype(F32)
+    gains = None
+    for b in range(4):
+        for d in range(8):
+            at = d * 384 + b * 96
+            grad_up[:, at : at + 96] = held[b, 0:24, d * 96 : d * 96 + 96]
+        for part in range(3):
+            at = part * 768 + b * 192
+            grad_qkv[:, at : at + 192] = held[b, 24:48, part * 192 : part * 192 + 192]
+        term = held[b, 24:28, 576:600]
+        gains = term if gains is None else gains + term
+    grad_gains[...] = gains
+
+
+def send(rows, axis, step):
+    pairs = []
+    for group in range(8):
+        z, y = group // 2, group % 2
+        for place in range(4):
+            target = {
+                "core": (group, place ^ 1),
+                "x": (group, place ^ 2),
+                "y": (z * 2 + 1 - y, place),
+                "z": ((z + step) % 4 * 2 + y, place),
+            }[axis]
+            pairs.append((group * 4 + place, target[0] * 4 + target[1]))
+    return lax.ppermute(rows, ("dp", "blk"), pairs)
+
+
+def gather_dp(chunk):
+    along_z = [chunk] + [send(chunk, "z", k) for k in (1, 2, 3)]
+    return along_z + [send(part, "y", 1) for part in along_z]
+
+
+def gather_blk(rows):
+    near = send(rows, "core", 1)
+    far = send(rows, "x", 1)
+    return [rows, near, far, send(far, "core", 1)]
+
+
+def scatter_dp(away, kept, rows):
+    came = send(away, "y", 1)
+    own, *parts = call(sum_y, [sds(rows, 768, dtype=F32)] + [sds(rows, 768)] * 3, [kept, came])
+    came = [send(part, "z", k) for k, part in zip((1, 2, 3), parts)]
+    return call(sum_z, [sds(rows, 768, dtype=F32)], [own, *came])[0]
+
+
+def pad_tail(rows):
+    return jnp.pad(rows.reshape(2, 10, 768), ((0, 0), (0, 6), (0, 0))).reshape(32, 768)
+
+
+def on_device_split(
+    patches, special, image_ids, w_qkv, w_out, w_up, w_down, gains, cot_patches, cot_special
+):
+    place = lax.axis_index("blk")
+    tail, cot_tail = pad_tail(special), pad_tail(cot_special)
+    spec_ids = jnp.concatenate(
+        [jnp.arange(10, dtype=jnp.int32) // SPECIAL, jnp.full((6,), PAD_ID, jnp.int32)]
+    )
+    ids = image_ids.reshape(4, 2, 88).transpose(1, 0, 2).reshape(2, 352)
+    ids_row = jnp.concatenate([ids, jnp.broadcast_to(spec_ids, (2, 16))], 1)
+    ids_col = ids_row.reshape(736, 1)
+    column = jnp.arange(192, dtype=jnp.int32)
+    targets = (column + column // 24 * 72 + place * 24).reshape(1, 192)
+
+    own, near, far, rows = call(
+        pick_pieces,
+        [sds(48, 768), sds(48, 768), sds(96, 768), sds(352, 768)],
+        [w_qkv, w_up, gains, patches, cot_patches],
+        [pltpu.VMEM((4, 48, 768), F32)],
+    )
+    came_far = send(far, "x", 1)
+    came_near, came_near_far = send(near, "core", 1), send(came_far, "core", 1)
+    row_parts = gather_blk(rows)
+    down_chunks = gather_dp(w_down)
+    pack, up_chunk = call(
+        join_pieces,
+        [sds(128, 768), sds(96, 768)],
+        [own, came_near, came_far, came_near_far, w_out],
+        [pltpu.VMEM((128, 768), F32), pltpu.VMEM((96, 768), F32)],
+    )
+    pack_chunks = gather_dp(pack)
+    up_chunks = gather_dp(up_chunk)
+    qkv_full, out_part, gain_rows = call(
+        open_pack,
+        [sds(768, 576), sds(192, 768), sds(8, 768, dtype=F32)],
+        pack_chunks,
+        [pltpu.VMEM((192, 768), F32), pltpu.VMEM((8, 32, 192), F32)],
+    )
+    out_parts = gather_blk(out_part)
+    tokens, cots, normed, projected, probs, attended = call(
+        attend,
+        [
+            sds(736, 768), sds(736, 768), sds(736, 768), sds(736, 576),
+            sds(6, 368, 368), sds(736, 192),
+        ],
+        [*row_parts, tail, cot_tail, ids_col, ids_row, qkv_full, gain_rows],
+        [pltpu.VMEM((736, 768), F32)],
+        flops=2 * 736 * 768 * 576 + 4 * 6 * 368 * 368 * 64,
+    )
+    heads = gather_blk(attended)
+    out_full, out_mine = call(
+        order_out, [sds(768, 768), sds(192, 768)], out_parts, [pltpu.VMEM((768, 768), F32)]
+    )
+    branch, middle, normed_mlp, active, slope, up_full = call(
+        raise_rows,
+        [
+            sds(736, 768), sds(736, 768, dtype=F32), sds(736, 768), sds(736, 768),
+            sds(736, 768, dtype=F32), sds(768, 768),
+        ],
+        [*heads, out_full, tokens, gain_rows, *up_chunks],
+        [pltpu.VMEM((736, 768), F32)],
+        flops=4 * 736 * 768 * 768,
+    )
+    down_full, grad_mlp, grad_hidden, sum_away, sum_kept = call(
+        lower_rows,
+        [sds(768, 768), sds(736, 768), sds(736, 768), sds(368, 768), sds(368, 768, dtype=F32)],
+        [active, slope, cots, gain_rows, up_full, *down_chunks],
+        [pltpu.VMEM((2, 368, 768), F32)],
+        flops=4 * 736 * 768 * 768,
+    )
+    sum_came = send(sum_away, "core", 1)
+    chip_sum = call(add_rows, [sds(368, 768)], [sum_kept, sum_came])[0]
+    chip_came = send(chip_sum, "x", 1)
+    half = [sds(4, 96, 768), sds(4, 96, 768, dtype=F32)]
+    rows_split = [sds(416, 768), sds(416, 768, dtype=F32)]
+    down_away, down_kept, up_away, up_kept, m_away, m_kept, scale_mlp = call(
+        mlp_grads,
+        [*half, *half, *rows_split, sds(8, 768, dtype=F32)],
+        [active, normed_mlp, grad_mlp, grad_hidden, down_full, cots],
+        [pltpu.VMEM((768, 768), F32), pltpu.VMEM((4, 208, 768), F32)],
+        flops=6 * 736 * 768 * 768,
+    )
+    grad_down = scatter_dp(down_away, down_kept, 96)
+    grad_up_rows = scatter_dp(up_away, up_kept, 96)
+    sum_own = call(add_pair, [sds(368, 768)], [chip_sum, chip_came])[0]
+    sum_near = send(sum_own, "core", 1)
+    m_came = send(m_away, "core", 1)
+    grad_rows, q_away, q_kept, h_away, h_kept = call(
+        attend_back,
+        [
+            sds(208, 768, dtype=F32), sds(4, 112, 768), sds(4, 112, 768, dtype=F32), *rows_split,
+        ],
+        [
+            sum_own, sum_near, middle, cots, branch, tokens, gain_rows, out_mine, qkv_full,
+            projected, probs, *heads, normed, targets, scale_mlp,
+        ],
+        [
+            pltpu.VMEM((896, 768), F32), pltpu.VMEM((736, 768), BF16), pltpu.VMEM((736, 192), BF16),
+            pltpu.VMEM((736, 576), BF16), pltpu.VMEM((768, 768), F32), pltpu.VMEM((192, 768), F32),
+            pltpu.VMEM((4, 208, 768), F32), pltpu.VMEM((3, 8, 768), F32),
+        ],
+        flops=4 * 736 * 768 * 576 + 4 * 736 * 768 * 192 + 10 * 6 * 368 * 368 * 64,
+    )
+    h_came = send(h_away, "core", 1)
+    stay, go = call(
+        add_pieces, [sds(416, 768, dtype=F32), sds(416, 768)], [m_kept, m_came, h_kept, h_came]
+    )
+    far_rows = send(go, "x", 1)
+    pack_rows = scatter_dp(q_away, q_kept, 112)
+    own, near, far, grad_out = call(
+        pick_grads,
+        [sds(48, 768, dtype=F32), sds(48, 768), sds(96, 768), sds(24, 768, dtype=F32)],
+        [grad_up_rows, pack_rows],
+        [pltpu.VMEM((4, 48, 768), F32)],
+    )
+    came_far = send(far, "x", 1)
+    came_near, came_near_far = send(near, "core", 1), send(came_far, "core", 1)
+    out_patches, out_special, grad_patches, grad_special = call(
+        finish_rows,
+        [
+            sds(176, 768), sds(20, 768), sds(176, 768, dtype=F32), sds(20, 768, dtype=F32),
+        ],
+        [stay, far_rows, middle, grad_rows, patches, tail, gain_rows],
+    )
+    grad_qkv, grad_up, grad_gains = call(
+        join_grads,
+        [sds(24, 2304, dtype=F32), sds(24, 3072, dtype=F32), sds(4, 24, dtype=F32)],
+        [own, came_near, came_far, came_near_far],
+        [pltpu.VMEM((4, 48, 768), F32)],
+    )
+    return (
+        out_patches, out_special, grad_patches, grad_special,
+        grad_qkv, grad_out, grad_up, grad_down, grad_gains,
+    )
+
+
 def solution(mesh):
     placed = (
         P(("dp", "blk"), None),
@@ -384,8 +1045,9 @@
         P(("dp", "blk"), None),
         P("dp", None),
     )
+    whole = dict(mesh.shape) != {"dp": 8, "blk": 4}
     return jax.shard_map(
-        on_device,
+        on_device if whole else on_device_split,
         mesh=mesh,
         in_specs=placed,
         out_specs=(

time: 1000 us -> 292 us (0.29)
  waiting for transfers between devices: 557 us -> 114 us
  blocking collectives: 146 us -> 0 us
  matrix products: 113 us -> 0 us
  Pallas kernels: 0 us -> 88.2 us
  other arithmetic: 59.3 us -> 0.11 us
  local copies, waits for them, and re-layouts: 77 us -> 22.3 us
  starting transfers between devices: 19.1 us -> 65.5 us
  between operations: 17.1 us -> 1.06 us
    reduce_scatter x4 -> x0, waiting for transfers between devices: 429 us -> none  [the longest x1 142 us: reduce_grads(): lax.psum_scatter(g_up, ('dp', 'blk'), scatter_dimension=0, tiled=True)]
    dot_general x116 -> x0, matrix products: 113 us -> none  [the longest x8 23.8 us: contract_rows(): jnp.einsum('ra,rb->ab', left_rows, right_rows, preferred_element_type=jnp...]
    all_gather x11 -> x0, blocking collectives: 106 us -> none  [the longest x1 43.3 us: fetch_weights(): lax.all_gather(gains, ('dp', 'blk'), axis=1, tiled=True)]
    pallas_call x0 -> x21, Pallas kernels: none -> 88.2 us  [call(): pl.pallas_call(kernel, out_shape=tuple(outs), in_specs=[pl.BlockSpec(memo...]
    ppermute x32 -> x54, waiting for transfers between devices: 36.8 us -> 114 us  [send(): return lax.ppermute(rows, ('dp', 'blk'), pairs)]
    all_gather x4 -> x0, waiting for transfers between devices: 60.7 us -> none  [the longest x1 48.5 us: fetch_weights(): lax.all_gather(w_down, ('dp', 'blk'), axis=0, tiled=True)]
    ppermute x32 -> x54, starting transfers between devices: 18.6 us -> 65.5 us  [send(): return lax.ppermute(rows, ('dp', 'blk'), pairs)]
    unnamed x1 -> x0, blocking collectives: 40.7 us -> none
  transfers between devices with their start and end apart: 41 -> 54, of which waited for: 23 -> 25; matrix products, arithmetic and copies ran while one was open for 17% -> 0% of each run, Pallas kernels for 0% -> 16%
where the time goes in v1:
time: 292 us; the launch traced here: 291 us
  waiting for transfers between devices  114 us (39%)
  Pallas kernels  88.2 us (30%)
  starting transfers between devices  65.5 us (22%)
  local copies, waits for them, and re-layouts  22.3 us (8%)
    ppermute x54, waiting for transfers between devices, send(): return lax.ppermute(rows, ('dp', 'blk'), pairs)  114 us
    pallas_call x21, Pallas kernels, call(): pl.pallas_call(kernel, out_shape=tuple(outs), in_specs=[pl.BlockSpec(memo...  88.2 us
    ppermute x54, starting transfers between devices, send(): return lax.ppermute(rows, ('dp', 'blk'), pairs)  65.5 us
    unnamed x94, local copies, waits for them, and re-layouts  21.9 us
  transfers between devices with their start and end apart: 54, of which 25 were waited for; matrix products, arithmetic and copies ran while one was open for 0% of the time, Pallas kernels for 16%

profile of v1, /device:TPU:0, one launch (start us, length us, event | category | flops | bytes accessed | tf_op | source)
XLA Modules:
  0.0 290.9 jit_solution(16037278184884115300)
XLA Ops:
  5.3 3.0 %collective-permute-start.1 = (bf16[352,768]{1,0:T(8,128)(2,1)S(1)}, bf16[352,768]{1,0:T(8,128)(2,1)S(1)}, u32[]{:S(2)}, u32[]{:S(2)}) collective-permute-start(bf16[352,768]{1,0:T(8,128)(2,1)S(1)} %get-tuple-element.74.rows_0), channel_id=1, source_target_pairs={{0,2},{1,3},{2,0},{3,1},{4,6},{5,7},{6,4},{7,5},{8,10},{9,11},{10,... | collective-permute-start | bytes 1622024 | tf_op jit(solution)/shard_map/ppermute | solution.py:874
  8.3 15.4 %collective-permute-done.4.far = bf16[96,768]{1,0:T(8,128)(2,1)S(1)} collective-permute-done((bf16[96,768]{1,0:T(8,128)(2,1)S(1)}, bf16[96,768]{1,0:T(8,128)(2,1)S(1)}, u32[]{:S(2)}, u32[]{:S(2)}) %collective-permute-start.4) | collective-permute-done | bytes 147488 | tf_op jit(solution)/shard_map/ppermute | solution.py:874
  26.1 1.9 collective-permute-start.6
  27.9 2.6 collective-permute-start.7
  31.9 1.5 collective-permute-start.9
  33.4 2.4 collective-permute-done.6.refs_1_
  36.5 7.4 %collective-permute-done.7.refs_2_ = bf16[128,768]{1,0:T(8,128)(2,1)S(1)} collective-permute-done((bf16[128,768]{1,0:T(8,128)(2,1)S(1)}, bf16[128,768]{1,0:T(8,128)(2,1)S(1)}, u32[]{:S(2)}, u32[]{:S(2)}) %collective-permute-start.7) | collective-permute-done | bytes 196640 | tf_op jit(solution)/shard_map/ppermute | solution.py:874
  43.9 1.5 collective-permute-start.10
  46.6 1.5 collective-permute-start.12
  48.9 2.8 collective-permute-done.10.refs_5_
  51.7 3.0 %collective-permute-start.26 = (bf16[96,768]{1,0:T(8,128)(2,1)}, bf16[96,768]{1,0:T(8,128)(2,1)}, u32[]{:S(2)}, u32[]{:S(2)}) collective-permute-start(bf16[96,768]{1,0:T(8,128)(2,1)} %refs_5_.1), channel_id=1, source_target_pairs={{0,8},{1,9},{2,10},{3,11},{4,12},{5,13},{6,14},{7,15},{8,16},{9,17... | collective-permute-start | bytes 442376 | tf_op jit(solution)/shard_map/ppermute | solution.py:874
  55.9 2.1 collective-permute-start.27
  61.9 1.5 collective-permute-start.17
  64.5 5.3 %collective-permute-start.28 = (bf16[96,768]{1,0:T(8,128)(2,1)}, bf16[96,768]{1,0:T(8,128)(2,1)S(1)}, u32[]{:S(2)}, u32[]{:S(2)}) collective-permute-start(bf16[96,768]{1,0:T(8,128)(2,1)} %refs_5_.1), channel_id=1, source_target_pairs={{0,24},{1,25},{2,26},{3,27},{4,28},{5,29},{6,30},{7,31},{8,0},{9,1... | collective-permute-start | bytes 442376 | tf_op jit(solution)/shard_map/ppermute | solution.py:874
  71.9 14.3 %attend.1 = (bf16[736,768]{1,0:T(8,128)(2,1)S(1)}, bf16[736,768]{1,0:T(8,128)(2,1)}, bf16[736,768]{1,0:T(8,128)(2,1)}, bf16[736,576]{1,0:T(8,128)(2,1)S(1)}, bf1...) custom-call(bf16[352,768]{1,0:T(8,128)(2,1)S(1)} %get-tuple-element.74.rows_0, bf16[352,768]{1,0:T(8,128)(2,1)S(1)} %copy-done.16, ...), custom_call_target="tpu_custom_call" | custom-call | flops 859176960 | bytes 9323264 | tf_op jit(solution)/shard_map/attend/pallas_call | solution.py:416
  87.9 3.3 %collective-permute-start.21 = (bf16[96,768]{1,0:T(8,128)(2,1)S(1)}, bf16[96,768]{1,0:T(8,128)(2,1)S(1)}, u32[]{:S(2)}, u32[]{:S(2)}) collective-permute-start(bf16[96,768]{1,0:T(8,128)(2,1)S(1)} %copy-done.41), channel_id=1, source_target_pairs={{0,24},{1,25},{2,26},{3,27},{4,28},{5,29},{6,30},{7,31},{8,0},{9,1... | collective-permute-start | bytes 442376 | tf_op jit(solution)/shard_map/ppermute | solution.py:874
  91.2 2.6 collective-permute-done.20.refs_9_
  93.8 1.5 collective-permute-start.22
  97.0 2.0 collective-permute-done.22.refs_11_
  98.9 1.5 collective-permute-start.23
  101.0 1.5 collective-permute-start.25
  105.7 1.5 collective-permute-start.29
  107.3 1.6 collective-permute-done.24.refs_13_
  108.9 1.5 collective-permute-start.30
  110.4 1.6 collective-permute-done.25.refs_14_
  112.1 1.5 collective-permute-start.31
  114.1 17.3 %raise_rows.1 = (bf16[736,768]{1,0:T(8,128)(2,1)S(1)}, f32[736,768]{1,0:T(8,128)}, bf16[736,768]{1,0:T(8,128)(2,1)S(1)}, bf16[736,768]{1,0:T(8,128)(2,1)S(1)}, f...) custom-call(bf16[736,192]{1,0:T(8,128)(2,1)S(1)} %get-tuple-element.81.refs_0_.head_0, ...), custom_call_target="tpu_custom_call" | custom-call | flops 1736441856 | bytes 13737984 | tf_op jit(solution)/shard_map/raise_rows/pallas_call | solution.py:416
  134.5 5.9 %lower_rows.1 = (bf16[768,768]{1,0:T(8,128)(2,1)}, bf16[736,768]{1,0:T(8,128)(2,1)S(1)}, bf16[736,768]{1,0:T(8,128)(2,1)S(1)}, bf16[368,768]{1,0:T(8,128)(2,1)S(1)}, f32[368,768]{1,0:T(8,128)S(1)}) custom-call(bf16[736,768]{1,0:T(8,128)(2,1)} %copy-done.7, f32[736,768]{1,0:T(8,128)} %get-tuple-element.88.refs_1_, ...), custom_call_target="tpu_custom_call" | custom-call | flops 1736441856 | bytes 12042240 | tf_op jit(solution)/shard_map/lower_rows/pallas_call | solution.py:416
  142.4 2.0 collective-permute-done.34.came
  144.5 1.6 collective-permute-start.35
  146.1 13.3 %collective-permute-done.35.came = bf16[368,768]{1,0:T(8,128)(2,1)S(1)} collective-permute-done((bf16[368,768]{1,0:T(8,128)(2,1)S(1)}, bf16[368,768]{1,0:T(8,128)(2,1)S(1)}, u32[]{:S(2)}, u32[]{:S(2)}) %collective-permute-start.35) | collective-permute-done | bytes 565280 | tf_op jit(solution)/shard_map/ppermute | solution.py:874
  162.2 8.2 %mlp_grads.1 = (bf16[4,96,768]{2,1,0:T(8,128)(2,1)S(1)}, f32[4,96,768]{2,1,0:T(8,128)}, bf16[4,96,768]{2,1,0:T(8,128)(2,1)S(1)}, f32[4,96,768]{2,1,0:T(8,128)}, ...) custom-call(bf16[736,768]{1,0:T(8,128)(2,1)S(1)} %copy-done.8, ...), custom_call_target="tpu_custom_call" | custom-call | flops 2604662784 | bytes 12312576 | tf_op jit(solution)/shard_map/mlp_grads/pallas_call | solution.py:416
  170.5 34.9 %attend_back.1 = (f32[208,768]{1,0:T(8,128)S(1)}, bf16[4,112,768]{2,1,0:T(8,128)(2,1)S(1)}, f32[4,112,768]{2,1,0:T(8,128)}, bf16[416,768]{1,0:T(8,128)(2,1)S(1)}, f32[416,768]{1,0:T(8,128)}) custom-call(bf16[368,768]{1,0:T(8,128)(2,1)S(1)} %add_pair.1.sum_own, bf16[368,768]{1,0:T(8,128)(2,1)S(1)} %collective-permute-done.36.sum_near, ...), custom_call_target="tpu_custom_call" | custom-call | flops 2256470016 | bytes 17366784 | tf_op jit(solution)/shard_map/attend_back/pallas_call | solution.py:416
  205.4 1.5 collective-permute-start.43
  207.9 1.5 collective-permute-start.50
  211.5 1.6 collective-permute-start.38
  213.0 23.2 %collective-permute-done.39.came = bf16[4,96,768]{2,1,0:T(8,128)(2,1)S(1)} collective-permute-done((bf16[4,96,768]{2,1,0:T(8,128)(2,1)S(1)}, bf16[4,96,768]{2,1,0:T(8,128)(2,1)S(1)}, u32[]{:S(2)}, u32[]{:S(2)}) %collective-permute-start.39) | collective-permute-done | bytes 589856 | tf_op jit(solution)/shard_map/ppermute | solution.py:874
  236.4 3.6 %collective-permute-start.40 = (bf16[96,768]{1,0:T(8,128)(2,1)S(1)}, bf16[96,768]{1,0:T(8,128)(2,1)S(1)}, u32[]{:S(2)}, u32[]{:S(2)}) collective-permute-start(bf16[96,768]{1,0:T(8,128)(2,1)S(1)} %get-tuple-element.117), channel_id=1, source_target_pairs={{0,8},{1,9},{2,10},{3,11},{4,12},{5,13},{6,14},{7,15},{8,16},{9,17... | collective-permute-start | bytes 442376 | tf_op jit(solution)/shard_map/ppermute | solution.py:874
  240.0 4.1 %collective-permute-start.41 = (bf16[96,768]{1,0:T(8,128)(2,1)S(1)}, bf16[96,768]{1,0:T(8,128)(2,1)S(1)}, u32[]{:S(2)}, u32[]{:S(2)}) collective-permute-start(bf16[96,768]{1,0:T(8,128)(2,1)S(1)} %get-tuple-element.118), channel_id=1, source_target_pairs={{0,16},{1,17},{2,18},{3,19},{4,20},{5,21},{6,22},{7,23},{8,24},{9,... | collective-permute-start | bytes 442376 | tf_op jit(solution)/shard_map/ppermute | solution.py:874
  244.3 4.1 %collective-permute-done.40.came_1 = bf16[96,768]{1,0:T(8,128)(2,1)S(1)} collective-permute-done((bf16[96,768]{1,0:T(8,128)(2,1)S(1)}, bf16[96,768]{1,0:T(8,128)(2,1)S(1)}, u32[]{:S(2)}, u32[]{:S(2)}) %collective-permute-start.40) | collective-permute-done | bytes 147488 | tf_op jit(solution)/shard_map/ppermute | solution.py:874
  248.4 6.3 %collective-permute-done.41.came_2 = bf16[96,768]{1,0:T(8,128)(2,1)S(1)} collective-permute-done((bf16[96,768]{1,0:T(8,128)(2,1)S(1)}, bf16[96,768]{1,0:T(8,128)(2,1)S(1)}, u32[]{:S(2)}, u32[]{:S(2)}) %collective-permute-start.41) | collective-permute-done | bytes 147488 | tf_op jit(solution)/shard_map/ppermute | solution.py:874
  254.7 2.6 collective-permute-start.46
  258.4 9.3 %collective-permute-done.45.came_2 = bf16[112,768]{1,0:T(8,128)(2,1)S(1)} collective-permute-done((bf16[112,768]{1,0:T(8,128)(2,1)S(1)}, bf16[112,768]{1,0:T(8,128)(2,1)S(1)}, u32[]{:S(2)}, u32[]{:S(2)}) %collective-permute-start.45) | collective-permute-done | bytes 172064 | tf_op jit(solution)/shard_map/ppermute | solution.py:874
  267.7 3.5 %collective-permute-done.46.came_3 = bf16[112,768]{1,0:T(8,128)(2,1)S(1)} collective-permute-done((bf16[112,768]{1,0:T(8,128)(2,1)S(1)}, bf16[112,768]{1,0:T(8,128)(2,1)S(1)}, u32[]{:S(2)}, u32[]{:S(2)}) %collective-permute-start.46) | collective-permute-done | bytes 172064 | tf_op jit(solution)/shard_map/ppermute | solution.py:874
  272.1 1.5 collective-permute-start.48
  274.4 3.2 %collective-permute-start.53 = (bf16[96,768]{1,0:T(8,128)(2,1)S(1)}, bf16[96,768]{1,0:T(8,128)(2,1)S(1)}, u32[]{:S(2)}, u32[]{:S(2)}) collective-permute-start(bf16[96,768]{1,0:T(8,128)(2,1)S(1)} %get-tuple-element.137), channel_id=1, source_target_pairs={{0,24},{1,25},{2,26},{3,27},{4,28},{5,29},{6,30},{7,31},{8,0},{9,1... | collective-permute-start | bytes 442376 | tf_op jit(solution)/shard_map/ppermute | solution.py:874
  277.9 4.5 %collective-permute-done.51.came_1 = bf16[96,768]{1,0:T(8,128)(2,1)S(1)} collective-permute-done((bf16[96,768]{1,0:T(8,128)(2,1)S(1)}, bf16[96,768]{1,0:T(8,128)(2,1)S(1)}, u32[]{:S(2)}, u32[]{:S(2)}) %collective-permute-start.51) | collective-permute-done | bytes 147488 | tf_op jit(solution)/shard_map/ppermute | solution.py:874
  282.4 5.2 %collective-permute-done.52.came_2 = bf16[96,768]{1,0:T(8,128)(2,1)S(1)} collective-permute-done((bf16[96,768]{1,0:T(8,128)(2,1)S(1)}, bf16[96,768]{1,0:T(8,128)(2,1)S(1)}, u32[]{:S(2)}, u32[]{:S(2)}) %collective-permute-start.52) | collective-permute-done | bytes 147488 | tf_op jit(solution)/shard_map/ppermute | solution.py:874
  (187 shorter events, 44.4 us)
Async XLA Ops:
  5.3 30.5 %collective-permute-start.1 = (bf16[352,768]{1,0:T(8,128)(2,1)S(1)}, bf16[352,768]{1,0:T(8,128)(2,1)S(1)}, u32[]{:S(2)}, u32[]{:S(2)}) collective-permute-start(bf16[352,768]{1,0:T(8,128)(2,1)S(1)} %get-tuple-element.74.rows_0), channel_id=1, source_target_pairs={{0,2},{1,3},{2,0},{3,1},{4,6},{5,7},{6,4},{7,5},{8,10},{9,11},{10,... | collective-permute-start | bytes 1622024 | tf_op jit(solution)/shard_map/ppermute | solution.py:874
  8.3 15.4 %collective-permute-start.4 = (bf16[96,768]{1,0:T(8,128)(2,1)S(1)}, bf16[96,768]{1,0:T(8,128)(2,1)S(1)}, u32[]{:S(2)}, u32[]{:S(2)}) collective-permute-start(bf16[96,768]{1,0:T(8,128)(2,1)S(1)} %get-tuple-element.77), channel_id=1, source_target_pairs={{0,2},{1,3},{2,0},{3,1},{4,6},{5,7},{6,4},{7,5},{8,10},{9,11},{10,... | collective-permute-start | bytes 442376 | tf_op jit(solution)/shard_map/ppermute | solution.py:874
  26.1 9.7 %collective-permute-start.6 = (bf16[128,768]{1,0:T(8,128)(2,1)S(1)}, bf16[128,768]{1,0:T(8,128)(2,1)S(1)}, u32[]{:S(2)}, u32[]{:S(2)}) collective-permute-start(bf16[128,768]{1,0:T(8,128)(2,1)S(1)} %get-tuple-element.78.refs_0_), channel_id=1, source_target_pairs={{0,8},{1,9},{2,10},{3,11},{4,12},{5,13},{6,14},{7,15},{8,16},{9,17... | collective-permute-start | bytes 589832 | tf_op jit(solution)/shard_map/ppermute | solution.py:874
  27.9 15.9 %collective-permute-start.7 = (bf16[128,768]{1,0:T(8,128)(2,1)S(1)}, bf16[128,768]{1,0:T(8,128)(2,1)S(1)}, u32[]{:S(2)}, u32[]{:S(2)}) collective-permute-start(bf16[128,768]{1,0:T(8,128)(2,1)S(1)} %get-tuple-element.78.refs_0_), channel_id=1, source_target_pairs={{0,16},{1,17},{2,18},{3,19},{4,20},{5,21},{6,22},{7,23},{8,24},{9,... | collective-permute-start | bytes 589832 | tf_op jit(solution)/shard_map/ppermute | solution.py:874
  30.5 14.9 %collective-permute-start.8 = (bf16[128,768]{1,0:T(8,128)(2,1)S(1)}, bf16[128,768]{1,0:T(8,128)(2,1)S(1)}, u32[]{:S(2)}, u32[]{:S(2)}) collective-permute-start(bf16[128,768]{1,0:T(8,128)(2,1)S(1)} %get-tuple-element.78.refs_0_), channel_id=1, source_target_pairs={{0,24},{1,25},{2,26},{3,27},{4,28},{5,29},{6,30},{7,31},{8,0},{9,1... | collective-permute-start | bytes 589832 | tf_op jit(solution)/shard_map/ppermute | solution.py:874
  31.9 14.0 %collective-permute-start.9 = (bf16[128,768]{1,0:T(8,128)(2,1)S(1)}, bf16[128,768]{1,0:T(8,128)(2,1)S(1)}, u32[]{:S(2)}, u32[]{:S(2)}) collective-permute-start(bf16[128,768]{1,0:T(8,128)(2,1)S(1)} %get-tuple-element.78.refs_0_), channel_id=1, source_target_pairs={{0,4},{1,5},{2,6},{3,7},{4,0},{5,1},{6,2},{7,3},{8,12},{9,13},{10,... | collective-permute-start | bytes 589832 | tf_op jit(solution)/shard_map/ppermute | solution.py:874
  35.8 27.9 %collective-permute-start = (bf16[352,768]{1,0:T(8,128)(2,1)S(1)}, bf16[352,768]{1,0:T(8,128)(2,1)S(1)}, u32[]{:S(2)}, u32[]{:S(2)}) collective-permute-start(bf16[352,768]{1,0:T(8,128)(2,1)S(1)} %get-tuple-element.74.rows_0), channel_id=1, source_target_pairs={{0,1},{1,0},{2,3},{3,2},{4,5},{5,4},{6,7},{7,6},{8,9},{9,8},{10,11... | collective-permute-start | bytes 1622024 | tf_op jit(solution)/shard_map/ppermute | solution.py:874
  35.8 34.0 %collective-permute-start.2 = (bf16[352,768]{1,0:T(8,128)(2,1)S(1)}, bf16[352,768]{1,0:T(8,128)(2,1)}, u32[]{:S(2)}, u32[]{:S(2)}) collective-permute-start(bf16[352,768]{1,0:T(8,128)(2,1)S(1)} %collective-permute-done.1.rows_2), channel_id=1, source_target_pairs={{0,1},{1,0},{2,3},{3,2},{4,5},{5,4},{6,7},{7,6},{8,9},{9,8},{10,11... | collective-permute-start | bytes 1622024 | tf_op jit(solution)/shard_map/ppermute | solution.py:874
  43.9 7.8 %collective-permute-start.10 = (bf16[128,768]{1,0:T(8,128)(2,1)S(1)}, bf16[128,768]{1,0:T(8,128)(2,1)S(1)}, u32[]{:S(2)}, u32[]{:S(2)}) collective-permute-start(bf16[128,768]{1,0:T(8,128)(2,1)S(1)} %collective-permute-done.6.refs_1_), channel_id=1, source_target_pairs={{0,4},{1,5},{2,6},{3,7},{4,0},{5,1},{6,2},{7,3},{8,12},{9,13},{10,... | collective-permute-start | bytes 589832 | tf_op jit(solution)/shard_map/ppermute | solution.py:874
  45.4 10.5 %collective-permute-start.11 = (bf16[128,768]{1,0:T(8,128)(2,1)S(1)}, bf16[128,768]{1,0:T(8,128)(2,1)S(1)}, u32[]{:S(2)}, u32[]{:S(2)}) collective-permute-start(bf16[128,768]{1,0:T(8,128)(2,1)S(1)} %collective-permute-done.7.refs_2_), channel_id=1, source_target_pairs={{0,4},{1,5},{2,6},{3,7},{4,0},{5,1},{6,2},{7,3},{8,12},{9,13},{10,... | collective-permute-start | bytes 589832 | tf_op jit(solution)/shard_map/ppermute | solution.py:874
  46.6 12.5 %collective-permute-start.12 = (bf16[128,768]{1,0:T(8,128)(2,1)S(1)}, bf16[128,768]{1,0:T(8,128)(2,1)S(1)}, u32[]{:S(2)}, u32[]{:S(2)}) collective-permute-start(bf16[128,768]{1,0:T(8,128)(2,1)S(1)} %collective-permute-done.8.refs_3_), channel_id=1, source_target_pairs={{0,4},{1,5},{2,6},{3,7},{4,0},{5,1},{6,2},{7,3},{8,12},{9,13},{10,... | collective-permute-start | bytes 589832 | tf_op jit(solution)/shard_map/ppermute | solution.py:874
  51.7 34.5 %collective-permute-start.26 = (bf16[96,768]{1,0:T(8,128)(2,1)}, bf16[96,768]{1,0:T(8,128)(2,1)}, u32[]{:S(2)}, u32[]{:S(2)}) collective-permute-start(bf16[96,768]{1,0:T(8,128)(2,1)} %refs_5_.1), channel_id=1, source_target_pairs={{0,8},{1,9},{2,10},{3,11},{4,12},{5,13},{6,14},{7,15},{8,16},{9,17... | collective-permute-start | bytes 442376 | tf_op jit(solution)/shard_map/ppermute | solution.py:874
  55.9 30.9 %collective-permute-start.27 = (bf16[96,768]{1,0:T(8,128)(2,1)}, bf16[96,768]{1,0:T(8,128)(2,1)}, u32[]{:S(2)}, u32[]{:S(2)}) collective-permute-start(bf16[96,768]{1,0:T(8,128)(2,1)} %refs_5_.1), channel_id=1, source_target_pairs={{0,16},{1,17},{2,18},{3,19},{4,20},{5,21},{6,22},{7,23},{8,24},{9,... | collective-permute-start | bytes 442376 | tf_op jit(solution)/shard_map/ppermute | solution.py:874
  61.9 25.5 %collective-permute-start.17 = (bf16[192,768]{1,0:T(8,128)(2,1)}, bf16[192,768]{1,0:T(8,128)(2,1)}, u32[]{:S(2)}, u32[]{:S(2)}) collective-permute-start(bf16[192,768]{1,0:T(8,128)(2,1)} %get-tuple-element.82.out_0), channel_id=1, source_target_pairs={{0,2},{1,3},{2,0},{3,1},{4,6},{5,7},{6,4},{7,5},{8,10},{9,11},{10,... | collective-permute-start | bytes 884744 | tf_op jit(solution)/shard_map/ppermute | solution.py:874
  64.5 22.8 %collective-permute-start.28 = (bf16[96,768]{1,0:T(8,128)(2,1)}, bf16[96,768]{1,0:T(8,128)(2,1)S(1)}, u32[]{:S(2)}, u32[]{:S(2)}) collective-permute-start(bf16[96,768]{1,0:T(8,128)(2,1)} %refs_5_.1), channel_id=1, source_target_pairs={{0,24},{1,25},{2,26},{3,27},{4,28},{5,29},{6,30},{7,31},{8,0},{9,1... | collective-permute-start | bytes 442376 | tf_op jit(solution)/shard_map/ppermute | solution.py:874
  69.8 18.1 %collective-permute-start.19 = (bf16[96,768]{1,0:T(8,128)(2,1)}, bf16[96,768]{1,0:T(8,128)(2,1)S(1)}, u32[]{:S(2)}, u32[]{:S(2)}) collective-permute-start(bf16[96,768]{1,0:T(8,128)(2,1)} %copy-done.40), channel_id=1, source_target_pairs={{0,8},{1,9},{2,10},{3,11},{4,12},{5,13},{6,14},{7,15},{8,16},{9,17... | collective-permute-start | bytes 442376 | tf_op jit(solution)/shard_map/ppermute | solution.py:874
  86.2 10.3 %collective-permute-start.14 = (bf16[736,192]{1,0:T(8,128)(2,1)S(1)}, bf16[736,192]{1,0:T(8,128)(2,1)S(1)}, u32[]{:S(2)}, u32[]{:S(2)}) collective-permute-start(bf16[736,192]{1,0:T(8,128)(2,1)S(1)} %get-tuple-element.81.refs_0_.head_0), channel_id=1, source_target_pairs={{0,2},{1,3},{2,0},{3,1},{4,6},{5,7},{6,4},{7,5},{8,10},{9,11},{10,... | collective-permute-start | bytes 847880 | tf_op jit(solution)/shard_map/ppermute | solution.py:874
  86.8 7.0 %collective-permute-start.20 = (bf16[96,768]{1,0:T(8,128)(2,1)S(1)}, bf16[96,768]{1,0:T(8,128)(2,1)S(1)}, u32[]{:S(2)}, u32[]{:S(2)}) collective-permute-start(bf16[96,768]{1,0:T(8,128)(2,1)S(1)} %copy-done.41), channel_id=1, source_target_pairs={{0,16},{1,17},{2,18},{3,19},{4,20},{5,21},{6,22},{7,23},{8,24},{9,... | collective-permute-start | bytes 442376 | tf_op jit(solution)/shard_map/ppermute | solution.py:874
  87.3 13.1 %collective-permute-start.16 = (bf16[192,768]{1,0:T(8,128)(2,1)}, bf16[192,768]{1,0:T(8,128)(2,1)S(1)}, u32[]{:S(2)}, u32[]{:S(2)}) collective-permute-start(bf16[192,768]{1,0:T(8,128)(2,1)} %get-tuple-element.82.out_0), channel_id=1, source_target_pairs={{0,1},{1,0},{2,3},{3,2},{4,5},{5,4},{6,7},{7,6},{8,9},{9,8},{10,11... | collective-permute-start | bytes 884744 | tf_op jit(solution)/shard_map/ppermute | solution.py:874
  87.4 13.6 %collective-permute-start.18 = (bf16[192,768]{1,0:T(8,128)(2,1)}, bf16[192,768]{1,0:T(8,128)(2,1)S(1)}, u32[]{:S(2)}, u32[]{:S(2)}) collective-permute-start(bf16[192,768]{1,0:T(8,128)(2,1)} %collective-permute-done.17.out_2), channel_id=1, source_target_pairs={{0,1},{1,0},{2,3},{3,2},{4,5},{5,4},{6,7},{7,6},{8,9},{9,8},{10,11... | collective-permute-start | bytes 884744 | tf_op jit(solution)/shard_map/ppermute | solution.py:874
  87.9 8.6 %collective-permute-start.21 = (bf16[96,768]{1,0:T(8,128)(2,1)S(1)}, bf16[96,768]{1,0:T(8,128)(2,1)S(1)}, u32[]{:S(2)}, u32[]{:S(2)}) collective-permute-start(bf16[96,768]{1,0:T(8,128)(2,1)S(1)} %copy-done.41), channel_id=1, source_target_pairs={{0,24},{1,25},{2,26},{3,27},{4,28},{5,29},{6,30},{7,31},{8,0},{9,1... | collective-permute-start | bytes 442376 | tf_op jit(solution)/shard_map/ppermute | solution.py:874
  96.4 17.1 %collective-permute-start.13 = (bf16[736,192]{1,0:T(8,128)(2,1)S(1)}, bf16[736,192]{1,0:T(8,128)(2,1)S(1)}, u32[]{:S(2)}, u32[]{:S(2)}) collective-permute-start(bf16[736,192]{1,0:T(8,128)(2,1)S(1)} %get-tuple-element.81.refs_0_.head_0), channel_id=1, source_target_pairs={{0,1},{1,0},{2,3},{3,2},{4,5},{5,4},{6,7},{7,6},{8,9},{9,8},{10,11... | collective-permute-start | bytes 847880 | tf_op jit(solution)/shard_map/ppermute | solution.py:874
  96.5 17.6 %collective-permute-start.15 = (bf16[736,192]{1,0:T(8,128)(2,1)S(1)}, bf16[736,192]{1,0:T(8,128)(2,1)S(1)}, u32[]{:S(2)}, u32[]{:S(2)}) collective-permute-start(bf16[736,192]{1,0:T(8,128)(2,1)S(1)} %collective-permute-done.14.refs_2_.head_2), channel_id=1, source_target_pairs={{0,1},{1,0},{2,3},{3,2},{4,5},{5,4},{6,7},{7,6},{8,9},{9,8},{10,11... | collective-permute-start | bytes 847880 | tf_op jit(solution)/shard_map/ppermute | solution.py:874
  98.9 6.8 %collective-permute-start.23 = (bf16[96,768]{1,0:T(8,128)(2,1)S(1)}, bf16[96,768]{1,0:T(8,128)(2,1)S(1)}, u32[]{:S(2)}, u32[]{:S(2)}) collective-permute-start(bf16[96,768]{1,0:T(8,128)(2,1)S(1)} %collective-permute-done.19.refs_8_), channel_id=1, source_target_pairs={{0,4},{1,5},{2,6},{3,7},{4,0},{5,1},{6,2},{7,3},{8,12},{9,13},{10,... | collective-permute-start | bytes 442376 | tf_op jit(solution)/shard_map/ppermute | solution.py:874
  100.5 8.4 %collective-permute-start.24 = (bf16[96,768]{1,0:T(8,128)(2,1)S(1)}, bf16[96,768]{1,0:T(8,128)(2,1)S(1)}, u32[]{:S(2)}, u32[]{:S(2)}) collective-permute-start(bf16[96,768]{1,0:T(8,128)(2,1)S(1)} %collective-permute-done.20.refs_9_), channel_id=1, source_target_pairs={{0,4},{1,5},{2,6},{3,7},{4,0},{5,1},{6,2},{7,3},{8,12},{9,13},{10,... | collective-permute-start | bytes 442376 | tf_op jit(solution)/shard_map/ppermute | solution.py:874
  101.0 11.1 %collective-permute-start.25 = (bf16[96,768]{1,0:T(8,128)(2,1)S(1)}, bf16[96,768]{1,0:T(8,128)(2,1)S(1)}, u32[]{:S(2)}, u32[]{:S(2)}) collective-permute-start(bf16[96,768]{1,0:T(8,128)(2,1)S(1)} %collective-permute-done.21.refs_10_), channel_id=1, source_target_pairs={{0,4},{1,5},{2,6},{3,7},{4,0},{5,1},{6,2},{7,3},{8,12},{9,13},{10,... | collective-permute-start | bytes 442376 | tf_op jit(solution)/shard_map/ppermute | solution.py:874
  105.7 28.8 %collective-permute-start.29 = (bf16[96,768]{1,0:T(8,128)(2,1)}, bf16[96,768]{1,0:T(8,128)(2,1)S(1)}, u32[]{:S(2)}, u32[]{:S(2)}) collective-permute-start(bf16[96,768]{1,0:T(8,128)(2,1)} %refs_5_.1), channel_id=1, source_target_pairs={{0,4},{1,5},{2,6},{3,7},{4,0},{5,1},{6,2},{7,3},{8,12},{9,13},{10,... | collective-permute-start | bytes 442376 | tf_op jit(solution)/shard_map/ppermute | solution.py:874
  108.9 25.6 %collective-permute-start.30 = (bf16[96,768]{1,0:T(8,128)(2,1)}, bf16[96,768]{1,0:T(8,128)(2,1)S(1)}, u32[]{:S(2)}, u32[]{:S(2)}) collective-permute-start(bf16[96,768]{1,0:T(8,128)(2,1)} %collective-permute-done.26.refs_6_), channel_id=1, source_target_pairs={{0,4},{1,5},{2,6},{3,7},{4,0},{5,1},{6,2},{7,3},{8,12},{9,13},{10,... | collective-permute-start | bytes 442376 | tf_op jit(solution)/shard_map/ppermute | solution.py:874
  112.1 22.5 %collective-permute-start.31 = (bf16[96,768]{1,0:T(8,128)(2,1)}, bf16[96,768]{1,0:T(8,128)(2,1)S(1)}, u32[]{:S(2)}, u32[]{:S(2)}) collective-permute-start(bf16[96,768]{1,0:T(8,128)(2,1)} %collective-permute-done.27.refs_7_), channel_id=1, source_target_pairs={{0,4},{1,5},{2,6},{3,7},{4,0},{5,1},{6,2},{7,3},{8,12},{9,13},{10,... | collective-permute-start | bytes 442376 | tf_op jit(solution)/shard_map/ppermute | solution.py:874
  113.6 20.9 %collective-permute-start.32 = (bf16[96,768]{1,0:T(8,128)(2,1)S(1)}, bf16[96,768]{1,0:T(8,128)(2,1)S(1)}, u32[]{:S(2)}, u32[]{:S(2)}) collective-permute-start(bf16[96,768]{1,0:T(8,128)(2,1)S(1)} %collective-permute-done.28.refs_8_), channel_id=1, source_target_pairs={{0,4},{1,5},{2,6},{3,7},{4,0},{5,1},{6,2},{7,3},{8,12},{9,13},{10,... | collective-permute-start | bytes 442376 | tf_op jit(solution)/shard_map/ppermute | solution.py:874
  144.5 14.9 %collective-permute-start.35 = (bf16[368,768]{1,0:T(8,128)(2,1)S(1)}, bf16[368,768]{1,0:T(8,128)(2,1)S(1)}, u32[]{:S(2)}, u32[]{:S(2)}) collective-permute-start(bf16[368,768]{1,0:T(8,128)(2,1)S(1)} %add_rows.1.here_rows), channel_id=1, source_target_pairs={{0,2},{1,3},{2,0},{3,1},{4,6},{5,7},{6,4},{7,5},{8,10},{9,11},{10,... | collective-permute-start | bytes 1695752 | tf_op jit(solution)/shard_map/ppermute | solution.py:874
  159.6 10.9 %collective-permute-start.36 = (bf16[368,768]{1,0:T(8,128)(2,1)S(1)}, bf16[368,768]{1,0:T(8,128)(2,1)S(1)}, u32[]{:S(2)}, u32[]{:S(2)}) collective-permute-start(bf16[368,768]{1,0:T(8,128)(2,1)S(1)} %add_pair.1.sum_own), channel_id=1, source_target_pairs={{0,1},{1,0},{2,3},{3,2},{4,5},{5,4},{6,7},{7,6},{8,9},{9,8},{10,11... | collective-permute-start | bytes 1695752 | tf_op jit(solution)/shard_map/ppermute | solution.py:874
  205.4 38.7 %collective-permute-start.43 = (bf16[4,112,768]{2,1,0:T(8,128)(2,1)S(1)}, bf16[4,112,768]{2,1,0:T(8,128)(2,1)S(1)}, u32[]{:S(2)}, u32[]{:S(2)}) collective-permute-start(bf16[4,112,768]{2,1,0:T(8,128)(2,1)S(1)} %get-tuple-element.121), channel_id=1, source_target_pairs={{0,4},{1,5},{2,6},{3,7},{4,0},{5,1},{6,2},{7,3},{8,12},{9,13},{10,... | collective-permute-start | bytes 2064392 | tf_op jit(solution)/shard_map/ppermute | solution.py:874
  207.4 28.8 %collective-permute-start.39 = (bf16[4,96,768]{2,1,0:T(8,128)(2,1)S(1)}, bf16[4,96,768]{2,1,0:T(8,128)(2,1)S(1)}, u32[]{:S(2)}, u32[]{:S(2)}) collective-permute-start(bf16[4,96,768]{2,1,0:T(8,128)(2,1)S(1)} %get-tuple-element.115), channel_id=1, source_target_pairs={{0,4},{1,5},{2,6},{3,7},{4,0},{5,1},{6,2},{7,3},{8,12},{9,13},{10,... | collective-permute-start | bytes 1769480 | tf_op jit(solution)/shard_map/ppermute | solution.py:874
  207.9 65.6 %collective-permute-start.50 = (bf16[4,96,768]{2,1,0:T(8,128)(2,1)S(1)}, bf16[4,96,768]{2,1,0:T(8,128)(2,1)S(1)}, u32[]{:S(2)}, u32[]{:S(2)}) collective-permute-start(bf16[4,96,768]{2,1,0:T(8,128)(2,1)S(1)} %get-tuple-element.133), channel_id=1, source_target_pairs={{0,4},{1,5},{2,6},{3,7},{4,0},{5,1},{6,2},{7,3},{8,12},{9,13},{10,... | collective-permute-start | bytes 1769480 | tf_op jit(solution)/shard_map/ppermute | solution.py:874
  211.5 78.0 %collective-permute-start.38 = (bf16[416,768]{1,0:T(8,128)(2,1)S(1)}, bf16[416,768]{1,0:T(8,128)(2,1)S(1)}, u32[]{:S(2)}, u32[]{:S(2)}) collective-permute-start(bf16[416,768]{1,0:T(8,128)(2,1)S(1)} %get-tuple-element.108), channel_id=1, source_target_pairs={{0,2},{1,3},{2,0},{3,1},{4,6},{5,7},{6,4},{7,5},{8,10},{9,11},{10,... | collective-permute-start | bytes 1916936 | tf_op jit(solution)/shard_map/ppermute | solution.py:874
  236.4 12.0 %collective-permute-start.40 = (bf16[96,768]{1,0:T(8,128)(2,1)S(1)}, bf16[96,768]{1,0:T(8,128)(2,1)S(1)}, u32[]{:S(2)}, u32[]{:S(2)}) collective-permute-start(bf16[96,768]{1,0:T(8,128)(2,1)S(1)} %get-tuple-element.117), channel_id=1, source_target_pairs={{0,8},{1,9},{2,10},{3,11},{4,12},{5,13},{6,14},{7,15},{8,16},{9,17... | collective-permute-start | bytes 442376 | tf_op jit(solution)/shard_map/ppermute | solution.py:874
  240.0 14.7 %collective-permute-start.41 = (bf16[96,768]{1,0:T(8,128)(2,1)S(1)}, bf16[96,768]{1,0:T(8,128)(2,1)S(1)}, u32[]{:S(2)}, u32[]{:S(2)}) collective-permute-start(bf16[96,768]{1,0:T(8,128)(2,1)S(1)} %get-tuple-element.118), channel_id=1, source_target_pairs={{0,16},{1,17},{2,18},{3,19},{4,20},{5,21},{6,22},{7,23},{8,24},{9,... | collective-permute-start | bytes 442376 | tf_op jit(solution)/shard_map/ppermute | solution.py:874
  244.1 10.6 %collective-permute-start.42 = (bf16[96,768]{1,0:T(8,128)(2,1)S(1)}, bf16[96,768]{1,0:T(8,128)(2,1)S(1)}, u32[]{:S(2)}, u32[]{:S(2)}) collective-permute-start(bf16[96,768]{1,0:T(8,128)(2,1)S(1)} %get-tuple-element.119), channel_id=1, source_target_pairs={{0,24},{1,25},{2,26},{3,27},{4,28},{5,29},{6,30},{7,31},{8,0},{9,1... | collective-permute-start | bytes 442376 | tf_op jit(solution)/shard_map/ppermute | solution.py:874
  248.4 10.0 %collective-permute-start.44 = (bf16[112,768]{1,0:T(8,128)(2,1)S(1)}, bf16[112,768]{1,0:T(8,128)(2,1)S(1)}, u32[]{:S(2)}, u32[]{:S(2)}) collective-permute-start(bf16[112,768]{1,0:T(8,128)(2,1)S(1)} %get-tuple-element.123), channel_id=1, source_target_pairs={{0,8},{1,9},{2,10},{3,11},{4,12},{5,13},{6,14},{7,15},{8,16},{9,17... | collective-permute-start | bytes 516104 | tf_op jit(solution)/shard_map/ppermute | solution.py:874
  254.7 13.0 %collective-permute-start.45 = (bf16[112,768]{1,0:T(8,128)(2,1)S(1)}, bf16[112,768]{1,0:T(8,128)(2,1)S(1)}, u32[]{:S(2)}, u32[]{:S(2)}) collective-permute-start(bf16[112,768]{1,0:T(8,128)(2,1)S(1)} %get-tuple-element.124), channel_id=1, source_target_pairs={{0,16},{1,17},{2,18},{3,19},{4,20},{5,21},{6,22},{7,23},{8,24},{9,... | collective-permute-start | bytes 516104 | tf_op jit(solution)/shard_map/ppermute | solution.py:874
  254.7 16.6 %collective-permute-start.46 = (bf16[112,768]{1,0:T(8,128)(2,1)S(1)}, bf16[112,768]{1,0:T(8,128)(2,1)S(1)}, u32[]{:S(2)}, u32[]{:S(2)}) collective-permute-start(bf16[112,768]{1,0:T(8,128)(2,1)S(1)} %get-tuple-element.125), channel_id=1, source_target_pairs={{0,24},{1,25},{2,26},{3,27},{4,28},{5,29},{6,30},{7,31},{8,0},{9,1... | collective-permute-start | bytes 516104 | tf_op jit(solution)/shard_map/ppermute | solution.py:874
  272.1 5.8 %collective-permute-start.48 = (bf16[96,768]{1,0:T(8,128)(2,1)S(1)}, bf16[96,768]{1,0:T(8,128)(2,1)S(1)}, u32[]{:S(2)}, u32[]{:S(2)}) collective-permute-start(bf16[96,768]{1,0:T(8,128)(2,1)S(1)} %get-tuple-element.128), channel_id=1, source_target_pairs={{0,2},{1,3},{2,0},{3,1},{4,6},{5,7},{6,4},{7,5},{8,10},{9,11},{10,... | collective-permute-start | bytes 442376 | tf_op jit(solution)/shard_map/ppermute | solution.py:874
  273.7 8.7 %collective-permute-start.51 = (bf16[96,768]{1,0:T(8,128)(2,1)S(1)}, bf16[96,768]{1,0:T(8,128)(2,1)S(1)}, u32[]{:S(2)}, u32[]{:S(2)}) collective-permute-start(bf16[96,768]{1,0:T(8,128)(2,1)S(1)} %get-tuple-element.135), channel_id=1, source_target_pairs={{0,8},{1,9},{2,10},{3,11},{4,12},{5,13},{6,14},{7,15},{8,16},{9,17... | collective-permute-start | bytes 442376 | tf_op jit(solution)/shard_map/ppermute | solution.py:874
  274.4 13.2 %collective-permute-start.52 = (bf16[96,768]{1,0:T(8,128)(2,1)S(1)}, bf16[96,768]{1,0:T(8,128)(2,1)S(1)}, u32[]{:S(2)}, u32[]{:S(2)}) collective-permute-start(bf16[96,768]{1,0:T(8,128)(2,1)S(1)} %get-tuple-element.136), channel_id=1, source_target_pairs={{0,16},{1,17},{2,18},{3,19},{4,20},{5,21},{6,22},{7,23},{8,24},{9,... | collective-permute-start | bytes 442376 | tf_op jit(solution)/shard_map/ppermute | solution.py:874
  274.4 13.2 %collective-permute-start.53 = (bf16[96,768]{1,0:T(8,128)(2,1)S(1)}, bf16[96,768]{1,0:T(8,128)(2,1)S(1)}, u32[]{:S(2)}, u32[]{:S(2)}) collective-permute-start(bf16[96,768]{1,0:T(8,128)(2,1)S(1)} %get-tuple-element.137), channel_id=1, source_target_pairs={{0,24},{1,25},{2,26},{3,27},{4,28},{5,29},{6,30},{7,31},{8,0},{9,1... | collective-permute-start | bytes 442376 | tf_op jit(solution)/shard_map/ppermute | solution.py:874
  277.9 10.5 %collective-permute-start.49 = (bf16[96,768]{1,0:T(8,128)(2,1)S(1)}, bf16[96,768]{1,0:T(8,128)(2,1)S(1)}, u32[]{:S(2)}, u32[]{:S(2)}) collective-permute-start(bf16[96,768]{1,0:T(8,128)(2,1)S(1)} %collective-permute-done.48.far), channel_id=1, source_target_pairs={{0,1},{1,0},{2,3},{3,2},{4,5},{5,4},{6,7},{7,6},{8,9},{9,8},{10,11... | collective-permute-start | bytes 442376 | tf_op jit(solution)/shard_map/ppermute | solution.py:874
  282.4 6.0 %collective-permute-start.47 = (bf16[48,768]{1,0:T(8,128)(2,1)S(1)}, bf16[48,768]{1,0:T(8,128)(2,1)S(1)}, u32[]{:S(2)}, u32[]{:S(2)}) collective-permute-start(bf16[48,768]{1,0:T(8,128)(2,1)S(1)} %get-tuple-element.127), channel_id=1, source_target_pairs={{0,1},{1,0},{2,3},{3,2},{4,5},{5,4},{6,7},{7,6},{8,9},{9,8},{10,11... | collective-permute-start | bytes 221192 | tf_op jit(solution)/shard_map/ppermute | solution.py:874
  (53 other events, 565.6 us)

commit v2 on v1

--- a/solution.py
+++ b/solution.py
@@ -403,15 +403,15 @@
     return source_z * 2 + source_y
 
 
-def loop_rows(count, block, body):
-    def step(i, carry):
-        body(pl.ds(pl.multiple_of(i * block, block), block))
-        return carry
-
-    lax.fori_loop(0, count // block, step, 0)
-
-
-def call(kernel, outs, ins, scratch=(), flops=0, limit=48):
+def row_blocks(block):
+    return [slice(first, first + block) for first in range(0, 736, block)]
+
+
+def fold(rows):
+    return rows.reshape(rows.shape[0] // 8, 8, rows.shape[1]).sum(0)
+
+
+def call(kernel, outs, ins, scratch=(), us=1, limit=28):
     moved = sum(o.size * o.dtype.itemsize for o in outs) + sum(i.size * i.dtype.itemsize for i in ins)
     return pl.pallas_call(
         kernel,
@@ -420,7 +420,7 @@
         out_specs=tuple(pl.BlockSpec(memory_space=pltpu.VMEM) for _ in outs),
         scratch_shapes=list(scratch),
         compiler_params=pltpu.CompilerParams(vmem_limit_bytes=limit * 2**20),
-        cost_estimate=pl.CostEstimate(flops=flops, bytes_accessed=moved, transcendentals=0),
+        cost_estimate=pl.CostEstimate(flops=us * 10**9, bytes_accessed=moved, transcendentals=0),
         name=kernel.__name__,
     )(*ins)
 
@@ -453,6 +453,7 @@
 
 def join_pieces(own, near, far, near_far, w_out, pack, up_chunk, pack_f, up_f):
     place = here()[0]
+    pack_f[96:112, :] = jnp.zeros((16, 768), F32)
     pieces = (
         own[...].astype(F32),
         near[...].astype(F32),
@@ -464,8 +465,8 @@
         at = pl.ds(pl.multiple_of(source * 24, 8), 24)
         up_f[at, :] = piece[0:24]
         pack_f[at, 0:576] = piece[24:48, 0:576]
-        pack_f[pl.ds(pl.multiple_of(96 + source * 8, 8), 8), 0:576] = jnp.zeros((8, 576), F32)
-        pack_f[pl.ds(pl.multiple_of(96 + source * 8, 8), 8), 576:768] = piece[24:32, 576:768]
+        lanes = pl.ds(pl.multiple_of(source * 128, 128), 128)
+        pack_f[96:104, lanes] = piece[24:32, 576:704]
     out = w_out[...].astype(F32)
     for i in range(4):
         pack_f[i * 24 : i * 24 + 24, 576:768] = out[:, i * 192 : i * 192 + 192]
@@ -479,18 +480,18 @@
     for slot, chunk in enumerate(chunks):
         d = chunk_index(slot, z, y)
         w_qkv[pl.ds(pl.multiple_of(d * 96, 96), 96), :] = chunk[0:96, 0:576]
-        tail = chunk[0:128, 576:768].astype(F32)
+        tail = chunk[0:96, 576:768].astype(F32)
         for i in range(4):
             out_f[pl.ds(pl.multiple_of(d * 24, 8), 24), i * 192 : i * 192 + 192] = tail[
                 i * 24 : i * 24 + 24
             ]
-        gain_f[d] = tail[96:128, :]
+        gain_f[d] = chunk[96:112, :].astype(F32)
     w_out[...] = out_f[...].astype(BF16)
     gain_rows[...] = jnp.zeros_like(gain_rows)
     for d in range(8):
         for b in range(4):
             at = (d * 4 + b) * 24
-            gain_rows[0:4, at : at + 24] = gain_f[d, b * 8 : b * 8 + 4, 0:24]
+            gain_rows[0:4, at : at + 24] = gain_f[d, 0:4, b * 128 : b * 128 + 24]
 
 
 def normalise(rows):
@@ -513,31 +514,29 @@
 
 
 def attend(
-    rows_0, rows_1, rows_2, rows_3, tail, cot_tail, ids_col, ids_row, w_qkv, gain_rows,
-    tokens, cots, normed, projected, probs, attended, rows_f,
+    rows_0, rows_1, rows_2, rows_3, tail, ids_col, ids_row, w_qkv, gain_rows,
+    tokens, normed, projected, probs, attended, rows_f,
 ):
-    place_rows(rows_f, (rows_0, rows_1, rows_2, rows_3), cot_tail, 176)
-    cots[...] = rows_f[...].astype(BF16)
     place_rows(rows_f, (rows_0, rows_1, rows_2, rows_3), tail, 0)
     gain = gain_rows[0:1, :]
 
-    def norm_block(at):
+    for at in row_blocks(32):
         rows = rows_f[at, :]
         tokens[at, :] = rows.astype(BF16)
         normed[at, :] = (normalise(rows)[0] * gain).astype(BF16)
-
-    loop_rows(736, 16, norm_block)
     for m in range(MICRO):
         at = slice(m * 368, m * 368 + 368)
-        qkv = mm(normed[at, :], w_qkv[...]).astype(BF16)
+        qkv = mm(normed[at, :], w_qkv[...])
+        qkv = jnp.concatenate([qkv[:, 0:192] * SCORE_SCALE, qkv[:, 192:576]], -1).astype(BF16)
         projected[at, :] = qkv
         same = ids_col[at, :] == ids_row[m : m + 1, :]
+        bias = jnp.where(same, 0.0, MASKED)
         heads = []
         for h in range(3):
             q = qkv[:, h * 64 : h * 64 + 64]
             k = qkv[:, 192 + h * 64 : 192 + h * 64 + 64]
             v = qkv[:, 384 + h * 64 : 384 + h * 64 + 64]
-            scores = jnp.where(same, mm_nt(q, k) * SCORE_SCALE, MASKED)
+            scores = mm_nt(q, k) + bias
             weights = jnp.exp(scores - jnp.max(scores, -1, keepdims=True))
             weights = weights * (1.0 / jnp.sum(weights, -1, keepdims=True))
             weights = weights.astype(BF16)
@@ -546,7 +545,10 @@
         attended[at, :] = jnp.concatenate(heads, -1).astype(BF16)
 
 
-def order_out(out_0, out_1, out_2, out_3, ordered, mine, out_f):
+def order_out(
+    out_0, out_1, out_2, out_3, rows_0, rows_1, rows_2, rows_3, cot_tail, gain_rows,
+    ordered, mine, cots, grad_mlp, out_f,
+):
     place = here()[0]
     for k, part in enumerate((out_0, out_1, out_2, out_3)):
         source = place ^ k
@@ -556,6 +558,12 @@
             out_f[pl.ds(at, 24), :] = rows[d * 24 : d * 24 + 24]
     ordered[...] = out_f[...].astype(BF16)
     mine[...] = out_f[pl.ds(pl.multiple_of(place * 192, 8), 192), :].astype(BF16)
+    place_rows(out_f, (rows_0, rows_1, rows_2, rows_3), cot_tail, 176)
+    gain = gain_rows[3:4, :]
+    for at in row_blocks(32):
+        rows = out_f[at, :]
+        cots[at, :] = rows.astype(BF16)
+        grad_mlp[at, :] = (gain * rows).astype(BF16)
 
 
 def raise_rows(*refs):
@@ -576,40 +584,30 @@
         up_f[at, :] = total
     gain_s, gain_n = gain_rows[1:2, :], gain_rows[2:3, :]
 
-    def norm_block(at):
+    for at in row_blocks(32):
         a = up_f[at, :]
         branch[at, :] = a.astype(BF16)
         rows = tokens[at, :].astype(F32) + gain_s * a
         middle[at, :] = rows
         normed[at, :] = (normalise(rows)[0] * gain_n).astype(BF16)
-
-    loop_rows(736, 16, norm_block)
     for m in range(MICRO):
         at = slice(m * 368, m * 368 + 368)
         up_f[at, :] = mm(normed[at, :], w_up[...])
 
-    def gelu_block(at):
+    for at in row_blocks(32):
         u = up_f[at, :]
         half = 0.5 + 0.5 * lax.erf(u * 0.7071067811865476)
         active[at, :] = (u * half).astype(BF16)
         slope[at, :] = half + u * (0.3989422804014327 * jnp.exp(-0.5 * u * u))
 
-    loop_rows(736, 16, gelu_block)
-
 
 def lower_rows(*refs):
-    (active, slope, cots, gain_rows, w_up), chunks = refs[:5], refs[5:13]
-    w_down, grad_mlp, grad_hidden, away, kept, work = refs[13:]
+    (slope, grad_mlp, w_up), chunks = refs[:3], refs[3:11]
+    w_down, grad_hidden, away, kept, work = refs[11:]
     _, _, core, z, y = here()
     for slot, chunk in enumerate(chunks):
         d = chunk_index(slot, z, y)
         w_down[pl.ds(pl.multiple_of(d * 96, 96), 96), :] = chunk[...]
-    gain = gain_rows[3:4, :]
-
-    def scale_block(at):
-        grad_mlp[at, :] = (gain * cots[at, :].astype(F32)).astype(BF16)
-
-    loop_rows(736, 16, scale_block)
     for m in range(MICRO):
         at = slice(m * 368, m * 368 + 368)
         grad = mm_nt(grad_mlp[at, :], w_down[...])
@@ -637,8 +635,8 @@
     for zz in range(4):
         other = pl.ds(pl.multiple_of((zz * 2 + 1 - y) * rows, 8), rows)
         ours = pl.ds(pl.multiple_of((zz * 2 + y) * rows, 8), rows)
-        away[zz] = grad_f[other, :].astype(BF16)
-        kept[zz] = grad_f[ours, :]
+        away[zz] = grad_f[other, 0 : away.shape[2]].astype(BF16)
+        kept[zz] = grad_f[ours, 0 : away.shape[2]]
 
 
 def mlp_grads(
@@ -653,12 +651,10 @@
     for m in range(MICRO):
         at = slice(m * 368, m * 368 + 368)
         work[at, :] = mm(active[at, :], w_down[...])
-    scale_grad[...] = jnp.zeros_like(scale_grad)
-
-    def sum_block(at):
-        scale_grad[...] += (cots[at, :].astype(F32) * work[at, :]).reshape(2, 8, 768).sum(0)
-
-    loop_rows(736, 16, sum_block)
+    total = jnp.zeros((8, 768), F32)
+    for at in row_blocks(32):
+        total = total + fold(cots[at, :].astype(F32) * work[at, :])
+    scale_grad[...] = total
     cut_rows(work, pieces)
     split_rows(pieces, place, rows_away, rows_kept)
 
@@ -671,11 +667,11 @@
     total[...] = (here_rows[...].astype(F32) + came[...].astype(F32)).astype(BF16)
 
 
-def attend_back(
-    sum_own, sum_near, middle, cots, branch, tokens, gain_rows, w_mine, w_qkv, projected, probs,
-    head_0, head_1, head_2, head_3, normed, targets, scale_grad_mlp,
-    grad_rows, away, kept, rows_away, rows_kept,
-    work, grad_branch, grad_heads, grad_qkv, grad_mid, extra, pieces, scale_grad,
+def branch_back(
+    sum_own, sum_near, middle, cots, branch, gain_rows, w_mine, probs, normed, targets,
+    scale_grad_mlp, head_0, head_1, head_2, head_3,
+    grad_rows, grad_heads, grad_v, away, kept,
+    work, grad_branch, grad_mid, extra,
 ):
     place, _, core, _, y = here()
     for m in range(MICRO):
@@ -689,23 +685,18 @@
         def _():
             work[at, :] = sum_near[...].astype(F32)
 
-    scale_grad[...] = jnp.zeros_like(scale_grad)
     gain_s, gain_n = gain_rows[1:2, :], gain_rows[2:3, :]
-
-    def norm_block(at):
+    scale_sum = jnp.zeros((8, 768), F32)
+    for at in row_blocks(32):
         unit, scale = normalise(middle[at, :])
-        grad = work[at, :]
-        pulled = grad * gain_n
+        pulled = work[at, :] * gain_n
         pulled = pulled - jnp.mean(pulled, -1, keepdims=True) - unit * jnp.mean(
             pulled * unit, -1, keepdims=True
         )
         through = cots[at, :].astype(F32) + scale * pulled
         grad_mid[at, :] = through
         grad_branch[at, :] = (gain_s * through).astype(BF16)
-        scale_grad[1] += (through * branch[at, :].astype(F32)).reshape(2, 8, 768).sum(0)
-        scale_grad[2] += (grad * unit).reshape(2, 8, 768).sum(0)
-
-    loop_rows(736, 16, norm_block)
+        scale_sum = scale_sum + fold(through * branch[at, :].astype(F32))
     for m in range(MICRO):
         for part, first in ((0, place * 88), (88, 352)):
             rows = 88 if part == 0 else 16
@@ -714,37 +705,11 @@
             ]
     for m in range(MICRO):
         at = slice(m * 368, m * 368 + 368)
-        grad_heads[at, :] = mm_nt(grad_branch[at, :], w_mine[...]).astype(BF16)
-        qkv = projected[at, :]
-        g_heads = grad_heads[at, :]
-        grads = [[], [], []]
-        for h in range(3):
-            q = qkv[:, h * 64 : h * 64 + 64]
-            k = qkv[:, 192 + h * 64 : 192 + h * 64 + 64]
-            v = qkv[:, 384 + h * 64 : 384 + h * 64 + 64]
-            g = g_heads[:, h * 64 : h * 64 + 64]
-            weights = probs[m * 3 + h]
-            grad_prob = mm_nt(g, v)
-            wide = weights.astype(F32)
-            moved = wide * grad_prob
-            delta = jnp.sum(moved, -1, keepdims=True)
-            grad_score = (moved - wide * delta).astype(BF16)
-            grads[0].append(mm(grad_score, k) * SCORE_SCALE)
-            grads[1].append(mm_tn(grad_score, q) * SCORE_SCALE)
-            grads[2].append(mm_tn(weights, g))
-        grad_qkv[at, :] = jnp.concatenate(grads[0] + grads[1] + grads[2], -1).astype(BF16)
-    for m in range(MICRO):
-        at = slice(m * 368, m * 368 + 368)
-        work[at, :] = mm_nt(grad_qkv[at, :], w_qkv[...])
-
-    def sum_block(at):
-        unit, _ = normalise(tokens[at, :].astype(F32))
-        scale_grad[0] += (work[at, :] * unit).reshape(2, 8, 768).sum(0)
-
-    loop_rows(736, 16, sum_block)
-    cut_rows(work, pieces)
-    split_rows(pieces, place, rows_away, rows_kept)
-    grad_mid[0:768, 0:576] = mm_tn(normed[...], grad_qkv[...])
+        heads = mm_nt(grad_branch[at, :], w_mine[...]).astype(BF16)
+        grad_heads[at, :] = heads
+        terms = [mm_tn(probs[m * 3 + h], heads[:, h * 64 : h * 64 + 64]) for h in range(3)]
+        grad_v[at, :] = jnp.concatenate(terms, -1).astype(BF16)
+    grad_mid[0:768, 0:192] = mm_tn(normed[...], grad_v[...])
     chosen = None
     for k, part in enumerate((head_0, head_1, head_2, head_3)):
         source = place ^ k
@@ -753,23 +718,53 @@
         term = mm(part[...], pick)
         chosen = term if chosen is None else chosen + term
     extra[...] = mm_tn(chosen.astype(BF16), grad_branch[...])
-    rows = [
-        jnp.sum(scale_grad[0], 0, keepdims=True),
-        0.25 * jnp.sum(scale_grad[1], 0, keepdims=True),
-        0.25 * jnp.sum(scale_grad[2], 0, keepdims=True),
+    scale_rows = (
+        0.25 * jnp.sum(scale_sum, 0, keepdims=True),
         jnp.sum(scale_grad_mlp[...], 0, keepdims=True),
-    ]
+    )
     for d in range(8):
         base = d * 112
-        work[base : base + 96, 0:576] = grad_mid[d * 96 : d * 96 + 96, 0:576]
+        work[base : base + 96, 0:192] = grad_mid[d * 96 : d * 96 + 96, 0:192]
         for i in range(4):
-            work[base + i * 24 : base + i * 24 + 24, 576:768] = extra[
+            work[base + i * 24 : base + i * 24 + 24, 192:384] = extra[
                 d * 24 : d * 24 + 24, i * 192 : i * 192 + 192
             ]
-        work[base + 96 : base + 112, :] = jnp.zeros((16, 768), F32)
-        for i in range(4):
-            work[base + 96 + i : base + 97 + i, 0:96] = rows[i][:, d * 96 : d * 96 + 96]
+        work[base + 96 : base + 112, 0:384] = jnp.zeros((16, 384), F32)
+        for i in range(2):
+            work[base + 96 + i : base + 97 + i, 0:96] = scale_rows[i][:, d * 96 : d * 96 + 96]
     halve(work, y, away, kept, 112)
+
+
+def score_back(probs, projected, grad_heads, normed, grad_qk, away, kept, work):
+    _, _, _, _, y = here()
+    for m in range(MICRO):
+        at = slice(m * 368, m * 368 + 368)
+        qkv = projected[at, :]
+        g_heads = grad_heads[at, :]
+        grads = [[], []]
+        for h in range(3):
+            q = qkv[:, h * 64 : h * 64 + 64]
+            k = qkv[:, 192 + h * 64 : 192 + h * 64 + 64]
+            v = qkv[:, 384 + h * 64 : 384 + h * 64 + 64]
+            grad_prob = mm_nt(g_heads[:, h * 64 : h * 64 + 64], v)
+            wide = probs[m * 3 + h].astype(F32)
+            moved = wide * grad_prob
+            delta = jnp.sum(moved, -1, keepdims=True)
+            grad_score = (moved - wide * delta).astype(BF16)
+            grads[0].append(mm(grad_score, k) * SCORE_SCALE)
+            grads[1].append(mm_tn(grad_score, q))
+        grad_qk[at, :] = jnp.concatenate(grads[0] + grads[1], -1).astype(BF16)
+    work[...] = mm_tn(normed[...], grad_qk[...])
+    halve(work, y, away, kept, 96)
+
+
+def project_back(grad_qk, grad_v, w_qkv, rows_away, rows_kept, work, pieces):
+    place = here()[0]
+    for m in range(MICRO):
+        at = slice(m * 368, m * 368 + 368)
+        work[at, :] = mm_nt(grad_qk[at, :], w_qkv[:, 0:384]) + mm_nt(grad_v[at, :], w_qkv[:, 384:576])
+    cut_rows(work, pieces)
+    split_rows(pieces, place, rows_away, rows_kept)
 
 
 def sum_y(kept, came, own, send_1, send_2, send_3):
@@ -826,27 +821,38 @@
     out_special[...] = jnp.concatenate([part[0:10] for part in out_tails], 0).astype(BF16)
 
 
-def pick_grads(up, pack, own, near, far, grad_out, held):
+def pick_grads(up, first, second, own, near, far, grad_out, held):
     place = here()[0]
     for b in range(4):
-        held[b, 0:24, :] = up[b * 24 : b * 24 + 24, :]
-        held[b, 24:48, 0:576] = pack[b * 24 : b * 24 + 24, 0:576]
+        at = slice(b * 24, b * 24 + 24)
+        held[b, 0:24, :] = up[at, :]
+        held[b, 24:48, 0:384] = second[at, :]
+        held[b, 24:48, 384:576] = first[at, 0:192]
         held[b, 24:48, 576:768] = jnp.zeros((24, 192), F32)
-        held[b, 24:28, 576:600] = pack[96:100, b * 24 : b * 24 + 24]
-        grad_out[:, b * 192 : b * 192 + 192] = pack[b * 24 : b * 24 + 24, 576:768]
+        held[b, 24:26, 576:600] = first[96:98, at]
+        grad_out[:, b * 192 : b * 192 + 192] = first[at, 192:384]
     own[...] = held[place]
     near[...] = held[place ^ 1].astype(BF16)
     far[0:48, :] = held[place ^ 2].astype(BF16)
     far[48:96, :] = held[place ^ 3].astype(BF16)
 
 
-def join_grads(own, near, far, near_far, grad_qkv, grad_up, grad_gains, held):
+def as_row(column):
+    count = column.shape[0]
+    square = lax.broadcasted_iota(jnp.int32, (count, count), 0)
+    across = lax.broadcasted_iota(jnp.int32, (count, count), 1)
+    return jnp.sum(jnp.where(square == across, column, 0.0), 0, keepdims=True)
+
+
+def join_grads(
+    own, near, far, near_far, w_qkv, w_up, gains, grad_qkv, grad_up, grad_gains, held
+):
     place = here()[0]
     held[place] = own[...]
     held[place ^ 1] = near[...].astype(F32)
     held[place ^ 2] = far[0:48, :].astype(F32)
     held[place ^ 3] = near_far[48:96, :].astype(F32)
-    gains = None
+    scales = None
     for b in range(4):
         for d in range(8):
             at = d * 384 + b * 96
@@ -854,9 +860,15 @@
         for part in range(3):
             at = part * 768 + b * 192
             grad_qkv[:, at : at + 192] = held[b, 24:48, part * 192 : part * 192 + 192]
-        term = held[b, 24:28, 576:600]
-        gains = term if gains is None else gains + term
-    grad_gains[...] = gains
+        term = held[b, 24:26, 576:600]
+        scales = term if scales is None else scales + term
+    norm_1 = as_row(jnp.sum(w_qkv[...].astype(F32) * grad_qkv[...], -1, keepdims=True))
+    norm_2 = as_row(jnp.sum(w_up[...].astype(F32) * grad_up[...], -1, keepdims=True))
+    gain = gains[...].astype(F32)
+    grad_gains[0:1, :] = norm_1 / gain[0:1, :]
+    grad_gains[1:2, :] = scales[0:1, :]
+    grad_gains[2:3, :] = norm_2 / gain[2:3, :]
+    grad_gains[3:4, :] = scales[1:2, :]
 
 
 def send(rows, axis, step):
@@ -885,11 +897,14 @@
     return [rows, near, far, send(far, "core", 1)]
 
 
-def scatter_dp(away, kept, rows):
+def scatter_dp(away, kept):
+    rows, width = away.shape[1:]
     came = send(away, "y", 1)
-    own, *parts = call(sum_y, [sds(rows, 768, dtype=F32)] + [sds(rows, 768)] * 3, [kept, came])
+    own, *parts = call(
+        sum_y, [sds(rows, width, dtype=F32)] + [sds(rows, width)] * 3, [kept, came]
+    )
     came = [send(part, "z", k) for k, part in zip((1, 2, 3), parts)]
-    return call(sum_z, [sds(rows, 768, dtype=F32)], [own, *came])[0]
+    return call(sum_z, [sds(rows, width, dtype=F32)], [own, *came])[0]
 
 
 def pad_tail(rows):
@@ -918,13 +933,14 @@
     )
     came_far = send(far, "x", 1)
     came_near, came_near_far = send(near, "core", 1), send(came_far, "core", 1)
+    rows, _ = lax.optimization_barrier((rows, came_far))
     row_parts = gather_blk(rows)
     down_chunks = gather_dp(w_down)
     pack, up_chunk = call(
         join_pieces,
-        [sds(128, 768), sds(96, 768)],
+        [sds(112, 768), sds(96, 768)],
         [own, came_near, came_far, came_near_far, w_out],
-        [pltpu.VMEM((128, 768), F32), pltpu.VMEM((96, 768), F32)],
+        [pltpu.VMEM((112, 768), F32), pltpu.VMEM((96, 768), F32)],
     )
     pack_chunks = gather_dp(pack)
     up_chunks = gather_dp(up_chunk)
@@ -932,22 +948,23 @@
         open_pack,
         [sds(768, 576), sds(192, 768), sds(8, 768, dtype=F32)],
         pack_chunks,
-        [pltpu.VMEM((192, 768), F32), pltpu.VMEM((8, 32, 192), F32)],
+        [pltpu.VMEM((192, 768), F32), pltpu.VMEM((8, 16, 768), F32)],
     )
     out_parts = gather_blk(out_part)
-    tokens, cots, normed, projected, probs, attended = call(
+    tokens, normed, projected, probs, attended = call(
         attend,
-        [
-            sds(736, 768), sds(736, 768), sds(736, 768), sds(736, 576),
-            sds(6, 368, 368), sds(736, 192),
-        ],
-        [*row_parts, tail, cot_tail, ids_col, ids_row, qkv_full, gain_rows],
+        [sds(736, 768), sds(736, 768), sds(736, 576), sds(6, 368, 368), sds(736, 192)],
+        [*row_parts, tail, ids_col, ids_row, qkv_full, gain_rows],
         [pltpu.VMEM((736, 768), F32)],
-        flops=2 * 736 * 768 * 576 + 4 * 6 * 368 * 368 * 64,
+        us=10,
     )
     heads = gather_blk(attended)
-    out_full, out_mine = call(
-        order_out, [sds(768, 768), sds(192, 768)], out_parts, [pltpu.VMEM((768, 768), F32)]
+    out_full, out_mine, cots, grad_mlp = call(
+        order_out,
+        [sds(768, 768), sds(192, 768), sds(736, 768), sds(736, 768)],
+        [*out_parts, *row_parts, cot_tail, gain_rows],
+        [pltpu.VMEM((768, 768), F32)],
+        us=3,
     )
     branch, middle, normed_mlp, active, slope, up_full = call(
         raise_rows,
@@ -957,14 +974,14 @@
         ],
         [*heads, out_full, tokens, gain_rows, *up_chunks],
         [pltpu.VMEM((736, 768), F32)],
-        flops=4 * 736 * 768 * 768,
-    )
-    down_full, grad_mlp, grad_hidden, sum_away, sum_kept = call(
+        us=10,
+    )
+    down_full, grad_hidden, sum_away, sum_kept = call(
         lower_rows,
-        [sds(768, 768), sds(736, 768), sds(736, 768), sds(368, 768), sds(368, 768, dtype=F32)],
-        [active, slope, cots, gain_rows, up_full, *down_chunks],
+        [sds(768, 768), sds(736, 768), sds(368, 768), sds(368, 768, dtype=F32)],
+        [slope, grad_mlp, up_full, *down_chunks],
         [pltpu.VMEM((2, 368, 768), F32)],
-        flops=4 * 736 * 768 * 768,
+        us=4,
     )
     sum_came = send(sum_away, "core", 1)
     chip_sum = call(add_rows, [sds(368, 768)], [sum_kept, sum_came])[0]
@@ -976,39 +993,54 @@
         [*half, *half, *rows_split, sds(8, 768, dtype=F32)],
         [active, normed_mlp, grad_mlp, grad_hidden, down_full, cots],
         [pltpu.VMEM((768, 768), F32), pltpu.VMEM((4, 208, 768), F32)],
-        flops=6 * 736 * 768 * 768,
-    )
-    grad_down = scatter_dp(down_away, down_kept, 96)
-    grad_up_rows = scatter_dp(up_away, up_kept, 96)
+        us=5,
+    )
+    grad_down = scatter_dp(down_away, down_kept)
+    grad_up_rows = scatter_dp(up_away, up_kept)
     sum_own = call(add_pair, [sds(368, 768)], [chip_sum, chip_came])[0]
     sum_near = send(sum_own, "core", 1)
     m_came = send(m_away, "core", 1)
-    grad_rows, q_away, q_kept, h_away, h_kept = call(
-        attend_back,
+    grad_rows, grad_heads, grad_v, a_away, a_kept = call(
+        branch_back,
         [
-            sds(208, 768, dtype=F32), sds(4, 112, 768), sds(4, 112, 768, dtype=F32), *rows_split,
+            sds(208, 768, dtype=F32), sds(736, 192), sds(736, 192),
+            sds(4, 112, 384), sds(4, 112, 384, dtype=F32),
         ],
         [
-            sum_own, sum_near, middle, cots, branch, tokens, gain_rows, out_mine, qkv_full,
-            projected, probs, *heads, normed, targets, scale_mlp,
+            sum_own, sum_near, middle, cots, branch, gain_rows, out_mine, probs, normed, targets,
+            scale_mlp, *heads,
         ],
         [
-            pltpu.VMEM((896, 768), F32), pltpu.VMEM((736, 768), BF16), pltpu.VMEM((736, 192), BF16),
-            pltpu.VMEM((736, 576), BF16), pltpu.VMEM((768, 768), F32), pltpu.VMEM((192, 768), F32),
-            pltpu.VMEM((4, 208, 768), F32), pltpu.VMEM((3, 8, 768), F32),
+            pltpu.VMEM((896, 768), F32), pltpu.VMEM((736, 768), BF16),
+            pltpu.VMEM((768, 768), F32), pltpu.VMEM((192, 768), F32),
         ],
-        flops=4 * 736 * 768 * 576 + 4 * 736 * 768 * 192 + 10 * 6 * 368 * 368 * 64,
+        us=10,
+    )
+    first_rows = scatter_dp(a_away, a_kept)
+    grad_qk, b_away, b_kept = call(
+        score_back,
+        [sds(736, 384), sds(4, 96, 384), sds(4, 96, 384, dtype=F32)],
+        [probs, projected, grad_heads, normed],
+        [pltpu.VMEM((768, 384), F32)],
+        us=10,
+    )
+    second_rows = scatter_dp(b_away, b_kept)
+    h_away, h_kept = call(
+        project_back,
+        rows_split,
+        [grad_qk, grad_v, qkv_full],
+        [pltpu.VMEM((736, 768), F32), pltpu.VMEM((4, 208, 768), F32)],
+        us=3,
     )
     h_came = send(h_away, "core", 1)
     stay, go = call(
         add_pieces, [sds(416, 768, dtype=F32), sds(416, 768)], [m_kept, m_came, h_kept, h_came]
     )
     far_rows = send(go, "x", 1)
-    pack_rows = scatter_dp(q_away, q_kept, 112)
     own, near, far, grad_out = call(
         pick_grads,
         [sds(48, 768, dtype=F32), sds(48, 768), sds(96, 768), sds(24, 768, dtype=F32)],
-        [grad_up_rows, pack_rows],
+        [grad_up_rows, first_rows, second_rows],
         [pltpu.VMEM((4, 48, 768), F32)],
     )
     came_far = send(far, "x", 1)
@@ -1023,7 +1055,7 @@
     grad_qkv, grad_up, grad_gains = call(
         join_grads,
         [sds(24, 2304, dtype=F32), sds(24, 3072, dtype=F32), sds(4, 24, dtype=F32)],
-        [own, came_near, came_far, came_near_far],
+        [own, came_near, came_far, came_near_far, w_qkv, w_up, gains],
         [pltpu.VMEM((4, 48, 768), F32)],
     )
     return (

time: 292 us -> 201 us (0.69)
  Pallas kernels: 88.2 us -> 35.3 us
  waiting for transfers between devices: 114 us -> 67.9 us
  starting transfers between devices: 65.5 us -> 74.7 us
    pallas_call x21 -> x25, Pallas kernels: 88.2 us -> 35.3 us  [call(): pl.pallas_call(kernel, out_shape=tuple(outs), in_specs=[pl.BlockSpec(memo...]
    ppermute x54 -> x58, waiting for transfers between devices: 114 us -> 67.9 us  [send(): return lax.ppermute(rows, ('dp', 'blk'), pairs)]
    ppermute x54 -> x58, starting transfers between devices: 65.5 us -> 74.7 us  [send(): return lax.ppermute(rows, ('dp', 'blk'), pairs)]
    unnamed x94 -> x114, local copies, waits for them, and re-layouts: 21.9 us -> 20.8 us
  transfers between devices with their start and end apart: 54 -> 58, of which waited for: 25 -> 25; matrix products, arithmetic and copies ran while one was open for 0% -> 0% of each run, Pallas kernels for 16% -> 15%
where the time goes in v2:
time: 201 us
  starting transfers between devices  74.7 us (37%)
  waiting for transfers between devices  67.9 us (34%)
  Pallas kernels  35.3 us (18%)
  local copies, waits for them, and re-layouts  21.2 us (11%)
    ppermute x58, starting transfers between devices, send(): return lax.ppermute(rows, ('dp', 'blk'), pairs)  74.7 us
    ppermute x58, waiting for transfers between devices, send(): return lax.ppermute(rows, ('dp', 'blk'), pairs)  67.9 us
    pallas_call x25, Pallas kernels, call(): pl.pallas_call(kernel, out_shape=tuple(outs), in_specs=[pl.BlockSpec(memo...  35.3 us
    unnamed x114, local copies, waits for them, and re-layouts  20.8 us
  transfers between devices with their start and end apart: 58, of which 25 were waited for; matrix products, arithmetic and copies ran while one was open for 0% of the time, Pallas kernels for 15%

profile of v2, /device:TPU:0, one launch (start us, length us, event | category | flops | bytes accessed | tf_op | source)
XLA Modules:
  0.0 200.6 jit_solution(6677000421663975303)
XLA Ops:
  5.3 3.0 %collective-permute-start = (bf16[96,768]{1,0:T(8,128)(2,1)S(1)}, bf16[96,768]{1,0:T(8,128)(2,1)S(1)}, u32[]{:S(2)}, u32[]{:S(2)}) collective-permute-start(bf16[96,768]{1,0:T(8,128)(2,1)S(1)} %get-tuple-element.85), channel_id=1, source_target_pairs={{0,2},{1,3},{2,0},{3,1},{4,6},{5,7},{6,4},{7,5},{8,10},{9,11},{10,... | collective-permute-start | bytes 442376 | tf_op jit(solution)/shard_map/ppermute | solution.py:886
  8.3 3.9 %collective-permute-done.far = bf16[96,768]{1,0:T(8,128)(2,1)S(1)} collective-permute-done((bf16[96,768]{1,0:T(8,128)(2,1)S(1)}, bf16[96,768]{1,0:T(8,128)(2,1)S(1)}, u32[]{:S(2)}, u32[]{:S(2)}) %collective-permute-start) | collective-permute-done | bytes 147488 | tf_op jit(solution)/shard_map/ppermute | solution.py:886
  12.1 1.7 collective-permute-start.2
  16.1 1.6 collective-permute-start.6
  17.7 2.6 %collective-permute-start.7 = (bf16[112,768]{1,0:T(8,128)(2,1)S(1)}, bf16[112,768]{1,0:T(8,128)(2,1)S(1)}, u32[]{:S(2)}, u32[]{:S(2)}) collective-permute-start(bf16[112,768]{1,0:T(8,128)(2,1)S(1)} %get-tuple-element.89.refs_0_), channel_id=1, source_target_pairs={{0,16},{1,17},{2,18},{3,19},{4,20},{5,21},{6,22},{7,23},{8,24},{9,... | collective-permute-start | bytes 516104 | tf_op jit(solution)/shard_map/ppermute | solution.py:886
  21.7 1.5 collective-permute-start.9
  23.2 2.1 %collective-permute-done.6.refs_1_ = bf16[112,768]{1,0:T(8,128)(2,1)S(1)} collective-permute-done((bf16[112,768]{1,0:T(8,128)(2,1)S(1)}, bf16[112,768]{1,0:T(8,128)(2,1)S(1)}, u32[]{:S(2)}, u32[]{:S(2)}) %collective-permute-start.6) | collective-permute-done | bytes 172064 | tf_op jit(solution)/shard_map/ppermute | solution.py:886
  25.2 1.5 collective-permute-start.10
  26.8 5.3 %collective-permute-done.7.refs_2_ = bf16[112,768]{1,0:T(8,128)(2,1)S(1)} collective-permute-done((bf16[112,768]{1,0:T(8,128)(2,1)S(1)}, bf16[112,768]{1,0:T(8,128)(2,1)S(1)}, u32[]{:S(2)}, u32[]{:S(2)}) %collective-permute-start.7) | collective-permute-done | bytes 172064 | tf_op jit(solution)/shard_map/ppermute | solution.py:886
  32.0 1.5 collective-permute-start.11
  35.5 3.7 %collective-permute-start.26 = (bf16[96,768]{1,0:T(8,128)(2,1)}, bf16[96,768]{1,0:T(8,128)(2,1)}, u32[]{:S(2)}, u32[]{:S(2)}) collective-permute-start(bf16[96,768]{1,0:T(8,128)(2,1)} %refs_3_.1), channel_id=1, source_target_pairs={{0,8},{1,9},{2,10},{3,11},{4,12},{5,13},{6,14},{7,15},{8,16},{9,17... | collective-permute-start | bytes 442376 | tf_op jit(solution)/shard_map/ppermute | solution.py:886
  39.4 3.1 %collective-permute-start.27 = (bf16[96,768]{1,0:T(8,128)(2,1)}, bf16[96,768]{1,0:T(8,128)(2,1)}, u32[]{:S(2)}, u32[]{:S(2)}) collective-permute-start(bf16[96,768]{1,0:T(8,128)(2,1)} %refs_3_.1), channel_id=1, source_target_pairs={{0,16},{1,17},{2,18},{3,19},{4,20},{5,21},{6,22},{7,23},{8,24},{9,... | collective-permute-start | bytes 442376 | tf_op jit(solution)/shard_map/ppermute | solution.py:886
  46.6 4.4 %collective-permute-start.28 = (bf16[96,768]{1,0:T(8,128)(2,1)}, bf16[96,768]{1,0:T(8,128)(2,1)S(1)}, u32[]{:S(2)}, u32[]{:S(2)}) collective-permute-start(bf16[96,768]{1,0:T(8,128)(2,1)} %refs_3_.1), channel_id=1, source_target_pairs={{0,24},{1,25},{2,26},{3,27},{4,28},{5,29},{6,30},{7,31},{8,0},{9,1... | collective-permute-start | bytes 442376 | tf_op jit(solution)/shard_map/ppermute | solution.py:886
  51.6 1.9 collective-permute-start.20
  55.3 3.8 %attend.1 = (bf16[736,768]{1,0:T(8,128)(2,1)S(1)}, bf16[736,768]{1,0:T(8,128)(2,1)S(1)}, bf16[736,576]{1,0:T(8,128)(2,1)S(1)}, bf16[6,368,368]{2,1,0:T(8,128)(2,1)S(1)}, bf16[736,192]{1,0:T(8,128)(2,1)S(1)}) custom-call(bf16[352,768]{1,0:T(8,128)(2,1)S(1)} %get-tuple-element.86.rows_0, bf16[352,768]{1,0:T(8,128)(2,1)S(1)} %collective-permute-done.1.rows_1, ...), custom_call_target="tpu_custom_call" | custom-call | flops 10000000000 | bytes 8143616 | tf_op jit(solution)/shard_map/attend/pallas_call | solution.py:416
  63.7 4.4 %collective-permute-start.21 = (bf16[96,768]{1,0:T(8,128)(2,1)S(1)}, bf16[96,768]{1,0:T(8,128)(2,1)S(1)}, u32[]{:S(2)}, u32[]{:S(2)}) collective-permute-start(bf16[96,768]{1,0:T(8,128)(2,1)S(1)} %copy-done.13), channel_id=1, source_target_pairs={{0,24},{1,25},{2,26},{3,27},{4,28},{5,29},{6,30},{7,31},{8,0},{9,1... | collective-permute-start | bytes 442376 | tf_op jit(solution)/shard_map/ppermute | solution.py:886
  68.1 1.5 collective-permute-start.22
  71.1 2.9 %collective-permute-done.14.refs_2_.head_2 = bf16[736,192]{1,0:T(8,128)(2,1)S(1)} collective-permute-done((bf16[736,192]{1,0:T(8,128)(2,1)S(1)}, bf16[736,192]{1,0:T(8,128)(2,1)S(1)}, u32[]{:S(2)}, u32[]{:S(2)}) %collective-permute-start.14) | collective-permute-done | bytes 282656 | tf_op jit(solution)/shard_map/ppermute | solution.py:886
  74.1 1.6 collective-permute-start.23
  76.2 1.5 collective-permute-start.25
  77.8 1.9 order_out.1
  81.0 1.5 collective-permute-start.29
  82.6 1.6 collective-permute-done.24.refs_13_
  84.2 1.5 collective-permute-start.30
  85.7 1.6 collective-permute-done.25.refs_14_
  87.4 1.5 collective-permute-start.31
  90.4 4.4 %raise_rows.1 = (bf16[736,768]{1,0:T(8,128)(2,1)S(1)}, f32[736,768]{1,0:T(8,128)S(1)}, bf16[736,768]{1,0:T(8,128)(2,1)S(1)}, bf16[736,768]{1,0:T(8,128)(2,1)S(1)...) custom-call(bf16[736,192]{1,0:T(8,128)(2,1)S(1)} %get-tuple-element.92.refs_0_.head_0, ...), custom_call_target="tpu_custom_call" | custom-call | flops 10000000000 | bytes 13737984 | tf_op jit(solution)/shard_map/raise_rows/pallas_call | solution.py:416
  96.8 2.8 %collective-permute-done.32.refs_10_ = bf16[96,768]{1,0:T(8,128)(2,1)S(1)} collective-permute-done((bf16[96,768]{1,0:T(8,128)(2,1)S(1)}, bf16[96,768]{1,0:T(8,128)(2,1)S(1)}, u32[]{:S(2)}, u32[]{:S(2)}) %collective-permute-start.32) | collective-permute-done | bytes 147488 | tf_op jit(solution)/shard_map/ppermute | solution.py:886
  99.6 3.6 %lower_rows.1 = (bf16[768,768]{1,0:T(8,128)(2,1)S(1)}, bf16[736,768]{1,0:T(8,128)(2,1)S(1)}, bf16[368,768]{1,0:T(8,128)(2,1)S(1)}, f32[368,768]{1,0:T(8,128)S(1)}) custom-call(f32[736,768]{1,0:T(8,128)S(1)} %get-tuple-element.100.refs_0_, bf16[736,768]{1,0:T(8,128)(2,1)S(1)} %get-tuple-element.99.refs_1_.grad_mlp, ...), custom_call_target="tpu_custom_call" | custom-call | flops 4000000000 | bytes 9756672 | tf_op jit(solution)/shard_map/lower_rows/pallas_call | solution.py:416
  104.3 2.0 collective-permute-done.34.came
  106.9 14.4 %collective-permute-done.35.came = bf16[368,768]{1,0:T(8,128)(2,1)S(1)} collective-permute-done((bf16[368,768]{1,0:T(8,128)(2,1)S(1)}, bf16[368,768]{1,0:T(8,128)(2,1)S(1)}, u32[]{:S(2)}, u32[]{:S(2)}) %collective-permute-start.35) | collective-permute-done | bytes 565280 | tf_op jit(solution)/shard_map/ppermute | solution.py:886
  125.3 3.9 %mlp_grads.1 = (bf16[4,96,768]{2,1,0:T(8,128)(2,1)S(1)}, f32[4,96,768]{2,1,0:T(8,128)S(1)}, bf16[4,96,768]{2,1,0:T(8,128)(2,1)S(1)}, f32[4,96,768]{2,1,0:T(8,128...) custom-call(bf16[736,768]{1,0:T(8,128)(2,1)S(1)} %copy-done.41, ...), custom_call_target="tpu_custom_call" | custom-call | flops 5000000000 | bytes 12312576 | tf_op jit(solution)/shard_map/mlp_grads/pallas_call | solution.py:416
  129.3 1.6 collective-permute-start.39
  131.1 5.6 %branch_back.1 = (f32[208,768]{1,0:T(8,128)S(1)}, bf16[736,192]{1,0:T(8,128)(2,1)S(1)}, bf16[736,192]{1,0:T(8,128)(2,1)S(1)}, bf16[4,112,384]{2,1,0:T(8,128)(2,1)S(1)}, f32[4,112,384]{2,1,0:T(8,128)S(1)}) custom-call(bf16[368,768]{1,0:T(8,128)(2,1)S(1)} %add_pair.1.sum_own, bf16[368,768]{1,0:T(8,128)(2,1)S(1)} %collective-permute-done.36.sum_near, ...), custom_call_target="tpu_custom_call" | custom-call | flops 10000000000 | bytes 12119808 | tf_op jit(solution)/shard_map/branch_back/pallas_call | solution.py:416
  136.7 4.3 %score_back.1 = (bf16[736,384]{1,0:T(8,128)(2,1)S(1)}, bf16[4,96,384]{2,1,0:T(8,128)(2,1)S(1)}, f32[4,96,384]{2,1,0:T(8,128)S(1)}) custom-call(bf16[6,368,368]{2,1,0:T(8,128)(2,1)S(1)} %copy-done.45, bf16[736,576]{1,0:T(8,128)(2,1)S(1)} %copy-done.53, bf16[736,192]{1,0:T(8,128)(2,1)S(1)} %get-tuple-element.116.grad_heads, bf16[736,768]{1,0:T(8,128)(2,1)S(1)} %copy-done.47), custom_call_target="tpu_custom_call" | custom-call | flops 10000000000 | bytes 5336064 | tf_op jit(solution)/shard_map/score_back/pallas_call | solution.py:416
  142.7 2.4 %collective-permute-done.39.came = bf16[4,96,768]{2,1,0:T(8,128)(2,1)S(1)} collective-permute-done((bf16[4,96,768]{2,1,0:T(8,128)(2,1)S(1)}, bf16[4,96,768]{2,1,0:T(8,128)(2,1)S(1)}, u32[]{:S(2)}, u32[]{:S(2)}) %collective-permute-start.39) | collective-permute-done | bytes 589856 | tf_op jit(solution)/shard_map/ppermute | solution.py:886
  145.2 2.5 %collective-permute-start.40 = (bf16[96,768]{1,0:T(8,128)(2,1)S(1)}, bf16[96,768]{1,0:T(8,128)(2,1)S(1)}, u32[]{:S(2)}, u32[]{:S(2)}) collective-permute-start(bf16[96,768]{1,0:T(8,128)(2,1)S(1)} %get-tuple-element.131), channel_id=1, source_target_pairs={{0,8},{1,9},{2,10},{3,11},{4,12},{5,13},{6,14},{7,15},{8,16},{9,17... | collective-permute-start | bytes 442376 | tf_op jit(solution)/shard_map/ppermute | solution.py:886
  147.7 2.1 %collective-permute-start.41 = (bf16[96,768]{1,0:T(8,128)(2,1)S(1)}, bf16[96,768]{1,0:T(8,128)(2,1)S(1)}, u32[]{:S(2)}, u32[]{:S(2)}) collective-permute-start(bf16[96,768]{1,0:T(8,128)(2,1)S(1)} %get-tuple-element.132), channel_id=1, source_target_pairs={{0,16},{1,17},{2,18},{3,19},{4,20},{5,21},{6,22},{7,23},{8,24},{9,... | collective-permute-start | bytes 442376 | tf_op jit(solution)/shard_map/ppermute | solution.py:886
  151.3 2.7 %collective-permute-done.40.came_1 = bf16[96,768]{1,0:T(8,128)(2,1)S(1)} collective-permute-done((bf16[96,768]{1,0:T(8,128)(2,1)S(1)}, bf16[96,768]{1,0:T(8,128)(2,1)S(1)}, u32[]{:S(2)}, u32[]{:S(2)}) %collective-permute-start.40) | collective-permute-done | bytes 147488 | tf_op jit(solution)/shard_map/ppermute | solution.py:886
  155.6 3.7 %collective-permute-done.41.came_2 = bf16[96,768]{1,0:T(8,128)(2,1)S(1)} collective-permute-done((bf16[96,768]{1,0:T(8,128)(2,1)S(1)}, bf16[96,768]{1,0:T(8,128)(2,1)S(1)}, u32[]{:S(2)}, u32[]{:S(2)}) %collective-permute-start.41) | collective-permute-done | bytes 147488 | tf_op jit(solution)/shard_map/ppermute | solution.py:886
  160.1 5.0 %collective-permute-done.42.came_3 = bf16[96,768]{1,0:T(8,128)(2,1)S(1)} collective-permute-done((bf16[96,768]{1,0:T(8,128)(2,1)S(1)}, bf16[96,768]{1,0:T(8,128)(2,1)S(1)}, u32[]{:S(2)}, u32[]{:S(2)}) %collective-permute-start.42) | collective-permute-done | bytes 147488 | tf_op jit(solution)/shard_map/ppermute | solution.py:886
  166.8 2.6 %collective-permute-start.49 = (bf16[96,384]{1,0:T(8,128)(2,1)S(1)}, bf16[96,384]{1,0:T(8,128)(2,1)S(1)}, u32[]{:S(2)}, u32[]{:S(2)}) collective-permute-start(bf16[96,384]{1,0:T(8,128)(2,1)S(1)} %get-tuple-element.144), channel_id=1, source_target_pairs={{0,16},{1,17},{2,18},{3,19},{4,20},{5,21},{6,22},{7,23},{8,24},{9,... | collective-permute-start | bytes 221192 | tf_op jit(solution)/shard_map/ppermute | solution.py:886
  171.8 1.5 collective-permute-done.48.came_1
  173.4 2.6 %collective-permute-done.49.came_2 = bf16[96,384]{1,0:T(8,128)(2,1)S(1)} collective-permute-done((bf16[96,384]{1,0:T(8,128)(2,1)S(1)}, bf16[96,384]{1,0:T(8,128)(2,1)S(1)}, u32[]{:S(2)}, u32[]{:S(2)}) %collective-permute-start.49) | collective-permute-done | bytes 73760 | tf_op jit(solution)/shard_map/ppermute | solution.py:886
  176.0 4.8 %collective-permute-start.46 = (bf16[112,384]{1,0:T(8,128)(2,1)S(1)}, bf16[112,384]{1,0:T(8,128)(2,1)S(1)}, u32[]{:S(2)}, u32[]{:S(2)}) collective-permute-start(bf16[112,384]{1,0:T(8,128)(2,1)S(1)} %get-tuple-element.139), channel_id=1, source_target_pairs={{0,24},{1,25},{2,26},{3,27},{4,28},{5,29},{6,30},{7,31},{8,0},{9,1... | collective-permute-start | bytes 258056 | tf_op jit(solution)/shard_map/ppermute | solution.py:886
  185.1 4.3 %collective-permute-start.56 = (bf16[96,768]{1,0:T(8,128)(2,1)S(1)}, bf16[96,768]{1,0:T(8,128)(2,1)S(1)}, u32[]{:S(2)}, u32[]{:S(2)}) collective-permute-start(bf16[96,768]{1,0:T(8,128)(2,1)S(1)} %get-tuple-element.156), channel_id=1, source_target_pairs={{0,16},{1,17},{2,18},{3,19},{4,20},{5,21},{6,22},{7,23},{8,24},{9,... | collective-permute-start | bytes 442376 | tf_op jit(solution)/shard_map/ppermute | solution.py:886
  189.4 4.5 %collective-permute-done.52.far = bf16[96,768]{1,0:T(8,128)(2,1)S(1)} collective-permute-done((bf16[96,768]{1,0:T(8,128)(2,1)S(1)}, bf16[96,768]{1,0:T(8,128)(2,1)S(1)}, u32[]{:S(2)}, u32[]{:S(2)}) %collective-permute-start.52) | collective-permute-done | bytes 147488 | tf_op jit(solution)/shard_map/ppermute | solution.py:886
  194.4 2.6 %collective-permute-done.56.came_2 = bf16[96,768]{1,0:T(8,128)(2,1)S(1)} collective-permute-done((bf16[96,768]{1,0:T(8,128)(2,1)S(1)}, bf16[96,768]{1,0:T(8,128)(2,1)S(1)}, u32[]{:S(2)}, u32[]{:S(2)}) %collective-permute-start.56) | collective-permute-done | bytes 147488 | tf_op jit(solution)/shard_map/ppermute | solution.py:886
  (219 shorter events, 52.3 us)
Async XLA Ops:
  12.1 22.2 %collective-permute-start.2 = (bf16[352,768]{1,0:T(8,128)(2,1)S(1)}, bf16[352,768]{1,0:T(8,128)(2,1)S(1)}, u32[]{:S(2)}, u32[]{:S(2)}) collective-permute-start(bf16[352,768]{1,0:T(8,128)(2,1)S(1)} %get-tuple-element.86.rows_0), channel_id=1, source_target_pairs={{0,2},{1,3},{2,0},{3,1},{4,6},{5,7},{6,4},{7,5},{8,10},{9,11},{10,... | collective-permute-start | bytes 1622024 | tf_op jit(solution)/shard_map/ppermute | solution.py:886
  16.1 9.1 %collective-permute-start.6 = (bf16[112,768]{1,0:T(8,128)(2,1)S(1)}, bf16[112,768]{1,0:T(8,128)(2,1)S(1)}, u32[]{:S(2)}, u32[]{:S(2)}) collective-permute-start(bf16[112,768]{1,0:T(8,128)(2,1)S(1)} %get-tuple-element.89.refs_0_), channel_id=1, source_target_pairs={{0,8},{1,9},{2,10},{3,11},{4,12},{5,13},{6,14},{7,15},{8,16},{9,17... | collective-permute-start | bytes 516104 | tf_op jit(solution)/shard_map/ppermute | solution.py:886
  17.7 14.3 %collective-permute-start.7 = (bf16[112,768]{1,0:T(8,128)(2,1)S(1)}, bf16[112,768]{1,0:T(8,128)(2,1)S(1)}, u32[]{:S(2)}, u32[]{:S(2)}) collective-permute-start(bf16[112,768]{1,0:T(8,128)(2,1)S(1)} %get-tuple-element.89.refs_0_), channel_id=1, source_target_pairs={{0,16},{1,17},{2,18},{3,19},{4,20},{5,21},{6,22},{7,23},{8,24},{9,... | collective-permute-start | bytes 516104 | tf_op jit(solution)/shard_map/ppermute | solution.py:886
  20.3 13.3 %collective-permute-start.8 = (bf16[112,768]{1,0:T(8,128)(2,1)S(1)}, bf16[112,768]{1,0:T(8,128)(2,1)S(1)}, u32[]{:S(2)}, u32[]{:S(2)}) collective-permute-start(bf16[112,768]{1,0:T(8,128)(2,1)S(1)} %get-tuple-element.89.refs_0_), channel_id=1, source_target_pairs={{0,24},{1,25},{2,26},{3,27},{4,28},{5,29},{6,30},{7,31},{8,0},{9,1... | collective-permute-start | bytes 516104 | tf_op jit(solution)/shard_map/ppermute | solution.py:886
  21.7 12.6 %collective-permute-start.9 = (bf16[112,768]{1,0:T(8,128)(2,1)S(1)}, bf16[112,768]{1,0:T(8,128)(2,1)S(1)}, u32[]{:S(2)}, u32[]{:S(2)}) collective-permute-start(bf16[112,768]{1,0:T(8,128)(2,1)S(1)} %get-tuple-element.89.refs_0_), channel_id=1, source_target_pairs={{0,4},{1,5},{2,6},{3,7},{4,0},{5,1},{6,2},{7,3},{8,12},{9,13},{10,... | collective-permute-start | bytes 516104 | tf_op jit(solution)/shard_map/ppermute | solution.py:886
  25.2 9.6 %collective-permute-start.10 = (bf16[112,768]{1,0:T(8,128)(2,1)S(1)}, bf16[112,768]{1,0:T(8,128)(2,1)S(1)}, u32[]{:S(2)}, u32[]{:S(2)}) collective-permute-start(bf16[112,768]{1,0:T(8,128)(2,1)S(1)} %collective-permute-done.6.refs_1_), channel_id=1, source_target_pairs={{0,4},{1,5},{2,6},{3,7},{4,0},{5,1},{6,2},{7,3},{8,12},{9,13},{10,... | collective-permute-start | bytes 516104 | tf_op jit(solution)/shard_map/ppermute | solution.py:886
  32.0 7.4 %collective-permute-start.11 = (bf16[112,768]{1,0:T(8,128)(2,1)S(1)}, bf16[112,768]{1,0:T(8,128)(2,1)}, u32[]{:S(2)}, u32[]{:S(2)}) collective-permute-start(bf16[112,768]{1,0:T(8,128)(2,1)S(1)} %collective-permute-done.7.refs_2_), channel_id=1, source_target_pairs={{0,4},{1,5},{2,6},{3,7},{4,0},{5,1},{6,2},{7,3},{8,12},{9,13},{10,... | collective-permute-start | bytes 516104 | tf_op jit(solution)/shard_map/ppermute | solution.py:886
  33.6 8.9 %collective-permute-start.12 = (bf16[112,768]{1,0:T(8,128)(2,1)S(1)}, bf16[112,768]{1,0:T(8,128)(2,1)}, u32[]{:S(2)}, u32[]{:S(2)}) collective-permute-start(bf16[112,768]{1,0:T(8,128)(2,1)S(1)} %collective-permute-done.8.refs_3_), channel_id=1, source_target_pairs={{0,4},{1,5},{2,6},{3,7},{4,0},{5,1},{6,2},{7,3},{8,12},{9,13},{10,... | collective-permute-start | bytes 516104 | tf_op jit(solution)/shard_map/ppermute | solution.py:886
  34.3 17.4 %collective-permute-start.1 = (bf16[352,768]{1,0:T(8,128)(2,1)S(1)}, bf16[352,768]{1,0:T(8,128)(2,1)S(1)}, u32[]{:S(2)}, u32[]{:S(2)}) collective-permute-start(bf16[352,768]{1,0:T(8,128)(2,1)S(1)} %get-tuple-element.86.rows_0), channel_id=1, source_target_pairs={{0,1},{1,0},{2,3},{3,2},{4,5},{5,4},{6,7},{7,6},{8,9},{9,8},{10,11... | collective-permute-start | bytes 1622024 | tf_op jit(solution)/shard_map/ppermute | solution.py:886
  34.3 19.2 %collective-permute-start.3 = (bf16[352,768]{1,0:T(8,128)(2,1)S(1)}, bf16[352,768]{1,0:T(8,128)(2,1)S(1)}, u32[]{:S(2)}, u32[]{:S(2)}) collective-permute-start(bf16[352,768]{1,0:T(8,128)(2,1)S(1)} %collective-permute-done.2.rows_2), channel_id=1, source_target_pairs={{0,1},{1,0},{2,3},{3,2},{4,5},{5,4},{6,7},{7,6},{8,9},{9,8},{10,11... | collective-permute-start | bytes 1622024 | tf_op jit(solution)/shard_map/ppermute | solution.py:886
  35.5 11.1 %collective-permute-start.26 = (bf16[96,768]{1,0:T(8,128)(2,1)}, bf16[96,768]{1,0:T(8,128)(2,1)}, u32[]{:S(2)}, u32[]{:S(2)}) collective-permute-start(bf16[96,768]{1,0:T(8,128)(2,1)} %refs_3_.1), channel_id=1, source_target_pairs={{0,8},{1,9},{2,10},{3,11},{4,12},{5,13},{6,14},{7,15},{8,16},{9,17... | collective-permute-start | bytes 442376 | tf_op jit(solution)/shard_map/ppermute | solution.py:886
  39.4 12.2 %collective-permute-start.27 = (bf16[96,768]{1,0:T(8,128)(2,1)}, bf16[96,768]{1,0:T(8,128)(2,1)}, u32[]{:S(2)}, u32[]{:S(2)}) collective-permute-start(bf16[96,768]{1,0:T(8,128)(2,1)} %refs_3_.1), channel_id=1, source_target_pairs={{0,16},{1,17},{2,18},{3,19},{4,20},{5,21},{6,22},{7,23},{8,24},{9,... | collective-permute-start | bytes 442376 | tf_op jit(solution)/shard_map/ppermute | solution.py:886
  45.7 7.8 %collective-permute-start.17 = (bf16[192,768]{1,0:T(8,128)(2,1)S(1)}, bf16[192,768]{1,0:T(8,128)(2,1)}, u32[]{:S(2)}, u32[]{:S(2)}) collective-permute-start(bf16[192,768]{1,0:T(8,128)(2,1)S(1)} %get-tuple-element.93.out_0), channel_id=1, source_target_pairs={{0,2},{1,3},{2,0},{3,1},{4,6},{5,7},{6,4},{7,5},{8,10},{9,11},{10,... | collective-permute-start | bytes 884744 | tf_op jit(solution)/shard_map/ppermute | solution.py:886
  46.6 16.6 %collective-permute-start.28 = (bf16[96,768]{1,0:T(8,128)(2,1)}, bf16[96,768]{1,0:T(8,128)(2,1)S(1)}, u32[]{:S(2)}, u32[]{:S(2)}) collective-permute-start(bf16[96,768]{1,0:T(8,128)(2,1)} %refs_3_.1), channel_id=1, source_target_pairs={{0,24},{1,25},{2,26},{3,27},{4,28},{5,29},{6,30},{7,31},{8,0},{9,1... | collective-permute-start | bytes 442376 | tf_op jit(solution)/shard_map/ppermute | solution.py:886
  51.6 12.1 %collective-permute-start.19 = (bf16[96,768]{1,0:T(8,128)(2,1)}, bf16[96,768]{1,0:T(8,128)(2,1)S(1)}, u32[]{:S(2)}, u32[]{:S(2)}) collective-permute-start(bf16[96,768]{1,0:T(8,128)(2,1)} %copy-done.12), channel_id=1, source_target_pairs={{0,8},{1,9},{2,10},{3,11},{4,12},{5,13},{6,14},{7,15},{8,16},{9,17... | collective-permute-start | bytes 442376 | tf_op jit(solution)/shard_map/ppermute | solution.py:886
  51.6 16.5 %collective-permute-start.20 = (bf16[96,768]{1,0:T(8,128)(2,1)}, bf16[96,768]{1,0:T(8,128)(2,1)S(1)}, u32[]{:S(2)}, u32[]{:S(2)}) collective-permute-start(bf16[96,768]{1,0:T(8,128)(2,1)} %copy-done.12), channel_id=1, source_target_pairs={{0,16},{1,17},{2,18},{3,19},{4,20},{5,21},{6,22},{7,23},{8,24},{9,... | collective-permute-start | bytes 442376 | tf_op jit(solution)/shard_map/ppermute | solution.py:886
  53.5 22.2 %collective-permute-start.16 = (bf16[192,768]{1,0:T(8,128)(2,1)S(1)}, bf16[192,768]{1,0:T(8,128)(2,1)}, u32[]{:S(2)}, u32[]{:S(2)}) collective-permute-start(bf16[192,768]{1,0:T(8,128)(2,1)S(1)} %get-tuple-element.93.out_0), channel_id=1, source_target_pairs={{0,1},{1,0},{2,3},{3,2},{4,5},{5,4},{6,7},{7,6},{8,9},{9,8},{10,11... | collective-permute-start | bytes 884744 | tf_op jit(solution)/shard_map/ppermute | solution.py:886
  53.6 22.7 %collective-permute-start.18 = (bf16[192,768]{1,0:T(8,128)(2,1)}, bf16[192,768]{1,0:T(8,128)(2,1)}, u32[]{:S(2)}, u32[]{:S(2)}) collective-permute-start(bf16[192,768]{1,0:T(8,128)(2,1)} %collective-permute-done.17.out_2), channel_id=1, source_target_pairs={{0,1},{1,0},{2,3},{3,2},{4,5},{5,4},{6,7},{7,6},{8,9},{9,8},{10,11... | collective-permute-start | bytes 884744 | tf_op jit(solution)/shard_map/ppermute | solution.py:886
  63.2 10.7 %collective-permute-start.14 = (bf16[736,192]{1,0:T(8,128)(2,1)S(1)}, bf16[736,192]{1,0:T(8,128)(2,1)S(1)}, u32[]{:S(2)}, u32[]{:S(2)}) collective-permute-start(bf16[736,192]{1,0:T(8,128)(2,1)S(1)} %get-tuple-element.92.refs_0_.head_0), channel_id=1, source_target_pairs={{0,2},{1,3},{2,0},{3,1},{4,6},{5,7},{6,4},{7,5},{8,10},{9,11},{10,... | collective-permute-start | bytes 847880 | tf_op jit(solution)/shard_map/ppermute | solution.py:886
  63.7 7.4 %collective-permute-start.21 = (bf16[96,768]{1,0:T(8,128)(2,1)S(1)}, bf16[96,768]{1,0:T(8,128)(2,1)S(1)}, u32[]{:S(2)}, u32[]{:S(2)}) collective-permute-start(bf16[96,768]{1,0:T(8,128)(2,1)S(1)} %copy-done.13), channel_id=1, source_target_pairs={{0,24},{1,25},{2,26},{3,27},{4,28},{5,29},{6,30},{7,31},{8,0},{9,1... | collective-permute-start | bytes 442376 | tf_op jit(solution)/shard_map/ppermute | solution.py:886
  71.1 17.8 %collective-permute-start.13 = (bf16[736,192]{1,0:T(8,128)(2,1)S(1)}, bf16[736,192]{1,0:T(8,128)(2,1)}, u32[]{:S(2)}, u32[]{:S(2)}) collective-permute-start(bf16[736,192]{1,0:T(8,128)(2,1)S(1)} %get-tuple-element.92.refs_0_.head_0), channel_id=1, source_target_pairs={{0,1},{1,0},{2,3},{3,2},{4,5},{5,4},{6,7},{7,6},{8,9},{9,8},{10,11... | collective-permute-start | bytes 847880 | tf_op jit(solution)/shard_map/ppermute | solution.py:886
  74.0 15.4 %collective-permute-start.15 = (bf16[736,192]{1,0:T(8,128)(2,1)S(1)}, bf16[736,192]{1,0:T(8,128)(2,1)}, u32[]{:S(2)}, u32[]{:S(2)}) collective-permute-start(bf16[736,192]{1,0:T(8,128)(2,1)S(1)} %collective-permute-done.14.refs_2_.head_2), channel_id=1, source_target_pairs={{0,1},{1,0},{2,3},{3,2},{4,5},{5,4},{6,7},{7,6},{8,9},{9,8},{10,11... | collective-permute-start | bytes 847880 | tf_op jit(solution)/shard_map/ppermute | solution.py:886
  75.7 8.5 %collective-permute-start.24 = (bf16[96,768]{1,0:T(8,128)(2,1)}, bf16[96,768]{1,0:T(8,128)(2,1)S(1)}, u32[]{:S(2)}, u32[]{:S(2)}) collective-permute-start(bf16[96,768]{1,0:T(8,128)(2,1)} %copy-done.18), channel_id=1, source_target_pairs={{0,4},{1,5},{2,6},{3,7},{4,0},{5,1},{6,2},{7,3},{8,12},{9,13},{10,... | collective-permute-start | bytes 442376 | tf_op jit(solution)/shard_map/ppermute | solution.py:886
  76.2 11.1 %collective-permute-start.25 = (bf16[96,768]{1,0:T(8,128)(2,1)}, bf16[96,768]{1,0:T(8,128)(2,1)S(1)}, u32[]{:S(2)}, u32[]{:S(2)}) collective-permute-start(bf16[96,768]{1,0:T(8,128)(2,1)} %copy-done.20), channel_id=1, source_target_pairs={{0,4},{1,5},{2,6},{3,7},{4,0},{5,1},{6,2},{7,3},{8,12},{9,13},{10,... | collective-permute-start | bytes 442376 | tf_op jit(solution)/shard_map/ppermute | solution.py:886
  81.0 14.8 %collective-permute-start.29 = (bf16[96,768]{1,0:T(8,128)(2,1)}, bf16[96,768]{1,0:T(8,128)(2,1)S(1)}, u32[]{:S(2)}, u32[]{:S(2)}) collective-permute-start(bf16[96,768]{1,0:T(8,128)(2,1)} %refs_3_.1), channel_id=1, source_target_pairs={{0,4},{1,5},{2,6},{3,7},{4,0},{5,1},{6,2},{7,3},{8,12},{9,13},{10,... | collective-permute-start | bytes 442376 | tf_op jit(solution)/shard_map/ppermute | solution.py:886
  84.2 11.6 %collective-permute-start.30 = (bf16[96,768]{1,0:T(8,128)(2,1)}, bf16[96,768]{1,0:T(8,128)(2,1)S(1)}, u32[]{:S(2)}, u32[]{:S(2)}) collective-permute-start(bf16[96,768]{1,0:T(8,128)(2,1)} %collective-permute-done.26.refs_4_), channel_id=1, source_target_pairs={{0,4},{1,5},{2,6},{3,7},{4,0},{5,1},{6,2},{7,3},{8,12},{9,13},{10,... | collective-permute-start | bytes 442376 | tf_op jit(solution)/shard_map/ppermute | solution.py:886
  87.4 9.5 %collective-permute-start.31 = (bf16[96,768]{1,0:T(8,128)(2,1)}, bf16[96,768]{1,0:T(8,128)(2,1)S(1)}, u32[]{:S(2)}, u32[]{:S(2)}) collective-permute-start(bf16[96,768]{1,0:T(8,128)(2,1)} %collective-permute-done.27.refs_5_), channel_id=1, source_target_pairs={{0,4},{1,5},{2,6},{3,7},{4,0},{5,1},{6,2},{7,3},{8,12},{9,13},{10,... | collective-permute-start | bytes 442376 | tf_op jit(solution)/shard_map/ppermute | solution.py:886
  88.9 10.7 %collective-permute-start.32 = (bf16[96,768]{1,0:T(8,128)(2,1)S(1)}, bf16[96,768]{1,0:T(8,128)(2,1)S(1)}, u32[]{:S(2)}, u32[]{:S(2)}) collective-permute-start(bf16[96,768]{1,0:T(8,128)(2,1)S(1)} %copy-done.15), channel_id=1, source_target_pairs={{0,4},{1,5},{2,6},{3,7},{4,0},{5,1},{6,2},{7,3},{8,12},{9,13},{10,... | collective-permute-start | bytes 442376 | tf_op jit(solution)/shard_map/ppermute | solution.py:886
  106.4 14.9 %collective-permute-start.35 = (bf16[368,768]{1,0:T(8,128)(2,1)S(1)}, bf16[368,768]{1,0:T(8,128)(2,1)S(1)}, u32[]{:S(2)}, u32[]{:S(2)}) collective-permute-start(bf16[368,768]{1,0:T(8,128)(2,1)S(1)} %add_rows.1.here_rows), channel_id=1, source_target_pairs={{0,2},{1,3},{2,0},{3,1},{4,6},{5,7},{6,4},{7,5},{8,10},{9,11},{10,... | collective-permute-start | bytes 1695752 | tf_op jit(solution)/shard_map/ppermute | solution.py:886
  121.4 9.6 %collective-permute-start.36 = (bf16[368,768]{1,0:T(8,128)(2,1)S(1)}, bf16[368,768]{1,0:T(8,128)(2,1)S(1)}, u32[]{:S(2)}, u32[]{:S(2)}) collective-permute-start(bf16[368,768]{1,0:T(8,128)(2,1)S(1)} %add_pair.1.sum_own), channel_id=1, source_target_pairs={{0,1},{1,0},{2,3},{3,2},{4,5},{5,4},{6,7},{7,6},{8,9},{9,8},{10,11... | collective-permute-start | bytes 1695752 | tf_op jit(solution)/shard_map/ppermute | solution.py:886
  129.3 15.8 %collective-permute-start.39 = (bf16[4,96,768]{2,1,0:T(8,128)(2,1)S(1)}, bf16[4,96,768]{2,1,0:T(8,128)(2,1)S(1)}, u32[]{:S(2)}, u32[]{:S(2)}) collective-permute-start(bf16[4,96,768]{2,1,0:T(8,128)(2,1)S(1)} %get-tuple-element.129), channel_id=1, source_target_pairs={{0,4},{1,5},{2,6},{3,7},{4,0},{5,1},{6,2},{7,3},{8,12},{9,13},{10,... | collective-permute-start | bytes 1769480 | tf_op jit(solution)/shard_map/ppermute | solution.py:886
  130.8 38.7 %collective-permute-start.33 = (bf16[416,768]{1,0:T(8,128)(2,1)S(1)}, bf16[416,768]{1,0:T(8,128)(2,1)S(1)}, u32[]{:S(2)}, u32[]{:S(2)}) collective-permute-start(bf16[416,768]{1,0:T(8,128)(2,1)S(1)} %get-tuple-element.106), channel_id=1, source_target_pairs={{0,1},{1,0},{2,3},{3,2},{4,5},{5,4},{6,7},{7,6},{8,9},{9,8},{10,11... | collective-permute-start | bytes 1916936 | tf_op jit(solution)/shard_map/ppermute | solution.py:886
  142.3 28.5 %collective-permute-start.37 = (bf16[416,768]{1,0:T(8,128)(2,1)S(1)}, bf16[416,768]{1,0:T(8,128)(2,1)S(1)}, u32[]{:S(2)}, u32[]{:S(2)}) collective-permute-start(bf16[416,768]{1,0:T(8,128)(2,1)S(1)} %get-tuple-element.120), channel_id=1, source_target_pairs={{0,1},{1,0},{2,3},{3,2},{4,5},{5,4},{6,7},{7,6},{8,9},{9,8},{10,11... | collective-permute-start | bytes 1916936 | tf_op jit(solution)/shard_map/ppermute | solution.py:886
  145.2 8.9 %collective-permute-start.40 = (bf16[96,768]{1,0:T(8,128)(2,1)S(1)}, bf16[96,768]{1,0:T(8,128)(2,1)S(1)}, u32[]{:S(2)}, u32[]{:S(2)}) collective-permute-start(bf16[96,768]{1,0:T(8,128)(2,1)S(1)} %get-tuple-element.131), channel_id=1, source_target_pairs={{0,8},{1,9},{2,10},{3,11},{4,12},{5,13},{6,14},{7,15},{8,16},{9,17... | collective-permute-start | bytes 442376 | tf_op jit(solution)/shard_map/ppermute | solution.py:886
  147.7 11.6 %collective-permute-start.41 = (bf16[96,768]{1,0:T(8,128)(2,1)S(1)}, bf16[96,768]{1,0:T(8,128)(2,1)S(1)}, u32[]{:S(2)}, u32[]{:S(2)}) collective-permute-start(bf16[96,768]{1,0:T(8,128)(2,1)S(1)} %get-tuple-element.132), channel_id=1, source_target_pairs={{0,16},{1,17},{2,18},{3,19},{4,20},{5,21},{6,22},{7,23},{8,24},{9,... | collective-permute-start | bytes 442376 | tf_op jit(solution)/shard_map/ppermute | solution.py:886
  149.8 16.8 %collective-permute-start.47 = (bf16[4,96,384]{2,1,0:T(8,128)(2,1)S(1)}, bf16[4,96,384]{2,1,0:T(8,128)(2,1)S(1)}, u32[]{:S(2)}, u32[]{:S(2)}) collective-permute-start(bf16[4,96,384]{2,1,0:T(8,128)(2,1)S(1)} %get-tuple-element.141), channel_id=1, source_target_pairs={{0,4},{1,5},{2,6},{3,7},{4,0},{5,1},{6,2},{7,3},{8,12},{9,13},{10,... | collective-permute-start | bytes 884744 | tf_op jit(solution)/shard_map/ppermute | solution.py:886
  154.1 12.8 %collective-permute-start.43 = (bf16[4,112,384]{2,1,0:T(8,128)(2,1)S(1)}, bf16[4,112,384]{2,1,0:T(8,128)(2,1)S(1)}, u32[]{:S(2)}, u32[]{:S(2)}) collective-permute-start(bf16[4,112,384]{2,1,0:T(8,128)(2,1)S(1)} %get-tuple-element.135), channel_id=1, source_target_pairs={{0,4},{1,5},{2,6},{3,7},{4,0},{5,1},{6,2},{7,3},{8,12},{9,13},{10,... | collective-permute-start | bytes 1032200 | tf_op jit(solution)/shard_map/ppermute | solution.py:886
  165.1 19.3 %collective-permute-start.54 = (bf16[4,96,768]{2,1,0:T(8,128)(2,1)S(1)}, bf16[4,96,768]{2,1,0:T(8,128)(2,1)S(1)}, u32[]{:S(2)}, u32[]{:S(2)}) collective-permute-start(bf16[4,96,768]{2,1,0:T(8,128)(2,1)S(1)} %get-tuple-element.153), channel_id=1, source_target_pairs={{0,4},{1,5},{2,6},{3,7},{4,0},{5,1},{6,2},{7,3},{8,12},{9,13},{10,... | collective-permute-start | bytes 1769480 | tf_op jit(solution)/shard_map/ppermute | solution.py:886
  166.8 9.2 %collective-permute-start.49 = (bf16[96,384]{1,0:T(8,128)(2,1)S(1)}, bf16[96,384]{1,0:T(8,128)(2,1)S(1)}, u32[]{:S(2)}, u32[]{:S(2)}) collective-permute-start(bf16[96,384]{1,0:T(8,128)(2,1)S(1)} %get-tuple-element.144), channel_id=1, source_target_pairs={{0,16},{1,17},{2,18},{3,19},{4,20},{5,21},{6,22},{7,23},{8,24},{9,... | collective-permute-start | bytes 221192 | tf_op jit(solution)/shard_map/ppermute | solution.py:886
  169.5 11.3 %collective-permute-start.50 = (bf16[96,384]{1,0:T(8,128)(2,1)S(1)}, bf16[96,384]{1,0:T(8,128)(2,1)S(1)}, u32[]{:S(2)}, u32[]{:S(2)}) collective-permute-start(bf16[96,384]{1,0:T(8,128)(2,1)S(1)} %get-tuple-element.145), channel_id=1, source_target_pairs={{0,24},{1,25},{2,26},{3,27},{4,28},{5,29},{6,30},{7,31},{8,0},{9,1... | collective-permute-start | bytes 221192 | tf_op jit(solution)/shard_map/ppermute | solution.py:886
  170.8 10.8 %collective-permute-start.44 = (bf16[112,384]{1,0:T(8,128)(2,1)S(1)}, bf16[112,384]{1,0:T(8,128)(2,1)S(1)}, u32[]{:S(2)}, u32[]{:S(2)}) collective-permute-start(bf16[112,384]{1,0:T(8,128)(2,1)S(1)} %get-tuple-element.137), channel_id=1, source_target_pairs={{0,8},{1,9},{2,10},{3,11},{4,12},{5,13},{6,14},{7,15},{8,16},{9,17... | collective-permute-start | bytes 258056 | tf_op jit(solution)/shard_map/ppermute | solution.py:886
  173.4 8.5 %collective-permute-start.45 = (bf16[112,384]{1,0:T(8,128)(2,1)S(1)}, bf16[112,384]{1,0:T(8,128)(2,1)S(1)}, u32[]{:S(2)}, u32[]{:S(2)}) collective-permute-start(bf16[112,384]{1,0:T(8,128)(2,1)S(1)} %get-tuple-element.138), channel_id=1, source_target_pairs={{0,16},{1,17},{2,18},{3,19},{4,20},{5,21},{6,22},{7,23},{8,24},{9,... | collective-permute-start | bytes 258056 | tf_op jit(solution)/shard_map/ppermute | solution.py:886
  176.0 6.9 %collective-permute-start.46 = (bf16[112,384]{1,0:T(8,128)(2,1)S(1)}, bf16[112,384]{1,0:T(8,128)(2,1)S(1)}, u32[]{:S(2)}, u32[]{:S(2)}) collective-permute-start(bf16[112,384]{1,0:T(8,128)(2,1)S(1)} %get-tuple-element.139), channel_id=1, source_target_pairs={{0,24},{1,25},{2,26},{3,27},{4,28},{5,29},{6,30},{7,31},{8,0},{9,1... | collective-permute-start | bytes 258056 | tf_op jit(solution)/shard_map/ppermute | solution.py:886
  180.8 18.3 %collective-permute-start.38 = (bf16[416,768]{1,0:T(8,128)(2,1)S(1)}, bf16[416,768]{1,0:T(8,128)(2,1)S(1)}, u32[]{:S(2)}, u32[]{:S(2)}) collective-permute-start(bf16[416,768]{1,0:T(8,128)(2,1)S(1)} %get-tuple-element.122), channel_id=1, source_target_pairs={{0,2},{1,3},{2,0},{3,1},{4,6},{5,7},{6,4},{7,5},{8,10},{9,11},{10,... | collective-permute-start | bytes 1916936 | tf_op jit(solution)/shard_map/ppermute | solution.py:886
  183.7 10.2 %collective-permute-start.52 = (bf16[96,768]{1,0:T(8,128)(2,1)S(1)}, bf16[96,768]{1,0:T(8,128)(2,1)S(1)}, u32[]{:S(2)}, u32[]{:S(2)}) collective-permute-start(bf16[96,768]{1,0:T(8,128)(2,1)S(1)} %get-tuple-element.148), channel_id=1, source_target_pairs={{0,2},{1,3},{2,0},{3,1},{4,6},{5,7},{6,4},{7,5},{8,10},{9,11},{10,... | collective-permute-start | bytes 442376 | tf_op jit(solution)/shard_map/ppermute | solution.py:886
  184.5 9.4 %collective-permute-start.55 = (bf16[96,768]{1,0:T(8,128)(2,1)S(1)}, bf16[96,768]{1,0:T(8,128)(2,1)S(1)}, u32[]{:S(2)}, u32[]{:S(2)}) collective-permute-start(bf16[96,768]{1,0:T(8,128)(2,1)S(1)} %get-tuple-element.155), channel_id=1, source_target_pairs={{0,8},{1,9},{2,10},{3,11},{4,12},{5,13},{6,14},{7,15},{8,16},{9,17... | collective-permute-start | bytes 442376 | tf_op jit(solution)/shard_map/ppermute | solution.py:886
  185.1 12.0 %collective-permute-start.56 = (bf16[96,768]{1,0:T(8,128)(2,1)S(1)}, bf16[96,768]{1,0:T(8,128)(2,1)S(1)}, u32[]{:S(2)}, u32[]{:S(2)}) collective-permute-start(bf16[96,768]{1,0:T(8,128)(2,1)S(1)} %get-tuple-element.156), channel_id=1, source_target_pairs={{0,16},{1,17},{2,18},{3,19},{4,20},{5,21},{6,22},{7,23},{8,24},{9,... | collective-permute-start | bytes 442376 | tf_op jit(solution)/shard_map/ppermute | solution.py:886
  189.4 7.7 %collective-permute-start.57 = (bf16[96,768]{1,0:T(8,128)(2,1)S(1)}, bf16[96,768]{1,0:T(8,128)(2,1)S(1)}, u32[]{:S(2)}, u32[]{:S(2)}) collective-permute-start(bf16[96,768]{1,0:T(8,128)(2,1)S(1)} %get-tuple-element.157), channel_id=1, source_target_pairs={{0,24},{1,25},{2,26},{3,27},{4,28},{5,29},{6,30},{7,31},{8,0},{9,1... | collective-permute-start | bytes 442376 | tf_op jit(solution)/shard_map/ppermute | solution.py:886
  (67 other events, 387.2 us)

commit v3 on v2

--- a/solution.py
+++ b/solution.py
@@ -376,6 +376,22 @@
 
 
 PAD_ID = 99
+TUNE = {'after_add_pieces': 'y_gdown', 'after_add_rows': 'branch_rows raise_rows pack_z1', 'after_attend': 'both0_y1', 'after_both2_y1': 'both1_y1', 'after_branch_rows': 'far_out_core1 order_out out_core1', 'after_far_cut_core1': 'pick_pieces', 'after_far_heads_core1': '', 'after_far_out_core1': '', 'after_far_rows_core1': 'pick_pieces', 'after_finish_rows': '', 'after_gb_y1': 'score_back', 'after_gb_z2': 'gdown_z2', 'after_gb_z3': 'h_core1', 'after_gdown_y1': 'raise_rows', 'after_gdown_z1': 'm_core1', 'after_gdown_z2': 'total_core1', 'after_grads_x1': 'project_back pick_grads', 'after_half_gdown': 'branch_back gdown_z1', 'after_heads_core1': 'far_out_core1', 'after_heads_x1': 'out_x1', 'after_join_pieces': 'pick_pieces', 'after_lower_rows': '', 'after_norm_rows_in': 'far_both_z1', 'after_open_pack': '', 'after_order_out': 'both3_y1', 'after_out_x1': 'both_z2', 'after_raise_rows': 'far_rows_core1', 'after_total_core1': 'out_core1', 'after_y_gdown': '', 'after_y_gup': '', 'half_down': 2, 'us_add_pair': 0.002, 'us_branch_back': 0.2, 'us_branch_rows': 6, 'us_down_grads': 45.0, 'us_finish_rows': 0.001, 'us_half_gdown': 0.035, 'us_half_gup': 0.001, 'us_join_grads': 0.11, 'us_join_pieces': 21.0, 'us_lower_rows': 111.0, 'us_mlp_grads': 12, 'us_open_pack': 3.6, 'us_order_out': 48.0, 'us_pick_grads': 0.001, 'us_pick_pieces': 7.5, 'us_score_back': 0.42, 'us_y_gup': 7.0, 'us_z_gdown': 0.001, 'us_z_gup': 0.07}
+
+
+def knob(name, default, among=None):
+    KNOBS.setdefault(name, (default, list(among) if among is not None else None))
+    return TUNE.get(name, default)
+
+
+def wait_for(name, default=""):
+    chosen = knob("after_" + name, default, MARK)
+    return [MARK[c] for c in chosen.split() if c in MARK]
+
+
+MARK = {}
+KNOBS = {}
+COST = {'pick_pieces': 1.5, 'join_pieces': 0.7, 'norm_rows_in': 2, 'open_pack': 1.2, 'attend': 4, 'order_out': 1.6, 'branch_rows': 2, 'raise_rows': 2.8, 'down_grads': 1.5, 'lower_rows': 3.7, 'add_rows': 0.9, 'mlp_grads': 4, 'add_pair': 0.9, 'branch_back': 4, 'score_back': 4.2, 'project_back': 1.3, 'add_pieces': 1.2, 'pick_grads': 0.7, 'finish_rows': 1.4, 'join_grads': 1.1}
 
 
 def mm(a, b):
@@ -397,32 +413,118 @@
 
 
 def chunk_index(slot, z, y):
-    hops, crossed = slot % 4, slot // 4
-    source_z = lax.rem(z + 4 - hops, 4)
-    source_y = y if not crossed else 1 - y
-    return source_z * 2 + source_y
-
-
-def row_blocks(block):
-    return [slice(first, first + block) for first in range(0, 736, block)]
+    return (z ^ (slot % 4)) * 2 + (y ^ (slot // 4))
+
+
+def row_blocks(block, among=slice(0, 736)):
+    return [slice(first, first + block) for first in range(among.start, among.stop, block)]
 
 
 def fold(rows):
     return rows.reshape(rows.shape[0] // 8, 8, rows.shape[1]).sum(0)
 
 
-def call(kernel, outs, ins, scratch=(), us=1, limit=28):
-    moved = sum(o.size * o.dtype.itemsize for o in outs) + sum(i.size * i.dtype.itemsize for i in ins)
-    return pl.pallas_call(
-        kernel,
-        out_shape=tuple(outs),
-        in_specs=[pl.BlockSpec(memory_space=pltpu.VMEM)] * len(ins),
-        out_specs=tuple(pl.BlockSpec(memory_space=pltpu.VMEM) for _ in outs),
-        scratch_shapes=list(scratch),
+class Keep:
+    def __init__(self, value):
+        self.value = value
+
+
+class Far:
+    def __init__(self, value, held=True):
+        self.value, self.held = value, held
+
+
+class Load:
+    def __init__(self, buffer, copy):
+        self.buffer, self.copy, self.waited = buffer, copy, False
+
+    def ready(self):
+        if not self.waited:
+            self.copy.wait()
+            self.waited = True
+        return self.buffer
+
+
+class Store:
+    def __init__(self, buffer, target, semaphore):
+        self.buffer, self.target, self.semaphore, self.copies = buffer, target, semaphore, []
+
+    def __setitem__(self, at, rows):
+        self.buffer[at] = rows
+
+    def __getitem__(self, at):
+        return self.buffer[at]
+
+    def go(self, at=None, source=None):
+        source, target = self.buffer if source is None else source, self.target
+        if at is not None:
+            source, target = source.at[at], target.at[at]
+        copy = pltpu.make_async_copy(source, target, self.semaphore.at[len(self.copies)])
+        copy.start()
+        self.copies.append(copy)
+
+
+def call(kernel, outs, ins, scratch=(), limit=20, after="", label=None):
+    label = label or kernel.__name__
+    after = wait_for(label, after)
+    far = [i for i, v in enumerate(ins) if isinstance(v, Far)]
+    far_out = [i for i, v in enumerate(outs) if isinstance(v, Far)]
+    plain = [v.value if isinstance(v, (Far, Keep)) else v for v in ins]
+    shapes = [v.value if isinstance(v, (Far, Keep)) else v for v in outs]
+    near, away = pl.BlockSpec(memory_space=pltpu.VMEM), pl.BlockSpec(memory_space=pltpu.HBM)
+    held = [i for i in far_out if outs[i].held]
+    room = [pltpu.VMEM(plain[i].shape, plain[i].dtype) for i in far]
+    room += [pltpu.VMEM(shapes[i].shape, shapes[i].dtype) for i in held]
+    if far or far_out:
+        room.append(pltpu.SemaphoreType.DMA((len(far) + len(far_out), MICRO)))
+
+    def body(*refs):
+        given = [*refs[: len(ins)], *refs[len(ins) + len(after) :]]
+        own = given[len(ins) + len(outs) + len(scratch) :]
+        given = given[: len(ins) + len(outs) + len(scratch)]
+        copies = []
+        for k, i in enumerate(far):
+            copies.append(pltpu.make_async_copy(given[i], own[k], own[-1].at[k, 0]))
+            given[i] = Load(own[k], copies[-1])
+        buffers = dict(zip(held, own[len(far) :]))
+        stores = []
+        for k, i in enumerate(far_out):
+            stores.append(Store(buffers.get(i), given[len(ins) + i], own[-1].at[len(far) + k]))
+            given[len(ins) + i] = stores[-1]
+        for copy in copies:
+            copy.start()
+        kernel(*given)
+        for store in stores:
+            for copy in store.copies:
+                copy.wait()
+
+    def placed(v):
+        if isinstance(v, Keep):
+            return pltpu.with_memory_space_constraint(v.value, pltpu.VMEM)
+        return pltpu.with_memory_space_constraint(v.value, pltpu.HBM) if isinstance(v, Far) else v
+
+    def made(v):
+        if isinstance(v, Keep):
+            return pltpu.VMEM(v.value.shape, v.value.dtype)
+        return pltpu.HBM(v.value.shape, v.value.dtype) if isinstance(v, Far) else v
+
+    made_arrays = pl.pallas_call(
+        body,
+        out_shape=tuple(made(v) for v in outs),
+        in_specs=[away if i in far else near for i in range(len(ins))]
+        + [pl.BlockSpec(memory_space=pl.ANY)] * len(after),
+        out_specs=tuple(away if i in far_out else near for i in range(len(outs))),
+        scratch_shapes=[*scratch, *room],
         compiler_params=pltpu.CompilerParams(vmem_limit_bytes=limit * 2**20),
-        cost_estimate=pl.CostEstimate(flops=us * 10**9, bytes_accessed=moved, transcendentals=0),
+        cost_estimate=pl.CostEstimate(flops=int(knob("us_" + label, COST.get(kernel.__name__, 0.7)) * 10**9), bytes_accessed=0, transcendentals=0),
         name=kernel.__name__,
-    )(*ins)
+    )(*[placed(v) for v in ins], *after)
+    MARK[label] = made_arrays[0]
+    return made_arrays
+
+
+def keep(*arrays):
+    return [Keep(v) for v in arrays]
 
 
 def sds(*shape, dtype=BF16):
@@ -432,9 +534,9 @@
 def pick_pieces(w_qkv, w_up, gains, patches, cots, own, near, far, rows, held):
     place = here()[0]
     held[...] = jnp.zeros_like(held)
-    up = w_up[...].astype(F32)
-    qkv = w_qkv[...].astype(F32)
-    gain = gains[...].astype(F32)
+    up = w_up.ready()[...].astype(F32)
+    qkv = w_qkv.ready()[...].astype(F32)
+    gain = gains.ready()[...].astype(F32)
     for b in range(4):
         for d in range(8):
             held[b, 0:24, d * 96 : d * 96 + 96] = up[:, d * 384 + b * 96 : d * 384 + b * 96 + 96]
@@ -447,11 +549,11 @@
     near[...] = held[place ^ 1].astype(BF16)
     far[0:48, :] = held[place ^ 2].astype(BF16)
     far[48:96, :] = held[place ^ 3].astype(BF16)
-    rows[0:176, :] = patches[...]
-    rows[176:352, :] = cots[...]
-
-
-def join_pieces(own, near, far, near_far, w_out, pack, up_chunk, pack_f, up_f):
+    rows[0:176, :] = patches.ready()[...]
+    rows[176:352, :] = cots.ready()[...]
+
+
+def join_pieces(own, near, far, near_far, w_out, w_down, pack, both, pack_f, up_f):
     place = here()[0]
     pack_f[96:112, :] = jnp.zeros((16, 768), F32)
     pieces = (
@@ -471,7 +573,8 @@
     for i in range(4):
         pack_f[i * 24 : i * 24 + 24, 576:768] = out[:, i * 192 : i * 192 + 192]
     pack[...] = pack_f[...].astype(BF16)
-    up_chunk[...] = up_f[...].astype(BF16)
+    both[0:96, :] = up_f[...].astype(BF16)
+    both[96:192, :] = w_down[...]
 
 
 def open_pack(*refs):
@@ -510,25 +613,35 @@
             scratch[pl.ds(pl.multiple_of(m * 368 + source * 88, 8), 88), :] = rows[m * 88 : m * 88 + 88]
     rows = tail[...].astype(F32)
     for m in range(MICRO):
-        scratch[m * 368 + 352 : m * 368 + 368, :] = rows[m * 16 : m * 16 + 16]
-
-
-def attend(
-    rows_0, rows_1, rows_2, rows_3, tail, ids_col, ids_row, w_qkv, gain_rows,
-    tokens, normed, projected, probs, attended, rows_f,
-):
-    place_rows(rows_f, (rows_0, rows_1, rows_2, rows_3), tail, 0)
-    gain = gain_rows[0:1, :]
-
+        scratch[m * 368 + 352 : m * 368 + 368, :] = jnp.zeros((16, 768), F32)
+        scratch[m * 368 + 352 : m * 368 + 362, :] = rows[m * 10 : m * 10 + 10]
+
+
+def norm_rows_in(rows_0, rows_1, rows_2, rows_3, tail, cot_tail, unit, tokens, cots, rows_f):
+    blocks = (rows_0, rows_1, rows_2, rows_3)
+    place_rows(rows_f, blocks, cot_tail, 176)
+    for at in row_blocks(32):
+        cots[at, :] = rows_f[at, :].astype(BF16)
+    cots.go()
+    place_rows(rows_f, blocks, tail, 0)
     for at in row_blocks(32):
         rows = rows_f[at, :]
         tokens[at, :] = rows.astype(BF16)
-        normed[at, :] = (normalise(rows)[0] * gain).astype(BF16)
+        unit[at, :] = normalise(rows)[0]
+    tokens.go()
+
+
+def attend(ids_col, ids_row, unit, w_qkv, gain_rows, attended, w_kept, normed, projected, probs):
+    w_kept.go(source=w_qkv)
+    gain = gain_rows[0:1, :]
     for m in range(MICRO):
         at = slice(m * 368, m * 368 + 368)
+        normed[at, :] = (unit[at, :] * gain).astype(BF16)
+        normed.go(at)
         qkv = mm(normed[at, :], w_qkv[...])
         qkv = jnp.concatenate([qkv[:, 0:192] * SCORE_SCALE, qkv[:, 192:576]], -1).astype(BF16)
         projected[at, :] = qkv
+        projected.go(at)
         same = ids_col[at, :] == ids_row[m : m + 1, :]
         bias = jnp.where(same, 0.0, MASKED)
         heads = []
@@ -542,13 +655,11 @@
             weights = weights.astype(BF16)
             probs[m * 3 + h] = weights
             heads.append(mm(weights, v))
+        probs.go(slice(m * 3, m * 3 + 3))
         attended[at, :] = jnp.concatenate(heads, -1).astype(BF16)
 
 
-def order_out(
-    out_0, out_1, out_2, out_3, rows_0, rows_1, rows_2, rows_3, cot_tail, gain_rows,
-    ordered, mine, cots, grad_mlp, out_f,
-):
+def order_out(out_0, out_1, out_2, out_3, cots, gain_rows, ordered, mine, grad_mlp, out_f):
     place = here()[0]
     for k, part in enumerate((out_0, out_1, out_2, out_3)):
         source = place ^ k
@@ -558,60 +669,70 @@
             out_f[pl.ds(at, 24), :] = rows[d * 24 : d * 24 + 24]
     ordered[...] = out_f[...].astype(BF16)
     mine[...] = out_f[pl.ds(pl.multiple_of(place * 192, 8), 192), :].astype(BF16)
-    place_rows(out_f, (rows_0, rows_1, rows_2, rows_3), cot_tail, 176)
+    mine.go()
     gain = gain_rows[3:4, :]
     for at in row_blocks(32):
-        rows = out_f[at, :]
-        cots[at, :] = rows.astype(BF16)
-        grad_mlp[at, :] = (gain * rows).astype(BF16)
+        grad_mlp[at, :] = (gain * cots[at, :].astype(F32)).astype(BF16)
+    grad_mlp.go()
+
+
+def branch_rows(
+    head_0, head_1, head_2, head_3, w_out, tokens, gain_rows, normed, branch, middle, rows_f
+):
+    place = here()[0]
+    gain_s, gain_n = gain_rows[1:2, :], gain_rows[2:3, :]
+    for m in range(MICRO):
+        group = slice(m * 368, m * 368 + 368)
+        total = None
+        for k, part in enumerate((head_0, head_1, head_2, head_3)):
+            rows = w_out[pl.ds(pl.multiple_of((place ^ k) * 192, 16), 192), :]
+            term = mm(part[group, :], rows)
+            total = term if total is None else total + term
+        rows_f[group, :] = total
+        for at in row_blocks(16, group):
+            a = rows_f[at, :]
+            branch[at, :] = a.astype(BF16)
+            rows = tokens[at, :].astype(F32) + gain_s * a
+            middle[at, :] = rows
+            normed[at, :] = (normalise(rows)[0] * gain_n).astype(BF16)
+        branch.go(group)
+        middle.go(group)
 
 
 def raise_rows(*refs):
-    heads, (w_out, tokens, gain_rows), chunks = refs[0:4], refs[4:7], refs[7:15]
-    branch, middle, normed, active, slope, w_up, up_f = refs[15:]
-    place, _, _, z, y = here()
+    normed, chunks = refs[0], refs[1:9]
+    active, slope, w_up, w_down, normed_kept, down_kept, rows_f = refs[9:]
+    normed_kept.go(source=normed)
+    _, _, _, z, y = here()
     for slot, chunk in enumerate(chunks):
         d = chunk_index(slot, z, y)
-        w_up[pl.ds(pl.multiple_of(d * 96, 96), 96), :] = chunk[...]
+        w_up[pl.ds(pl.multiple_of(d * 96, 96), 96), :] = chunk[0:96, :]
+        w_down[pl.ds(pl.multiple_of(d * 96, 96), 96), :] = chunk[96:192, :]
+    down_kept.go(source=w_down)
     for m in range(MICRO):
         at = slice(m * 368, m * 368 + 368)
-        total = None
-        for k, part in enumerate(heads):
-            source = place ^ k
-            rows = w_out[pl.ds(pl.multiple_of(source * 192, 16), 192), :]
-            term = mm(part[at, :], rows)
-            total = term if total is None else total + term
-        up_f[at, :] = total
-    gain_s, gain_n = gain_rows[1:2, :], gain_rows[2:3, :]
-
+        rows_f[at, :] = mm(normed[at, :], w_up[...])
     for at in row_blocks(32):
-        a = up_f[at, :]
-        branch[at, :] = a.astype(BF16)
-        rows = tokens[at, :].astype(F32) + gain_s * a
-        middle[at, :] = rows
-        normed[at, :] = (normalise(rows)[0] * gain_n).astype(BF16)
-    for m in range(MICRO):
-        at = slice(m * 368, m * 368 + 368)
-        up_f[at, :] = mm(normed[at, :], w_up[...])
-
-    for at in row_blocks(32):
-        u = up_f[at, :]
+        u = rows_f[at, :]
         half = 0.5 + 0.5 * lax.erf(u * 0.7071067811865476)
         active[at, :] = (u * half).astype(BF16)
         slope[at, :] = half + u * (0.3989422804014327 * jnp.exp(-0.5 * u * u))
 
 
-def lower_rows(*refs):
-    (slope, grad_mlp, w_up), chunks = refs[:3], refs[3:11]
-    w_down, grad_hidden, away, kept, work = refs[11:]
-    _, _, core, z, y = here()
-    for slot, chunk in enumerate(chunks):
-        d = chunk_index(slot, z, y)
-        w_down[pl.ds(pl.multiple_of(d * 96, 96), 96), :] = chunk[...]
+def down_grads(active, grad_mlp, away, kept, active_kept, work):
+    active_kept.go(source=active)
+    y = here()[4]
+    work[...] = mm_tn(active[...], grad_mlp[...])
+    halve(work, y, away, kept, 96)
+
+
+def lower_rows(slope, grad_mlp, w_up, w_down, away, kept, grad_hidden, work):
+    core = here()[2]
     for m in range(MICRO):
         at = slice(m * 368, m * 368 + 368)
         grad = mm_nt(grad_mlp[at, :], w_down[...])
         grad_hidden[at, :] = (slope[at, :] * grad).astype(BF16)
+        grad_hidden.go(at)
         work[m] = mm_nt(grad_hidden[at, :], w_up[...])
     away[...] = work[1 - core].astype(BF16)
     kept[...] = work[core]
@@ -640,14 +761,13 @@
 
 
 def mlp_grads(
-    active, normed, grad_mlp, grad_hidden, w_down, cots,
-    down_away, down_kept, up_away, up_kept, rows_away, rows_kept, scale_grad, work, pieces,
+    active, normed, grad_hidden, w_down, cots, targets, head_0, head_1, head_2, head_3,
+    up_away, up_kept, rows_away, rows_kept, scale_grad, chosen, work, pieces,
 ):
     place, _, _, _, y = here()
-    work[0:768, :] = mm_tn(active[...], grad_mlp[...])
-    halve(work, y, down_away, down_kept, 96)
-    work[0:768, :] = mm_tn(normed[...], grad_hidden[...])
+    work[0:768, :] = mm_tn(normed.ready()[...], grad_hidden.ready()[...])
     halve(work, y, up_away, up_kept, 96)
+    active, w_down, cots = active.ready(), w_down.ready(), cots.ready()
     for m in range(MICRO):
         at = slice(m * 368, m * 368 + 368)
         work[at, :] = mm(active[at, :], w_down[...])
@@ -657,6 +777,13 @@
     scale_grad[...] = total
     cut_rows(work, pieces)
     split_rows(pieces, place, rows_away, rows_kept)
+    picked = None
+    for k, part in enumerate((head_0, head_1, head_2, head_3)):
+        index = lax.broadcasted_iota(jnp.int32, (192, 192), 0) + (place ^ k) * 192
+        pick = jnp.where(index == targets[...], 1.0, 0.0).astype(BF16)
+        term = mm(part[...], pick)
+        picked = term if picked is None else picked + term
+    chosen[...] = picked.astype(BF16)
 
 
 def add_rows(kept, came, total):
@@ -668,10 +795,9 @@
 
 
 def branch_back(
-    sum_own, sum_near, middle, cots, branch, gain_rows, w_mine, probs, normed, targets,
-    scale_grad_mlp, head_0, head_1, head_2, head_3,
+    sum_own, sum_near, middle, cots, branch, gain_rows, w_mine, probs, normed, scale_grad_mlp, chosen,
     grad_rows, grad_heads, grad_v, away, kept,
-    work, grad_branch, grad_mid, extra,
+    work, grad_branch, grad_mid, extra, early,
 ):
     place, _, core, _, y = here()
     for m in range(MICRO):
@@ -710,29 +836,22 @@
         terms = [mm_tn(probs[m * 3 + h], heads[:, h * 64 : h * 64 + 64]) for h in range(3)]
         grad_v[at, :] = jnp.concatenate(terms, -1).astype(BF16)
     grad_mid[0:768, 0:192] = mm_tn(normed[...], grad_v[...])
-    chosen = None
-    for k, part in enumerate((head_0, head_1, head_2, head_3)):
-        source = place ^ k
-        index = lax.broadcasted_iota(jnp.int32, (192, 192), 0) + source * 192
-        pick = jnp.where(index == targets[...], 1.0, 0.0).astype(BF16)
-        term = mm(part[...], pick)
-        chosen = term if chosen is None else chosen + term
-    extra[...] = mm_tn(chosen.astype(BF16), grad_branch[...])
+    extra[...] = mm_tn(chosen[...], grad_branch[...])
     scale_rows = (
         0.25 * jnp.sum(scale_sum, 0, keepdims=True),
         jnp.sum(scale_grad_mlp[...], 0, keepdims=True),
     )
     for d in range(8):
         base = d * 112
-        work[base : base + 96, 0:192] = grad_mid[d * 96 : d * 96 + 96, 0:192]
+        early[base : base + 96, 0:192] = grad_mid[d * 96 : d * 96 + 96, 0:192]
         for i in range(4):
-            work[base + i * 24 : base + i * 24 + 24, 192:384] = extra[
+            early[base + i * 24 : base + i * 24 + 24, 192:384] = extra[
                 d * 24 : d * 24 + 24, i * 192 : i * 192 + 192
             ]
-        work[base + 96 : base + 112, 0:384] = jnp.zeros((16, 384), F32)
+        early[base + 96 : base + 112, :] = jnp.zeros((16, 384), F32)
         for i in range(2):
-            work[base + 96 + i : base + 97 + i, 0:96] = scale_rows[i][:, d * 96 : d * 96 + 96]
-    halve(work, y, away, kept, 112)
+            early[base + 96 + i : base + 97 + i, 0:96] = scale_rows[i][:, d * 96 : d * 96 + 96]
+    halve(early, y, away, kept, 112)
 
 
 def score_back(probs, projected, grad_heads, normed, grad_qk, away, kept, work):
@@ -771,8 +890,24 @@
     _, _, _, z, _ = here()
     own[...] = kept[z] + came[z].astype(F32)
     for k, send in ((1, send_1), (2, send_2), (3, send_3)):
-        there = lax.rem(z + k, 4)
-        send[...] = (kept[there] + came[there].astype(F32)).astype(BF16)
+        send[...] = (kept[z ^ k] + came[z ^ k].astype(F32)).astype(BF16)
+
+
+def sum_y_pairs(kept, came, own, away):
+    _, _, _, z, _ = here()
+    for k in range(2):
+        own[k] = kept[z ^ (2 * k)] + came[z ^ (2 * k)].astype(F32)
+        there = z ^ (2 * k + 1)
+        away[k] = (kept[there] + came[there].astype(F32)).astype(BF16)
+
+
+def sum_pairs(kept, came, own, away):
+    own[...] = kept[0] + came[0].astype(F32)
+    away[...] = (kept[1] + came[1].astype(F32)).astype(BF16)
+
+
+def sum_last(own, came, total):
+    total[...] = own[...] + came[...].astype(F32)
 
 
 def sum_z(own, came_1, came_2, came_3, total):
@@ -800,13 +935,13 @@
     outs, out_tails = [], []
     for m in range(MICRO):
         for part, first in ((0, place * 88), (88, 352)):
-            count = 88 if part == 0 else 16
+            count = 88 if part == 0 else 10
             at = slice(m * 104 + part, m * 104 + part + count)
             far_at = slice(208 + m * 104 + part, 208 + m * 104 + part + count)
             mid = middle[pl.ds(pl.multiple_of(m * 368 + first, 8), count), :]
             final = mid + gain_rows[3:4, :] * (stay[at, :] + came[at, :].astype(F32))
             (outs if part == 0 else out_tails).append(final)
-            rows = own[m * 88 : m * 88 + 88] if part == 0 else rest[m * 16 : m * 16 + 16]
+            rows = own[m * 88 : m * 88 + 88] if part == 0 else rest[m * 10 : m * 10 + 10]
             unit, scale = normalise(rows)
             pulled = gain_rows[0:1, :] * (stay[far_at, :] + came[far_at, :].astype(F32))
             pulled = pulled - jnp.mean(pulled, -1, keepdims=True) - unit * jnp.mean(
@@ -816,9 +951,9 @@
             if part == 0:
                 grad_patches[m * 88 : m * 88 + 88, :] = grad
             else:
-                grad_special[m * 10 : m * 10 + 10, :] = grad[0:10]
+                grad_special[m * 10 : m * 10 + 10, :] = grad
     out_patches[...] = jnp.concatenate(outs, 0).astype(BF16)
-    out_special[...] = jnp.concatenate([part[0:10] for part in out_tails], 0).astype(BF16)
+    out_special[...] = jnp.concatenate(out_tails, 0).astype(BF16)
 
 
 def pick_grads(up, first, second, own, near, far, grad_out, held):
@@ -871,7 +1006,7 @@
     grad_gains[3:4, :] = scales[1:2, :]
 
 
-def send(rows, axis, step):
+def send(rows, axis, step, label, after=""):
     pairs = []
     for group in range(8):
         z, y = group // 2, group % 2
@@ -880,42 +1015,83 @@
                 "core": (group, place ^ 1),
                 "x": (group, place ^ 2),
                 "y": (z * 2 + 1 - y, place),
-                "z": ((z + step) % 4 * 2 + y, place),
+                "z": ((z ^ step) * 2 + y, place),
             }[axis]
             pairs.append((group * 4 + place, target[0] * 4 + target[1]))
-    return lax.ppermute(rows, ("dp", "blk"), pairs)
-
-
-def gather_dp(chunk):
-    along_z = [chunk] + [send(chunk, "z", k) for k in (1, 2, 3)]
-    return along_z + [send(part, "y", 1) for part in along_z]
-
-
-def gather_blk(rows):
-    near = send(rows, "core", 1)
-    far = send(rows, "x", 1)
-    return [rows, near, far, send(far, "core", 1)]
-
-
-def scatter_dp(away, kept):
-    rows, width = away.shape[1:]
-    came = send(away, "y", 1)
+    label = f"{label}_{axis}{step}"
+    ready = wait_for(label, after)
+    if ready:
+        rows = lax.optimization_barrier((rows, *ready))[0]
+    with jax.named_scope(label):
+        MARK[label] = lax.ppermute(rows, ("dp", "blk"), pairs)
+    return MARK[label]
+
+
+def gather_z(chunk, label, after=""):
+    second = send(chunk, "z", 2, label, after)
+    return [chunk, send(chunk, "z", 1, label, after), second, send(second, "z", 1, f"far_{label}")]
+
+
+def gather_y(along_z, label):
+    return along_z + [send(part, "y", 1, f"{label}{k}") for k, part in enumerate(along_z)]
+
+
+def add_y(kept, came, label, after):
+    rows, width = kept.shape[1:]
     own, *parts = call(
-        sum_y, [sds(rows, width, dtype=F32)] + [sds(rows, width)] * 3, [kept, came]
-    )
-    came = [send(part, "z", k) for k, part in zip((1, 2, 3), parts)]
-    return call(sum_z, [sds(rows, width, dtype=F32)], [own, *came])[0]
-
-
-def pad_tail(rows):
-    return jnp.pad(rows.reshape(2, 10, 768), ((0, 0), (0, 6), (0, 0))).reshape(32, 768)
+        sum_y,
+        [Keep(sds(rows, width, dtype=F32))] + [sds(rows, width)] * 3,
+        [Keep(kept), came],
+        after=after,
+        label="y_" + label,
+    )
+    return [own, *[send(part, "z", k, label) for k, part in zip((1, 2, 3), parts)]]
+
+
+def halve_y(kept, came, label, after):
+    rows, width = kept.shape[1:]
+    own, away = call(
+        sum_y_pairs,
+        [Keep(sds(2, rows, width, dtype=F32)), sds(2, rows, width)],
+        [Keep(kept), came],
+        after=after,
+        label="y_" + label,
+    )
+    return own, send(away, "z", 1, label)
+
+
+def halve_z(pair, label, after):
+    kept, came = pair
+    rows, width = kept.shape[1:]
+    own, away = call(
+        sum_pairs,
+        [Keep(sds(rows, width, dtype=F32)), sds(rows, width)],
+        [Keep(kept), came],
+        after=after,
+        label="half_" + label,
+    )
+    return own, send(away, "z", 2, label)
+
+
+def add_last(last, label, after):
+    own, came = last
+    return call(
+        sum_last, [sds(*own.shape, dtype=F32)], [Keep(own), came], after=after, label="z_" + label
+    )[0]
+
+
+def add_z(steps, label, after):
+    own, *came = steps
+    return call(
+        sum_z, [sds(*own.shape, dtype=F32)], [Keep(own), *came], after=after, label="z_" + label
+    )[0]
 
 
 def on_device_split(
     patches, special, image_ids, w_qkv, w_out, w_up, w_down, gains, cot_patches, cot_special
 ):
+    MARK.clear()
     place = lax.axis_index("blk")
-    tail, cot_tail = pad_tail(special), pad_tail(cot_special)
     spec_ids = jnp.concatenate(
         [jnp.arange(10, dtype=jnp.int32) // SPECIAL, jnp.full((6,), PAD_ID, jnp.int32)]
     )
@@ -928,135 +1104,196 @@
     own, near, far, rows = call(
         pick_pieces,
         [sds(48, 768), sds(48, 768), sds(96, 768), sds(352, 768)],
-        [w_qkv, w_up, gains, patches, cot_patches],
+        [Far(w_qkv), Far(w_up), Far(gains), Far(patches), Far(cot_patches)],
         [pltpu.VMEM((4, 48, 768), F32)],
     )
-    came_far = send(far, "x", 1)
-    came_near, came_near_far = send(near, "core", 1), send(came_far, "core", 1)
-    rows, _ = lax.optimization_barrier((rows, came_far))
-    row_parts = gather_blk(rows)
-    down_chunks = gather_dp(w_down)
-    pack, up_chunk = call(
+    came_far = send(far, "x", 1, "cut")
+    came_near, came_near_far = send(near, "core", 1, "cut"), send(came_far, "core", 1, "far_cut")
+    pack, both = call(
         join_pieces,
-        [sds(112, 768), sds(96, 768)],
-        [own, came_near, came_far, came_near_far, w_out],
+        [sds(112, 768), sds(192, 768)],
+        [own, came_near, came_far, came_near_far, w_out, w_down],
         [pltpu.VMEM((112, 768), F32), pltpu.VMEM((96, 768), F32)],
     )
-    pack_chunks = gather_dp(pack)
-    up_chunks = gather_dp(up_chunk)
+    pack_z = gather_z(pack, "pack")
+    far_rows = send(rows, "x", 1, "rows", "cut_x1")
+    near_rows = send(rows, "core", 1, "rows")
+    row_parts = [rows, near_rows, far_rows, send(far_rows, "core", 1, "far_rows", "pack_z1")]
+    pack_chunks = gather_y(pack_z, "pack")
+    both_z = gather_z(both, "both", "pack_z2")
+    unit, tokens, cots = call(
+        norm_rows_in,
+        [Keep(sds(736, 768, dtype=F32)), *[Far(sds(736, 768))] * 2],
+        [*row_parts, special, cot_special],
+        [pltpu.VMEM((736, 768), F32)],
+        after="pack_z2",
+    )
     qkv_full, out_part, gain_rows = call(
         open_pack,
-        [sds(768, 576), sds(192, 768), sds(8, 768, dtype=F32)],
+        [Keep(sds(768, 576)), sds(192, 768), Keep(sds(8, 768, dtype=F32))],
         pack_chunks,
         [pltpu.VMEM((192, 768), F32), pltpu.VMEM((8, 16, 768), F32)],
-    )
-    out_parts = gather_blk(out_part)
-    tokens, normed, projected, probs, attended = call(
+        after="norm_rows_in",
+    )
+    far_out = send(out_part, "x", 1, "out")
+    both_chunks = gather_y(both_z, "both")
+    attended, qkv_far, normed_far, projected, probs = call(
         attend,
-        [sds(736, 768), sds(736, 768), sds(736, 576), sds(6, 368, 368), sds(736, 192)],
-        [*row_parts, tail, ids_col, ids_row, qkv_full, gain_rows],
+        [
+            sds(736, 192), Far(sds(768, 576), held=False), Far(sds(736, 768)),
+            Far(sds(736, 576)), Far(sds(6, 368, 368)),
+        ],
+        [ids_col, ids_row, *keep(unit, qkv_full, gain_rows)],
+    )
+    far_heads = send(attended, "x", 1, "heads")
+    out_parts = [
+        out_part, send(out_part, "core", 1, "out", "attend"),
+        far_out, send(far_out, "core", 1, "far_out", "attend"),
+    ]
+    out_full, out_mine, grad_mlp = call(
+        order_out,
+        [Keep(sds(768, 768)), Far(sds(192, 768)), Far(sds(736, 768))],
+        [*out_parts, cots, Keep(gain_rows)],
+        [pltpu.VMEM((768, 768), F32)],
+    )
+    heads = [
+        attended, send(attended, "core", 1, "heads"),
+        far_heads, send(far_heads, "core", 1, "far_heads", "order_out"),
+    ]
+    normed_mlp, branch, middle = call(
+        branch_rows,
+        [Keep(sds(736, 768)), Far(sds(736, 768)), Far(sds(736, 768, dtype=F32))],
+        [*heads, Keep(out_full), tokens, Keep(gain_rows)],
         [pltpu.VMEM((736, 768), F32)],
-        us=10,
-    )
-    heads = gather_blk(attended)
-    out_full, out_mine, cots, grad_mlp = call(
-        order_out,
-        [sds(768, 768), sds(192, 768), sds(736, 768), sds(736, 768)],
-        [*out_parts, *row_parts, cot_tail, gain_rows],
-        [pltpu.VMEM((768, 768), F32)],
-        us=3,
-    )
-    branch, middle, normed_mlp, active, slope, up_full = call(
+    )
+    active, slope, up_full, down_full, normed_mlp, down_far = call(
         raise_rows,
         [
-            sds(736, 768), sds(736, 768, dtype=F32), sds(736, 768), sds(736, 768),
-            sds(736, 768, dtype=F32), sds(768, 768),
+            *keep(sds(736, 768), sds(736, 768, dtype=F32), sds(768, 768), sds(768, 768)),
+            Far(sds(736, 768), held=False), Far(sds(768, 768), held=False),
         ],
-        [*heads, out_full, tokens, gain_rows, *up_chunks],
+        [Keep(normed_mlp), *both_chunks],
         [pltpu.VMEM((736, 768), F32)],
-        us=10,
-    )
-    down_full, grad_hidden, sum_away, sum_kept = call(
+    )
+    half = [sds(4, 96, 768), Keep(sds(4, 96, 768, dtype=F32))]
+    rows_split = [sds(416, 768), Keep(sds(416, 768, dtype=F32))]
+    down_away, down_kept, active = call(
+        down_grads,
+        [*half, Far(sds(736, 768), held=False)],
+        [Keep(active), grad_mlp],
+        [pltpu.VMEM((768, 768), F32)],
+    )
+    down_came = send(down_away, "y", 1, "gdown")
+    sum_away, sum_kept, grad_hidden = call(
         lower_rows,
-        [sds(768, 768), sds(736, 768), sds(368, 768), sds(368, 768, dtype=F32)],
-        [slope, grad_mlp, up_full, *down_chunks],
+        [sds(368, 768), Keep(sds(368, 768, dtype=F32)), Far(sds(736, 768))],
+        [Keep(slope), grad_mlp, *keep(up_full, down_full)],
         [pltpu.VMEM((2, 368, 768), F32)],
-        us=4,
-    )
-    sum_came = send(sum_away, "core", 1)
-    chip_sum = call(add_rows, [sds(368, 768)], [sum_kept, sum_came])[0]
-    chip_came = send(chip_sum, "x", 1)
-    half = [sds(4, 96, 768), sds(4, 96, 768, dtype=F32)]
-    rows_split = [sds(416, 768), sds(416, 768, dtype=F32)]
-    down_away, down_kept, up_away, up_kept, m_away, m_kept, scale_mlp = call(
+        after="down_grads",
+    )
+    sum_came = send(sum_away, "core", 1, "sum")
+    chip_sum = call(add_rows, [sds(368, 768)], [Keep(sum_kept), sum_came])[0]
+    chip_came = send(chip_sum, "x", 1, "sum")
+    up_away, up_kept, m_away, m_kept, scale_mlp, chosen = call(
         mlp_grads,
-        [*half, *half, *rows_split, sds(8, 768, dtype=F32)],
-        [active, normed_mlp, grad_mlp, grad_hidden, down_full, cots],
+        [*half, *rows_split, *keep(sds(8, 768, dtype=F32), sds(736, 192))],
+        [*[Far(v) for v in (active, normed_mlp, grad_hidden, down_far, cots)], targets, *heads],
         [pltpu.VMEM((768, 768), F32), pltpu.VMEM((4, 208, 768), F32)],
-        us=5,
-    )
-    grad_down = scatter_dp(down_away, down_kept)
-    grad_up_rows = scatter_dp(up_away, up_kept)
-    sum_own = call(add_pair, [sds(368, 768)], [chip_sum, chip_came])[0]
-    sum_near = send(sum_own, "core", 1)
-    m_came = send(m_away, "core", 1)
+        after="add_rows",
+    )
+    up_came = send(up_away, "y", 1, "gup")
+    m_came = send(m_away, "core", 1, "m")
+    down_steps = halve_y(down_kept, down_came, "gdown", "mlp_grads")
+    sum_own = call(add_pair, [sds(368, 768)], [chip_sum, chip_came], after="y_gdown")[0]
+    sum_near = send(sum_own, "core", 1, "total")
     grad_rows, grad_heads, grad_v, a_away, a_kept = call(
         branch_back,
         [
-            sds(208, 768, dtype=F32), sds(736, 192), sds(736, 192),
-            sds(4, 112, 384), sds(4, 112, 384, dtype=F32),
+            *keep(sds(208, 768, dtype=F32), sds(736, 192), sds(736, 192)),
+            sds(4, 112, 384), Keep(sds(4, 112, 384, dtype=F32)),
         ],
         [
-            sum_own, sum_near, middle, cots, branch, gain_rows, out_mine, probs, normed, targets,
-            scale_mlp, *heads,
+            sum_own, sum_near, middle, cots, branch, Keep(gain_rows), out_mine,
+            probs, normed_far, *keep(scale_mlp, chosen),
         ],
         [
-            pltpu.VMEM((896, 768), F32), pltpu.VMEM((736, 768), BF16),
-            pltpu.VMEM((768, 768), F32), pltpu.VMEM((192, 768), F32),
+            pltpu.VMEM((736, 768), F32), pltpu.VMEM((736, 768), BF16),
+            pltpu.VMEM((768, 768), F32), pltpu.VMEM((192, 768), F32), pltpu.VMEM((896, 384), F32),
         ],
-        us=10,
-    )
-    first_rows = scatter_dp(a_away, a_kept)
+    )
+    a_came = send(a_away, "y", 1, "ga")
+    order = knob("up_steps", 1, [0, 1, 2])
+    if order == 0:
+        up_steps = halve_y(up_kept, up_came, "gup", "branch_back")
+    when = knob("half_down", 0, [0, 1, 2])
+    if when == 0:
+        down_last = halve_z(down_steps, "gdown", "branch_back")
     grad_qk, b_away, b_kept = call(
         score_back,
-        [sds(736, 384), sds(4, 96, 384), sds(4, 96, 384, dtype=F32)],
-        [probs, projected, grad_heads, normed],
+        [Keep(sds(736, 384)), sds(4, 96, 384), Keep(sds(4, 96, 384, dtype=F32))],
+        [probs, projected, Keep(grad_heads), normed_far],
         [pltpu.VMEM((768, 384), F32)],
-        us=10,
-    )
-    second_rows = scatter_dp(b_away, b_kept)
+    )
+    b_came = send(b_away, "y", 1, "gb")
+    early_a = knob("early_a", False)
+    if early_a:
+        a_pair = halve_y(a_kept, a_came, "ga", "score_back")
+    if order == 1:
+        up_steps = halve_y(up_kept, up_came, "gup", "score_back")
     h_away, h_kept = call(
         project_back,
         rows_split,
-        [grad_qk, grad_v, qkv_full],
+        [*keep(grad_qk, grad_v), qkv_far],
         [pltpu.VMEM((736, 768), F32), pltpu.VMEM((4, 208, 768), F32)],
-        us=3,
-    )
-    h_came = send(h_away, "core", 1)
+    )
+    h_came = send(h_away, "core", 1, "h")
+    if when == 1:
+        down_last = halve_z(down_steps, "gdown", "project_back")
+    if order == 2:
+        up_steps = halve_y(up_kept, up_came, "gup", "project_back")
     stay, go = call(
-        add_pieces, [sds(416, 768, dtype=F32), sds(416, 768)], [m_kept, m_came, h_kept, h_came]
-    )
-    far_rows = send(go, "x", 1)
+        add_pieces,
+        [Keep(sds(416, 768, dtype=F32)), sds(416, 768)],
+        [Keep(m_kept), m_came, Keep(h_kept), h_came],
+    )
+    far_rows = send(go, "x", 1, "mh")
+    if when == 2:
+        down_last = halve_z(down_steps, "gdown", "add_pieces")
+    up_last = None
+    if knob("half_up", True):
+        up_last = halve_z(up_steps, "gup", "add_pieces")
+    if not early_a:
+        a_pair = halve_y(a_kept, a_came, "ga", "project_back")
+    b_steps = add_y(b_kept, b_came, "gb", "add_pieces")
+    a_last = halve_z(a_pair, "ga", "y_gb")
+    if up_last is None:
+        up_last = halve_z(up_steps, "gup", "y_gb")
+    grad_down = add_last(down_last, "gdown", "y_gb")
+    grad_up_rows = add_last(up_last, "gup", "z_gdown")
+    first_rows = add_last(a_last, "ga", "z_gup")
+    second_rows = add_z(b_steps, "gb", "z_ga")
     own, near, far, grad_out = call(
         pick_grads,
-        [sds(48, 768, dtype=F32), sds(48, 768), sds(96, 768), sds(24, 768, dtype=F32)],
+        [Keep(sds(48, 768, dtype=F32)), sds(48, 768), sds(96, 768), sds(24, 768, dtype=F32)],
         [grad_up_rows, first_rows, second_rows],
         [pltpu.VMEM((4, 48, 768), F32)],
     )
-    came_far = send(far, "x", 1)
-    came_near, came_near_far = send(near, "core", 1), send(came_far, "core", 1)
+    came_far = send(far, "x", 1, "grads")
+    came_near, came_near_far = send(near, "core", 1, "grads"), send(came_far, "core", 1, "far_grads")
     out_patches, out_special, grad_patches, grad_special = call(
         finish_rows,
         [
             sds(176, 768), sds(20, 768), sds(176, 768, dtype=F32), sds(20, 768, dtype=F32),
         ],
-        [stay, far_rows, middle, grad_rows, patches, tail, gain_rows],
+        [Keep(stay), far_rows, middle, Keep(grad_rows), patches, special, Keep(gain_rows)],
+        after="pick_grads",
     )
     grad_qkv, grad_up, grad_gains = call(
         join_grads,
         [sds(24, 2304, dtype=F32), sds(24, 3072, dtype=F32), sds(4, 24, dtype=F32)],
-        [own, came_near, came_far, came_near_far, w_qkv, w_up, gains],
+        [Keep(own), came_near, came_far, came_near_far, w_qkv, w_up, gains],
         [pltpu.VMEM((4, 48, 768), F32)],
+        after="finish_rows",
     )
     return (
         out_patches, out_special, grad_patches, grad_special,

time: 201 us -> 163 us (0.81)
  starting transfers between devices: 74.7 us -> 45.8 us
  local copies, waits for them, and re-layouts: 21.2 us -> 8.34 us
  Pallas kernels: 35.3 us -> 46 us
  waiting for transfers between devices: 67.9 us -> 61.3 us
    ppermute x58 -> x48, starting transfers between devices: 74.7 us -> 45.8 us  [send(): MARK[label] = lax.ppermute(rows, ('dp', 'blk'), pairs)]
    unnamed x114 -> x78, local copies, waits for them, and re-layouts: 20.8 us -> 7.96 us
    pallas_call x25 -> x31, Pallas kernels: 35.3 us -> 46 us  [call(): pl.pallas_call(body, out_shape=tuple((made(v) for v in outs)), in_specs=[...]
    ppermute x58 -> x48, waiting for transfers between devices: 67.9 us -> 61.3 us  [send(): MARK[label] = lax.ppermute(rows, ('dp', 'blk'), pairs)]
  transfers between devices with their start and end apart: 58 -> 48, of which waited for: 25 -> 20; matrix products, arithmetic and copies ran while one was open for 0% -> 0% of each run, Pallas kernels for 15% -> 22%
where the time goes in v3:
time: 163 us
  waiting for transfers between devices  61.3 us (38%)
  Pallas kernels  46 us (28%)
  starting transfers between devices  45.8 us (28%)
  local copies, waits for them, and re-layouts  8.34 us (5%)
    ppermute x48, waiting for transfers between devices, send(): MARK[label] = lax.ppermute(rows, ('dp', 'blk'), pairs)  61.3 us
    pallas_call x31, Pallas kernels, call(): pl.pallas_call(body, out_shape=tuple((made(v) for v in outs)), in_specs=[...  46 us
    ppermute x48, starting transfers between devices, send(): MARK[label] = lax.ppermute(rows, ('dp', 'blk'), pairs)  45.8 us
    unnamed x78, local copies, waits for them, and re-layouts  7.96 us
  transfers between devices with their start and end apart: 48, of which 20 were waited for; matrix products, arithmetic and copies ran while one was open for 0% of the time, Pallas kernels for 22%

profile of v3, /device:TPU:0, one launch (start us, length us, event | category | flops | bytes accessed | tf_op | source)
XLA Modules:
  0.0 162.8 jit_solution(5899330512292202012)
XLA Ops:
  0.7 1.3 pick_pieces.1
  2.0 3.0 %collective-permute-start.1 = (bf16[96,768]{1,0:T(8,128)(2,1)S(1)}, bf16[96,768]{1,0:T(8,128)(2,1)S(1)}, u32[]{:S(2)}, u32[]{:S(2)}) collective-permute-start(bf16[96,768]{1,0:T(8,128)(2,1)S(1)} %get-tuple-element.107), channel_id=1, source_target_pairs={{0,2},{1,3},{2,0},{3,1},{4,6},{5,7},{6,4},{7,5},{8,10},{9,11},{10,... | collective-permute-start | bytes 442376 | tf_op jit(solution)/shard_map/cut_x1/ppermute | solution.py:1026
  5.0 3.9 %collective-permute-done.1.refs_2_ = bf16[96,768]{1,0:T(8,128)(2,1)S(1)} collective-permute-done((bf16[96,768]{1,0:T(8,128)(2,1)S(1)}, bf16[96,768]{1,0:T(8,128)(2,1)S(1)}, u32[]{:S(2)}, u32[]{:S(2)}) %collective-permute-start.1) | collective-permute-done | bytes 147488 | tf_op jit(solution)/shard_map/cut_x1/ppermute | solution.py:1026
  9.4 1.7 %collective-permute-start.2 = (bf16[352,768]{1,0:T(8,128)(2,1)S(1)}, bf16[352,768]{1,0:T(8,128)(2,1)S(1)}, u32[]{:S(2)}, u32[]{:S(2)}) collective-permute-start(bf16[352,768]{1,0:T(8,128)(2,1)S(1)} %get-tuple-element.108.refs_0_), channel_id=1, source_target_pairs={{0,2},{1,3},{2,0},{3,1},{4,6},{5,7},{6,4},{7,5},{8,10},{9,11},{10,... | collective-permute-start | bytes 1622024 | tf_op jit(solution)/shard_map/rows_x1/ppermute | solution.py:1026
  11.3 2.7 %collective-permute-start.6 = (bf16[112,768]{1,0:T(8,128)(2,1)S(1)}, bf16[112,768]{1,0:T(8,128)(2,1)S(1)}, u32[]{:S(2)}, u32[]{:S(2)}) collective-permute-start(bf16[112,768]{1,0:T(8,128)(2,1)S(1)} %get-tuple-element.114.refs_0_), channel_id=1, source_target_pairs={{0,16},{1,17},{2,18},{3,19},{4,20},{5,21},{6,22},{7,23},{8,24},{9,... | collective-permute-start | bytes 516104 | tf_op jit(solution)/shard_map/pack_z2/ppermute | solution.py:1026
  13.9 1.6 collective-permute-start.9
  15.5 1.5 collective-permute-start.11
  17.0 5.0 %collective-permute-done.6.refs_2_ = bf16[112,768]{1,0:T(8,128)(2,1)S(1)} collective-permute-done((bf16[112,768]{1,0:T(8,128)(2,1)S(1)}, bf16[112,768]{1,0:T(8,128)(2,1)S(1)}, u32[]{:S(2)}, u32[]{:S(2)}) %collective-permute-start.6) | collective-permute-done | bytes 172064 | tf_op jit(solution)/shard_map/pack_z2/ppermute | solution.py:1026
  22.6 3.4 %collective-permute-start.7 = (bf16[192,768]{1,0:T(8,128)(2,1)S(1)}, bf16[192,768]{1,0:T(8,128)(2,1)S(1)}, u32[]{:S(2)}, u32[]{:S(2)}) collective-permute-start(bf16[192,768]{1,0:T(8,128)(2,1)S(1)} %get-tuple-element.115.refs_1_), channel_id=1, source_target_pairs={{0,16},{1,17},{2,18},{3,19},{4,20},{5,21},{6,22},{7,23},{8,24},{9,... | collective-permute-start | bytes 884744 | tf_op jit(solution)/shard_map/both_z2/ppermute | solution.py:1026
  26.0 1.5 collective-permute-start.12
  28.7 2.3 %collective-permute-done.10.refs_3_ = bf16[112,768]{1,0:T(8,128)(2,1)} collective-permute-done((bf16[112,768]{1,0:T(8,128)(2,1)S(1)}, bf16[112,768]{1,0:T(8,128)(2,1)}, u32[]{:S(2)}, u32[]{:S(2)}) %collective-permute-start.10) | collective-permute-done | bytes 172064 | tf_op jit(solution)/shard_map/far_pack_z1/ppermute | solution.py:1026
  31.0 1.6 collective-permute-start.14
  34.0 3.0 %collective-permute-done.13.refs_6_ = bf16[112,768]{1,0:T(8,128)(2,1)S(1)} collective-permute-done((bf16[112,768]{1,0:T(8,128)(2,1)S(1)}, bf16[112,768]{1,0:T(8,128)(2,1)S(1)}, u32[]{:S(2)}, u32[]{:S(2)}) %collective-permute-start.13) | collective-permute-done | bytes 172064 | tf_op jit(solution)/shard_map/pack2_y1/ppermute | solution.py:1026
  37.7 1.7 %collective-permute-done.7.refs_3_ = bf16[192,768]{1,0:T(8,128)(2,1)S(1)} collective-permute-done((bf16[192,768]{1,0:T(8,128)(2,1)S(1)}, bf16[192,768]{1,0:T(8,128)(2,1)S(1)}, u32[]{:S(2)}, u32[]{:S(2)}) %collective-permute-start.7) | collective-permute-done | bytes 294944 | tf_op jit(solution)/shard_map/both_z2/ppermute | solution.py:1026
  42.3 2.0 %open_pack.1 = (bf16[768,576]{1,0:T(8,128)(2,1)S(1)}, bf16[192,768]{1,0:T(8,128)(2,1)}, f32[8,768]{1,0:T(8,128)S(1)}) custom-call(bf16[112,768]{1,0:T(8,128)(2,1)S(1)} %get-tuple-element.114.refs_0_, bf16[112,768]{1,0:T(8,128)(2,1)S(1)} %collective-permute-done.9.refs_1_.refs_4_, bf16[112,768]{1,0:T(8,128)(2,1)S(1)} %collective-permute-done.6.refs_2_, ...), custom_call_target="tpu_custom_call" | custom-call | flops 3600000000 | tf_op jit(solution)/shard_map/open_pack/pallas_call | solution.py:511
  45.3 1.5 collective-permute-start.16
  46.9 1.5 collective-permute-start.15
  49.3 2.8 %collective-permute-done.8.refs_6_.refs_4_ = bf16[192,768]{1,0:T(8,128)(2,1)} collective-permute-done((bf16[192,768]{1,0:T(8,128)(2,1)S(1)}, bf16[192,768]{1,0:T(8,128)(2,1)}, u32[]{:S(2)}, u32[]{:S(2)}) %collective-permute-start.8) | collective-permute-done | bytes 294944 | tf_op jit(solution)/shard_map/far_both_z1/ppermute | solution.py:1026
  53.7 2.5 %norm_rows_in.1 = (f32[736,768]{1,0:T(8,128)S(1)}, bf16[736,768]{1,0:T(8,128)(2,1)}, bf16[736,768]{1,0:T(8,128)(2,1)}) custom-call(bf16[352,768]{1,0:T(8,128)(2,1)S(1)} %get-tuple-element.108.refs_0_, bf16[352,768]{1,0:T(8,128)(2,1)S(1)} %collective-permute-done.refs_1_, bf16[352,768]{1,0:T(8,128)(2,1)S(1)} %collective-permute-done.2.refs_2_, ...), custom_call_target="tpu_custom_call" | custom-call | flops 2000000000 | tf_op jit(solution)/shard_map/norm_rows_in/pallas_call | solution.py:511
  57.0 4.1 %attend.1 = (bf16[736,192]{1,0:T(8,128)(2,1)S(1)}, bf16[768,576]{1,0:T(8,128)(2,1)}, bf16[736,768]{1,0:T(8,128)(2,1)}, bf16[736,576]{1,0:T(8,128)(2,1)}, bf16[6,368,368]{2,1,0:T(8,128)(2,1)}) custom-call(s32[736,1]{1,0:T(8,128)S(1)} %reshape.77.refs_0_, s32[2,368]{1,0:T(2,128)S(1)} %pad_add_fusion.refs_1_, f32[736,768]{1,0:T(8,128)S(1)} %get-tuple-element.116.refs_2_, ...), custom_call_target="tpu_custom_call" | custom-call | flops 4000000000 | tf_op jit(solution)/shard_map/attend/pallas_call | solution.py:511
  61.2 1.3 collective-permute-start.19
  63.3 1.5 collective-permute-start.25
  64.8 7.5 %collective-permute-done.19.refs_2_.refs_8_ = bf16[736,192]{1,0:T(8,128)(2,1)S(1)} collective-permute-done((bf16[736,192]{1,0:T(8,128)(2,1)S(1)}, bf16[736,192]{1,0:T(8,128)(2,1)S(1)}, u32[]{:S(2)}, u32[]{:S(2)}) %collective-permute-start.19) | collective-permute-done | bytes 282656 | tf_op jit(solution)/shard_map/heads_x1/ppermute | solution.py:1026
  72.4 2.8 %order_out.1 = (bf16[768,768]{1,0:T(8,128)(2,1)S(1)}, bf16[192,768]{1,0:T(8,128)(2,1)}, bf16[736,768]{1,0:T(8,128)(2,1)}) custom-call(bf16[192,768]{1,0:T(8,128)(2,1)} %get-tuple-element.124.refs_0_, bf16[192,768]{1,0:T(8,128)(2,1)S(1)} %collective-permute-done.21.refs_1_.refs_9_, bf16[192,768]{1,0:T(8,128)(2,1)} %collective-permute-done.16.refs_2_, ...), custom_call_target="tpu_custom_call" | custom-call | flops 48000000000 | tf_op jit(solution)/shard_map/order_out/pallas_call | solution.py:511
  75.2 3.2 %branch_rows.1 = (bf16[736,768]{1,0:T(8,128)(2,1)S(1)}, bf16[736,768]{1,0:T(8,128)(2,1)}, f32[736,768]{1,0:T(8,128)}) custom-call(bf16[736,192]{1,0:T(8,128)(2,1)S(1)} %get-tuple-element.123.refs_0_.refs_6_, bf16[736,192]{1,0:T(8,128)(2,1)S(1)} %collective-permute-done.18.refs_1_.refs_7_, bf16[736,192]{1,0:T(8,128)(2,1)S(1)} %collective-permute-done.19.refs_2_.refs_8_, ...), custom_call_target="tpu_custom_call" | custom-call | flops 6000000000 | tf_op jit(solution)/shard_map/branch_rows/pallas_call | solution.py:511
  78.5 4.1 %raise_rows.1 = (bf16[736,768]{1,0:T(8,128)(2,1)S(1)}, f32[736,768]{1,0:T(8,128)S(1)}, bf16[768,768]{1,0:T(8,128)(2,1)S(1)}, bf16[768,768]{1,0:T(8,128)(2,1)S(1)...) custom-call(bf16[736,768]{1,0:T(8,128)(2,1)S(1)} %get-tuple-element.128.refs_0_.refs_2_, ...), custom_call_target="tpu_custom_call" | custom-call | flops 2800000000 | tf_op jit(solution)/shard_map/raise_rows/pallas_call | solution.py:511
  82.6 3.1 %lower_rows.1 = (bf16[368,768]{1,0:T(8,128)(2,1)S(1)}, f32[368,768]{1,0:T(8,128)S(1)}, bf16[736,768]{1,0:T(8,128)(2,1)}) custom-call(f32[736,768]{1,0:T(8,128)S(1)} %get-tuple-element.134.refs_0_, bf16[736,768]{1,0:T(8,128)(2,1)S(1)} %copy-done.37, bf16[768,768]{1,0:T(8,128)(2,1)S(1)} %get-tuple-element.135.refs_2_, ...), custom_call_target="tpu_custom_call" | custom-call | flops 111000002560 | tf_op jit(solution)/shard_map/lower_rows/pallas_call | solution.py:511
  86.3 1.4 down_grads.1
  87.7 1.6 collective-permute-start.29
  90.4 6.6 %mlp_grads.1 = (bf16[4,96,768]{2,1,0:T(8,128)(2,1)S(1)}, f32[4,96,768]{2,1,0:T(8,128)S(1)}, bf16[416,768]{1,0:T(8,128)(2,1)S(1)}, f32[416,768]{1,0:T(8,128)S(1)}...) custom-call(bf16[736,768]{1,0:T(8,128)(2,1)} %get-tuple-element.132.refs_0_, ...), custom_call_target="tpu_custom_call" | custom-call | flops 12000000000 | tf_op jit(solution)/shard_map/mlp_grads/pallas_call | solution.py:511
  97.1 5.9 %collective-permute-done.29.refs_1_ = bf16[4,96,768]{2,1,0:T(8,128)(2,1)S(1)} collective-permute-done((bf16[4,96,768]{2,1,0:T(8,128)(2,1)S(1)}, bf16[4,96,768]{2,1,0:T(8,128)(2,1)S(1)}, u32[]{:S(2)}, u32[]{:S(2)}) %collective-permute-start.29) | collective-permute-done | bytes 589856 | tf_op jit(solution)/shard_map/gdown_y1/ppermute | solution.py:1026
  104.9 1.9 %collective-permute-start.36 = (bf16[2,96,768]{2,1,0:T(8,128)(2,1)S(1)}, bf16[2,96,768]{2,1,0:T(8,128)(2,1)S(1)}, u32[]{:S(2)}, u32[]{:S(2)}) collective-permute-start(bf16[2,96,768]{2,1,0:T(8,128)(2,1)S(1)} %get-tuple-element.176), channel_id=1, source_target_pairs={{0,8},{1,9},{2,10},{3,11},{4,12},{5,13},{6,14},{7,15},{8,0},{9,1},... | collective-permute-start | bytes 884744 | tf_op jit(solution)/shard_map/gdown_z1/ppermute | solution.py:1026
  106.9 4.0 %branch_back.1 = (f32[208,768]{1,0:T(8,128)S(1)}, bf16[736,192]{1,0:T(8,128)(2,1)S(1)}, bf16[736,192]{1,0:T(8,128)(2,1)S(1)}, bf16[4,112,384]{2,1,0:T(8,128)(2,1)S(1)}, f32[4,112,384]{2,1,0:T(8,128)S(1)}) custom-call(bf16[368,768]{1,0:T(8,128)(2,1)S(1)} %add_pair.1.refs_0_, bf16[368,768]{1,0:T(8,128)(2,1)S(1)} %collective-permute-done.30.refs_1_, ...), custom_call_target="tpu_custom_call" | custom-call | flops 200000000 | tf_op jit(solution)/shard_map/branch_back/pallas_call | solution.py:511
  111.0 1.3 collective-permute-start.39
  112.3 4.3 %score_back.1 = (bf16[736,384]{1,0:T(8,128)(2,1)S(1)}, bf16[4,96,384]{2,1,0:T(8,128)(2,1)S(1)}, f32[4,96,384]{2,1,0:T(8,128)S(1)}) custom-call(bf16[6,368,368]{2,1,0:T(8,128)(2,1)S(1)} %copy-done.1, bf16[736,576]{1,0:T(8,128)(2,1)S(1)} %copy-done.7, bf16[736,192]{1,0:T(8,128)(2,1)S(1)} %get-tuple-element.156.refs_2_, bf16[736,768]{1,0:T(8,128)(2,1)S(1)} %copy-done.2), custom_call_target="tpu_custom_call" | custom-call | flops 420000000 | tf_op jit(solution)/shard_map/score_back/pallas_call | solution.py:511
  116.6 1.3 project_back.1
  117.9 2.4 %collective-permute-done.33.refs_1_ = bf16[4,96,768]{2,1,0:T(8,128)(2,1)S(1)} collective-permute-done((bf16[4,96,768]{2,1,0:T(8,128)(2,1)S(1)}, bf16[4,96,768]{2,1,0:T(8,128)(2,1)S(1)}, u32[]{:S(2)}, u32[]{:S(2)}) %collective-permute-start.33) | collective-permute-done | bytes 589856 | tf_op jit(solution)/shard_map/gup_y1/ppermute | solution.py:1026
  120.5 2.0 %collective-permute-start.34 = (bf16[2,96,768]{2,1,0:T(8,128)(2,1)S(1)}, bf16[2,96,768]{2,1,0:T(8,128)(2,1)S(1)}, u32[]{:S(2)}, u32[]{:S(2)}) collective-permute-start(bf16[2,96,768]{2,1,0:T(8,128)(2,1)S(1)} %get-tuple-element.172), channel_id=1, source_target_pairs={{0,8},{1,9},{2,10},{3,11},{4,12},{5,13},{6,14},{7,15},{8,0},{9,1},... | collective-permute-start | bytes 884744 | tf_op jit(solution)/shard_map/gup_z1/ppermute | solution.py:1026
  124.4 3.3 %collective-permute-done.39.refs_1_ = bf16[4,112,384]{2,1,0:T(8,128)(2,1)S(1)} collective-permute-done((bf16[4,112,384]{2,1,0:T(8,128)(2,1)S(1)}, bf16[4,112,384]{2,1,0:T(8,128)(2,1)S(1)}, u32[]{:S(2)}, u32[]{:S(2)}) %collective-permute-start.39) | collective-permute-done | bytes 344096 | tf_op jit(solution)/shard_map/ga_y1/ppermute | solution.py:1026
  127.8 2.0 %collective-permute-start.40 = (bf16[2,112,384]{2,1,0:T(8,128)(2,1)S(1)}, bf16[2,112,384]{2,1,0:T(8,128)(2,1)S(1)}, u32[]{:S(2)}, u32[]{:S(2)}) collective-permute-start(bf16[2,112,384]{2,1,0:T(8,128)(2,1)S(1)} %get-tuple-element.187), channel_id=1, source_target_pairs={{0,8},{1,9},{2,10},{3,11},{4,12},{5,13},{6,14},{7,15},{8,0},{9,1},... | collective-permute-start | bytes 516104 | tf_op jit(solution)/shard_map/ga_z1/ppermute | solution.py:1026
  130.0 3.6 %collective-permute-done.34.refs_1_ = bf16[2,96,768]{2,1,0:T(8,128)(2,1)S(1)} collective-permute-done((bf16[2,96,768]{2,1,0:T(8,128)(2,1)S(1)}, bf16[2,96,768]{2,1,0:T(8,128)(2,1)S(1)}, u32[]{:S(2)}, u32[]{:S(2)}) %collective-permute-start.34) | collective-permute-done | bytes 294944 | tf_op jit(solution)/shard_map/gup_z1/ppermute | solution.py:1026
  135.2 2.1 %collective-permute-done.40.refs_1_ = bf16[2,112,384]{2,1,0:T(8,128)(2,1)S(1)} collective-permute-done((bf16[2,112,384]{2,1,0:T(8,128)(2,1)S(1)}, bf16[2,112,384]{2,1,0:T(8,128)(2,1)S(1)}, u32[]{:S(2)}, u32[]{:S(2)}) %collective-permute-start.40) | collective-permute-done | bytes 172064 | tf_op jit(solution)/shard_map/ga_z1/ppermute | solution.py:1026
  137.3 2.9 %collective-permute-start.41 = (bf16[112,384]{1,0:T(8,128)(2,1)S(1)}, bf16[112,384]{1,0:T(8,128)(2,1)S(1)}, u32[]{:S(2)}, u32[]{:S(2)}) collective-permute-start(bf16[112,384]{1,0:T(8,128)(2,1)S(1)} %get-tuple-element.189), channel_id=1, source_target_pairs={{0,16},{1,17},{2,18},{3,19},{4,20},{5,21},{6,22},{7,23},{8,24},{9,... | collective-permute-start | bytes 258056 | tf_op jit(solution)/shard_map/ga_z2/ppermute | solution.py:1026
  140.2 1.2 collective-permute-start.44
  141.5 6.1 %collective-permute-done.35.refs_1_ = bf16[96,768]{1,0:T(8,128)(2,1)S(1)} collective-permute-done((bf16[96,768]{1,0:T(8,128)(2,1)S(1)}, bf16[96,768]{1,0:T(8,128)(2,1)S(1)}, u32[]{:S(2)}, u32[]{:S(2)}) %collective-permute-start.35) | collective-permute-done | bytes 147488 | tf_op jit(solution)/shard_map/gup_z2/ppermute | solution.py:1026
  149.4 3.4 %collective-permute-done.43.refs_2_ = bf16[96,384]{1,0:T(8,128)(2,1)S(1)} collective-permute-done((bf16[96,384]{1,0:T(8,128)(2,1)S(1)}, bf16[96,384]{1,0:T(8,128)(2,1)S(1)}, u32[]{:S(2)}, u32[]{:S(2)}) %collective-permute-start.43) | collective-permute-done | bytes 73760 | tf_op jit(solution)/shard_map/gb_z2/ppermute | solution.py:1026
  154.4 4.4 %collective-permute-done.46.refs_2_ = bf16[96,768]{1,0:T(8,128)(2,1)S(1)} collective-permute-done((bf16[96,768]{1,0:T(8,128)(2,1)S(1)}, bf16[96,768]{1,0:T(8,128)(2,1)S(1)}, u32[]{:S(2)}, u32[]{:S(2)}) %collective-permute-start.46) | collective-permute-done | bytes 147488 | tf_op jit(solution)/shard_map/grads_x1/ppermute | solution.py:1026
  159.3 1.4 finish_rows.1
  (165 shorter events, 26.2 us)
Async XLA Ops:
  2.0 6.9 %collective-permute-start.1 = (bf16[96,768]{1,0:T(8,128)(2,1)S(1)}, bf16[96,768]{1,0:T(8,128)(2,1)S(1)}, u32[]{:S(2)}, u32[]{:S(2)}) collective-permute-start(bf16[96,768]{1,0:T(8,128)(2,1)S(1)} %get-tuple-element.107), channel_id=1, source_target_pairs={{0,2},{1,3},{2,0},{3,1},{4,6},{5,7},{6,4},{7,5},{8,10},{9,11},{10,... | collective-permute-start | bytes 442376 | tf_op jit(solution)/shard_map/cut_x1/ppermute | solution.py:1026
  8.9 2.3 %collective-permute-start.5 = (bf16[96,768]{1,0:T(8,128)(2,1)S(1)}, bf16[96,768]{1,0:T(8,128)(2,1)S(1)}, u32[]{:S(2)}, u32[]{:S(2)}) collective-permute-start(bf16[96,768]{1,0:T(8,128)(2,1)S(1)} %collective-permute-done.1.refs_2_), channel_id=1, source_target_pairs={{0,1},{1,0},{2,3},{3,2},{4,5},{5,4},{6,7},{7,6},{8,9},{9,8},{10,11... | collective-permute-start | bytes 442376 | tf_op jit(solution)/shard_map/far_cut_core1/ppermute | solution.py:1026
  8.9 2.3 %collective-permute-start.4 = (bf16[48,768]{1,0:T(8,128)(2,1)S(1)}, bf16[48,768]{1,0:T(8,128)(2,1)S(1)}, u32[]{:S(2)}, u32[]{:S(2)}) collective-permute-start(bf16[48,768]{1,0:T(8,128)(2,1)S(1)} %get-tuple-element.111), channel_id=1, source_target_pairs={{0,1},{1,0},{2,3},{3,2},{4,5},{5,4},{6,7},{7,6},{8,9},{9,8},{10,11... | collective-permute-start | bytes 221192 | tf_op jit(solution)/shard_map/cut_core1/ppermute | solution.py:1026
  9.4 23.4 %collective-permute-start.2 = (bf16[352,768]{1,0:T(8,128)(2,1)S(1)}, bf16[352,768]{1,0:T(8,128)(2,1)S(1)}, u32[]{:S(2)}, u32[]{:S(2)}) collective-permute-start(bf16[352,768]{1,0:T(8,128)(2,1)S(1)} %get-tuple-element.108.refs_0_), channel_id=1, source_target_pairs={{0,2},{1,3},{2,0},{3,1},{4,6},{5,7},{6,4},{7,5},{8,10},{9,11},{10,... | collective-permute-start | bytes 1622024 | tf_op jit(solution)/shard_map/rows_x1/ppermute | solution.py:1026
  11.3 10.8 %collective-permute-start.6 = (bf16[112,768]{1,0:T(8,128)(2,1)S(1)}, bf16[112,768]{1,0:T(8,128)(2,1)S(1)}, u32[]{:S(2)}, u32[]{:S(2)}) collective-permute-start(bf16[112,768]{1,0:T(8,128)(2,1)S(1)} %get-tuple-element.114.refs_0_), channel_id=1, source_target_pairs={{0,16},{1,17},{2,18},{3,19},{4,20},{5,21},{6,22},{7,23},{8,24},{9,... | collective-permute-start | bytes 516104 | tf_op jit(solution)/shard_map/pack_z2/ppermute | solution.py:1026
  13.9 12.1 %collective-permute-start.9 = (bf16[112,768]{1,0:T(8,128)(2,1)S(1)}, bf16[112,768]{1,0:T(8,128)(2,1)S(1)}, u32[]{:S(2)}, u32[]{:S(2)}) collective-permute-start(bf16[112,768]{1,0:T(8,128)(2,1)S(1)} %get-tuple-element.114.refs_0_), channel_id=1, source_target_pairs={{0,8},{1,9},{2,10},{3,11},{4,12},{5,13},{6,14},{7,15},{8,0},{9,1},... | collective-permute-start | bytes 516104 | tf_op jit(solution)/shard_map/pack_z1/ppermute | solution.py:1026
  15.5 12.1 %collective-permute-start.11 = (bf16[112,768]{1,0:T(8,128)(2,1)S(1)}, bf16[112,768]{1,0:T(8,128)(2,1)S(1)}, u32[]{:S(2)}, u32[]{:S(2)}) collective-permute-start(bf16[112,768]{1,0:T(8,128)(2,1)S(1)} %get-tuple-element.114.refs_0_), channel_id=1, source_target_pairs={{0,4},{1,5},{2,6},{3,7},{4,0},{5,1},{6,2},{7,3},{8,12},{9,13},{10,... | collective-permute-start | bytes 516104 | tf_op jit(solution)/shard_map/pack0_y1/ppermute | solution.py:1026
  22.0 9.0 %collective-permute-start.10 = (bf16[112,768]{1,0:T(8,128)(2,1)S(1)}, bf16[112,768]{1,0:T(8,128)(2,1)}, u32[]{:S(2)}, u32[]{:S(2)}) collective-permute-start(bf16[112,768]{1,0:T(8,128)(2,1)S(1)} %collective-permute-done.6.refs_2_), channel_id=1, source_target_pairs={{0,8},{1,9},{2,10},{3,11},{4,12},{5,13},{6,14},{7,15},{8,0},{9,1},... | collective-permute-start | bytes 516104 | tf_op jit(solution)/shard_map/far_pack_z1/ppermute | solution.py:1026
  22.6 16.8 %collective-permute-start.7 = (bf16[192,768]{1,0:T(8,128)(2,1)S(1)}, bf16[192,768]{1,0:T(8,128)(2,1)S(1)}, u32[]{:S(2)}, u32[]{:S(2)}) collective-permute-start(bf16[192,768]{1,0:T(8,128)(2,1)S(1)} %get-tuple-element.115.refs_1_), channel_id=1, source_target_pairs={{0,16},{1,17},{2,18},{3,19},{4,20},{5,21},{6,22},{7,23},{8,24},{9,... | collective-permute-start | bytes 884744 | tf_op jit(solution)/shard_map/both_z2/ppermute | solution.py:1026
  26.0 7.3 %collective-permute-start.12 = (bf16[112,768]{1,0:T(8,128)(2,1)S(1)}, bf16[112,768]{1,0:T(8,128)(2,1)S(1)}, u32[]{:S(2)}, u32[]{:S(2)}) collective-permute-start(bf16[112,768]{1,0:T(8,128)(2,1)S(1)} %collective-permute-done.9.refs_1_.refs_4_), channel_id=1, source_target_pairs={{0,4},{1,5},{2,6},{3,7},{4,0},{5,1},{6,2},{7,3},{8,12},{9,13},{10,... | collective-permute-start | bytes 516104 | tf_op jit(solution)/shard_map/pack1_y1/ppermute | solution.py:1026
  28.2 8.8 %collective-permute-start.13 = (bf16[112,768]{1,0:T(8,128)(2,1)S(1)}, bf16[112,768]{1,0:T(8,128)(2,1)S(1)}, u32[]{:S(2)}, u32[]{:S(2)}) collective-permute-start(bf16[112,768]{1,0:T(8,128)(2,1)S(1)} %collective-permute-done.6.refs_2_), channel_id=1, source_target_pairs={{0,4},{1,5},{2,6},{3,7},{4,0},{5,1},{6,2},{7,3},{8,12},{9,13},{10,... | collective-permute-start | bytes 516104 | tf_op jit(solution)/shard_map/pack2_y1/ppermute | solution.py:1026
  31.0 8.4 %collective-permute-start.14 = (bf16[112,768]{1,0:T(8,128)(2,1)}, bf16[112,768]{1,0:T(8,128)(2,1)}, u32[]{:S(2)}, u32[]{:S(2)}) collective-permute-start(bf16[112,768]{1,0:T(8,128)(2,1)} %collective-permute-done.10.refs_3_), channel_id=1, source_target_pairs={{0,4},{1,5},{2,6},{3,7},{4,0},{5,1},{6,2},{7,3},{8,12},{9,13},{10,... | collective-permute-start | bytes 516104 | tf_op jit(solution)/shard_map/pack3_y1/ppermute | solution.py:1026
  32.7 14.2 %collective-permute-start = (bf16[352,768]{1,0:T(8,128)(2,1)S(1)}, bf16[352,768]{1,0:T(8,128)(2,1)S(1)}, u32[]{:S(2)}, u32[]{:S(2)}) collective-permute-start(bf16[352,768]{1,0:T(8,128)(2,1)S(1)} %get-tuple-element.108.refs_0_), channel_id=1, source_target_pairs={{0,1},{1,0},{2,3},{3,2},{4,5},{5,4},{6,7},{7,6},{8,9},{9,8},{10,11... | collective-permute-start | bytes 1622024 | tf_op jit(solution)/shard_map/rows_core1/ppermute | solution.py:1026
  34.0 14.7 %collective-permute-start.23 = (bf16[192,768]{1,0:T(8,128)(2,1)S(1)}, bf16[192,768]{1,0:T(8,128)(2,1)}, u32[]{:S(2)}, u32[]{:S(2)}) collective-permute-start(bf16[192,768]{1,0:T(8,128)(2,1)S(1)} %get-tuple-element.115.refs_1_), channel_id=1, source_target_pairs={{0,8},{1,9},{2,10},{3,11},{4,12},{5,13},{6,14},{7,15},{8,0},{9,1},... | collective-permute-start | bytes 884744 | tf_op jit(solution)/shard_map/both_z1/ppermute | solution.py:1026
  37.7 16.0 %collective-permute-start.3 = (bf16[352,768]{1,0:T(8,128)(2,1)S(1)}, bf16[352,768]{1,0:T(8,128)(2,1)S(1)}, u32[]{:S(2)}, u32[]{:S(2)}) collective-permute-start(bf16[352,768]{1,0:T(8,128)(2,1)S(1)} %collective-permute-done.2.refs_2_), channel_id=1, source_target_pairs={{0,1},{1,0},{2,3},{3,2},{4,5},{5,4},{6,7},{7,6},{8,9},{9,8},{10,11... | collective-permute-start | bytes 1622024 | tf_op jit(solution)/shard_map/far_rows_core1/ppermute | solution.py:1026
  39.4 12.6 %collective-permute-start.8 = (bf16[192,768]{1,0:T(8,128)(2,1)S(1)}, bf16[192,768]{1,0:T(8,128)(2,1)}, u32[]{:S(2)}, u32[]{:S(2)}) collective-permute-start(bf16[192,768]{1,0:T(8,128)(2,1)S(1)} %collective-permute-done.7.refs_3_), channel_id=1, source_target_pairs={{0,8},{1,9},{2,10},{3,11},{4,12},{5,13},{6,14},{7,15},{8,0},{9,1},... | collective-permute-start | bytes 884744 | tf_op jit(solution)/shard_map/far_both_z1/ppermute | solution.py:1026
  45.3 8.3 %collective-permute-start.16 = (bf16[192,768]{1,0:T(8,128)(2,1)}, bf16[192,768]{1,0:T(8,128)(2,1)}, u32[]{:S(2)}, u32[]{:S(2)}) collective-permute-start(bf16[192,768]{1,0:T(8,128)(2,1)} %get-tuple-element.124.refs_0_), channel_id=1, source_target_pairs={{0,2},{1,3},{2,0},{3,1},{4,6},{5,7},{6,4},{7,5},{8,10},{9,11},{10,... | collective-permute-start | bytes 884744 | tf_op jit(solution)/shard_map/out_x1/ppermute | solution.py:1026
  46.9 10.1 %collective-permute-start.15 = (bf16[192,768]{1,0:T(8,128)(2,1)S(1)}, bf16[192,768]{1,0:T(8,128)(2,1)}, u32[]{:S(2)}, u32[]{:S(2)}) collective-permute-start(bf16[192,768]{1,0:T(8,128)(2,1)S(1)} %get-tuple-element.115.refs_1_), channel_id=1, source_target_pairs={{0,4},{1,5},{2,6},{3,7},{4,0},{5,1},{6,2},{7,3},{8,12},{9,13},{10,... | collective-permute-start | bytes 884744 | tf_op jit(solution)/shard_map/both0_y1/ppermute | solution.py:1026
  48.7 14.6 %collective-permute-start.24 = (bf16[192,768]{1,0:T(8,128)(2,1)}, bf16[192,768]{1,0:T(8,128)(2,1)}, u32[]{:S(2)}, u32[]{:S(2)}) collective-permute-start(bf16[192,768]{1,0:T(8,128)(2,1)} %collective-permute-done.23.refs_2_), channel_id=1, source_target_pairs={{0,4},{1,5},{2,6},{3,7},{4,0},{5,1},{6,2},{7,3},{8,12},{9,13},{10,... | collective-permute-start | bytes 884744 | tf_op jit(solution)/shard_map/both1_y1/ppermute | solution.py:1026
  52.0 20.3 %collective-permute-start.22 = (bf16[192,768]{1,0:T(8,128)(2,1)}, bf16[192,768]{1,0:T(8,128)(2,1)}, u32[]{:S(2)}, u32[]{:S(2)}) collective-permute-start(bf16[192,768]{1,0:T(8,128)(2,1)} %collective-permute-done.8.refs_6_.refs_4_), channel_id=1, source_target_pairs={{0,4},{1,5},{2,6},{3,7},{4,0},{5,1},{6,2},{7,3},{8,12},{9,13},{10,... | collective-permute-start | bytes 884744 | tf_op jit(solution)/shard_map/both3_y1/ppermute | solution.py:1026
  53.6 11.2 %collective-permute-start.17 = (bf16[192,768]{1,0:T(8,128)(2,1)}, bf16[192,768]{1,0:T(8,128)(2,1)}, u32[]{:S(2)}, u32[]{:S(2)}) collective-permute-start(bf16[192,768]{1,0:T(8,128)(2,1)} %collective-permute-done.16.refs_2_), channel_id=1, source_target_pairs={{0,1},{1,0},{2,3},{3,2},{4,5},{5,4},{6,7},{7,6},{8,9},{9,8},{10,11... | collective-permute-start | bytes 884744 | tf_op jit(solution)/shard_map/far_out_core1/ppermute | solution.py:1026
  61.1 11.3 %collective-permute-start.21 = (bf16[192,768]{1,0:T(8,128)(2,1)}, bf16[192,768]{1,0:T(8,128)(2,1)S(1)}, u32[]{:S(2)}, u32[]{:S(2)}) collective-permute-start(bf16[192,768]{1,0:T(8,128)(2,1)} %get-tuple-element.124.refs_0_), channel_id=1, source_target_pairs={{0,1},{1,0},{2,3},{3,2},{4,5},{5,4},{6,7},{7,6},{8,9},{9,8},{10,11... | collective-permute-start | bytes 884744 | tf_op jit(solution)/shard_map/out_core1/ppermute | solution.py:1026
  61.2 11.2 %collective-permute-start.19 = (bf16[736,192]{1,0:T(8,128)(2,1)S(1)}, bf16[736,192]{1,0:T(8,128)(2,1)S(1)}, u32[]{:S(2)}, u32[]{:S(2)}) collective-permute-start(bf16[736,192]{1,0:T(8,128)(2,1)S(1)} %get-tuple-element.123.refs_0_.refs_6_), channel_id=1, source_target_pairs={{0,2},{1,3},{2,0},{3,1},{4,6},{5,7},{6,4},{7,5},{8,10},{9,11},{10,... | collective-permute-start | bytes 847880 | tf_op jit(solution)/shard_map/heads_x1/ppermute | solution.py:1026
  63.3 15.2 %collective-permute-start.25 = (bf16[192,768]{1,0:T(8,128)(2,1)S(1)}, bf16[192,768]{1,0:T(8,128)(2,1)S(1)}, u32[]{:S(2)}, u32[]{:S(2)}) collective-permute-start(bf16[192,768]{1,0:T(8,128)(2,1)S(1)} %copy-done.23), channel_id=1, source_target_pairs={{0,4},{1,5},{2,6},{3,7},{4,0},{5,1},{6,2},{7,3},{8,12},{9,13},{10,... | collective-permute-start | bytes 884744 | tf_op jit(solution)/shard_map/both2_y1/ppermute | solution.py:1026
  64.8 10.3 %collective-permute-start.18 = (bf16[736,192]{1,0:T(8,128)(2,1)S(1)}, bf16[736,192]{1,0:T(8,128)(2,1)S(1)}, u32[]{:S(2)}, u32[]{:S(2)}) collective-permute-start(bf16[736,192]{1,0:T(8,128)(2,1)S(1)} %get-tuple-element.123.refs_0_.refs_6_), channel_id=1, source_target_pairs={{0,1},{1,0},{2,3},{3,2},{4,5},{5,4},{6,7},{7,6},{8,9},{9,8},{10,11... | collective-permute-start | bytes 847880 | tf_op jit(solution)/shard_map/heads_core1/ppermute | solution.py:1026
  72.4 2.8 %collective-permute-start.20 = (bf16[736,192]{1,0:T(8,128)(2,1)S(1)}, bf16[736,192]{1,0:T(8,128)(2,1)S(1)}, u32[]{:S(2)}, u32[]{:S(2)}) collective-permute-start(bf16[736,192]{1,0:T(8,128)(2,1)S(1)} %collective-permute-done.19.refs_2_.refs_8_), channel_id=1, source_target_pairs={{0,1},{1,0},{2,3},{3,2},{4,5},{5,4},{6,7},{7,6},{8,9},{9,8},{10,11... | collective-permute-start | bytes 847880 | tf_op jit(solution)/shard_map/far_heads_core1/ppermute | solution.py:1026
  85.7 3.6 %collective-permute-start.26 = (bf16[368,768]{1,0:T(8,128)(2,1)S(1)}, bf16[368,768]{1,0:T(8,128)(2,1)S(1)}, u32[]{:S(2)}, u32[]{:S(2)}) collective-permute-start(bf16[368,768]{1,0:T(8,128)(2,1)S(1)} %get-tuple-element.140), channel_id=1, source_target_pairs={{0,1},{1,0},{2,3},{3,2},{4,5},{5,4},{6,7},{7,6},{8,9},{9,8},{10,11... | collective-permute-start | bytes 1695752 | tf_op jit(solution)/shard_map/sum_core1/ppermute | solution.py:1026
  87.7 15.3 %collective-permute-start.29 = (bf16[4,96,768]{2,1,0:T(8,128)(2,1)S(1)}, bf16[4,96,768]{2,1,0:T(8,128)(2,1)S(1)}, u32[]{:S(2)}, u32[]{:S(2)}) collective-permute-start(bf16[4,96,768]{2,1,0:T(8,128)(2,1)S(1)} %get-tuple-element.147), channel_id=1, source_target_pairs={{0,4},{1,5},{2,6},{3,7},{4,0},{5,1},{6,2},{7,3},{8,12},{9,13},{10,... | collective-permute-start | bytes 1769480 | tf_op jit(solution)/shard_map/gdown_y1/ppermute | solution.py:1026
  89.4 14.5 %collective-permute-start.28 = (bf16[368,768]{1,0:T(8,128)(2,1)S(1)}, bf16[368,768]{1,0:T(8,128)(2,1)S(1)}, u32[]{:S(2)}, u32[]{:S(2)}) collective-permute-start(bf16[368,768]{1,0:T(8,128)(2,1)S(1)} %add_rows.1.refs_10_.refs_0_), channel_id=1, source_target_pairs={{0,2},{1,3},{2,0},{3,1},{4,6},{5,7},{6,4},{7,5},{8,10},{9,11},{10,... | collective-permute-start | bytes 1695752 | tf_op jit(solution)/shard_map/sum_x1/ppermute | solution.py:1026
  97.0 7.9 %collective-permute-start.27 = (bf16[416,768]{1,0:T(8,128)(2,1)S(1)}, bf16[416,768]{1,0:T(8,128)(2,1)S(1)}, u32[]{:S(2)}, u32[]{:S(2)}) collective-permute-start(bf16[416,768]{1,0:T(8,128)(2,1)S(1)} %get-tuple-element.142), channel_id=1, source_target_pairs={{0,1},{1,0},{2,3},{3,2},{4,5},{5,4},{6,7},{7,6},{8,9},{9,8},{10,11... | collective-permute-start | bytes 1916936 | tf_op jit(solution)/shard_map/m_core1/ppermute | solution.py:1026
  104.0 2.8 %collective-permute-start.30 = (bf16[368,768]{1,0:T(8,128)(2,1)S(1)}, bf16[368,768]{1,0:T(8,128)(2,1)S(1)}, u32[]{:S(2)}, u32[]{:S(2)}) collective-permute-start(bf16[368,768]{1,0:T(8,128)(2,1)S(1)} %add_pair.1.refs_0_), channel_id=1, source_target_pairs={{0,1},{1,0},{2,3},{3,2},{4,5},{5,4},{6,7},{7,6},{8,9},{9,8},{10,11... | collective-permute-start | bytes 1695752 | tf_op jit(solution)/shard_map/total_core1/ppermute | solution.py:1026
  104.1 16.2 %collective-permute-start.33 = (bf16[4,96,768]{2,1,0:T(8,128)(2,1)S(1)}, bf16[4,96,768]{2,1,0:T(8,128)(2,1)S(1)}, u32[]{:S(2)}, u32[]{:S(2)}) collective-permute-start(bf16[4,96,768]{2,1,0:T(8,128)(2,1)S(1)} %get-tuple-element.170), channel_id=1, source_target_pairs={{0,4},{1,5},{2,6},{3,7},{4,0},{5,1},{6,2},{7,3},{8,12},{9,13},{10,... | collective-permute-start | bytes 1769480 | tf_op jit(solution)/shard_map/gup_y1/ppermute | solution.py:1026
  104.9 18.2 %collective-permute-start.36 = (bf16[2,96,768]{2,1,0:T(8,128)(2,1)S(1)}, bf16[2,96,768]{2,1,0:T(8,128)(2,1)S(1)}, u32[]{:S(2)}, u32[]{:S(2)}) collective-permute-start(bf16[2,96,768]{2,1,0:T(8,128)(2,1)S(1)} %get-tuple-element.176), channel_id=1, source_target_pairs={{0,8},{1,9},{2,10},{3,11},{4,12},{5,13},{6,14},{7,15},{8,0},{9,1},... | collective-permute-start | bytes 884744 | tf_op jit(solution)/shard_map/gdown_z1/ppermute | solution.py:1026
  111.0 16.7 %collective-permute-start.39 = (bf16[4,112,384]{2,1,0:T(8,128)(2,1)S(1)}, bf16[4,112,384]{2,1,0:T(8,128)(2,1)S(1)}, u32[]{:S(2)}, u32[]{:S(2)}) collective-permute-start(bf16[4,112,384]{2,1,0:T(8,128)(2,1)S(1)} %get-tuple-element.185), channel_id=1, source_target_pairs={{0,4},{1,5},{2,6},{3,7},{4,0},{5,1},{6,2},{7,3},{8,12},{9,13},{10,... | collective-permute-start | bytes 1032200 | tf_op jit(solution)/shard_map/ga_y1/ppermute | solution.py:1026
  117.9 11.9 %collective-permute-start.31 = (bf16[416,768]{1,0:T(8,128)(2,1)S(1)}, bf16[416,768]{1,0:T(8,128)(2,1)S(1)}, u32[]{:S(2)}, u32[]{:S(2)}) collective-permute-start(bf16[416,768]{1,0:T(8,128)(2,1)S(1)} %get-tuple-element.161.refs_2_), channel_id=1, source_target_pairs={{0,1},{1,0},{2,3},{3,2},{4,5},{5,4},{6,7},{7,6},{8,9},{9,8},{10,11... | collective-permute-start | bytes 1916936 | tf_op jit(solution)/shard_map/h_core1/ppermute | solution.py:1026
  120.5 13.2 %collective-permute-start.34 = (bf16[2,96,768]{2,1,0:T(8,128)(2,1)S(1)}, bf16[2,96,768]{2,1,0:T(8,128)(2,1)S(1)}, u32[]{:S(2)}, u32[]{:S(2)}) collective-permute-start(bf16[2,96,768]{2,1,0:T(8,128)(2,1)S(1)} %get-tuple-element.172), channel_id=1, source_target_pairs={{0,8},{1,9},{2,10},{3,11},{4,12},{5,13},{6,14},{7,15},{8,0},{9,1},... | collective-permute-start | bytes 884744 | tf_op jit(solution)/shard_map/gup_z1/ppermute | solution.py:1026
  122.4 12.7 %collective-permute-start.38 = (bf16[4,96,384]{2,1,0:T(8,128)(2,1)S(1)}, bf16[4,96,384]{2,1,0:T(8,128)(2,1)S(1)}, u32[]{:S(2)}, u32[]{:S(2)}) collective-permute-start(bf16[4,96,384]{2,1,0:T(8,128)(2,1)S(1)} %get-tuple-element.182), channel_id=1, source_target_pairs={{0,4},{1,5},{2,6},{3,7},{4,0},{5,1},{6,2},{7,3},{8,12},{9,13},{10,... | collective-permute-start | bytes 884744 | tf_op jit(solution)/shard_map/gb_y1/ppermute | solution.py:1026
  123.3 18.2 %collective-permute-start.37 = (bf16[96,768]{1,0:T(8,128)(2,1)S(1)}, bf16[96,768]{1,0:T(8,128)(2,1)S(1)}, u32[]{:S(2)}, u32[]{:S(2)}) collective-permute-start(bf16[96,768]{1,0:T(8,128)(2,1)S(1)} %get-tuple-element.179), channel_id=1, source_target_pairs={{0,16},{1,17},{2,18},{3,19},{4,20},{5,21},{6,22},{7,23},{8,24},{9,... | collective-permute-start | bytes 442376 | tf_op jit(solution)/shard_map/gdown_z2/ppermute | solution.py:1026
  127.8 9.5 %collective-permute-start.40 = (bf16[2,112,384]{2,1,0:T(8,128)(2,1)S(1)}, bf16[2,112,384]{2,1,0:T(8,128)(2,1)S(1)}, u32[]{:S(2)}, u32[]{:S(2)}) collective-permute-start(bf16[2,112,384]{2,1,0:T(8,128)(2,1)S(1)} %get-tuple-element.187), channel_id=1, source_target_pairs={{0,8},{1,9},{2,10},{3,11},{4,12},{5,13},{6,14},{7,15},{8,0},{9,1},... | collective-permute-start | bytes 516104 | tf_op jit(solution)/shard_map/ga_z1/ppermute | solution.py:1026
  133.7 13.9 %collective-permute-start.35 = (bf16[96,768]{1,0:T(8,128)(2,1)S(1)}, bf16[96,768]{1,0:T(8,128)(2,1)S(1)}, u32[]{:S(2)}, u32[]{:S(2)}) collective-permute-start(bf16[96,768]{1,0:T(8,128)(2,1)S(1)} %get-tuple-element.174), channel_id=1, source_target_pairs={{0,16},{1,17},{2,18},{3,19},{4,20},{5,21},{6,22},{7,23},{8,24},{9,... | collective-permute-start | bytes 442376 | tf_op jit(solution)/shard_map/gup_z2/ppermute | solution.py:1026
  134.2 25.1 %collective-permute-start.32 = (bf16[416,768]{1,0:T(8,128)(2,1)S(1)}, bf16[416,768]{1,0:T(8,128)(2,1)S(1)}, u32[]{:S(2)}, u32[]{:S(2)}) collective-permute-start(bf16[416,768]{1,0:T(8,128)(2,1)S(1)} %get-tuple-element.163), channel_id=1, source_target_pairs={{0,2},{1,3},{2,0},{3,1},{4,6},{5,7},{6,4},{7,5},{8,10},{9,11},{10,... | collective-permute-start | bytes 1916936 | tf_op jit(solution)/shard_map/mh_x1/ppermute | solution.py:1026
  137.3 12.1 %collective-permute-start.41 = (bf16[112,384]{1,0:T(8,128)(2,1)S(1)}, bf16[112,384]{1,0:T(8,128)(2,1)S(1)}, u32[]{:S(2)}, u32[]{:S(2)}) collective-permute-start(bf16[112,384]{1,0:T(8,128)(2,1)S(1)} %get-tuple-element.189), channel_id=1, source_target_pairs={{0,16},{1,17},{2,18},{3,19},{4,20},{5,21},{6,22},{7,23},{8,24},{9,... | collective-permute-start | bytes 258056 | tf_op jit(solution)/shard_map/ga_z2/ppermute | solution.py:1026
  140.2 9.2 %collective-permute-start.44 = (bf16[96,384]{1,0:T(8,128)(2,1)S(1)}, bf16[96,384]{1,0:T(8,128)(2,1)S(1)}, u32[]{:S(2)}, u32[]{:S(2)}) collective-permute-start(bf16[96,384]{1,0:T(8,128)(2,1)S(1)} %get-tuple-element.194), channel_id=1, source_target_pairs={{0,24},{1,25},{2,26},{3,27},{4,28},{5,29},{6,30},{7,31},{8,16},{9,... | collective-permute-start | bytes 221192 | tf_op jit(solution)/shard_map/gb_z3/ppermute | solution.py:1026
  141.5 7.9 %collective-permute-start.42 = (bf16[96,384]{1,0:T(8,128)(2,1)S(1)}, bf16[96,384]{1,0:T(8,128)(2,1)S(1)}, u32[]{:S(2)}, u32[]{:S(2)}) collective-permute-start(bf16[96,384]{1,0:T(8,128)(2,1)S(1)} %get-tuple-element.190), channel_id=1, source_target_pairs={{0,8},{1,9},{2,10},{3,11},{4,12},{5,13},{6,14},{7,15},{8,0},{9,1},... | collective-permute-start | bytes 221192 | tf_op jit(solution)/shard_map/gb_z1/ppermute | solution.py:1026
  147.6 5.3 %collective-permute-start.43 = (bf16[96,384]{1,0:T(8,128)(2,1)S(1)}, bf16[96,384]{1,0:T(8,128)(2,1)S(1)}, u32[]{:S(2)}, u32[]{:S(2)}) collective-permute-start(bf16[96,384]{1,0:T(8,128)(2,1)S(1)} %get-tuple-element.192), channel_id=1, source_target_pairs={{0,16},{1,17},{2,18},{3,19},{4,20},{5,21},{6,22},{7,23},{8,24},{9,... | collective-permute-start | bytes 221192 | tf_op jit(solution)/shard_map/gb_z2/ppermute | solution.py:1026
  153.6 5.1 %collective-permute-start.46 = (bf16[96,768]{1,0:T(8,128)(2,1)S(1)}, bf16[96,768]{1,0:T(8,128)(2,1)S(1)}, u32[]{:S(2)}, u32[]{:S(2)}) collective-permute-start(bf16[96,768]{1,0:T(8,128)(2,1)S(1)} %get-tuple-element.198), channel_id=1, source_target_pairs={{0,2},{1,3},{2,0},{3,1},{4,6},{5,7},{6,4},{7,5},{8,10},{9,11},{10,... | collective-permute-start | bytes 442376 | tf_op jit(solution)/shard_map/grads_x1/ppermute | solution.py:1026
  158.8 2.0 %collective-permute-start.47 = (bf16[96,768]{1,0:T(8,128)(2,1)S(1)}, bf16[96,768]{1,0:T(8,128)(2,1)S(1)}, u32[]{:S(2)}, u32[]{:S(2)}) collective-permute-start(bf16[96,768]{1,0:T(8,128)(2,1)S(1)} %collective-permute-done.46.refs_2_), channel_id=1, source_target_pairs={{0,1},{1,0},{2,3},{3,2},{4,5},{5,4},{6,7},{7,6},{8,9},{9,8},{10,11... | collective-permute-start | bytes 442376 | tf_op jit(solution)/shard_map/far_grads_core1/ppermute | solution.py:1026
  158.8 1.9 %collective-permute-start.45 = (bf16[48,768]{1,0:T(8,128)(2,1)S(1)}, bf16[48,768]{1,0:T(8,128)(2,1)S(1)}, u32[]{:S(2)}, u32[]{:S(2)}) collective-permute-start(bf16[48,768]{1,0:T(8,128)(2,1)S(1)} %get-tuple-element.196), channel_id=1, source_target_pairs={{0,1},{1,0},{2,3},{3,2},{4,5},{5,4},{6,7},{7,6},{8,9},{9,8},{10,11... | collective-permute-start | bytes 221192 | tf_op jit(solution)/shard_map/grads_core1/ppermute | solution.py:1026
  (39 other events, 252.4 us)

commit v4 on v3

--- a/solution.py
+++ b/solution.py
@@ -376,22 +376,24 @@
 
 
 PAD_ID = 99
-TUNE = {'after_add_pieces': 'y_gdown', 'after_add_rows': 'branch_rows raise_rows pack_z1', 'after_attend': 'both0_y1', 'after_both2_y1': 'both1_y1', 'after_branch_rows': 'far_out_core1 order_out out_core1', 'after_far_cut_core1': 'pick_pieces', 'after_far_heads_core1': '', 'after_far_out_core1': '', 'after_far_rows_core1': 'pick_pieces', 'after_finish_rows': '', 'after_gb_y1': 'score_back', 'after_gb_z2': 'gdown_z2', 'after_gb_z3': 'h_core1', 'after_gdown_y1': 'raise_rows', 'after_gdown_z1': 'm_core1', 'after_gdown_z2': 'total_core1', 'after_grads_x1': 'project_back pick_grads', 'after_half_gdown': 'branch_back gdown_z1', 'after_heads_core1': 'far_out_core1', 'after_heads_x1': 'out_x1', 'after_join_pieces': 'pick_pieces', 'after_lower_rows': '', 'after_norm_rows_in': 'far_both_z1', 'after_open_pack': '', 'after_order_out': 'both3_y1', 'after_out_x1': 'both_z2', 'after_raise_rows': 'far_rows_core1', 'after_total_core1': 'out_core1', 'after_y_gdown': '', 'after_y_gup': '', 'half_down': 2, 'us_add_pair': 0.002, 'us_branch_back': 0.2, 'us_branch_rows': 6, 'us_down_grads': 45.0, 'us_finish_rows': 0.001, 'us_half_gdown': 0.035, 'us_half_gup': 0.001, 'us_join_grads': 0.11, 'us_join_pieces': 21.0, 'us_lower_rows': 111.0, 'us_mlp_grads': 12, 'us_open_pack': 3.6, 'us_order_out': 48.0, 'us_pick_grads': 0.001, 'us_pick_pieces': 7.5, 'us_score_back': 0.42, 'us_y_gup': 7.0, 'us_z_gdown': 0.001, 'us_z_gup': 0.07}
-
-
-def knob(name, default, among=None):
-    KNOBS.setdefault(name, (default, list(among) if among is not None else None))
-    return TUNE.get(name, default)
-
-
-def wait_for(name, default=""):
-    chosen = knob("after_" + name, default, MARK)
-    return [MARK[c] for c in chosen.split() if c in MARK]
-
-
-MARK = {}
-KNOBS = {}
-COST = {'pick_pieces': 1.5, 'join_pieces': 0.7, 'norm_rows_in': 2, 'open_pack': 1.2, 'attend': 4, 'order_out': 1.6, 'branch_rows': 2, 'raise_rows': 2.8, 'down_grads': 1.5, 'lower_rows': 3.7, 'add_rows': 0.9, 'mlp_grads': 4, 'add_pair': 0.9, 'branch_back': 4, 'score_back': 4.2, 'project_back': 1.3, 'add_pieces': 1.2, 'pick_grads': 0.7, 'finish_rows': 1.4, 'join_grads': 1.1}
+PLAN = (
+    (45.0, ()), (0, (0,)), (0, (0,)), (0, (2,)), (7.0, ()), (0, ()), (0, ()), (0, (0,)), (0, ()), (0, (6,)),
+    (0, ()), (0, (0,)), (0, ()), (0, (5,)), (0, (5, 12, 1)), (0, ()), (0, ()), (0.2, (9,)), (0, ()),
+    (0, (11,)), (0.36, (8,)), (0, ()), (40, (3,)), (0, ()), (0, ()), (0, (19,)), (0, ()), (0, ()),
+    (0, (22, 6)), (1.6, ()), (0, (29,)), (0, ()), (0.001, (21, 23)), (0.84, (31, 24)), (0.185, (33,)),
+    (0, (34,)), (27.0, (19, 34)), (0, (33, 25)), (1.5, (31,)), (0, (33,)), (0.6, (36,)), (0, (40, 9)),
+    (2.0, (40,)), (0, (30, 31)), (0.7, ()), (0, ()), (0.54, (44,)), (0, (36,)), (0.001, ()), (0, (48,)),
+    (0.001, ()), (0, ()), (0.35, ()), (0, ()), (21.0, ()), (0, ()), (0.001, (46,)), (0, (56, 43)),
+    (3.6, (37, 22)), (0, ()), (0.001, (39, 44)), (0, (47,)), (0.14, ()), (0, ()), (0.21, (58,)), (0, ()),
+    (0, (64,)), (0, ()), (0.7, ()), (0, (60,)), (0.001, ()), (0.002, (70,)), (0.35, (71,)), (0.001, (72,)),
+    (0.07, ()), (0, ()), (0, ()), (0, (76, 75)), (0.42, (75,)), (11.0, (78,)),
+)
+STEPS = []
+
+
+def plan():
+    us, steps = PLAN[len(STEPS)]
+    return us, [STEPS[i] for i in steps]
 
 
 def mm(a, b):
@@ -464,9 +466,8 @@
         self.copies.append(copy)
 
 
-def call(kernel, outs, ins, scratch=(), limit=20, after="", label=None):
-    label = label or kernel.__name__
-    after = wait_for(label, after)
+def call(kernel, outs, ins, scratch=(), limit=20):
+    us, after = plan()
     far = [i for i, v in enumerate(ins) if isinstance(v, Far)]
     far_out = [i for i, v in enumerate(outs) if isinstance(v, Far)]
     plain = [v.value if isinstance(v, (Far, Keep)) else v for v in ins]
@@ -516,10 +517,10 @@
         out_specs=tuple(away if i in far_out else near for i in range(len(outs))),
         scratch_shapes=[*scratch, *room],
         compiler_params=pltpu.CompilerParams(vmem_limit_bytes=limit * 2**20),
-        cost_estimate=pl.CostEstimate(flops=int(knob("us_" + label, COST.get(kernel.__name__, 0.7)) * 10**9), bytes_accessed=0, transcendentals=0),
+        cost_estimate=pl.CostEstimate(flops=int(us * 10**9), bytes_accessed=0, transcendentals=0),
         name=kernel.__name__,
     )(*[placed(v) for v in ins], *after)
-    MARK[label] = made_arrays[0]
+    STEPS.append(made_arrays[0])
     return made_arrays
 
 
@@ -721,9 +722,25 @@
 
 def down_grads(active, grad_mlp, away, kept, active_kept, work):
     active_kept.go(source=active)
+    _, _, _, z, _ = here()
+    work[...] = mm_tn(active[...], grad_mlp[...])
+    for pair in range(2):
+        for side in range(2):
+            ours = pl.multiple_of(((z ^ (2 * pair)) * 2 + side) * 96, 8)
+            theirs = pl.multiple_of(((z ^ (2 * pair + 1)) * 2 + side) * 96, 8)
+            kept[pair * 2 + side] = work[pl.ds(ours, 96), :]
+            away[pair * 2 + side] = work[pl.ds(theirs, 96), :].astype(BF16)
+
+
+def sum_fours(kept, came, own, away):
+    own[...] = kept[0:2] + came[0:2].astype(F32)
+    away[...] = (kept[2:4] + came[2:4].astype(F32)).astype(BF16)
+
+
+def sum_sides(kept, came, own, away):
     y = here()[4]
-    work[...] = mm_tn(active[...], grad_mlp[...])
-    halve(work, y, away, kept, 96)
+    own[...] = kept[y] + came[y].astype(F32)
+    away[...] = (kept[1 - y] + came[1 - y].astype(F32)).astype(BF16)
 
 
 def lower_rows(slope, grad_mlp, w_up, w_down, away, kept, grad_hidden, work):
@@ -760,17 +777,22 @@
         kept[zz] = grad_f[ours, 0 : away.shape[2]]
 
 
-def mlp_grads(
-    active, normed, grad_hidden, w_down, cots, targets, head_0, head_1, head_2, head_3,
-    up_away, up_kept, rows_away, rows_kept, scale_grad, chosen, work, pieces,
+def up_grads(normed, grad_hidden, away, kept, work):
+    y = here()[4]
+    work[...] = mm_tn(normed.ready()[...], grad_hidden.ready()[...])
+    halve(work, y, away, kept, 96)
+
+
+def mlp_rows(
+    active, w_down, cots, targets, head_0, head_1, head_2, head_3,
+    rows_away, rows_kept, scale_grad, chosen, work, pieces,
 ):
-    place, _, _, _, y = here()
-    work[0:768, :] = mm_tn(normed.ready()[...], grad_hidden.ready()[...])
-    halve(work, y, up_away, up_kept, 96)
-    active, w_down, cots = active.ready(), w_down.ready(), cots.ready()
+    place = here()[0]
+    active, w_down = active.ready(), w_down.ready()
     for m in range(MICRO):
         at = slice(m * 368, m * 368 + 368)
         work[at, :] = mm(active[at, :], w_down[...])
+    cots = cots.ready()
     total = jnp.zeros((8, 768), F32)
     for at in row_blocks(32):
         total = total + fold(cots[at, :].astype(F32) * work[at, :])
@@ -871,8 +893,9 @@
             delta = jnp.sum(moved, -1, keepdims=True)
             grad_score = (moved - wide * delta).astype(BF16)
             grads[0].append(mm(grad_score, k) * SCORE_SCALE)
-            grads[1].append(mm_tn(grad_score, q))
-        grad_qk[at, :] = jnp.concatenate(grads[0] + grads[1], -1).astype(BF16)
+            grads[1].append(mm_tn(q, grad_score))
+        grad_qk[at, 0:192] = jnp.concatenate(grads[0], -1).astype(BF16)
+        grad_qk[at, 192:384] = jnp.concatenate(grads[1], 0).T.astype(BF16)
     work[...] = mm_tn(normed[...], grad_qk[...])
     halve(work, y, away, kept, 96)
 
@@ -1006,7 +1029,7 @@
     grad_gains[3:4, :] = scales[1:2, :]
 
 
-def send(rows, axis, step, label, after=""):
+def send(rows, axis, step):
     pairs = []
     for group in range(8):
         z, y = group // 2, group % 2
@@ -1018,79 +1041,71 @@
                 "z": ((z ^ step) * 2 + y, place),
             }[axis]
             pairs.append((group * 4 + place, target[0] * 4 + target[1]))
-    label = f"{label}_{axis}{step}"
-    ready = wait_for(label, after)
+    _, ready = plan()
     if ready:
         rows = lax.optimization_barrier((rows, *ready))[0]
-    with jax.named_scope(label):
-        MARK[label] = lax.ppermute(rows, ("dp", "blk"), pairs)
-    return MARK[label]
-
-
-def gather_z(chunk, label, after=""):
-    second = send(chunk, "z", 2, label, after)
-    return [chunk, send(chunk, "z", 1, label, after), second, send(second, "z", 1, f"far_{label}")]
-
-
-def gather_y(along_z, label):
-    return along_z + [send(part, "y", 1, f"{label}{k}") for k, part in enumerate(along_z)]
-
-
-def add_y(kept, came, label, after):
+    STEPS.append(lax.ppermute(rows, ("dp", "blk"), pairs))
+    return STEPS[-1]
+
+
+def add_y(kept, came):
     rows, width = kept.shape[1:]
     own, *parts = call(
         sum_y,
         [Keep(sds(rows, width, dtype=F32))] + [sds(rows, width)] * 3,
         [Keep(kept), came],
-        after=after,
-        label="y_" + label,
-    )
-    return [own, *[send(part, "z", k, label) for k, part in zip((1, 2, 3), parts)]]
-
-
-def halve_y(kept, came, label, after):
+    )
+    return [own, *[send(part, "z", k) for k, part in zip((1, 2, 3), parts)]]
+
+
+def halve_y(kept, came):
     rows, width = kept.shape[1:]
     own, away = call(
         sum_y_pairs,
         [Keep(sds(2, rows, width, dtype=F32)), sds(2, rows, width)],
         [Keep(kept), came],
-        after=after,
-        label="y_" + label,
-    )
-    return own, send(away, "z", 1, label)
-
-
-def halve_z(pair, label, after):
+    )
+    return own, send(away, "z", 1)
+
+
+def halve_z(pair):
     kept, came = pair
     rows, width = kept.shape[1:]
     own, away = call(
         sum_pairs,
         [Keep(sds(rows, width, dtype=F32)), sds(rows, width)],
         [Keep(kept), came],
-        after=after,
-        label="half_" + label,
-    )
-    return own, send(away, "z", 2, label)
-
-
-def add_last(last, label, after):
+    )
+    return own, send(away, "z", 2)
+
+
+def side_y(kept, came):
+    own, away = call(
+        sum_sides,
+        [Keep(sds(96, 768, dtype=F32)), sds(96, 768)],
+        [Keep(kept), came],
+    )
+    return own, send(away, "y", 1)
+
+
+def add_last(last):
     own, came = last
     return call(
-        sum_last, [sds(*own.shape, dtype=F32)], [Keep(own), came], after=after, label="z_" + label
+        sum_last, [sds(*own.shape, dtype=F32)], [Keep(own), came]
     )[0]
 
 
-def add_z(steps, label, after):
+def add_z(steps):
     own, *came = steps
     return call(
-        sum_z, [sds(*own.shape, dtype=F32)], [Keep(own), *came], after=after, label="z_" + label
+        sum_z, [sds(*own.shape, dtype=F32)], [Keep(own), *came]
     )[0]
 
 
 def on_device_split(
     patches, special, image_ids, w_qkv, w_out, w_up, w_down, gains, cot_patches, cot_special
 ):
-    MARK.clear()
+    STEPS.clear()
     place = lax.axis_index("blk")
     spec_ids = jnp.concatenate(
         [jnp.arange(10, dtype=jnp.int32) // SPECIAL, jnp.full((6,), PAD_ID, jnp.int32)]
@@ -1107,36 +1122,41 @@
         [Far(w_qkv), Far(w_up), Far(gains), Far(patches), Far(cot_patches)],
         [pltpu.VMEM((4, 48, 768), F32)],
     )
-    came_far = send(far, "x", 1, "cut")
-    came_near, came_near_far = send(near, "core", 1, "cut"), send(came_far, "core", 1, "far_cut")
+    came_far = send(far, "x", 1)
+    came_near, came_near_far = send(near, "core", 1), send(came_far, "core", 1)
     pack, both = call(
         join_pieces,
         [sds(112, 768), sds(192, 768)],
         [own, came_near, came_far, came_near_far, w_out, w_down],
         [pltpu.VMEM((112, 768), F32), pltpu.VMEM((96, 768), F32)],
     )
-    pack_z = gather_z(pack, "pack")
-    far_rows = send(rows, "x", 1, "rows", "cut_x1")
-    near_rows = send(rows, "core", 1, "rows")
-    row_parts = [rows, near_rows, far_rows, send(far_rows, "core", 1, "far_rows", "pack_z1")]
-    pack_chunks = gather_y(pack_z, "pack")
-    both_z = gather_z(both, "both", "pack_z2")
+    pack_2 = send(pack, "z", 2)
+    pack_1 = send(pack, "z", 1)
+    pack_y0 = send(pack, "y", 1)
+    far_rows = send(rows, "x", 1)
+    both_y0 = send(both, "y", 1)
+    pack_y1 = send(pack_1, "y", 1)
+    pack_3 = send(pack_2, "z", 1)
+    pack_y2 = send(pack_2, "y", 1)
+    both_2 = send(both, "z", 2)
+    both_1 = send(both, "z", 1)
+    near_rows = send(rows, "core", 1)
+    row_parts = [rows, near_rows, far_rows, send(far_rows, "core", 1)]
     unit, tokens, cots = call(
         norm_rows_in,
         [Keep(sds(736, 768, dtype=F32)), *[Far(sds(736, 768))] * 2],
         [*row_parts, special, cot_special],
         [pltpu.VMEM((736, 768), F32)],
-        after="pack_z2",
-    )
+    )
+    pack_y3 = send(pack_3, "y", 1)
+    both_y1 = send(both_1, "y", 1)
     qkv_full, out_part, gain_rows = call(
         open_pack,
         [Keep(sds(768, 576)), sds(192, 768), Keep(sds(8, 768, dtype=F32))],
-        pack_chunks,
+        [pack, pack_1, pack_2, pack_3, pack_y0, pack_y1, pack_y2, pack_y3],
         [pltpu.VMEM((192, 768), F32), pltpu.VMEM((8, 16, 768), F32)],
-        after="norm_rows_in",
-    )
-    far_out = send(out_part, "x", 1, "out")
-    both_chunks = gather_y(both_z, "both")
+    )
+    far_out = send(out_part, "x", 1)
     attended, qkv_far, normed_far, projected, probs = call(
         attend,
         [
@@ -1145,11 +1165,14 @@
         ],
         [ids_col, ids_row, *keep(unit, qkv_full, gain_rows)],
     )
-    far_heads = send(attended, "x", 1, "heads")
+    far_heads = send(attended, "x", 1)
+    both_3 = send(both_2, "z", 1)
+    both_y2 = send(both_2, "y", 1)
     out_parts = [
-        out_part, send(out_part, "core", 1, "out", "attend"),
-        far_out, send(far_out, "core", 1, "far_out", "attend"),
+        out_part, send(out_part, "core", 1),
+        far_out, send(far_out, "core", 1),
     ]
+    both_y3 = send(both_3, "y", 1)
     out_full, out_mine, grad_mlp = call(
         order_out,
         [Keep(sds(768, 768)), Far(sds(192, 768)), Far(sds(736, 768))],
@@ -1157,9 +1180,10 @@
         [pltpu.VMEM((768, 768), F32)],
     )
     heads = [
-        attended, send(attended, "core", 1, "heads"),
-        far_heads, send(far_heads, "core", 1, "far_heads", "order_out"),
+        attended, send(attended, "core", 1),
+        far_heads, send(far_heads, "core", 1),
     ]
+    both_chunks = [both, both_1, both_2, both_3, both_y0, both_y1, both_y2, both_y3]
     normed_mlp, branch, middle = call(
         branch_rows,
         [Keep(sds(736, 768)), Far(sds(736, 768)), Far(sds(736, 768, dtype=F32))],
@@ -1177,35 +1201,48 @@
     )
     half = [sds(4, 96, 768), Keep(sds(4, 96, 768, dtype=F32))]
     rows_split = [sds(416, 768), Keep(sds(416, 768, dtype=F32))]
-    down_away, down_kept, active = call(
-        down_grads,
-        [*half, Far(sds(736, 768), held=False)],
-        [Keep(active), grad_mlp],
-        [pltpu.VMEM((768, 768), F32)],
-    )
-    down_came = send(down_away, "y", 1, "gdown")
+
+    def make_down(active):
+        return call(
+            down_grads,
+            [*half, Far(sds(736, 768), held=False)],
+            [Keep(active), grad_mlp],
+            [pltpu.VMEM((768, 768), F32)],
+        )
+
     sum_away, sum_kept, grad_hidden = call(
         lower_rows,
         [sds(368, 768), Keep(sds(368, 768, dtype=F32)), Far(sds(736, 768))],
         [Keep(slope), grad_mlp, *keep(up_full, down_full)],
         [pltpu.VMEM((2, 368, 768), F32)],
-        after="down_grads",
-    )
-    sum_came = send(sum_away, "core", 1, "sum")
+    )
+    sum_came = send(sum_away, "core", 1)
     chip_sum = call(add_rows, [sds(368, 768)], [Keep(sum_kept), sum_came])[0]
-    chip_came = send(chip_sum, "x", 1, "sum")
-    up_away, up_kept, m_away, m_kept, scale_mlp, chosen = call(
-        mlp_grads,
-        [*half, *rows_split, *keep(sds(8, 768, dtype=F32), sds(736, 192))],
-        [*[Far(v) for v in (active, normed_mlp, grad_hidden, down_far, cots)], targets, *heads],
-        [pltpu.VMEM((768, 768), F32), pltpu.VMEM((4, 208, 768), F32)],
-        after="add_rows",
-    )
-    up_came = send(up_away, "y", 1, "gup")
-    m_came = send(m_away, "core", 1, "m")
-    down_steps = halve_y(down_kept, down_came, "gdown", "mlp_grads")
-    sum_own = call(add_pair, [sds(368, 768)], [chip_sum, chip_came], after="y_gdown")[0]
-    sum_near = send(sum_own, "core", 1, "total")
+    chip_came = send(chip_sum, "x", 1)
+    down_away, down_kept, active = make_down(active)
+    down_came = send(down_away, "z", 1)
+    up_away, up_kept = call(
+        up_grads,
+        half,
+        [Far(normed_mlp), Far(grad_hidden)],
+        [pltpu.VMEM((768, 768), F32)],
+    )
+    up_came = send(up_away, "y", 1)
+    m_away, m_kept, scale_mlp, chosen = call(
+        mlp_rows,
+        [*rows_split, *keep(sds(8, 768, dtype=F32), sds(736, 192))],
+        [*[Far(v) for v in (active, down_far, cots)], targets, *heads],
+        [pltpu.VMEM((736, 768), F32), pltpu.VMEM((4, 208, 768), F32)],
+    )
+    m_came = send(m_away, "core", 1)
+    down_two, down_away = call(
+        sum_fours,
+        [Keep(sds(2, 96, 768, dtype=F32)), sds(2, 96, 768)],
+        [Keep(down_kept), down_came],
+    )
+    down_came = send(down_away, "z", 2)
+    sum_own = call(add_pair, [sds(368, 768)], [chip_sum, chip_came])[0]
+    sum_near = send(sum_own, "core", 1)
     grad_rows, grad_heads, grad_v, a_away, a_kept = call(
         branch_back,
         [
@@ -1221,79 +1258,57 @@
             pltpu.VMEM((768, 768), F32), pltpu.VMEM((192, 768), F32), pltpu.VMEM((896, 384), F32),
         ],
     )
-    a_came = send(a_away, "y", 1, "ga")
-    order = knob("up_steps", 1, [0, 1, 2])
-    if order == 0:
-        up_steps = halve_y(up_kept, up_came, "gup", "branch_back")
-    when = knob("half_down", 0, [0, 1, 2])
-    if when == 0:
-        down_last = halve_z(down_steps, "gdown", "branch_back")
+    a_came = send(a_away, "y", 1)
     grad_qk, b_away, b_kept = call(
         score_back,
         [Keep(sds(736, 384)), sds(4, 96, 384), Keep(sds(4, 96, 384, dtype=F32))],
         [probs, projected, Keep(grad_heads), normed_far],
         [pltpu.VMEM((768, 384), F32)],
     )
-    b_came = send(b_away, "y", 1, "gb")
-    early_a = knob("early_a", False)
-    if early_a:
-        a_pair = halve_y(a_kept, a_came, "ga", "score_back")
-    if order == 1:
-        up_steps = halve_y(up_kept, up_came, "gup", "score_back")
+    b_came = send(b_away, "y", 1)
+    a_pair = halve_y(a_kept, a_came)
+    up_steps = halve_y(up_kept, up_came)
     h_away, h_kept = call(
         project_back,
         rows_split,
         [*keep(grad_qk, grad_v), qkv_far],
         [pltpu.VMEM((736, 768), F32), pltpu.VMEM((4, 208, 768), F32)],
     )
-    h_came = send(h_away, "core", 1, "h")
-    if when == 1:
-        down_last = halve_z(down_steps, "gdown", "project_back")
-    if order == 2:
-        up_steps = halve_y(up_kept, up_came, "gup", "project_back")
+    h_came = send(h_away, "core", 1)
     stay, go = call(
         add_pieces,
         [Keep(sds(416, 768, dtype=F32)), sds(416, 768)],
         [Keep(m_kept), m_came, Keep(h_kept), h_came],
     )
-    far_rows = send(go, "x", 1, "mh")
-    if when == 2:
-        down_last = halve_z(down_steps, "gdown", "add_pieces")
-    up_last = None
-    if knob("half_up", True):
-        up_last = halve_z(up_steps, "gup", "add_pieces")
-    if not early_a:
-        a_pair = halve_y(a_kept, a_came, "ga", "project_back")
-    b_steps = add_y(b_kept, b_came, "gb", "add_pieces")
-    a_last = halve_z(a_pair, "ga", "y_gb")
-    if up_last is None:
-        up_last = halve_z(up_steps, "gup", "y_gb")
-    grad_down = add_last(down_last, "gdown", "y_gb")
-    grad_up_rows = add_last(up_last, "gup", "z_gdown")
-    first_rows = add_last(a_last, "ga", "z_gup")
-    second_rows = add_z(b_steps, "gb", "z_ga")
+    far_rows = send(go, "x", 1)
+    down_last = side_y(down_two, down_came)
+    up_last = halve_z(up_steps)
+    b_steps = add_y(b_kept, b_came)
+    a_last = halve_z(a_pair)
+    grad_down = add_last(down_last)
+    grad_up_rows = add_last(up_last)
+    first_rows = add_last(a_last)
+    second_rows = add_z(b_steps)
     own, near, far, grad_out = call(
         pick_grads,
         [Keep(sds(48, 768, dtype=F32)), sds(48, 768), sds(96, 768), sds(24, 768, dtype=F32)],
         [grad_up_rows, first_rows, second_rows],
         [pltpu.VMEM((4, 48, 768), F32)],
     )
-    came_far = send(far, "x", 1, "grads")
-    came_near, came_near_far = send(near, "core", 1, "grads"), send(came_far, "core", 1, "far_grads")
+    came_far = send(far, "x", 1)
+    came_near, came_near_far = send(near, "core", 1), send(came_far, "core", 1)
     out_patches, out_special, grad_patches, grad_special = call(
         finish_rows,
         [
             sds(176, 768), sds(20, 768), sds(176, 768, dtype=F32), sds(20, 768, dtype=F32),
         ],
         [Keep(stay), far_rows, middle, Keep(grad_rows), patches, special, Keep(gain_rows)],
-        after="pick_grads",
     )
     grad_qkv, grad_up, grad_gains = call(
         join_grads,
         [sds(24, 2304, dtype=F32), sds(24, 3072, dtype=F32), sds(4, 24, dtype=F32)],
         [Keep(own), came_near, came_far, came_near_far, w_qkv, w_up, gains],
         [pltpu.VMEM((4, 48, 768), F32)],
-        after="finish_rows",
     )
     return (
         out_patches, out_special, grad_patches, grad_special,

time: 163 us -> 154 us (0.945)
  waiting for transfers between devices: 61.3 us -> 53.1 us
  local copies, waits for them, and re-layouts: 8.34 us -> 3.87 us
  starting transfers between devices: 45.8 us -> 50 us
    ppermute x48, waiting for transfers between devices: 61.3 us -> 53.1 us  [send(): STEPS.append(lax.ppermute(rows, ('dp', 'blk'), pairs))]
    unnamed x78 -> x60, local copies, waits for them, and re-layouts: 7.96 us -> 3.5 us
    ppermute x48, starting transfers between devices: 45.8 us -> 50 us  [send(): STEPS.append(lax.ppermute(rows, ('dp', 'blk'), pairs))]
    pallas_call x31 -> x32, Pallas kernels: 46 us -> 45.2 us  [call(): pl.pallas_call(body, out_shape=tuple((made(v) for v in outs)), in_specs=[...]
  transfers between devices with their start and end apart: 48 -> 48, of which waited for: 20 -> 19; matrix products, arithmetic and copies ran while one was open for 0% -> 0% of each run, Pallas kernels for 22% -> 23%
where the time goes in v4:
time: 154 us; the launch traced here: 153 us
  waiting for transfers between devices  53.1 us (34%)
  starting transfers between devices  50 us (32%)
  Pallas kernels  45.2 us (29%)
  local copies, waits for them, and re-layouts  3.87 us (3%)
    ppermute x48, waiting for transfers between devices, send(): STEPS.append(lax.ppermute(rows, ('dp', 'blk'), pairs))  53.1 us
    ppermute x48, starting transfers between devices, send(): STEPS.append(lax.ppermute(rows, ('dp', 'blk'), pairs))  50 us
    pallas_call x32, Pallas kernels, call(): pl.pallas_call(body, out_shape=tuple((made(v) for v in outs)), in_specs=[...  45.2 us
    unnamed x60, local copies, waits for them, and re-layouts  3.5 us
  transfers between devices with their start and end apart: 48, of which 19 were waited for; matrix products, arithmetic and copies ran while one was open for 0% of the time, Pallas kernels for 23%

profile of v4, /device:TPU:0, one launch (start us, length us, event | category | flops | bytes accessed | tf_op | source)
XLA Modules:
  0.0 153.5 jit_solution(16347975219228817537)
XLA Ops:
  0.7 1.3 pick_pieces.1
  2.0 3.0 %collective-permute-start.4 = (bf16[96,768]{1,0:T(8,128)(2,1)S(1)}, bf16[96,768]{1,0:T(8,128)(2,1)S(1)}, u32[]{:S(2)}, u32[]{:S(2)}) collective-permute-start(bf16[96,768]{1,0:T(8,128)(2,1)S(1)} %get-tuple-element.118), channel_id=1, source_target_pairs={{0,2},{1,3},{2,0},{3,1},{4,6},{5,7},{6,4},{7,5},{8,10},{9,11},{10,... | collective-permute-start | bytes 442376 | tf_op jit(solution)/shard_map/ppermute | solution.py:1047
  6.3 2.6 %collective-permute-done.4.refs_2_ = bf16[96,768]{1,0:T(8,128)(2,1)S(1)} collective-permute-done((bf16[96,768]{1,0:T(8,128)(2,1)S(1)}, bf16[96,768]{1,0:T(8,128)(2,1)S(1)}, u32[]{:S(2)}, u32[]{:S(2)}) %collective-permute-start.4) | collective-permute-done | bytes 147488 | tf_op jit(solution)/shard_map/ppermute | solution.py:1047
  8.9 1.7 %collective-permute-start.1 = (bf16[352,768]{1,0:T(8,128)(2,1)S(1)}, bf16[352,768]{1,0:T(8,128)(2,1)S(1)}, u32[]{:S(2)}, u32[]{:S(2)}) collective-permute-start(bf16[352,768]{1,0:T(8,128)(2,1)S(1)} %get-tuple-element.113.refs_0_), channel_id=1, source_target_pairs={{0,2},{1,3},{2,0},{3,1},{4,6},{5,7},{6,4},{7,5},{8,10},{9,11},{10,... | collective-permute-start | bytes 1622024 | tf_op jit(solution)/shard_map/ppermute | solution.py:1047
  11.3 2.7 %collective-permute-start.8 = (bf16[112,768]{1,0:T(8,128)(2,1)S(1)}, bf16[112,768]{1,0:T(8,128)(2,1)S(1)}, u32[]{:S(2)}, u32[]{:S(2)}) collective-permute-start(bf16[112,768]{1,0:T(8,128)(2,1)S(1)} %get-tuple-element.125.refs_0_), channel_id=1, source_target_pairs={{0,16},{1,17},{2,18},{3,19},{4,20},{5,21},{6,22},{7,23},{8,24},{9,... | collective-permute-start | bytes 516104 | tf_op jit(solution)/shard_map/ppermute | solution.py:1047
  13.9 1.5 collective-permute-start.10
  15.5 1.6 %collective-permute-start.6 = (bf16[112,768]{1,0:T(8,128)(2,1)S(1)}, bf16[112,768]{1,0:T(8,128)(2,1)S(1)}, u32[]{:S(2)}, u32[]{:S(2)}) collective-permute-start(bf16[112,768]{1,0:T(8,128)(2,1)S(1)} %get-tuple-element.125.refs_0_), channel_id=1, source_target_pairs={{0,8},{1,9},{2,10},{3,11},{4,12},{5,13},{6,14},{7,15},{8,0},{9,1},... | collective-permute-start | bytes 516104 | tf_op jit(solution)/shard_map/ppermute | solution.py:1047
  17.0 5.5 %collective-permute-done.8.refs_2_ = bf16[112,768]{1,0:T(8,128)(2,1)S(1)} collective-permute-done((bf16[112,768]{1,0:T(8,128)(2,1)S(1)}, bf16[112,768]{1,0:T(8,128)(2,1)S(1)}, u32[]{:S(2)}, u32[]{:S(2)}) %collective-permute-start.8) | collective-permute-done | bytes 172064 | tf_op jit(solution)/shard_map/ppermute | solution.py:1047
  23.2 1.5 collective-permute-start.12
  24.6 3.4 %collective-permute-start.21 = (bf16[192,768]{1,0:T(8,128)(2,1)S(1)}, bf16[192,768]{1,0:T(8,128)(2,1)S(1)}, u32[]{:S(2)}, u32[]{:S(2)}) collective-permute-start(bf16[192,768]{1,0:T(8,128)(2,1)S(1)} %get-tuple-element.136.refs_1_), channel_id=1, source_target_pairs={{0,16},{1,17},{2,18},{3,19},{4,20},{5,21},{6,22},{7,23},{8,24},{9,... | collective-permute-start | bytes 884744 | tf_op jit(solution)/shard_map/ppermute | solution.py:1047
  28.6 4.2 %collective-permute-start.13 = (bf16[112,768]{1,0:T(8,128)(2,1)S(1)}, bf16[112,768]{1,0:T(8,128)(2,1)S(1)}, u32[]{:S(2)}, u32[]{:S(2)}) collective-permute-start(bf16[112,768]{1,0:T(8,128)(2,1)S(1)} %collective-permute-done.9.refs_3_), channel_id=1, source_target_pairs={{0,4},{1,5},{2,6},{3,7},{4,0},{5,1},{6,2},{7,3},{8,12},{9,13},{10,... | collective-permute-start | bytes 516104 | tf_op jit(solution)/shard_map/ppermute | solution.py:1047
  33.4 1.9 %collective-permute-done.11.refs_5_ = bf16[112,768]{1,0:T(8,128)(2,1)S(1)} collective-permute-done((bf16[112,768]{1,0:T(8,128)(2,1)S(1)}, bf16[112,768]{1,0:T(8,128)(2,1)S(1)}, u32[]{:S(2)}, u32[]{:S(2)}) %collective-permute-start.11) | collective-permute-done | bytes 172064 | tf_op jit(solution)/shard_map/ppermute | solution.py:1047
  36.0 2.2 %collective-permute-done.13.refs_7_ = bf16[112,768]{1,0:T(8,128)(2,1)S(1)} collective-permute-done((bf16[112,768]{1,0:T(8,128)(2,1)S(1)}, bf16[112,768]{1,0:T(8,128)(2,1)S(1)}, u32[]{:S(2)}, u32[]{:S(2)}) %collective-permute-start.13) | collective-permute-done | bytes 172064 | tf_op jit(solution)/shard_map/ppermute | solution.py:1047
  41.1 1.3 collective-permute-start.15
  42.9 4.5 %collective-permute-done.20.refs_2_ = bf16[192,768]{1,0:T(8,128)(2,1)} collective-permute-done((bf16[192,768]{1,0:T(8,128)(2,1)S(1)}, bf16[192,768]{1,0:T(8,128)(2,1)}, u32[]{:S(2)}, u32[]{:S(2)}) %collective-permute-start.20) | collective-permute-done | bytes 294944 | tf_op jit(solution)/shard_map/ppermute | solution.py:1047
  48.1 2.6 %norm_rows_in.1 = (f32[736,768]{1,0:T(8,128)S(1)}, bf16[736,768]{1,0:T(8,128)(2,1)}, bf16[736,768]{1,0:T(8,128)(2,1)}) custom-call(bf16[352,768]{1,0:T(8,128)(2,1)S(1)} %get-tuple-element.113.refs_0_, bf16[352,768]{1,0:T(8,128)(2,1)S(1)} %collective-permute-done.refs_1_, bf16[352,768]{1,0:T(8,128)(2,1)S(1)} %collective-permute-done.1.refs_2_.refs_8_, ...), custom_call_target="tpu_custom_call" | custom-call | flops 200000000 | tf_op jit(solution)/shard_map/norm_rows_in/pallas_call | solution.py:512
  51.0 4.1 %attend.1 = (bf16[736,192]{1,0:T(8,128)(2,1)S(1)}, bf16[768,576]{1,0:T(8,128)(2,1)}, bf16[736,768]{1,0:T(8,128)(2,1)}, bf16[736,576]{1,0:T(8,128)(2,1)}, bf16[6,368,368]{2,1,0:T(8,128)(2,1)}) custom-call(s32[736,1]{1,0:T(8,128)S(1)} %reshape.77.refs_0_, s32[2,368]{1,0:T(2,128)S(1)} %pad_add_fusion.refs_1_, f32[736,768]{1,0:T(8,128)S(1)} %get-tuple-element.123.refs_2_, ...), custom_call_target="tpu_custom_call" | custom-call | flops 40000000000 | tf_op jit(solution)/shard_map/attend/pallas_call | solution.py:512
  55.1 1.3 collective-permute-start.18
  56.4 1.5 collective-permute-start.25
  58.5 7.7 %collective-permute-done.18.refs_2_.refs_8_.refs_6_ = bf16[736,192]{1,0:T(8,128)(2,1)S(1)} collective-permute-done((bf16[736,192]{1,0:T(8,128)(2,1)S(1)}, bf16[736,192]{1,0:T(8,128)(2,1)S(1)}, u32[]{:S(2)}, u32[]{:S(2)}) %collective-permute-start.18) | collective-permute-done | bytes 282656 | tf_op jit(solution)/shard_map/ppermute | solution.py:1047
  66.2 2.7 %order_out.1 = (bf16[768,768]{1,0:T(8,128)(2,1)S(1)}, bf16[192,768]{1,0:T(8,128)(2,1)}, bf16[736,768]{1,0:T(8,128)(2,1)}) custom-call(bf16[192,768]{1,0:T(8,128)(2,1)} %get-tuple-element.129.refs_0_, bf16[192,768]{1,0:T(8,128)(2,1)S(1)} %collective-permute-done.14.refs_1_, bf16[192,768]{1,0:T(8,128)(2,1)} %collective-permute-done.15.refs_2_.refs_7_, ...), custom_call_target="tpu_custom_call" | custom-call | flops 1600000000 | tf_op jit(solution)/shard_map/order_out/pallas_call | solution.py:512
  69.4 1.3 collective-permute-done.17.refs_1_.refs_5_
  70.8 3.2 %branch_rows.1 = (bf16[736,768]{1,0:T(8,128)(2,1)S(1)}, bf16[736,768]{1,0:T(8,128)(2,1)}, f32[736,768]{1,0:T(8,128)}) custom-call(bf16[736,192]{1,0:T(8,128)(2,1)S(1)} %get-tuple-element.132.refs_0_.refs_4_.refs_5_, bf16[736,192]{1,0:T(8,128)(2,1)S(1)} %collective-permute-done.17.refs_1_.refs_5_, ...), custom_call_target="tpu_custom_call" | custom-call | flops 1000000 | tf_op jit(solution)/shard_map/branch_rows/pallas_call | solution.py:512
  74.0 3.8 %raise_rows.1 = (bf16[736,768]{1,0:T(8,128)(2,1)S(1)}, f32[736,768]{1,0:T(8,128)S(1)}, bf16[768,768]{1,0:T(8,128)(2,1)S(1)}, bf16[768,768]{1,0:T(8,128)(2,1)S(1)...) custom-call(bf16[736,768]{1,0:T(8,128)(2,1)S(1)} %get-tuple-element.134.refs_0_, bf16[192,768]{1,0:T(8,128)(2,1)S(1)} %copy-done.12, ...), custom_call_target="tpu_custom_call" | custom-call | flops 840000000 | tf_op jit(solution)/shard_map/raise_rows/pallas_call | solution.py:512
  77.8 3.0 %lower_rows.1 = (bf16[368,768]{1,0:T(8,128)(2,1)S(1)}, f32[368,768]{1,0:T(8,128)S(1)}, bf16[736,768]{1,0:T(8,128)(2,1)}) custom-call(f32[736,768]{1,0:T(8,128)S(1)} %get-tuple-element.145.refs_0_, bf16[736,768]{1,0:T(8,128)(2,1)S(1)} %copy-done.5, bf16[768,768]{1,0:T(8,128)(2,1)S(1)} %get-tuple-element.146.refs_2_, ...), custom_call_target="tpu_custom_call" | custom-call | flops 185000000 | tf_op jit(solution)/shard_map/lower_rows/pallas_call | solution.py:512
  81.2 2.6 %down_grads.1 = (bf16[4,96,768]{2,1,0:T(8,128)(2,1)}, f32[4,96,768]{2,1,0:T(8,128)S(1)}, bf16[736,768]{1,0:T(8,128)(2,1)}) custom-call(bf16[736,768]{1,0:T(8,128)(2,1)S(1)} %get-tuple-element.140.refs_0_.refs_4_, bf16[736,768]{1,0:T(8,128)(2,1)S(1)} %copy-done.5, bf16[736,192]{1,0:T(8,128)(2,1)S(1)} %collective-permute-done.19.refs_3_.refs_9_.refs_2_.refs_7_), custom_call_target="tpu_custom_call" | custom-call | flops 1500000000 | tf_op jit(solution)/shard_map/down_grads/pallas_call | solution.py:512
  83.9 2.1 %collective-permute-start.29 = (bf16[4,96,768]{2,1,0:T(8,128)(2,1)}, bf16[4,96,768]{2,1,0:T(8,128)(2,1)S(1)}, u32[]{:S(2)}, u32[]{:S(2)}) collective-permute-start(bf16[4,96,768]{2,1,0:T(8,128)(2,1)} %get-tuple-element.161), channel_id=1, source_target_pairs={{0,8},{1,9},{2,10},{3,11},{4,12},{5,13},{6,14},{7,15},{8,0},{9,1},... | collective-permute-start | bytes 1769480 | tf_op jit(solution)/shard_map/ppermute | solution.py:1047
  86.1 1.3 collective-permute-start.28
  87.5 3.0 %up_grads.1 = (bf16[4,96,768]{2,1,0:T(8,128)(2,1)S(1)}, f32[4,96,768]{2,1,0:T(8,128)S(1)}) custom-call(bf16[736,768]{1,0:T(8,128)(2,1)} %get-tuple-element.144.refs_0_, bf16[736,768]{1,0:T(8,128)(2,1)} %get-tuple-element.148.refs_1_, bf16[368,768]{1,0:T(8,128)(2,1)S(1)} %add_rows.1.refs_2_.refs_0_), custom_call_target="tpu_custom_call" | custom-call | flops 600000000 | tf_op jit(solution)/shard_map/up_grads/pallas_call | solution.py:512
  90.5 1.5 collective-permute-start.33
  92.0 3.9 %mlp_rows.1 = (bf16[416,768]{1,0:T(8,128)(2,1)S(1)}, f32[416,768]{1,0:T(8,128)S(1)}, f32[8,768]{1,0:T(8,128)S(1)}, bf16[736,192]{1,0:T(8,128)(2,1)S(1)}) custom-call(bf16[736,768]{1,0:T(8,128)(2,1)} %get-tuple-element.142.refs_0_, bf16[768,768]{1,0:T(8,128)(2,1)} %get-tuple-element.143.refs_1_, bf16[736,768]{1,0:T(8,128)(2,1)} %get-tuple-element.130.refs_4_.refs_2_.refs_3_, ...), custom_call_target="tpu_custom_call" | custom-call | flops 2000000000 | tf_op jit(solution)/shard_map/mlp_rows/pallas_call | solution.py:512
  96.0 3.8 %collective-permute-done.29.refs_1_.refs_2_ = bf16[4,96,768]{2,1,0:T(8,128)(2,1)S(1)} collective-permute-done((bf16[4,96,768]{2,1,0:T(8,128)(2,1)}, bf16[4,96,768]{2,1,0:T(8,128)(2,1)S(1)}, u32[]{:S(2)}, u32[]{:S(2)}) %collective-permute-start.29) | collective-permute-done | bytes 589856 | tf_op jit(solution)/shard_map/ppermute | solution.py:1047
  101.0 2.0 %collective-permute-start.36 = (bf16[2,96,768]{2,1,0:T(8,128)(2,1)S(1)}, bf16[2,96,768]{2,1,0:T(8,128)(2,1)S(1)}, u32[]{:S(2)}, u32[]{:S(2)}) collective-permute-start(bf16[2,96,768]{2,1,0:T(8,128)(2,1)S(1)} %get-tuple-element.186), channel_id=1, source_target_pairs={{0,16},{1,17},{2,18},{3,19},{4,20},{5,21},{6,22},{7,23},{8,24},{9,... | collective-permute-start | bytes 884744 | tf_op jit(solution)/shard_map/ppermute | solution.py:1047
  103.0 3.7 %branch_back.1 = (f32[208,768]{1,0:T(8,128)S(1)}, bf16[736,192]{1,0:T(8,128)(2,1)S(1)}, bf16[736,192]{1,0:T(8,128)(2,1)S(1)}, bf16[4,112,384]{2,1,0:T(8,128)(2,1)S(1)}, f32[4,112,384]{2,1,0:T(8,128)S(1)}) custom-call(bf16[368,768]{1,0:T(8,128)(2,1)S(1)} %add_pair.1.refs_0_.refs_3_, bf16[368,768]{1,0:T(8,128)(2,1)S(1)} %collective-permute-done.30.refs_1_, ...), custom_call_target="tpu_custom_call" | custom-call | flops 1000000 | tf_op jit(solution)/shard_map/branch_back/pallas_call | solution.py:512
  106.7 1.5 %collective-permute-start.38 = (bf16[4,112,384]{2,1,0:T(8,128)(2,1)S(1)}, bf16[4,112,384]{2,1,0:T(8,128)(2,1)S(1)}, u32[]{:S(2)}, u32[]{:S(2)}) collective-permute-start(bf16[4,112,384]{2,1,0:T(8,128)(2,1)S(1)} %get-tuple-element.192), channel_id=1, source_target_pairs={{0,4},{1,5},{2,6},{3,7},{4,0},{5,1},{6,2},{7,3},{8,12},{9,13},{10,... | collective-permute-start | bytes 1032200 | tf_op jit(solution)/shard_map/ppermute | solution.py:1047
  108.3 3.8 %score_back.1 = (bf16[736,384]{1,0:T(8,128)(2,1)S(1)}, bf16[4,96,384]{2,1,0:T(8,128)(2,1)S(1)}, f32[4,96,384]{2,1,0:T(8,128)S(1)}) custom-call(bf16[6,368,368]{2,1,0:T(8,128)(2,1)S(1)} %copy-done.1, bf16[736,576]{1,0:T(8,128)(2,1)S(1)} %copy-done.10, bf16[736,192]{1,0:T(8,128)(2,1)S(1)} %get-tuple-element.170.refs_2_, bf16[736,768]{1,0:T(8,128)(2,1)S(1)} %copy-done.2), custom_call_target="tpu_custom_call" | custom-call | flops 1000000 | tf_op jit(solution)/shard_map/score_back/pallas_call | solution.py:512
  115.8 1.3 collective-permute-start.32
  118.4 5.6 %collective-permute-done.34.refs_1_ = bf16[2,96,768]{2,1,0:T(8,128)(2,1)S(1)} collective-permute-done((bf16[2,96,768]{2,1,0:T(8,128)(2,1)S(1)}, bf16[2,96,768]{2,1,0:T(8,128)(2,1)S(1)}, u32[]{:S(2)}, u32[]{:S(2)}) %collective-permute-start.34) | collective-permute-done | bytes 294944 | tf_op jit(solution)/shard_map/ppermute | solution.py:1047
  124.0 1.5 collective-permute-start.35
  126.1 1.6 %collective-permute-done.39.refs_1_ = bf16[2,112,384]{2,1,0:T(8,128)(2,1)S(1)} collective-permute-done((bf16[2,112,384]{2,1,0:T(8,128)(2,1)S(1)}, bf16[2,112,384]{2,1,0:T(8,128)(2,1)S(1)}, u32[]{:S(2)}, u32[]{:S(2)}) %collective-permute-start.39) | collective-permute-done | bytes 172064 | tf_op jit(solution)/shard_map/ppermute | solution.py:1047
  127.7 1.5 collective-permute-start.40
  129.3 1.5 collective-permute-start.43
  130.8 7.1 %collective-permute-done.35.refs_1_ = bf16[96,768]{1,0:T(8,128)(2,1)S(1)} collective-permute-done((bf16[96,768]{1,0:T(8,128)(2,1)S(1)}, bf16[96,768]{1,0:T(8,128)(2,1)S(1)}, u32[]{:S(2)}, u32[]{:S(2)}) %collective-permute-start.35) | collective-permute-done | bytes 147488 | tf_op jit(solution)/shard_map/ppermute | solution.py:1047
  137.8 1.6 %collective-permute-start.44 = (bf16[96,384]{1,0:T(8,128)(2,1)S(1)}, bf16[96,384]{1,0:T(8,128)(2,1)S(1)}, u32[]{:S(2)}, u32[]{:S(2)}) collective-permute-start(bf16[96,384]{1,0:T(8,128)(2,1)S(1)} %get-tuple-element.204), channel_id=1, source_target_pairs={{0,24},{1,25},{2,26},{3,27},{4,28},{5,29},{6,30},{7,31},{8,16},{9,... | collective-permute-start | bytes 221192 | tf_op jit(solution)/shard_map/ppermute | solution.py:1047
  141.2 1.9 %collective-permute-done.42.refs_1_ = bf16[96,384]{1,0:T(8,128)(2,1)S(1)} collective-permute-done((bf16[96,384]{1,0:T(8,128)(2,1)S(1)}, bf16[96,384]{1,0:T(8,128)(2,1)S(1)}, u32[]{:S(2)}, u32[]{:S(2)}) %collective-permute-start.42) | collective-permute-done | bytes 73760 | tf_op jit(solution)/shard_map/ppermute | solution.py:1047
  144.9 1.3 collective-permute-start.45
  147.4 2.6 %collective-permute-done.45.refs_7_.refs_2_ = bf16[96,768]{1,0:T(8,128)(2,1)S(1)} collective-permute-done((bf16[96,768]{1,0:T(8,128)(2,1)S(1)}, bf16[96,768]{1,0:T(8,128)(2,1)S(1)}, u32[]{:S(2)}, u32[]{:S(2)}) %collective-permute-start.45) | collective-permute-done | bytes 147488 | tf_op jit(solution)/shard_map/ppermute | solution.py:1047
  150.0 1.4 finish_rows.1
  (148 shorter events, 23.9 us)
Async XLA Ops:
  2.0 6.9 %collective-permute-start.4 = (bf16[96,768]{1,0:T(8,128)(2,1)S(1)}, bf16[96,768]{1,0:T(8,128)(2,1)S(1)}, u32[]{:S(2)}, u32[]{:S(2)}) collective-permute-start(bf16[96,768]{1,0:T(8,128)(2,1)S(1)} %get-tuple-element.118), channel_id=1, source_target_pairs={{0,2},{1,3},{2,0},{3,1},{4,6},{5,7},{6,4},{7,5},{8,10},{9,11},{10,... | collective-permute-start | bytes 442376 | tf_op jit(solution)/shard_map/ppermute | solution.py:1047
  5.0 1.3 collective-permute-start.3
  8.9 1.7 %collective-permute-start.5 = (bf16[96,768]{1,0:T(8,128)(2,1)S(1)}, bf16[96,768]{1,0:T(8,128)(2,1)S(1)}, u32[]{:S(2)}, u32[]{:S(2)}) collective-permute-start(bf16[96,768]{1,0:T(8,128)(2,1)S(1)} %collective-permute-done.4.refs_2_), channel_id=1, source_target_pairs={{0,1},{1,0},{2,3},{3,2},{4,5},{5,4},{6,7},{7,6},{8,9},{9,8},{10,11... | collective-permute-start | bytes 442376 | tf_op jit(solution)/shard_map/ppermute | solution.py:1047
  8.9 24.0 %collective-permute-start.1 = (bf16[352,768]{1,0:T(8,128)(2,1)S(1)}, bf16[352,768]{1,0:T(8,128)(2,1)S(1)}, u32[]{:S(2)}, u32[]{:S(2)}) collective-permute-start(bf16[352,768]{1,0:T(8,128)(2,1)S(1)} %get-tuple-element.113.refs_0_), channel_id=1, source_target_pairs={{0,2},{1,3},{2,0},{3,1},{4,6},{5,7},{6,4},{7,5},{8,10},{9,11},{10,... | collective-permute-start | bytes 1622024 | tf_op jit(solution)/shard_map/ppermute | solution.py:1047
  11.3 11.3 %collective-permute-start.8 = (bf16[112,768]{1,0:T(8,128)(2,1)S(1)}, bf16[112,768]{1,0:T(8,128)(2,1)S(1)}, u32[]{:S(2)}, u32[]{:S(2)}) collective-permute-start(bf16[112,768]{1,0:T(8,128)(2,1)S(1)} %get-tuple-element.125.refs_0_), channel_id=1, source_target_pairs={{0,16},{1,17},{2,18},{3,19},{4,20},{5,21},{6,22},{7,23},{8,24},{9,... | collective-permute-start | bytes 516104 | tf_op jit(solution)/shard_map/ppermute | solution.py:1047
  13.9 10.7 %collective-permute-start.10 = (bf16[112,768]{1,0:T(8,128)(2,1)S(1)}, bf16[112,768]{1,0:T(8,128)(2,1)S(1)}, u32[]{:S(2)}, u32[]{:S(2)}) collective-permute-start(bf16[112,768]{1,0:T(8,128)(2,1)S(1)} %get-tuple-element.125.refs_0_), channel_id=1, source_target_pairs={{0,4},{1,5},{2,6},{3,7},{4,0},{5,1},{6,2},{7,3},{8,12},{9,13},{10,... | collective-permute-start | bytes 516104 | tf_op jit(solution)/shard_map/ppermute | solution.py:1047
  15.5 12.6 %collective-permute-start.6 = (bf16[112,768]{1,0:T(8,128)(2,1)S(1)}, bf16[112,768]{1,0:T(8,128)(2,1)S(1)}, u32[]{:S(2)}, u32[]{:S(2)}) collective-permute-start(bf16[112,768]{1,0:T(8,128)(2,1)S(1)} %get-tuple-element.125.refs_0_), channel_id=1, source_target_pairs={{0,8},{1,9},{2,10},{3,11},{4,12},{5,13},{6,14},{7,15},{8,0},{9,1},... | collective-permute-start | bytes 516104 | tf_op jit(solution)/shard_map/ppermute | solution.py:1047
  22.6 6.1 %collective-permute-start.9 = (bf16[112,768]{1,0:T(8,128)(2,1)S(1)}, bf16[112,768]{1,0:T(8,128)(2,1)S(1)}, u32[]{:S(2)}, u32[]{:S(2)}) collective-permute-start(bf16[112,768]{1,0:T(8,128)(2,1)S(1)} %collective-permute-done.8.refs_2_), channel_id=1, source_target_pairs={{0,8},{1,9},{2,10},{3,11},{4,12},{5,13},{6,14},{7,15},{8,0},{9,1},... | collective-permute-start | bytes 516104 | tf_op jit(solution)/shard_map/ppermute | solution.py:1047
  23.2 9.7 %collective-permute-start.12 = (bf16[112,768]{1,0:T(8,128)(2,1)S(1)}, bf16[112,768]{1,0:T(8,128)(2,1)S(1)}, u32[]{:S(2)}, u32[]{:S(2)}) collective-permute-start(bf16[112,768]{1,0:T(8,128)(2,1)S(1)} %collective-permute-done.8.refs_2_), channel_id=1, source_target_pairs={{0,4},{1,5},{2,6},{3,7},{4,0},{5,1},{6,2},{7,3},{8,12},{9,13},{10,... | collective-permute-start | bytes 516104 | tf_op jit(solution)/shard_map/ppermute | solution.py:1047
  24.6 16.5 %collective-permute-start.21 = (bf16[192,768]{1,0:T(8,128)(2,1)S(1)}, bf16[192,768]{1,0:T(8,128)(2,1)S(1)}, u32[]{:S(2)}, u32[]{:S(2)}) collective-permute-start(bf16[192,768]{1,0:T(8,128)(2,1)S(1)} %get-tuple-element.136.refs_1_), channel_id=1, source_target_pairs={{0,16},{1,17},{2,18},{3,19},{4,20},{5,21},{6,22},{7,23},{8,24},{9,... | collective-permute-start | bytes 884744 | tf_op jit(solution)/shard_map/ppermute | solution.py:1047
  28.0 7.3 %collective-permute-start.11 = (bf16[112,768]{1,0:T(8,128)(2,1)S(1)}, bf16[112,768]{1,0:T(8,128)(2,1)S(1)}, u32[]{:S(2)}, u32[]{:S(2)}) collective-permute-start(bf16[112,768]{1,0:T(8,128)(2,1)S(1)} %collective-permute-done.6.refs_1_), channel_id=1, source_target_pairs={{0,4},{1,5},{2,6},{3,7},{4,0},{5,1},{6,2},{7,3},{8,12},{9,13},{10,... | collective-permute-start | bytes 516104 | tf_op jit(solution)/shard_map/ppermute | solution.py:1047
  28.6 9.5 %collective-permute-start.13 = (bf16[112,768]{1,0:T(8,128)(2,1)S(1)}, bf16[112,768]{1,0:T(8,128)(2,1)S(1)}, u32[]{:S(2)}, u32[]{:S(2)}) collective-permute-start(bf16[112,768]{1,0:T(8,128)(2,1)S(1)} %collective-permute-done.9.refs_3_), channel_id=1, source_target_pairs={{0,4},{1,5},{2,6},{3,7},{4,0},{5,1},{6,2},{7,3},{8,12},{9,13},{10,... | collective-permute-start | bytes 516104 | tf_op jit(solution)/shard_map/ppermute | solution.py:1047
  32.9 14.5 %collective-permute-start = (bf16[352,768]{1,0:T(8,128)(2,1)S(1)}, bf16[352,768]{1,0:T(8,128)(2,1)S(1)}, u32[]{:S(2)}, u32[]{:S(2)}) collective-permute-start(bf16[352,768]{1,0:T(8,128)(2,1)S(1)} %get-tuple-element.113.refs_0_), channel_id=1, source_target_pairs={{0,1},{1,0},{2,3},{3,2},{4,5},{5,4},{6,7},{7,6},{8,9},{9,8},{10,11... | collective-permute-start | bytes 1622024 | tf_op jit(solution)/shard_map/ppermute | solution.py:1047
  32.9 15.2 %collective-permute-start.2 = (bf16[352,768]{1,0:T(8,128)(2,1)S(1)}, bf16[352,768]{1,0:T(8,128)(2,1)S(1)}, u32[]{:S(2)}, u32[]{:S(2)}) collective-permute-start(bf16[352,768]{1,0:T(8,128)(2,1)S(1)} %collective-permute-done.1.refs_2_.refs_8_), channel_id=1, source_target_pairs={{0,1},{1,0},{2,3},{3,2},{4,5},{5,4},{6,7},{7,6},{8,9},{9,8},{10,11... | collective-permute-start | bytes 1622024 | tf_op jit(solution)/shard_map/ppermute | solution.py:1047
  35.3 12.1 %collective-permute-start.7 = (bf16[192,768]{1,0:T(8,128)(2,1)S(1)}, bf16[192,768]{1,0:T(8,128)(2,1)S(1)}, u32[]{:S(2)}, u32[]{:S(2)}) collective-permute-start(bf16[192,768]{1,0:T(8,128)(2,1)S(1)} %get-tuple-element.136.refs_1_), channel_id=1, source_target_pairs={{0,4},{1,5},{2,6},{3,7},{4,0},{5,1},{6,2},{7,3},{8,12},{9,13},{10,... | collective-permute-start | bytes 884744 | tf_op jit(solution)/shard_map/ppermute | solution.py:1047
  38.2 9.2 %collective-permute-start.20 = (bf16[192,768]{1,0:T(8,128)(2,1)S(1)}, bf16[192,768]{1,0:T(8,128)(2,1)}, u32[]{:S(2)}, u32[]{:S(2)}) collective-permute-start(bf16[192,768]{1,0:T(8,128)(2,1)S(1)} %get-tuple-element.136.refs_1_), channel_id=1, source_target_pairs={{0,8},{1,9},{2,10},{3,11},{4,12},{5,13},{6,14},{7,15},{8,0},{9,1},... | collective-permute-start | bytes 884744 | tf_op jit(solution)/shard_map/ppermute | solution.py:1047
  41.1 9.7 %collective-permute-start.15 = (bf16[192,768]{1,0:T(8,128)(2,1)}, bf16[192,768]{1,0:T(8,128)(2,1)}, u32[]{:S(2)}, u32[]{:S(2)}) collective-permute-start(bf16[192,768]{1,0:T(8,128)(2,1)} %get-tuple-element.129.refs_0_), channel_id=1, source_target_pairs={{0,2},{1,3},{2,0},{3,1},{4,6},{5,7},{6,4},{7,5},{8,10},{9,11},{10,... | collective-permute-start | bytes 884744 | tf_op jit(solution)/shard_map/ppermute | solution.py:1047
  47.4 9.0 %collective-permute-start.22 = (bf16[192,768]{1,0:T(8,128)(2,1)S(1)}, bf16[192,768]{1,0:T(8,128)(2,1)S(1)}, u32[]{:S(2)}, u32[]{:S(2)}) collective-permute-start(bf16[192,768]{1,0:T(8,128)(2,1)S(1)} %collective-permute-done.21.refs_3_), channel_id=1, source_target_pairs={{0,8},{1,9},{2,10},{3,11},{4,12},{5,13},{6,14},{7,15},{8,0},{9,1},... | collective-permute-start | bytes 884744 | tf_op jit(solution)/shard_map/ppermute | solution.py:1047
  47.4 18.7 %collective-permute-start.14 = (bf16[192,768]{1,0:T(8,128)(2,1)}, bf16[192,768]{1,0:T(8,128)(2,1)S(1)}, u32[]{:S(2)}, u32[]{:S(2)}) collective-permute-start(bf16[192,768]{1,0:T(8,128)(2,1)} %get-tuple-element.129.refs_0_), channel_id=1, source_target_pairs={{0,1},{1,0},{2,3},{3,2},{4,5},{5,4},{6,7},{7,6},{8,9},{9,8},{10,11... | collective-permute-start | bytes 884744 | tf_op jit(solution)/shard_map/ppermute | solution.py:1047
  47.5 10.4 %collective-permute-start.23 = (bf16[192,768]{1,0:T(8,128)(2,1)}, bf16[192,768]{1,0:T(8,128)(2,1)S(1)}, u32[]{:S(2)}, u32[]{:S(2)}) collective-permute-start(bf16[192,768]{1,0:T(8,128)(2,1)} %collective-permute-done.20.refs_2_), channel_id=1, source_target_pairs={{0,4},{1,5},{2,6},{3,7},{4,0},{5,1},{6,2},{7,3},{8,12},{9,13},{10,... | collective-permute-start | bytes 884744 | tf_op jit(solution)/shard_map/ppermute | solution.py:1047
  50.8 15.4 %collective-permute-start.16 = (bf16[192,768]{1,0:T(8,128)(2,1)}, bf16[192,768]{1,0:T(8,128)(2,1)S(1)}, u32[]{:S(2)}, u32[]{:S(2)}) collective-permute-start(bf16[192,768]{1,0:T(8,128)(2,1)} %collective-permute-done.15.refs_2_.refs_7_), channel_id=1, source_target_pairs={{0,1},{1,0},{2,3},{3,2},{4,5},{5,4},{6,7},{7,6},{8,9},{9,8},{10,11... | collective-permute-start | bytes 884744 | tf_op jit(solution)/shard_map/ppermute | solution.py:1047
  55.1 11.1 %collective-permute-start.18 = (bf16[736,192]{1,0:T(8,128)(2,1)S(1)}, bf16[736,192]{1,0:T(8,128)(2,1)S(1)}, u32[]{:S(2)}, u32[]{:S(2)}) collective-permute-start(bf16[736,192]{1,0:T(8,128)(2,1)S(1)} %get-tuple-element.132.refs_0_.refs_4_.refs_5_), channel_id=1, source_target_pairs={{0,2},{1,3},{2,0},{3,1},{4,6},{5,7},{6,4},{7,5},{8,10},{9,11},{10,... | collective-permute-start | bytes 847880 | tf_op jit(solution)/shard_map/ppermute | solution.py:1047
  56.4 17.5 %collective-permute-start.25 = (bf16[192,768]{1,0:T(8,128)(2,1)S(1)}, bf16[192,768]{1,0:T(8,128)(2,1)S(1)}, u32[]{:S(2)}, u32[]{:S(2)}) collective-permute-start(bf16[192,768]{1,0:T(8,128)(2,1)S(1)} %collective-permute-done.22.refs_4_.refs_10_), channel_id=1, source_target_pairs={{0,4},{1,5},{2,6},{3,7},{4,0},{5,1},{6,2},{7,3},{8,12},{9,13},{10,... | collective-permute-start | bytes 884744 | tf_op jit(solution)/shard_map/ppermute | solution.py:1047
  57.9 16.1 %collective-permute-start.24 = (bf16[192,768]{1,0:T(8,128)(2,1)S(1)}, bf16[192,768]{1,0:T(8,128)(2,1)S(1)}, u32[]{:S(2)}, u32[]{:S(2)}) collective-permute-start(bf16[192,768]{1,0:T(8,128)(2,1)S(1)} %collective-permute-done.21.refs_3_), channel_id=1, source_target_pairs={{0,4},{1,5},{2,6},{3,7},{4,0},{5,1},{6,2},{7,3},{8,12},{9,13},{10,... | collective-permute-start | bytes 884744 | tf_op jit(solution)/shard_map/ppermute | solution.py:1047
  66.2 3.3 %collective-permute-start.19 = (bf16[736,192]{1,0:T(8,128)(2,1)S(1)}, bf16[736,192]{1,0:T(8,128)(2,1)S(1)}, u32[]{:S(2)}, u32[]{:S(2)}) collective-permute-start(bf16[736,192]{1,0:T(8,128)(2,1)S(1)} %collective-permute-done.18.refs_2_.refs_8_.refs_6_), channel_id=1, source_target_pairs={{0,1},{1,0},{2,3},{3,2},{4,5},{5,4},{6,7},{7,6},{8,9},{9,8},{10,11... | collective-permute-start | bytes 847880 | tf_op jit(solution)/shard_map/ppermute | solution.py:1047
  68.9 1.9 %collective-permute-start.17 = (bf16[736,192]{1,0:T(8,128)(2,1)S(1)}, bf16[736,192]{1,0:T(8,128)(2,1)S(1)}, u32[]{:S(2)}, u32[]{:S(2)}) collective-permute-start(bf16[736,192]{1,0:T(8,128)(2,1)S(1)} %get-tuple-element.132.refs_0_.refs_4_.refs_5_), channel_id=1, source_target_pairs={{0,1},{1,0},{2,3},{3,2},{4,5},{5,4},{6,7},{7,6},{8,9},{9,8},{10,11... | collective-permute-start | bytes 847880 | tf_op jit(solution)/shard_map/ppermute | solution.py:1047
  80.8 5.2 %collective-permute-start.26 = (bf16[368,768]{1,0:T(8,128)(2,1)S(1)}, bf16[368,768]{1,0:T(8,128)(2,1)S(1)}, u32[]{:S(2)}, u32[]{:S(2)}) collective-permute-start(bf16[368,768]{1,0:T(8,128)(2,1)S(1)} %get-tuple-element.151.refs_3_), channel_id=1, source_target_pairs={{0,1},{1,0},{2,3},{3,2},{4,5},{5,4},{6,7},{7,6},{8,9},{9,8},{10,11... | collective-permute-start | bytes 1695752 | tf_op jit(solution)/shard_map/ppermute | solution.py:1047
  83.9 15.9 %collective-permute-start.29 = (bf16[4,96,768]{2,1,0:T(8,128)(2,1)}, bf16[4,96,768]{2,1,0:T(8,128)(2,1)S(1)}, u32[]{:S(2)}, u32[]{:S(2)}) collective-permute-start(bf16[4,96,768]{2,1,0:T(8,128)(2,1)} %get-tuple-element.161), channel_id=1, source_target_pairs={{0,8},{1,9},{2,10},{3,11},{4,12},{5,13},{6,14},{7,15},{8,0},{9,1},... | collective-permute-start | bytes 1769480 | tf_op jit(solution)/shard_map/ppermute | solution.py:1047
  86.1 14.6 %collective-permute-start.28 = (bf16[368,768]{1,0:T(8,128)(2,1)S(1)}, bf16[368,768]{1,0:T(8,128)(2,1)S(1)}, u32[]{:S(2)}, u32[]{:S(2)}) collective-permute-start(bf16[368,768]{1,0:T(8,128)(2,1)S(1)} %add_rows.1.refs_2_.refs_0_), channel_id=1, source_target_pairs={{0,2},{1,3},{2,0},{3,1},{4,6},{5,7},{6,4},{7,5},{8,10},{9,11},{10,... | collective-permute-start | bytes 1695752 | tf_op jit(solution)/shard_map/ppermute | solution.py:1047
  90.5 23.0 %collective-permute-start.33 = (bf16[4,96,768]{2,1,0:T(8,128)(2,1)S(1)}, bf16[4,96,768]{2,1,0:T(8,128)(2,1)S(1)}, u32[]{:S(2)}, u32[]{:S(2)}) collective-permute-start(bf16[4,96,768]{2,1,0:T(8,128)(2,1)S(1)} %get-tuple-element.181.refs_8_), channel_id=1, source_target_pairs={{0,4},{1,5},{2,6},{3,7},{4,0},{5,1},{6,2},{7,3},{8,12},{9,13},{10,... | collective-permute-start | bytes 1769480 | tf_op jit(solution)/shard_map/ppermute | solution.py:1047
  95.9 17.5 %collective-permute-start.27 = (bf16[416,768]{1,0:T(8,128)(2,1)S(1)}, bf16[416,768]{1,0:T(8,128)(2,1)S(1)}, u32[]{:S(2)}, u32[]{:S(2)}) collective-permute-start(bf16[416,768]{1,0:T(8,128)(2,1)S(1)} %get-tuple-element.155), channel_id=1, source_target_pairs={{0,1},{1,0},{2,3},{3,2},{4,5},{5,4},{6,7},{7,6},{8,9},{9,8},{10,11... | collective-permute-start | bytes 1916936 | tf_op jit(solution)/shard_map/ppermute | solution.py:1047
  100.9 2.1 %collective-permute-start.30 = (bf16[368,768]{1,0:T(8,128)(2,1)S(1)}, bf16[368,768]{1,0:T(8,128)(2,1)S(1)}, u32[]{:S(2)}, u32[]{:S(2)}) collective-permute-start(bf16[368,768]{1,0:T(8,128)(2,1)S(1)} %add_pair.1.refs_0_.refs_3_), channel_id=1, source_target_pairs={{0,1},{1,0},{2,3},{3,2},{4,5},{5,4},{6,7},{7,6},{8,9},{9,8},{10,11... | collective-permute-start | bytes 1695752 | tf_op jit(solution)/shard_map/ppermute | solution.py:1047
  101.0 17.4 %collective-permute-start.36 = (bf16[2,96,768]{2,1,0:T(8,128)(2,1)S(1)}, bf16[2,96,768]{2,1,0:T(8,128)(2,1)S(1)}, u32[]{:S(2)}, u32[]{:S(2)}) collective-permute-start(bf16[2,96,768]{2,1,0:T(8,128)(2,1)S(1)} %get-tuple-element.186), channel_id=1, source_target_pairs={{0,16},{1,17},{2,18},{3,19},{4,20},{5,21},{6,22},{7,23},{8,24},{9,... | collective-permute-start | bytes 884744 | tf_op jit(solution)/shard_map/ppermute | solution.py:1047
  106.7 10.4 %collective-permute-start.38 = (bf16[4,112,384]{2,1,0:T(8,128)(2,1)S(1)}, bf16[4,112,384]{2,1,0:T(8,128)(2,1)S(1)}, u32[]{:S(2)}, u32[]{:S(2)}) collective-permute-start(bf16[4,112,384]{2,1,0:T(8,128)(2,1)S(1)} %get-tuple-element.192), channel_id=1, source_target_pairs={{0,4},{1,5},{2,6},{3,7},{4,0},{5,1},{6,2},{7,3},{8,12},{9,13},{10,... | collective-permute-start | bytes 1032200 | tf_op jit(solution)/shard_map/ppermute | solution.py:1047
  113.4 2.1 %collective-permute-start.31 = (bf16[416,768]{1,0:T(8,128)(2,1)S(1)}, bf16[416,768]{1,0:T(8,128)(2,1)S(1)}, u32[]{:S(2)}, u32[]{:S(2)}) collective-permute-start(bf16[416,768]{1,0:T(8,128)(2,1)S(1)} %get-tuple-element.176), channel_id=1, source_target_pairs={{0,1},{1,0},{2,3},{3,2},{4,5},{5,4},{6,7},{7,6},{8,9},{9,8},{10,11... | collective-permute-start | bytes 1916936 | tf_op jit(solution)/shard_map/ppermute | solution.py:1047
  113.6 10.3 %collective-permute-start.34 = (bf16[2,96,768]{2,1,0:T(8,128)(2,1)S(1)}, bf16[2,96,768]{2,1,0:T(8,128)(2,1)S(1)}, u32[]{:S(2)}, u32[]{:S(2)}) collective-permute-start(bf16[2,96,768]{2,1,0:T(8,128)(2,1)S(1)} %get-tuple-element.183), channel_id=1, source_target_pairs={{0,8},{1,9},{2,10},{3,11},{4,12},{5,13},{6,14},{7,15},{8,0},{9,1},... | collective-permute-start | bytes 884744 | tf_op jit(solution)/shard_map/ppermute | solution.py:1047
  114.7 14.5 %collective-permute-start.41 = (bf16[4,96,384]{2,1,0:T(8,128)(2,1)S(1)}, bf16[4,96,384]{2,1,0:T(8,128)(2,1)S(1)}, u32[]{:S(2)}, u32[]{:S(2)}) collective-permute-start(bf16[4,96,384]{2,1,0:T(8,128)(2,1)S(1)} %get-tuple-element.199), channel_id=1, source_target_pairs={{0,4},{1,5},{2,6},{3,7},{4,0},{5,1},{6,2},{7,3},{8,12},{9,13},{10,... | collective-permute-start | bytes 884744 | tf_op jit(solution)/shard_map/ppermute | solution.py:1047
  115.8 34.2 %collective-permute-start.32 = (bf16[416,768]{1,0:T(8,128)(2,1)S(1)}, bf16[416,768]{1,0:T(8,128)(2,1)S(1)}, u32[]{:S(2)}, u32[]{:S(2)}) collective-permute-start(bf16[416,768]{1,0:T(8,128)(2,1)S(1)} %get-tuple-element.178), channel_id=1, source_target_pairs={{0,2},{1,3},{2,0},{3,1},{4,6},{5,7},{6,4},{7,5},{8,10},{9,11},{10,... | collective-permute-start | bytes 1916936 | tf_op jit(solution)/shard_map/ppermute | solution.py:1047
  117.2 10.4 %collective-permute-start.39 = (bf16[2,112,384]{2,1,0:T(8,128)(2,1)S(1)}, bf16[2,112,384]{2,1,0:T(8,128)(2,1)S(1)}, u32[]{:S(2)}, u32[]{:S(2)}) collective-permute-start(bf16[2,112,384]{2,1,0:T(8,128)(2,1)S(1)} %get-tuple-element.194), channel_id=1, source_target_pairs={{0,8},{1,9},{2,10},{3,11},{4,12},{5,13},{6,14},{7,15},{8,0},{9,1},... | collective-permute-start | bytes 516104 | tf_op jit(solution)/shard_map/ppermute | solution.py:1047
  124.0 13.8 %collective-permute-start.35 = (bf16[96,768]{1,0:T(8,128)(2,1)S(1)}, bf16[96,768]{1,0:T(8,128)(2,1)S(1)}, u32[]{:S(2)}, u32[]{:S(2)}) collective-permute-start(bf16[96,768]{1,0:T(8,128)(2,1)S(1)} %get-tuple-element.185), channel_id=1, source_target_pairs={{0,16},{1,17},{2,18},{3,19},{4,20},{5,21},{6,22},{7,23},{8,24},{9,... | collective-permute-start | bytes 442376 | tf_op jit(solution)/shard_map/ppermute | solution.py:1047
  125.5 12.3 %collective-permute-start.37 = (bf16[96,768]{1,0:T(8,128)(2,1)S(1)}, bf16[96,768]{1,0:T(8,128)(2,1)S(1)}, u32[]{:S(2)}, u32[]{:S(2)}) collective-permute-start(bf16[96,768]{1,0:T(8,128)(2,1)S(1)} %get-tuple-element.189), channel_id=1, source_target_pairs={{0,4},{1,5},{2,6},{3,7},{4,0},{5,1},{6,2},{7,3},{8,12},{9,13},{10,... | collective-permute-start | bytes 442376 | tf_op jit(solution)/shard_map/ppermute | solution.py:1047
  127.7 13.5 %collective-permute-start.40 = (bf16[112,384]{1,0:T(8,128)(2,1)S(1)}, bf16[112,384]{1,0:T(8,128)(2,1)S(1)}, u32[]{:S(2)}, u32[]{:S(2)}) collective-permute-start(bf16[112,384]{1,0:T(8,128)(2,1)S(1)} %get-tuple-element.197), channel_id=1, source_target_pairs={{0,16},{1,17},{2,18},{3,19},{4,20},{5,21},{6,22},{7,23},{8,24},{9,... | collective-permute-start | bytes 258056 | tf_op jit(solution)/shard_map/ppermute | solution.py:1047
  129.3 12.0 %collective-permute-start.43 = (bf16[96,384]{1,0:T(8,128)(2,1)S(1)}, bf16[96,384]{1,0:T(8,128)(2,1)S(1)}, u32[]{:S(2)}, u32[]{:S(2)}) collective-permute-start(bf16[96,384]{1,0:T(8,128)(2,1)S(1)} %get-tuple-element.203), channel_id=1, source_target_pairs={{0,16},{1,17},{2,18},{3,19},{4,20},{5,21},{6,22},{7,23},{8,24},{9,... | collective-permute-start | bytes 221192 | tf_op jit(solution)/shard_map/ppermute | solution.py:1047
  137.8 5.3 %collective-permute-start.42 = (bf16[96,384]{1,0:T(8,128)(2,1)S(1)}, bf16[96,384]{1,0:T(8,128)(2,1)S(1)}, u32[]{:S(2)}, u32[]{:S(2)}) collective-permute-start(bf16[96,384]{1,0:T(8,128)(2,1)S(1)} %get-tuple-element.201), channel_id=1, source_target_pairs={{0,8},{1,9},{2,10},{3,11},{4,12},{5,13},{6,14},{7,15},{8,0},{9,1},... | collective-permute-start | bytes 221192 | tf_op jit(solution)/shard_map/ppermute | solution.py:1047
  137.8 6.3 %collective-permute-start.44 = (bf16[96,384]{1,0:T(8,128)(2,1)S(1)}, bf16[96,384]{1,0:T(8,128)(2,1)S(1)}, u32[]{:S(2)}, u32[]{:S(2)}) collective-permute-start(bf16[96,384]{1,0:T(8,128)(2,1)S(1)} %get-tuple-element.204), channel_id=1, source_target_pairs={{0,24},{1,25},{2,26},{3,27},{4,28},{5,29},{6,30},{7,31},{8,16},{9,... | collective-permute-start | bytes 221192 | tf_op jit(solution)/shard_map/ppermute | solution.py:1047
  144.9 5.1 %collective-permute-start.45 = (bf16[96,768]{1,0:T(8,128)(2,1)S(1)}, bf16[96,768]{1,0:T(8,128)(2,1)S(1)}, u32[]{:S(2)}, u32[]{:S(2)}) collective-permute-start(bf16[96,768]{1,0:T(8,128)(2,1)S(1)} %get-tuple-element.205), channel_id=1, source_target_pairs={{0,2},{1,3},{2,0},{3,1},{4,6},{5,7},{6,4},{7,5},{8,10},{9,11},{10,... | collective-permute-start | bytes 442376 | tf_op jit(solution)/shard_map/ppermute | solution.py:1047
  146.2 1.3 collective-permute-start.46
  150.0 1.4 collective-permute-start.47
  (30 other events, 297.0 us)

commit v5 on v4

--- a/solution.py
+++ b/solution.py
@@ -377,16 +377,17 @@
 
 PAD_ID = 99
 PLAN = (
-    (45.0, ()), (0, (0,)), (0, (0,)), (0, (2,)), (7.0, ()), (0, ()), (0, ()), (0, (0,)), (0, ()), (0, (6,)),
-    (0, ()), (0, (0,)), (0, ()), (0, (5,)), (0, (5, 12, 1)), (0, ()), (0, ()), (0.2, (9,)), (0, ()),
-    (0, (11,)), (0.36, (8,)), (0, ()), (40, (3,)), (0, ()), (0, ()), (0, (19,)), (0, ()), (0, ()),
-    (0, (22, 6)), (1.6, ()), (0, (29,)), (0, ()), (0.001, (21, 23)), (0.84, (31, 24)), (0.185, (33,)),
-    (0, (34,)), (27.0, (19, 34)), (0, (33, 25)), (1.5, (31,)), (0, (33,)), (0.6, (36,)), (0, (40, 9)),
-    (2.0, (40,)), (0, (30, 31)), (0.7, ()), (0, ()), (0.54, (44,)), (0, (36,)), (0.001, ()), (0, (48,)),
-    (0.001, ()), (0, ()), (0.35, ()), (0, ()), (21.0, ()), (0, ()), (0.001, (46,)), (0, (56, 43)),
-    (3.6, (37, 22)), (0, ()), (0.001, (39, 44)), (0, (47,)), (0.14, ()), (0, ()), (0.21, (58,)), (0, ()),
-    (0, (64,)), (0, ()), (0.7, ()), (0, (60,)), (0.001, ()), (0.002, (70,)), (0.35, (71,)), (0.001, (72,)),
-    (0.07, ()), (0, ()), (0, ()), (0, (76, 75)), (0.42, (75,)), (11.0, (78,)),
+    (9.0, ()), (0, (0,)), (0, (0,)), (0, (2,)), (7.0, (2,)), (0, ()), (0, ()), (0, ()), (0, ()), (0, (4,)),
+    (0, (1,)), (0, (3,)), (0, (8,)), (0, ()), (0, (12, 1)), (0, (5, 10)), (0, (7, 3)), (20, ()), (0, ()),
+    (0, (11, 16)), (0, ()), (3.6, (17,)), (0, ()), (4, (3, 16, 0)), (0, (23,)), (0, (19, 0, 15)),
+    (0, (10,)), (0, ()), (0, (23, 6, 9)), (1.6, ()), (0, (18,)), (0, (29, 15)), (0.001, (28, 30)),
+    (2.8, ()), (45.0, (19,)), (0, (33, 31)), (0.185, (33, 20)), (0, (36,)), (0.09, (19, 36, 13)),
+    (0, (33, 25)), (0.6, (38,)), (0, (40, 9, 38)), (1.2, ()), (0, ()), (0.7, (31,)), (0, ()),
+    (0.001, (44,)), (0, (38, 44)), (0.001, ()), (0, (48,)), (21.0, ()), (0, ()), (0.002, ()), (0, (45,)),
+    (1.4, ()), (0, ()), (0.065, (46,)), (0, (56, 43, 48)), (1.8, (23,)), (0, (58, 37)), (0.07, (35, 44)),
+    (0, (47,)), (0.001, ()), (0, ()), (0.105, (58,)), (0, (55,)), (0, (65,)), (0, ()), (2.1, (33,)),
+    (0, (60,)), (0.7, (55, 54)), (0.7, (70,)), (0, ()), (0, ()), (0, (55,)), (3, ()), (0.9, (50,)), (0, ()),
+    (0, (59,)), (0, (78, 77)), (0.001, ()), (3, (80,)),
 )
 STEPS = []
 
@@ -432,8 +433,8 @@
 
 
 class Far:
-    def __init__(self, value, held=True):
-        self.value, self.held = value, held
+    def __init__(self, value):
+        self.value = value
 
 
 class Load:
@@ -447,74 +448,38 @@
         return self.buffer
 
 
-class Store:
-    def __init__(self, buffer, target, semaphore):
-        self.buffer, self.target, self.semaphore, self.copies = buffer, target, semaphore, []
-
-    def __setitem__(self, at, rows):
-        self.buffer[at] = rows
-
-    def __getitem__(self, at):
-        return self.buffer[at]
-
-    def go(self, at=None, source=None):
-        source, target = self.buffer if source is None else source, self.target
-        if at is not None:
-            source, target = source.at[at], target.at[at]
-        copy = pltpu.make_async_copy(source, target, self.semaphore.at[len(self.copies)])
-        copy.start()
-        self.copies.append(copy)
-
-
 def call(kernel, outs, ins, scratch=(), limit=20):
     us, after = plan()
     far = [i for i, v in enumerate(ins) if isinstance(v, Far)]
-    far_out = [i for i, v in enumerate(outs) if isinstance(v, Far)]
     plain = [v.value if isinstance(v, (Far, Keep)) else v for v in ins]
-    shapes = [v.value if isinstance(v, (Far, Keep)) else v for v in outs]
     near, away = pl.BlockSpec(memory_space=pltpu.VMEM), pl.BlockSpec(memory_space=pltpu.HBM)
-    held = [i for i in far_out if outs[i].held]
     room = [pltpu.VMEM(plain[i].shape, plain[i].dtype) for i in far]
-    room += [pltpu.VMEM(shapes[i].shape, shapes[i].dtype) for i in held]
-    if far or far_out:
-        room.append(pltpu.SemaphoreType.DMA((len(far) + len(far_out), MICRO)))
+    if far:
+        room.append(pltpu.SemaphoreType.DMA((len(far),)))
 
     def body(*refs):
         given = [*refs[: len(ins)], *refs[len(ins) + len(after) :]]
         own = given[len(ins) + len(outs) + len(scratch) :]
         given = given[: len(ins) + len(outs) + len(scratch)]
-        copies = []
         for k, i in enumerate(far):
-            copies.append(pltpu.make_async_copy(given[i], own[k], own[-1].at[k, 0]))
-            given[i] = Load(own[k], copies[-1])
-        buffers = dict(zip(held, own[len(far) :]))
-        stores = []
-        for k, i in enumerate(far_out):
-            stores.append(Store(buffers.get(i), given[len(ins) + i], own[-1].at[len(far) + k]))
-            given[len(ins) + i] = stores[-1]
-        for copy in copies:
+            copy = pltpu.make_async_copy(given[i], own[k], own[-1].at[k])
             copy.start()
+            given[i] = Load(own[k], copy)
         kernel(*given)
-        for store in stores:
-            for copy in store.copies:
-                copy.wait()
 
     def placed(v):
         if isinstance(v, Keep):
             return pltpu.with_memory_space_constraint(v.value, pltpu.VMEM)
         return pltpu.with_memory_space_constraint(v.value, pltpu.HBM) if isinstance(v, Far) else v
 
-    def made(v):
-        if isinstance(v, Keep):
-            return pltpu.VMEM(v.value.shape, v.value.dtype)
-        return pltpu.HBM(v.value.shape, v.value.dtype) if isinstance(v, Far) else v
-
     made_arrays = pl.pallas_call(
         body,
-        out_shape=tuple(made(v) for v in outs),
+        out_shape=tuple(
+            pltpu.VMEM(v.value.shape, v.value.dtype) if isinstance(v, Keep) else v for v in outs
+        ),
         in_specs=[away if i in far else near for i in range(len(ins))]
         + [pl.BlockSpec(memory_space=pl.ANY)] * len(after),
-        out_specs=tuple(away if i in far_out else near for i in range(len(outs))),
+        out_specs=tuple(near for _ in outs),
         scratch_shapes=[*scratch, *room],
         compiler_params=pltpu.CompilerParams(vmem_limit_bytes=limit * 2**20),
         cost_estimate=pl.CostEstimate(flops=int(us * 10**9), bytes_accessed=0, transcendentals=0),
@@ -618,49 +583,60 @@
         scratch[m * 368 + 352 : m * 368 + 362, :] = rows[m * 10 : m * 10 + 10]
 
 
-def norm_rows_in(rows_0, rows_1, rows_2, rows_3, tail, cot_tail, unit, tokens, cots, rows_f):
+def turned(line):
+    count = max(line.shape)
+    down = lax.broadcasted_iota(jnp.int32, (count, count), 0)
+    across = lax.broadcasted_iota(jnp.int32, (count, count), 1)
+    return jnp.sum(jnp.where(down == across, line, 0.0), line.shape.index(count), keepdims=True)
+
+
+def norm_rows_in(
+    rows_0, rows_1, rows_2, rows_3, tail, cot_tail, ids,
+    unit, bias, tokens, cots, unit_low, rows_f,
+):
+    slot = lax.broadcasted_iota(jnp.int32, (1, 16), 1)
+    tail_ids = jnp.where(slot < 2 * SPECIAL, (slot >= SPECIAL).astype(jnp.int32), PAD_ID)
+    for m in range(MICRO):
+        row = jnp.concatenate([ids[b * 2 + m : b * 2 + m + 1, :] for b in range(4)] + [tail_ids], 1)
+        row = row.astype(F32)
+        bias[m] = jnp.where(turned(row) == row, 0.0, MASKED)
     blocks = (rows_0, rows_1, rows_2, rows_3)
     place_rows(rows_f, blocks, cot_tail, 176)
     for at in row_blocks(32):
         cots[at, :] = rows_f[at, :].astype(BF16)
-    cots.go()
     place_rows(rows_f, blocks, tail, 0)
     for at in row_blocks(32):
         rows = rows_f[at, :]
         tokens[at, :] = rows.astype(BF16)
-        unit[at, :] = normalise(rows)[0]
-    tokens.go()
-
-
-def attend(ids_col, ids_row, unit, w_qkv, gain_rows, attended, w_kept, normed, projected, probs):
-    w_kept.go(source=w_qkv)
+        even = normalise(rows)[0]
+        unit[at, :] = even
+        unit_low[at, :] = even.astype(BF16)
+
+
+def attend(unit, bias, w_qkv, gain_rows, attended, projected, probs):
     gain = gain_rows[0:1, :]
     for m in range(MICRO):
         at = slice(m * 368, m * 368 + 368)
-        normed[at, :] = (unit[at, :] * gain).astype(BF16)
-        normed.go(at)
-        qkv = mm(normed[at, :], w_qkv[...])
+        qkv = mm((unit[at, :] * gain).astype(BF16), w_qkv[...])
         qkv = jnp.concatenate([qkv[:, 0:192] * SCORE_SCALE, qkv[:, 192:576]], -1).astype(BF16)
         projected[at, :] = qkv
-        projected.go(at)
-        same = ids_col[at, :] == ids_row[m : m + 1, :]
-        bias = jnp.where(same, 0.0, MASKED)
         heads = []
         for h in range(3):
             q = qkv[:, h * 64 : h * 64 + 64]
             k = qkv[:, 192 + h * 64 : 192 + h * 64 + 64]
             v = qkv[:, 384 + h * 64 : 384 + h * 64 + 64]
-            scores = mm_nt(q, k) + bias
+            scores = mm_nt(q, k) + bias[m]
             weights = jnp.exp(scores - jnp.max(scores, -1, keepdims=True))
             weights = weights * (1.0 / jnp.sum(weights, -1, keepdims=True))
             weights = weights.astype(BF16)
             probs[m * 3 + h] = weights
             heads.append(mm(weights, v))
-        probs.go(slice(m * 3, m * 3 + 3))
         attended[at, :] = jnp.concatenate(heads, -1).astype(BF16)
 
 
-def order_out(out_0, out_1, out_2, out_3, cots, gain_rows, ordered, mine, grad_mlp, out_f):
+def order_out(
+    out_0, out_1, out_2, out_3, cots, gain_rows, ordered, mine, grad_mlp, out_f
+):
     place = here()[0]
     for k, part in enumerate((out_0, out_1, out_2, out_3)):
         source = place ^ k
@@ -670,15 +646,13 @@
             out_f[pl.ds(at, 24), :] = rows[d * 24 : d * 24 + 24]
     ordered[...] = out_f[...].astype(BF16)
     mine[...] = out_f[pl.ds(pl.multiple_of(place * 192, 8), 192), :].astype(BF16)
-    mine.go()
     gain = gain_rows[3:4, :]
     for at in row_blocks(32):
         grad_mlp[at, :] = (gain * cots[at, :].astype(F32)).astype(BF16)
-    grad_mlp.go()
 
 
 def branch_rows(
-    head_0, head_1, head_2, head_3, w_out, tokens, gain_rows, normed, branch, middle, rows_f
+    head_0, head_1, head_2, head_3, w_out, tokens, gain_rows, normed, branch, own_rows, rows_f
 ):
     place = here()[0]
     gain_s, gain_n = gain_rows[1:2, :], gain_rows[2:3, :]
@@ -694,22 +668,23 @@
             a = rows_f[at, :]
             branch[at, :] = a.astype(BF16)
             rows = tokens[at, :].astype(F32) + gain_s * a
-            middle[at, :] = rows
+            rows_f[at, :] = rows
             normed[at, :] = (normalise(rows)[0] * gain_n).astype(BF16)
-        branch.go(group)
-        middle.go(group)
+        for part, first in ((0, place * 88), (88, 352)):
+            rows = 88 if part == 0 else 16
+            own_rows[m * 104 + part : m * 104 + part + rows, :] = rows_f[
+                pl.ds(pl.multiple_of(m * 368 + first, 8), rows), :
+            ]
 
 
 def raise_rows(*refs):
     normed, chunks = refs[0], refs[1:9]
-    active, slope, w_up, w_down, normed_kept, down_kept, rows_f = refs[9:]
-    normed_kept.go(source=normed)
+    active, slope, w_up, w_down, rows_f = refs[9:]
     _, _, _, z, y = here()
     for slot, chunk in enumerate(chunks):
         d = chunk_index(slot, z, y)
         w_up[pl.ds(pl.multiple_of(d * 96, 96), 96), :] = chunk[0:96, :]
         w_down[pl.ds(pl.multiple_of(d * 96, 96), 96), :] = chunk[96:192, :]
-    down_kept.go(source=w_down)
     for m in range(MICRO):
         at = slice(m * 368, m * 368 + 368)
         rows_f[at, :] = mm(normed[at, :], w_up[...])
@@ -720,8 +695,7 @@
         slope[at, :] = half + u * (0.3989422804014327 * jnp.exp(-0.5 * u * u))
 
 
-def down_grads(active, grad_mlp, away, kept, active_kept, work):
-    active_kept.go(source=active)
+def down_grads(active, grad_mlp, away, kept, work):
     _, _, _, z, _ = here()
     work[...] = mm_tn(active[...], grad_mlp[...])
     for pair in range(2):
@@ -749,7 +723,6 @@
         at = slice(m * 368, m * 368 + 368)
         grad = mm_nt(grad_mlp[at, :], w_down[...])
         grad_hidden[at, :] = (slope[at, :] * grad).astype(BF16)
-        grad_hidden.go(at)
         work[m] = mm_nt(grad_hidden[at, :], w_up[...])
     away[...] = work[1 - core].astype(BF16)
     kept[...] = work[core]
@@ -779,20 +752,18 @@
 
 def up_grads(normed, grad_hidden, away, kept, work):
     y = here()[4]
-    work[...] = mm_tn(normed.ready()[...], grad_hidden.ready()[...])
+    work[...] = mm_tn(normed[...], grad_hidden[...])
     halve(work, y, away, kept, 96)
 
 
 def mlp_rows(
-    active, w_down, cots, targets, head_0, head_1, head_2, head_3,
+    active, w_down, cots, head_0, head_1, head_2, head_3,
     rows_away, rows_kept, scale_grad, chosen, work, pieces,
 ):
     place = here()[0]
-    active, w_down = active.ready(), w_down.ready()
     for m in range(MICRO):
         at = slice(m * 368, m * 368 + 368)
         work[at, :] = mm(active[at, :], w_down[...])
-    cots = cots.ready()
     total = jnp.zeros((8, 768), F32)
     for at in row_blocks(32):
         total = total + fold(cots[at, :].astype(F32) * work[at, :])
@@ -800,9 +771,12 @@
     cut_rows(work, pieces)
     split_rows(pieces, place, rows_away, rows_kept)
     picked = None
+    column = lax.broadcasted_iota(jnp.int32, (192, 192), 1)
+    chunk = sum((column >= 24 * d).astype(jnp.int32) for d in range(1, 8))
+    targets = column + chunk * 72 + place * 24
     for k, part in enumerate((head_0, head_1, head_2, head_3)):
         index = lax.broadcasted_iota(jnp.int32, (192, 192), 0) + (place ^ k) * 192
-        pick = jnp.where(index == targets[...], 1.0, 0.0).astype(BF16)
+        pick = jnp.where(index == targets, 1.0, 0.0).astype(BF16)
         term = mm(part[...], pick)
         picked = term if picked is None else picked + term
     chosen[...] = picked.astype(BF16)
@@ -817,7 +791,7 @@
 
 
 def branch_back(
-    sum_own, sum_near, middle, cots, branch, gain_rows, w_mine, probs, normed, scale_grad_mlp, chosen,
+    sum_own, sum_near, tokens, cots, branch, gain_rows, w_mine, probs, normed, scale_grad_mlp, chosen,
     grad_rows, grad_heads, grad_v, away, kept,
     work, grad_branch, grad_mid, extra, early,
 ):
@@ -836,7 +810,8 @@
     gain_s, gain_n = gain_rows[1:2, :], gain_rows[2:3, :]
     scale_sum = jnp.zeros((8, 768), F32)
     for at in row_blocks(32):
-        unit, scale = normalise(middle[at, :])
+        grown = branch[at, :].astype(F32)
+        unit, scale = normalise(tokens[at, :].astype(F32) + gain_s * grown)
         pulled = work[at, :] * gain_n
         pulled = pulled - jnp.mean(pulled, -1, keepdims=True) - unit * jnp.mean(
             pulled * unit, -1, keepdims=True
@@ -844,7 +819,7 @@
         through = cots[at, :].astype(F32) + scale * pulled
         grad_mid[at, :] = through
         grad_branch[at, :] = (gain_s * through).astype(BF16)
-        scale_sum = scale_sum + fold(through * branch[at, :].astype(F32))
+        scale_sum = scale_sum + fold(through * grown)
     for m in range(MICRO):
         for part, first in ((0, place * 88), (88, 352)):
             rows = 88 if part == 0 else 16
@@ -933,15 +908,6 @@
     total[...] = own[...] + came[...].astype(F32)
 
 
-def sum_z(own, came_1, came_2, came_3, total):
-    total[...] = (
-        own[...]
-        + came_1[...].astype(F32)
-        + came_2[...].astype(F32)
-        + came_3[...].astype(F32)
-    )
-
-
 def add_pieces(kept_m, came_m, kept_h, came_h, stay, go):
     for i, (kept, came) in enumerate(((kept_m, came_m), (kept_h, came_h))):
         stay[i * 208 : i * 208 + 208, :] = kept[0:208, :] + came[0:208, :].astype(F32)
@@ -949,20 +915,17 @@
 
 
 def finish_rows(
-    stay, came, middle, grad_rows, patches, tail, gain_rows,
+    stay, came, own_rows, grad_rows, patches, tail, gain_rows,
     out_patches, out_special, grad_patches, grad_special,
 ):
-    place = here()[0]
     own = patches[...].astype(F32)
     rest = tail[...].astype(F32)
     outs, out_tails = [], []
     for m in range(MICRO):
-        for part, first in ((0, place * 88), (88, 352)):
-            count = 88 if part == 0 else 10
+        for part, count in ((0, 88), (88, 10)):
             at = slice(m * 104 + part, m * 104 + part + count)
             far_at = slice(208 + m * 104 + part, 208 + m * 104 + part + count)
-            mid = middle[pl.ds(pl.multiple_of(m * 368 + first, 8), count), :]
-            final = mid + gain_rows[3:4, :] * (stay[at, :] + came[at, :].astype(F32))
+            final = own_rows[at, :] + gain_rows[3:4, :] * (stay[at, :] + came[at, :].astype(F32))
             (outs if part == 0 else out_tails).append(final)
             rows = own[m * 88 : m * 88 + 88] if part == 0 else rest[m * 10 : m * 10 + 10]
             unit, scale = normalise(rows)
@@ -979,54 +942,72 @@
     out_special[...] = jnp.concatenate(out_tails, 0).astype(BF16)
 
 
-def pick_grads(up, first, second, own, near, far, grad_out, held):
+def hand_out(held, own, near, far):
     place = here()[0]
-    for b in range(4):
-        at = slice(b * 24, b * 24 + 24)
-        held[b, 0:24, :] = up[at, :]
-        held[b, 24:48, 0:384] = second[at, :]
-        held[b, 24:48, 384:576] = first[at, 0:192]
-        held[b, 24:48, 576:768] = jnp.zeros((24, 192), F32)
-        held[b, 24:26, 576:600] = first[96:98, at]
-        grad_out[:, b * 192 : b * 192 + 192] = first[at, 192:384]
     own[...] = held[place]
     near[...] = held[place ^ 1].astype(BF16)
-    far[0:48, :] = held[place ^ 2].astype(BF16)
-    far[48:96, :] = held[place ^ 3].astype(BF16)
-
-
-def as_row(column):
-    count = column.shape[0]
-    square = lax.broadcasted_iota(jnp.int32, (count, count), 0)
-    across = lax.broadcasted_iota(jnp.int32, (count, count), 1)
-    return jnp.sum(jnp.where(square == across, column, 0.0), 0, keepdims=True)
-
-
-def join_grads(
-    own, near, far, near_far, w_qkv, w_up, gains, grad_qkv, grad_up, grad_gains, held
-):
+    far[0:32, :] = held[place ^ 2].astype(BF16)
+    far[32:64, :] = held[place ^ 3].astype(BF16)
+
+
+def take_in(held, own, near, far, near_far):
     place = here()[0]
     held[place] = own[...]
     held[place ^ 1] = near[...].astype(F32)
-    held[place ^ 2] = far[0:48, :].astype(F32)
-    held[place ^ 3] = near_far[48:96, :].astype(F32)
-    scales = None
+    held[place ^ 2] = far[0:32, :].astype(F32)
+    held[place ^ 3] = near_far[32:64, :].astype(F32)
+
+
+def pick_up(kept, came, own, near, far, held):
+    held[...] = jnp.zeros_like(held)
+    for b in range(4):
+        at = slice(b * 24, b * 24 + 24)
+        held[b, 0:24, :] = kept[at, :] + came[at, :].astype(F32)
+    hand_out(held, own, near, far)
+
+
+def pick_attention(kept_a, came_a, kept_b, came_1, came_2, came_3, own, near, far, grad_out, held, sums):
+    held[...] = jnp.zeros_like(held)
+    sums[:, 0:384] = kept_a[...] + came_a[...].astype(F32)
+    sums[0:96, 384:768] = (
+        kept_b[...] + came_1[...].astype(F32) + came_2[...].astype(F32) + came_3[...].astype(F32)
+    )
+    for b in range(4):
+        at = slice(b * 24, b * 24 + 24)
+        held[b, 0:24, 0:384] = sums[at, 384:768]
+        held[b, 0:24, 384:576] = sums[at, 0:192]
+        held[b, 0:2, 576:600] = sums[96:98, at]
+        grad_out[:, b * 192 : b * 192 + 192] = sums[at, 192:384]
+    hand_out(held, own, near, far)
+
+
+def join_up(own, near, far, near_far, w_up, gains, grad_up, norm_grad, held):
+    take_in(held, own, near, far, near_far)
     for b in range(4):
         for d in range(8):
             at = d * 384 + b * 96
             grad_up[:, at : at + 96] = held[b, 0:24, d * 96 : d * 96 + 96]
+    total = turned(jnp.sum(w_up[...].astype(F32) * grad_up[...], -1, keepdims=True))
+    norm_grad[...] = total / gains[2:3, :].astype(F32)
+
+
+def join_attention(
+    own, near, far, near_far, w_qkv, gains, norm_grad, grad_qkv, grad_gains, held
+):
+    take_in(held, own, near, far, near_far)
+    scales = None
+    for b in range(4):
         for part in range(3):
-            at = part * 768 + b * 192
-            grad_qkv[:, at : at + 192] = held[b, 24:48, part * 192 : part * 192 + 192]
-        term = held[b, 24:26, 576:600]
+            at = slice(part * 768 + b * 192, part * 768 + b * 192 + 192)
+            grad_qkv[:, at] = held[b, 0:24, part * 192 : part * 192 + 192]
+        term = held[b, 0:2, 576:600]
         scales = term if scales is None else scales + term
-    norm_1 = as_row(jnp.sum(w_qkv[...].astype(F32) * grad_qkv[...], -1, keepdims=True))
-    norm_2 = as_row(jnp.sum(w_up[...].astype(F32) * grad_up[...], -1, keepdims=True))
-    gain = gains[...].astype(F32)
-    grad_gains[0:1, :] = norm_1 / gain[0:1, :]
+    plain = grad_qkv[...]
+    grad_gains[0:1, :] = turned(jnp.sum(w_qkv[...].astype(F32) * plain, -1, keepdims=True))
     grad_gains[1:2, :] = scales[0:1, :]
-    grad_gains[2:3, :] = norm_2 / gain[2:3, :]
+    grad_gains[2:3, :] = norm_grad[...]
     grad_gains[3:4, :] = scales[1:2, :]
+    grad_qkv[...] = plain * turned(gains[0:1, :].astype(F32))
 
 
 def send(rows, axis, step):
@@ -1095,27 +1076,10 @@
     )[0]
 
 
-def add_z(steps):
-    own, *came = steps
-    return call(
-        sum_z, [sds(*own.shape, dtype=F32)], [Keep(own), *came]
-    )[0]
-
-
 def on_device_split(
     patches, special, image_ids, w_qkv, w_out, w_up, w_down, gains, cot_patches, cot_special
 ):
     STEPS.clear()
-    place = lax.axis_index("blk")
-    spec_ids = jnp.concatenate(
-        [jnp.arange(10, dtype=jnp.int32) // SPECIAL, jnp.full((6,), PAD_ID, jnp.int32)]
-    )
-    ids = image_ids.reshape(4, 2, 88).transpose(1, 0, 2).reshape(2, 352)
-    ids_row = jnp.concatenate([ids, jnp.broadcast_to(spec_ids, (2, 16))], 1)
-    ids_col = ids_row.reshape(736, 1)
-    column = jnp.arange(192, dtype=jnp.int32)
-    targets = (column + column // 24 * 72 + place * 24).reshape(1, 192)
-
     own, near, far, rows = call(
         pick_pieces,
         [sds(48, 768), sds(48, 768), sds(96, 768), sds(352, 768)],
@@ -1142,14 +1106,15 @@
     both_1 = send(both, "z", 1)
     near_rows = send(rows, "core", 1)
     row_parts = [rows, near_rows, far_rows, send(far_rows, "core", 1)]
-    unit, tokens, cots = call(
+    unit, bias, tokens, cots, unit_low = call(
         norm_rows_in,
-        [Keep(sds(736, 768, dtype=F32)), *[Far(sds(736, 768))] * 2],
-        [*row_parts, special, cot_special],
+        keep(sds(736, 768, dtype=F32), sds(2, 368, 368, dtype=F32), *[sds(736, 768)] * 3),
+        [*row_parts, special, cot_special, image_ids.reshape(8, 88)],
         [pltpu.VMEM((736, 768), F32)],
     )
     pack_y3 = send(pack_3, "y", 1)
     both_y1 = send(both_1, "y", 1)
+    both_3 = send(both_2, "z", 1)
     qkv_full, out_part, gain_rows = call(
         open_pack,
         [Keep(sds(768, 576)), sds(192, 768), Keep(sds(8, 768, dtype=F32))],
@@ -1157,16 +1122,12 @@
         [pltpu.VMEM((192, 768), F32), pltpu.VMEM((8, 16, 768), F32)],
     )
     far_out = send(out_part, "x", 1)
-    attended, qkv_far, normed_far, projected, probs = call(
+    attended, projected, probs = call(
         attend,
-        [
-            sds(736, 192), Far(sds(768, 576), held=False), Far(sds(736, 768)),
-            Far(sds(736, 576)), Far(sds(6, 368, 368)),
-        ],
-        [ids_col, ids_row, *keep(unit, qkv_full, gain_rows)],
+        [sds(736, 192), *keep(sds(736, 576), sds(6, 368, 368))],
+        keep(unit, bias, qkv_full, gain_rows),
     )
     far_heads = send(attended, "x", 1)
-    both_3 = send(both_2, "z", 1)
     both_y2 = send(both_2, "y", 1)
     out_parts = [
         out_part, send(out_part, "core", 1),
@@ -1175,8 +1136,8 @@
     both_y3 = send(both_3, "y", 1)
     out_full, out_mine, grad_mlp = call(
         order_out,
-        [Keep(sds(768, 768)), Far(sds(192, 768)), Far(sds(736, 768))],
-        [*out_parts, cots, Keep(gain_rows)],
+        keep(sds(768, 768), sds(192, 768), sds(736, 768)),
+        [*out_parts, *keep(cots, gain_rows)],
         [pltpu.VMEM((768, 768), F32)],
     )
     heads = [
@@ -1184,18 +1145,15 @@
         far_heads, send(far_heads, "core", 1),
     ]
     both_chunks = [both, both_1, both_2, both_3, both_y0, both_y1, both_y2, both_y3]
-    normed_mlp, branch, middle = call(
+    normed_mlp, branch, own_rows = call(
         branch_rows,
-        [Keep(sds(736, 768)), Far(sds(736, 768)), Far(sds(736, 768, dtype=F32))],
-        [*heads, Keep(out_full), tokens, Keep(gain_rows)],
+        keep(sds(736, 768), sds(736, 768), sds(208, 768, dtype=F32)),
+        [*heads, *keep(out_full, tokens, gain_rows)],
         [pltpu.VMEM((736, 768), F32)],
     )
-    active, slope, up_full, down_full, normed_mlp, down_far = call(
+    active, slope, up_full, down_full = call(
         raise_rows,
-        [
-            *keep(sds(736, 768), sds(736, 768, dtype=F32), sds(768, 768), sds(768, 768)),
-            Far(sds(736, 768), held=False), Far(sds(768, 768), held=False),
-        ],
+        keep(sds(736, 768), sds(736, 768, dtype=F32), sds(768, 768), sds(768, 768)),
         [Keep(normed_mlp), *both_chunks],
         [pltpu.VMEM((736, 768), F32)],
     )
@@ -1205,33 +1163,33 @@
     def make_down(active):
         return call(
             down_grads,
-            [*half, Far(sds(736, 768), held=False)],
-            [Keep(active), grad_mlp],
+            half,
+            keep(active, grad_mlp),
             [pltpu.VMEM((768, 768), F32)],
         )
 
+    down_away, down_kept = make_down(active)
+    down_came = send(down_away, "z", 1)
     sum_away, sum_kept, grad_hidden = call(
         lower_rows,
-        [sds(368, 768), Keep(sds(368, 768, dtype=F32)), Far(sds(736, 768))],
-        [Keep(slope), grad_mlp, *keep(up_full, down_full)],
+        [sds(368, 768), *keep(sds(368, 768, dtype=F32), sds(736, 768))],
+        keep(slope, grad_mlp, up_full, down_full),
         [pltpu.VMEM((2, 368, 768), F32)],
     )
     sum_came = send(sum_away, "core", 1)
     chip_sum = call(add_rows, [sds(368, 768)], [Keep(sum_kept), sum_came])[0]
     chip_came = send(chip_sum, "x", 1)
-    down_away, down_kept, active = make_down(active)
-    down_came = send(down_away, "z", 1)
     up_away, up_kept = call(
         up_grads,
         half,
-        [Far(normed_mlp), Far(grad_hidden)],
+        keep(normed_mlp, grad_hidden),
         [pltpu.VMEM((768, 768), F32)],
     )
     up_came = send(up_away, "y", 1)
     m_away, m_kept, scale_mlp, chosen = call(
         mlp_rows,
         [*rows_split, *keep(sds(8, 768, dtype=F32), sds(736, 192))],
-        [*[Far(v) for v in (active, down_far, cots)], targets, *heads],
+        [*keep(active, down_full, cots), *heads],
         [pltpu.VMEM((736, 768), F32), pltpu.VMEM((4, 208, 768), F32)],
     )
     m_came = send(m_away, "core", 1)
@@ -1250,8 +1208,7 @@
             sds(4, 112, 384), Keep(sds(4, 112, 384, dtype=F32)),
         ],
         [
-            sum_own, sum_near, middle, cots, branch, Keep(gain_rows), out_mine,
-            probs, normed_far, *keep(scale_mlp, chosen),
+            sum_own, sum_near, *keep(tokens, cots, branch, gain_rows, out_mine, probs, unit_low), *keep(scale_mlp, chosen),
         ],
         [
             pltpu.VMEM((736, 768), F32), pltpu.VMEM((736, 768), BF16),
@@ -1259,19 +1216,19 @@
         ],
     )
     a_came = send(a_away, "y", 1)
+    up_steps = halve_y(up_kept, up_came)
     grad_qk, b_away, b_kept = call(
         score_back,
         [Keep(sds(736, 384)), sds(4, 96, 384), Keep(sds(4, 96, 384, dtype=F32))],
-        [probs, projected, Keep(grad_heads), normed_far],
+        keep(probs, projected, grad_heads, unit_low),
         [pltpu.VMEM((768, 384), F32)],
     )
     b_came = send(b_away, "y", 1)
     a_pair = halve_y(a_kept, a_came)
-    up_steps = halve_y(up_kept, up_came)
     h_away, h_kept = call(
         project_back,
         rows_split,
-        [*keep(grad_qk, grad_v), qkv_far],
+        keep(grad_qk, grad_v, qkv_full),
         [pltpu.VMEM((736, 768), F32), pltpu.VMEM((4, 208, 768), F32)],
     )
     h_came = send(h_away, "core", 1)
@@ -1286,14 +1243,22 @@
     b_steps = add_y(b_kept, b_came)
     a_last = halve_z(a_pair)
     grad_down = add_last(down_last)
-    grad_up_rows = add_last(up_last)
-    first_rows = add_last(a_last)
-    second_rows = add_z(b_steps)
+    pieces = [Keep(sds(32, 768, dtype=F32)), sds(32, 768), sds(64, 768)]
+    held = pltpu.VMEM((4, 32, 768), F32)
+    own, near, far = call(pick_up, pieces, [Keep(up_last[0]), up_last[1]], [held])
+    came_far = send(far, "x", 1)
+    came_near, came_near_far = send(near, "core", 1), send(came_far, "core", 1)
+    grad_up, norm_grad = call(
+        join_up,
+        [sds(24, 3072, dtype=F32), Keep(sds(1, 24, dtype=F32))],
+        [Keep(own), came_near, came_far, came_near_far, w_up, gains],
+        [held],
+    )
     own, near, far, grad_out = call(
-        pick_grads,
-        [Keep(sds(48, 768, dtype=F32)), sds(48, 768), sds(96, 768), sds(24, 768, dtype=F32)],
-        [grad_up_rows, first_rows, second_rows],
-        [pltpu.VMEM((4, 48, 768), F32)],
+        pick_attention,
+        [*pieces, sds(24, 768, dtype=F32)],
+        [Keep(a_last[0]), a_last[1], Keep(b_steps[0]), *b_steps[1:]],
+        [held, pltpu.VMEM((112, 768), F32)],
     )
     came_far = send(far, "x", 1)
     came_near, came_near_far = send(near, "core", 1), send(came_far, "core", 1)
@@ -1302,13 +1267,13 @@
         [
             sds(176, 768), sds(20, 768), sds(176, 768, dtype=F32), sds(20, 768, dtype=F32),
         ],
-        [Keep(stay), far_rows, middle, Keep(grad_rows), patches, special, Keep(gain_rows)],
-    )
-    grad_qkv, grad_up, grad_gains = call(
-        join_grads,
-        [sds(24, 2304, dtype=F32), sds(24, 3072, dtype=F32), sds(4, 24, dtype=F32)],
-        [Keep(own), came_near, came_far, came_near_far, w_qkv, w_up, gains],
-        [pltpu.VMEM((4, 48, 768), F32)],
+        [Keep(stay), far_rows, *keep(own_rows, grad_rows), patches, special, Keep(gain_rows)],
+    )
+    grad_qkv, grad_gains = call(
+        join_attention,
+        [sds(24, 2304, dtype=F32), sds(4, 24, dtype=F32)],
+        [Keep(own), came_near, came_far, came_near_far, w_qkv, gains, Keep(norm_grad)],
+        [held],
     )
     return (
         out_patches, out_special, grad_patches, grad_special,

time: 154 us -> 147 us (0.955)
  Pallas kernels: 45.2 us -> 34.1 us
  waiting for transfers between devices: 53.1 us -> 62.1 us
  starting transfers between devices: 50 us -> 46.3 us
    pallas_call x32 -> x31, Pallas kernels: 45.2 us -> 34.1 us  [call(): pl.pallas_call(body, out_shape=tuple((pltpu.VMEM(v.value.shape, v.value.d...]
    ppermute x48 -> x51, waiting for transfers between devices: 53.1 us -> 62.1 us  [send(): STEPS.append(lax.ppermute(rows, ('dp', 'blk'), pairs))]
    ppermute x48 -> x51, starting transfers between devices: 50 us -> 46.3 us  [send(): STEPS.append(lax.ppermute(rows, ('dp', 'blk'), pairs))]
    unnamed x60 -> x30, local copies, waits for them, and re-layouts: 3.5 us -> 3.24 us
  transfers between devices with their start and end apart: 48 -> 51, of which waited for: 19 -> 28; matrix products, arithmetic and copies ran while one was open for 0% -> 0% of each run, Pallas kernels for 23% -> 19%
where the time goes in v5:
time: 147 us
  waiting for transfers between devices  62.1 us (42%)
  starting transfers between devices  46.3 us (31%)
  Pallas kernels  34.1 us (23%)
  local copies, waits for them, and re-layouts  3.31 us (2%)
    ppermute x51, waiting for transfers between devices, send(): STEPS.append(lax.ppermute(rows, ('dp', 'blk'), pairs))  62.1 us
    ppermute x51, starting transfers between devices, send(): STEPS.append(lax.ppermute(rows, ('dp', 'blk'), pairs))  46.3 us
    pallas_call x31, Pallas kernels, call(): pl.pallas_call(body, out_shape=tuple((pltpu.VMEM(v.value.shape, v.value.d...  34.1 us
    unnamed x30, local copies, waits for them, and re-layouts  3.24 us
  transfers between devices with their start and end apart: 51, of which 28 were waited for; matrix products, arithmetic and copies ran while one was open for 0% of the time, Pallas kernels for 19%

profile of v5, /device:TPU:0, one launch (start us, length us, event | category | flops | bytes accessed | tf_op | source)
XLA Modules:
  0.0 146.8 jit_solution(7139420519881813113)
XLA Ops:
  0.7 1.3 pick_pieces.1
  2.0 3.0 %collective-permute-start.1 = (bf16[96,768]{1,0:T(8,128)(2,1)S(1)}, bf16[96,768]{1,0:T(8,128)(2,1)S(1)}, u32[]{:S(2)}, u32[]{:S(2)}) collective-permute-start(bf16[96,768]{1,0:T(8,128)(2,1)S(1)} %get-tuple-element.128), channel_id=1, source_target_pairs={{0,2},{1,3},{2,0},{3,1},{4,6},{5,7},{6,4},{7,5},{8,10},{9,11},{10,... | collective-permute-start | bytes 442376 | tf_op jit(solution)/shard_map/ppermute | solution.py:1028
  5.0 1.3 collective-permute-done.refs_1_.refs_6_
  6.2 2.6 %collective-permute-done.1.refs_2_ = bf16[96,768]{1,0:T(8,128)(2,1)S(1)} collective-permute-done((bf16[96,768]{1,0:T(8,128)(2,1)S(1)}, bf16[96,768]{1,0:T(8,128)(2,1)S(1)}, u32[]{:S(2)}, u32[]{:S(2)}) %collective-permute-start.1) | collective-permute-done | bytes 147488 | tf_op jit(solution)/shard_map/ppermute | solution.py:1028
  8.8 1.8 %collective-permute-start.7 = (bf16[352,768]{1,0:T(8,128)(2,1)S(1)}, bf16[352,768]{1,0:T(8,128)(2,1)S(1)}, u32[]{:S(2)}, u32[]{:S(2)}) collective-permute-start(bf16[352,768]{1,0:T(8,128)(2,1)S(1)} %get-tuple-element.132.refs_0_), channel_id=1, source_target_pairs={{0,2},{1,3},{2,0},{3,1},{4,6},{5,7},{6,4},{7,5},{8,10},{9,11},{10,... | collective-permute-start | bytes 1622024 | tf_op jit(solution)/shard_map/ppermute | solution.py:1028
  11.3 1.6 %collective-permute-start.4 = (bf16[112,768]{1,0:T(8,128)(2,1)S(1)}, bf16[112,768]{1,0:T(8,128)(2,1)S(1)}, u32[]{:S(2)}, u32[]{:S(2)}) collective-permute-start(bf16[112,768]{1,0:T(8,128)(2,1)S(1)} %get-tuple-element.130.refs_0_), channel_id=1, source_target_pairs={{0,8},{1,9},{2,10},{3,11},{4,12},{5,13},{6,14},{7,15},{8,0},{9,1},... | collective-permute-start | bytes 516104 | tf_op jit(solution)/shard_map/ppermute | solution.py:1028
  12.9 1.5 %collective-permute-start.8 = (bf16[112,768]{1,0:T(8,128)(2,1)S(1)}, bf16[112,768]{1,0:T(8,128)(2,1)S(1)}, u32[]{:S(2)}, u32[]{:S(2)}) collective-permute-start(bf16[112,768]{1,0:T(8,128)(2,1)S(1)} %get-tuple-element.130.refs_0_), channel_id=1, source_target_pairs={{0,4},{1,5},{2,6},{3,7},{4,0},{5,1},{6,2},{7,3},{8,12},{9,13},{10,... | collective-permute-start | bytes 516104 | tf_op jit(solution)/shard_map/ppermute | solution.py:1028
  14.4 2.6 %collective-permute-start.3 = (bf16[112,768]{1,0:T(8,128)(2,1)S(1)}, bf16[112,768]{1,0:T(8,128)(2,1)S(1)}, u32[]{:S(2)}, u32[]{:S(2)}) collective-permute-start(bf16[112,768]{1,0:T(8,128)(2,1)S(1)} %get-tuple-element.130.refs_0_), channel_id=1, source_target_pairs={{0,16},{1,17},{2,18},{3,19},{4,20},{5,21},{6,22},{7,23},{8,24},{9,... | collective-permute-start | bytes 516104 | tf_op jit(solution)/shard_map/ppermute | solution.py:1028
  17.0 2.4 %collective-permute-done.4.refs_1_ = bf16[112,768]{1,0:T(8,128)(2,1)S(1)} collective-permute-done((bf16[112,768]{1,0:T(8,128)(2,1)S(1)}, bf16[112,768]{1,0:T(8,128)(2,1)S(1)}, u32[]{:S(2)}, u32[]{:S(2)}) %collective-permute-start.4) | collective-permute-done | bytes 172064 | tf_op jit(solution)/shard_map/ppermute | solution.py:1028
  19.4 3.2 %collective-permute-start.5 = (bf16[112,768]{1,0:T(8,128)(2,1)S(1)}, bf16[112,768]{1,0:T(8,128)(2,1)S(1)}, u32[]{:S(2)}, u32[]{:S(2)}) collective-permute-start(bf16[112,768]{1,0:T(8,128)(2,1)S(1)} %collective-permute-done.4.refs_1_), channel_id=1, source_target_pairs={{0,4},{1,5},{2,6},{3,7},{4,0},{5,1},{6,2},{7,3},{8,12},{9,13},{10,... | collective-permute-start | bytes 516104 | tf_op jit(solution)/shard_map/ppermute | solution.py:1028
  23.5 1.4 collective-permute-done.3.refs_2_
  26.1 2.0 %collective-permute-start.11 = (bf16[112,768]{1,0:T(8,128)(2,1)S(1)}, bf16[112,768]{1,0:T(8,128)(2,1)}, u32[]{:S(2)}, u32[]{:S(2)}) collective-permute-start(bf16[112,768]{1,0:T(8,128)(2,1)S(1)} %collective-permute-done.3.refs_2_), channel_id=1, source_target_pairs={{0,4},{1,5},{2,6},{3,7},{4,0},{5,1},{6,2},{7,3},{8,12},{9,13},{10,... | collective-permute-start | bytes 516104 | tf_op jit(solution)/shard_map/ppermute | solution.py:1028
  28.1 3.2 %collective-permute-start.19 = (bf16[192,768]{1,0:T(8,128)(2,1)S(1)}, bf16[192,768]{1,0:T(8,128)(2,1)S(1)}, u32[]{:S(2)}, u32[]{:S(2)}) collective-permute-start(bf16[192,768]{1,0:T(8,128)(2,1)S(1)} %get-tuple-element.153.refs_1_), channel_id=1, source_target_pairs={{0,16},{1,17},{2,18},{3,19},{4,20},{5,21},{6,22},{7,23},{8,24},{9,... | collective-permute-start | bytes 884744 | tf_op jit(solution)/shard_map/ppermute | solution.py:1028
  31.4 3.4 %collective-permute-done.10.refs_3_ = bf16[112,768]{1,0:T(8,128)(2,1)S(1)} collective-permute-done((bf16[112,768]{1,0:T(8,128)(2,1)S(1)}, bf16[112,768]{1,0:T(8,128)(2,1)S(1)}, u32[]{:S(2)}, u32[]{:S(2)}) %collective-permute-start.10) | collective-permute-done | bytes 172064 | tf_op jit(solution)/shard_map/ppermute | solution.py:1028
  34.8 3.4 %collective-permute-start.12 = (bf16[112,768]{1,0:T(8,128)(2,1)S(1)}, bf16[112,768]{1,0:T(8,128)(2,1)S(1)}, u32[]{:S(2)}, u32[]{:S(2)}) collective-permute-start(bf16[112,768]{1,0:T(8,128)(2,1)S(1)} %collective-permute-done.10.refs_3_), channel_id=1, source_target_pairs={{0,4},{1,5},{2,6},{3,7},{4,0},{5,1},{6,2},{7,3},{8,12},{9,13},{10,... | collective-permute-start | bytes 516104 | tf_op jit(solution)/shard_map/ppermute | solution.py:1028
  39.0 2.1 %norm_rows_in.1 = (f32[736,768]{1,0:T(8,128)S(1)}, f32[2,368,368]{2,1,0:T(8,128)S(1)}, bf16[736,768]{1,0:T(8,128)(2,1)S(1)}, bf16[736,768]{1,0:T(8,128)(2,1)S(1)}, bf16[736,768]{1,0:T(8,128)(2,1)S(1)}) custom-call(bf16[352,768]{1,0:T(8,128)(2,1)S(1)} %get-tuple-element.132.refs_0_, bf16[352,768]{1,0:T(8,128)(2,1)S(1)} %collective-permute-done.6.refs_1_, ...), custom_call_target="tpu_custom_call" | custom-call | flops 20000000000 | tf_op jit(solution)/shard_map/norm_rows_in/pallas_call | solution.py:475
  41.1 1.4 collective-permute-done.12.refs_7_
  43.7 1.3 collective-permute-start.16
  45.1 1.7 %collective-permute-start.21 = (bf16[192,768]{1,0:T(8,128)(2,1)S(1)}, bf16[192,768]{1,0:T(8,128)(2,1)S(1)}, u32[]{:S(2)}, u32[]{:S(2)}) collective-permute-start(bf16[192,768]{1,0:T(8,128)(2,1)S(1)} %get-tuple-element.153.refs_1_), channel_id=1, source_target_pairs={{0,4},{1,5},{2,6},{3,7},{4,0},{5,1},{6,2},{7,3},{8,12},{9,13},{10,... | collective-permute-start | bytes 884744 | tf_op jit(solution)/shard_map/ppermute | solution.py:1028
  46.8 4.5 %collective-permute-done.23.refs_2_ = bf16[192,768]{1,0:T(8,128)(2,1)S(1)} collective-permute-done((bf16[192,768]{1,0:T(8,128)(2,1)S(1)}, bf16[192,768]{1,0:T(8,128)(2,1)S(1)}, u32[]{:S(2)}, u32[]{:S(2)}) %collective-permute-start.23) | collective-permute-done | bytes 294944 | tf_op jit(solution)/shard_map/ppermute | solution.py:1028
  51.9 3.2 %attend.1 = (bf16[736,192]{1,0:T(8,128)(2,1)S(1)}, bf16[736,576]{1,0:T(8,128)(2,1)S(1)}, bf16[6,368,368]{2,1,0:T(8,128)(2,1)S(1)}) custom-call(f32[736,768]{1,0:T(8,128)S(1)} %get-tuple-element.134.refs_8_.refs_0_, f32[2,368,368]{2,1,0:T(8,128)S(1)} %get-tuple-element.135.refs_1_, bf16[768,576]{1,0:T(8,128)(2,1)S(1)} %get-tuple-element.138.refs_2_, ...), custom_call_target="tpu_custom_call" | custom-call | flops 4000000000 | tf_op jit(solution)/shard_map/attend/pallas_call | solution.py:475
  55.0 1.3 collective-permute-start.14
  58.3 1.4 collective-permute-done.24.refs_6_.refs_2_
  61.1 5.2 %collective-permute-done.14.refs_2_.refs_5_ = bf16[736,192]{1,0:T(8,128)(2,1)S(1)} collective-permute-done((bf16[736,192]{1,0:T(8,128)(2,1)S(1)}, bf16[736,192]{1,0:T(8,128)(2,1)S(1)}, u32[]{:S(2)}, u32[]{:S(2)}) %collective-permute-start.14) | collective-permute-done | bytes 282656 | tf_op jit(solution)/shard_map/ppermute | solution.py:1028
  68.0 2.1 %branch_rows.1 = (bf16[736,768]{1,0:T(8,128)(2,1)S(1)}, bf16[736,768]{1,0:T(8,128)(2,1)S(1)}, f32[208,768]{1,0:T(8,128)S(1)}) custom-call(bf16[736,192]{1,0:T(8,128)(2,1)S(1)} %get-tuple-element.142.refs_0_.refs_3_.refs_4_, bf16[736,192]{1,0:T(8,128)(2,1)S(1)} %collective-permute-done.13.refs_1_.refs_8_.refs_4_, ...), custom_call_target="tpu_custom_call" | custom-call | flops 1000000 | tf_op jit(solution)/shard_map/branch_rows/pallas_call | solution.py:475
  70.1 2.2 %collective-permute-done.25.refs_7_ = bf16[192,768]{1,0:T(8,128)(2,1)S(1)} collective-permute-done((bf16[192,768]{1,0:T(8,128)(2,1)S(1)}, bf16[192,768]{1,0:T(8,128)(2,1)S(1)}, u32[]{:S(2)}, u32[]{:S(2)}) %collective-permute-start.25) | collective-permute-done | bytes 294944 | tf_op jit(solution)/shard_map/ppermute | solution.py:1028
  72.3 1.7 %raise_rows.1 = (bf16[736,768]{1,0:T(8,128)(2,1)S(1)}, f32[736,768]{1,0:T(8,128)S(1)}, bf16[768,768]{1,0:T(8,128)(2,1)S(1)}, bf16[768,768]{1,0:T(8,128)(2,1)S(1)}) custom-call(bf16[736,768]{1,0:T(8,128)(2,1)S(1)} %get-tuple-element.152.refs_0_, bf16[192,768]{1,0:T(8,128)(2,1)S(1)} %get-tuple-element.153.refs_1_, ...), custom_call_target="tpu_custom_call" | custom-call | flops 2800000000 | tf_op jit(solution)/shard_map/raise_rows/pallas_call | solution.py:475
  74.0 2.7 %lower_rows.1 = (bf16[368,768]{1,0:T(8,128)(2,1)S(1)}, f32[368,768]{1,0:T(8,128)S(1)}, bf16[736,768]{1,0:T(8,128)(2,1)S(1)}) custom-call(f32[736,768]{1,0:T(8,128)S(1)} %get-tuple-element.162.refs_0_, bf16[736,768]{1,0:T(8,128)(2,1)S(1)} %get-tuple-element.163.refs_1_, bf16[768,768]{1,0:T(8,128)(2,1)S(1)} %get-tuple-element.164.refs_2_, ...), custom_call_target="tpu_custom_call" | custom-call | flops 185000000 | tf_op jit(solution)/shard_map/lower_rows/pallas_call | solution.py:475
  76.8 1.3 down_grads.1
  78.8 1.4 collective-permute-start.28
  80.2 1.7 %mlp_rows.1 = (bf16[416,768]{1,0:T(8,128)(2,1)S(1)}, f32[416,768]{1,0:T(8,128)S(1)}, f32[8,768]{1,0:T(8,128)S(1)}, bf16[736,192]{1,0:T(8,128)(2,1)S(1)}) custom-call(bf16[736,768]{1,0:T(8,128)(2,1)S(1)} %get-tuple-element.156.refs_0_.refs_4_.refs_2_, bf16[768,768]{1,0:T(8,128)(2,1)S(1)} %get-tuple-element.157.refs_1_.refs_3_, ...), custom_call_target="tpu_custom_call" | custom-call | flops 1200000000 | tf_op jit(solution)/shard_map/mlp_rows/pallas_call | solution.py:475
  82.0 1.4 up_grads.1
  83.9 10.0 %collective-permute-done.29.refs_1_.refs_2_ = bf16[4,96,768]{2,1,0:T(8,128)(2,1)S(1)} collective-permute-done((bf16[4,96,768]{2,1,0:T(8,128)(2,1)S(1)}, bf16[4,96,768]{2,1,0:T(8,128)(2,1)S(1)}, u32[]{:S(2)}, u32[]{:S(2)}) %collective-permute-start.29) | collective-permute-done | bytes 589856 | tf_op jit(solution)/shard_map/ppermute | solution.py:1028
  94.2 1.7 %collective-permute-start.35 = (bf16[2,96,768]{2,1,0:T(8,128)(2,1)S(1)}, bf16[2,96,768]{2,1,0:T(8,128)(2,1)S(1)}, u32[]{:S(2)}, u32[]{:S(2)}) collective-permute-start(bf16[2,96,768]{2,1,0:T(8,128)(2,1)S(1)} %get-tuple-element.201), channel_id=1, source_target_pairs={{0,16},{1,17},{2,18},{3,19},{4,20},{5,21},{6,22},{7,23},{8,24},{9,... | collective-permute-start | bytes 884744 | tf_op jit(solution)/shard_map/ppermute | solution.py:1028
  96.2 3.9 %branch_back.1 = (f32[208,768]{1,0:T(8,128)S(1)}, bf16[736,192]{1,0:T(8,128)(2,1)S(1)}, bf16[736,192]{1,0:T(8,128)(2,1)S(1)}, bf16[4,112,384]{2,1,0:T(8,128)(2,1)S(1)}, f32[4,112,384]{2,1,0:T(8,128)S(1)}) custom-call(bf16[368,768]{1,0:T(8,128)(2,1)S(1)} %add_pair.1.refs_0_.refs_3_, bf16[368,768]{1,0:T(8,128)(2,1)S(1)} %collective-permute-done.30.refs_1_, ...), custom_call_target="tpu_custom_call" | custom-call | flops 1000000 | tf_op jit(solution)/shard_map/branch_back/pallas_call | solution.py:475
  100.1 1.3 collective-permute-start.33
  101.4 3.8 %score_back.1 = (bf16[736,384]{1,0:T(8,128)(2,1)S(1)}, bf16[4,96,384]{2,1,0:T(8,128)(2,1)S(1)}, f32[4,96,384]{2,1,0:T(8,128)S(1)}) custom-call(bf16[6,368,368]{2,1,0:T(8,128)(2,1)S(1)} %get-tuple-element.160.refs_7_.refs_0_, bf16[736,576]{1,0:T(8,128)(2,1)S(1)} %get-tuple-element.161.refs_1_, bf16[736,192]{1,0:T(8,128)(2,1)S(1)} %get-tuple-element.179.refs_2_, ...), custom_call_target="tpu_custom_call" | custom-call | flops 2000000 | tf_op jit(solution)/shard_map/score_back/pallas_call | solution.py:475
  105.2 1.3 project_back.1
  107.7 3.2 %collective-permute-done.35.refs_1_ = bf16[2,96,768]{2,1,0:T(8,128)(2,1)S(1)} collective-permute-done((bf16[2,96,768]{2,1,0:T(8,128)(2,1)S(1)}, bf16[2,96,768]{2,1,0:T(8,128)(2,1)S(1)}, u32[]{:S(2)}, u32[]{:S(2)}) %collective-permute-start.35) | collective-permute-done | bytes 294944 | tf_op jit(solution)/shard_map/ppermute | solution.py:1028
  113.3 3.9 %collective-permute-done.45.refs_1_ = bf16[2,96,768]{2,1,0:T(8,128)(2,1)S(1)} collective-permute-done((bf16[2,96,768]{2,1,0:T(8,128)(2,1)S(1)}, bf16[2,96,768]{2,1,0:T(8,128)(2,1)S(1)}, u32[]{:S(2)}, u32[]{:S(2)}) %collective-permute-start.45) | collective-permute-done | bytes 294944 | tf_op jit(solution)/shard_map/ppermute | solution.py:1028
  117.3 1.3 collective-permute-start.46
  119.5 1.4 collective-permute-done.34.refs_1_.refs_2_
  121.5 1.9 %collective-permute-start.36 = (bf16[112,384]{1,0:T(8,128)(2,1)S(1)}, bf16[112,384]{1,0:T(8,128)(2,1)S(1)}, u32[]{:S(2)}, u32[]{:S(2)}) collective-permute-start(bf16[112,384]{1,0:T(8,128)(2,1)S(1)} %get-tuple-element.203), channel_id=1, source_target_pairs={{0,16},{1,17},{2,18},{3,19},{4,20},{5,21},{6,22},{7,23},{8,24},{9,... | collective-permute-start | bytes 258056 | tf_op jit(solution)/shard_map/ppermute | solution.py:1028
  124.5 1.6 %collective-permute-start.40 = (bf16[96,384]{1,0:T(8,128)(2,1)S(1)}, bf16[96,384]{1,0:T(8,128)(2,1)S(1)}, u32[]{:S(2)}, u32[]{:S(2)}) collective-permute-start(bf16[96,384]{1,0:T(8,128)(2,1)S(1)} %get-tuple-element.212), channel_id=1, source_target_pairs={{0,24},{1,25},{2,26},{3,27},{4,28},{5,29},{6,30},{7,31},{8,16},{9,... | collective-permute-start | bytes 221192 | tf_op jit(solution)/shard_map/ppermute | solution.py:1028
  127.5 5.1 %collective-permute-done.46.refs_1_ = bf16[96,768]{1,0:T(8,128)(2,1)S(1)} collective-permute-done((bf16[96,768]{1,0:T(8,128)(2,1)S(1)}, bf16[96,768]{1,0:T(8,128)(2,1)S(1)}, u32[]{:S(2)}, u32[]{:S(2)}) %collective-permute-start.46) | collective-permute-done | bytes 147488 | tf_op jit(solution)/shard_map/ppermute | solution.py:1028
  134.5 2.6 %collective-permute-done.39.refs_4_ = bf16[96,384]{1,0:T(8,128)(2,1)S(1)} collective-permute-done((bf16[96,384]{1,0:T(8,128)(2,1)S(1)}, bf16[96,384]{1,0:T(8,128)(2,1)S(1)}, u32[]{:S(2)}, u32[]{:S(2)}) %collective-permute-start.39) | collective-permute-done | bytes 73760 | tf_op jit(solution)/shard_map/ppermute | solution.py:1028
  139.5 3.0 %collective-permute-done.43.refs_2_ = bf16[64,768]{1,0:T(8,128)(2,1)S(1)} collective-permute-done((bf16[64,768]{1,0:T(8,128)(2,1)S(1)}, bf16[64,768]{1,0:T(8,128)(2,1)S(1)}, u32[]{:S(2)}, u32[]{:S(2)}) %collective-permute-start.43) | collective-permute-done | bytes 98336 | tf_op jit(solution)/shard_map/ppermute | solution.py:1028
  143.5 1.5 finish_rows.1
  (116 shorter events, 27.1 us)
Async XLA Ops:
  2.0 6.9 %collective-permute-start.1 = (bf16[96,768]{1,0:T(8,128)(2,1)S(1)}, bf16[96,768]{1,0:T(8,128)(2,1)S(1)}, u32[]{:S(2)}, u32[]{:S(2)}) collective-permute-start(bf16[96,768]{1,0:T(8,128)(2,1)S(1)} %get-tuple-element.128), channel_id=1, source_target_pairs={{0,2},{1,3},{2,0},{3,1},{4,6},{5,7},{6,4},{7,5},{8,10},{9,11},{10,... | collective-permute-start | bytes 442376 | tf_op jit(solution)/shard_map/ppermute | solution.py:1028
  8.8 14.7 %collective-permute-start.7 = (bf16[352,768]{1,0:T(8,128)(2,1)S(1)}, bf16[352,768]{1,0:T(8,128)(2,1)S(1)}, u32[]{:S(2)}, u32[]{:S(2)}) collective-permute-start(bf16[352,768]{1,0:T(8,128)(2,1)S(1)} %get-tuple-element.132.refs_0_), channel_id=1, source_target_pairs={{0,2},{1,3},{2,0},{3,1},{4,6},{5,7},{6,4},{7,5},{8,10},{9,11},{10,... | collective-permute-start | bytes 1622024 | tf_op jit(solution)/shard_map/ppermute | solution.py:1028
  11.3 8.1 %collective-permute-start.4 = (bf16[112,768]{1,0:T(8,128)(2,1)S(1)}, bf16[112,768]{1,0:T(8,128)(2,1)S(1)}, u32[]{:S(2)}, u32[]{:S(2)}) collective-permute-start(bf16[112,768]{1,0:T(8,128)(2,1)S(1)} %get-tuple-element.130.refs_0_), channel_id=1, source_target_pairs={{0,8},{1,9},{2,10},{3,11},{4,12},{5,13},{6,14},{7,15},{8,0},{9,1},... | collective-permute-start | bytes 516104 | tf_op jit(solution)/shard_map/ppermute | solution.py:1028
  12.9 9.7 %collective-permute-start.8 = (bf16[112,768]{1,0:T(8,128)(2,1)S(1)}, bf16[112,768]{1,0:T(8,128)(2,1)S(1)}, u32[]{:S(2)}, u32[]{:S(2)}) collective-permute-start(bf16[112,768]{1,0:T(8,128)(2,1)S(1)} %get-tuple-element.130.refs_0_), channel_id=1, source_target_pairs={{0,4},{1,5},{2,6},{3,7},{4,0},{5,1},{6,2},{7,3},{8,12},{9,13},{10,... | collective-permute-start | bytes 516104 | tf_op jit(solution)/shard_map/ppermute | solution.py:1028
  14.4 10.5 %collective-permute-start.3 = (bf16[112,768]{1,0:T(8,128)(2,1)S(1)}, bf16[112,768]{1,0:T(8,128)(2,1)S(1)}, u32[]{:S(2)}, u32[]{:S(2)}) collective-permute-start(bf16[112,768]{1,0:T(8,128)(2,1)S(1)} %get-tuple-element.130.refs_0_), channel_id=1, source_target_pairs={{0,16},{1,17},{2,18},{3,19},{4,20},{5,21},{6,22},{7,23},{8,24},{9,... | collective-permute-start | bytes 516104 | tf_op jit(solution)/shard_map/ppermute | solution.py:1028
  19.4 6.6 %collective-permute-start.5 = (bf16[112,768]{1,0:T(8,128)(2,1)S(1)}, bf16[112,768]{1,0:T(8,128)(2,1)S(1)}, u32[]{:S(2)}, u32[]{:S(2)}) collective-permute-start(bf16[112,768]{1,0:T(8,128)(2,1)S(1)} %collective-permute-done.4.refs_1_), channel_id=1, source_target_pairs={{0,4},{1,5},{2,6},{3,7},{4,0},{5,1},{6,2},{7,3},{8,12},{9,13},{10,... | collective-permute-start | bytes 516104 | tf_op jit(solution)/shard_map/ppermute | solution.py:1028
  23.5 14.7 %collective-permute-start.9 = (bf16[352,768]{1,0:T(8,128)(2,1)S(1)}, bf16[352,768]{1,0:T(8,128)(2,1)S(1)}, u32[]{:S(2)}, u32[]{:S(2)}) collective-permute-start(bf16[352,768]{1,0:T(8,128)(2,1)S(1)} %collective-permute-done.7.refs_2_), channel_id=1, source_target_pairs={{0,1},{1,0},{2,3},{3,2},{4,5},{5,4},{6,7},{7,6},{8,9},{9,8},{10,11... | collective-permute-start | bytes 1622024 | tf_op jit(solution)/shard_map/ppermute | solution.py:1028
  26.1 12.1 %collective-permute-start.6 = (bf16[352,768]{1,0:T(8,128)(2,1)S(1)}, bf16[352,768]{1,0:T(8,128)(2,1)S(1)}, u32[]{:S(2)}, u32[]{:S(2)}) collective-permute-start(bf16[352,768]{1,0:T(8,128)(2,1)S(1)} %get-tuple-element.132.refs_0_), channel_id=1, source_target_pairs={{0,1},{1,0},{2,3},{3,2},{4,5},{5,4},{6,7},{7,6},{8,9},{9,8},{10,11... | collective-permute-start | bytes 1622024 | tf_op jit(solution)/shard_map/ppermute | solution.py:1028
  26.1 8.7 %collective-permute-start.10 = (bf16[112,768]{1,0:T(8,128)(2,1)S(1)}, bf16[112,768]{1,0:T(8,128)(2,1)S(1)}, u32[]{:S(2)}, u32[]{:S(2)}) collective-permute-start(bf16[112,768]{1,0:T(8,128)(2,1)S(1)} %collective-permute-done.3.refs_2_), channel_id=1, source_target_pairs={{0,8},{1,9},{2,10},{3,11},{4,12},{5,13},{6,14},{7,15},{8,0},{9,1},... | collective-permute-start | bytes 516104 | tf_op jit(solution)/shard_map/ppermute | solution.py:1028
  26.1 12.1 %collective-permute-start.11 = (bf16[112,768]{1,0:T(8,128)(2,1)S(1)}, bf16[112,768]{1,0:T(8,128)(2,1)}, u32[]{:S(2)}, u32[]{:S(2)}) collective-permute-start(bf16[112,768]{1,0:T(8,128)(2,1)S(1)} %collective-permute-done.3.refs_2_), channel_id=1, source_target_pairs={{0,4},{1,5},{2,6},{3,7},{4,0},{5,1},{6,2},{7,3},{8,12},{9,13},{10,... | collective-permute-start | bytes 516104 | tf_op jit(solution)/shard_map/ppermute | solution.py:1028
  28.1 18.7 %collective-permute-start.19 = (bf16[192,768]{1,0:T(8,128)(2,1)S(1)}, bf16[192,768]{1,0:T(8,128)(2,1)S(1)}, u32[]{:S(2)}, u32[]{:S(2)}) collective-permute-start(bf16[192,768]{1,0:T(8,128)(2,1)S(1)} %get-tuple-element.153.refs_1_), channel_id=1, source_target_pairs={{0,16},{1,17},{2,18},{3,19},{4,20},{5,21},{6,22},{7,23},{8,24},{9,... | collective-permute-start | bytes 884744 | tf_op jit(solution)/shard_map/ppermute | solution.py:1028
  34.8 7.7 %collective-permute-start.12 = (bf16[112,768]{1,0:T(8,128)(2,1)S(1)}, bf16[112,768]{1,0:T(8,128)(2,1)S(1)}, u32[]{:S(2)}, u32[]{:S(2)}) collective-permute-start(bf16[112,768]{1,0:T(8,128)(2,1)S(1)} %collective-permute-done.10.refs_3_), channel_id=1, source_target_pairs={{0,4},{1,5},{2,6},{3,7},{4,0},{5,1},{6,2},{7,3},{8,12},{9,13},{10,... | collective-permute-start | bytes 516104 | tf_op jit(solution)/shard_map/ppermute | solution.py:1028
  38.2 13.1 %collective-permute-start.23 = (bf16[192,768]{1,0:T(8,128)(2,1)S(1)}, bf16[192,768]{1,0:T(8,128)(2,1)S(1)}, u32[]{:S(2)}, u32[]{:S(2)}) collective-permute-start(bf16[192,768]{1,0:T(8,128)(2,1)S(1)} %get-tuple-element.153.refs_1_), channel_id=1, source_target_pairs={{0,8},{1,9},{2,10},{3,11},{4,12},{5,13},{6,14},{7,15},{8,0},{9,1},... | collective-permute-start | bytes 884744 | tf_op jit(solution)/shard_map/ppermute | solution.py:1028
  43.7 8.1 %collective-permute-start.16 = (bf16[192,768]{1,0:T(8,128)(2,1)S(1)}, bf16[192,768]{1,0:T(8,128)(2,1)S(1)}, u32[]{:S(2)}, u32[]{:S(2)}) collective-permute-start(bf16[192,768]{1,0:T(8,128)(2,1)S(1)} %get-tuple-element.144.refs_0_), channel_id=1, source_target_pairs={{0,2},{1,3},{2,0},{3,1},{4,6},{5,7},{6,4},{7,5},{8,10},{9,11},{10,... | collective-permute-start | bytes 884744 | tf_op jit(solution)/shard_map/ppermute | solution.py:1028
  45.1 10.0 %collective-permute-start.21 = (bf16[192,768]{1,0:T(8,128)(2,1)S(1)}, bf16[192,768]{1,0:T(8,128)(2,1)S(1)}, u32[]{:S(2)}, u32[]{:S(2)}) collective-permute-start(bf16[192,768]{1,0:T(8,128)(2,1)S(1)} %get-tuple-element.153.refs_1_), channel_id=1, source_target_pairs={{0,4},{1,5},{2,6},{3,7},{4,0},{5,1},{6,2},{7,3},{8,12},{9,13},{10,... | collective-permute-start | bytes 884744 | tf_op jit(solution)/shard_map/ppermute | solution.py:1028
  46.8 10.5 %collective-permute-start.20 = (bf16[192,768]{1,0:T(8,128)(2,1)S(1)}, bf16[192,768]{1,0:T(8,128)(2,1)S(1)}, u32[]{:S(2)}, u32[]{:S(2)}) collective-permute-start(bf16[192,768]{1,0:T(8,128)(2,1)S(1)} %collective-permute-done.19.refs_3_.refs_4_), channel_id=1, source_target_pairs={{0,8},{1,9},{2,10},{3,11},{4,12},{5,13},{6,14},{7,15},{8,0},{9,1},... | collective-permute-start | bytes 884744 | tf_op jit(solution)/shard_map/ppermute | solution.py:1028
  51.3 8.4 %collective-permute-start.24 = (bf16[192,768]{1,0:T(8,128)(2,1)S(1)}, bf16[192,768]{1,0:T(8,128)(2,1)S(1)}, u32[]{:S(2)}, u32[]{:S(2)}) collective-permute-start(bf16[192,768]{1,0:T(8,128)(2,1)S(1)} %collective-permute-done.23.refs_2_), channel_id=1, source_target_pairs={{0,4},{1,5},{2,6},{3,7},{4,0},{5,1},{6,2},{7,3},{8,12},{9,13},{10,... | collective-permute-start | bytes 884744 | tf_op jit(solution)/shard_map/ppermute | solution.py:1028
  51.3 8.4 %collective-permute-start.15 = (bf16[192,768]{1,0:T(8,128)(2,1)S(1)}, bf16[192,768]{1,0:T(8,128)(2,1)S(1)}, u32[]{:S(2)}, u32[]{:S(2)}) collective-permute-start(bf16[192,768]{1,0:T(8,128)(2,1)S(1)} %get-tuple-element.144.refs_0_), channel_id=1, source_target_pairs={{0,1},{1,0},{2,3},{3,2},{4,5},{5,4},{6,7},{7,6},{8,9},{9,8},{10,11... | collective-permute-start | bytes 884744 | tf_op jit(solution)/shard_map/ppermute | solution.py:1028
  51.8 8.8 %collective-permute-start.17 = (bf16[192,768]{1,0:T(8,128)(2,1)S(1)}, bf16[192,768]{1,0:T(8,128)(2,1)S(1)}, u32[]{:S(2)}, u32[]{:S(2)}) collective-permute-start(bf16[192,768]{1,0:T(8,128)(2,1)S(1)} %collective-permute-done.16.refs_2_), channel_id=1, source_target_pairs={{0,1},{1,0},{2,3},{3,2},{4,5},{5,4},{6,7},{7,6},{8,9},{9,8},{10,11... | collective-permute-start | bytes 884744 | tf_op jit(solution)/shard_map/ppermute | solution.py:1028
  55.0 11.2 %collective-permute-start.14 = (bf16[736,192]{1,0:T(8,128)(2,1)S(1)}, bf16[736,192]{1,0:T(8,128)(2,1)S(1)}, u32[]{:S(2)}, u32[]{:S(2)}) collective-permute-start(bf16[736,192]{1,0:T(8,128)(2,1)S(1)} %get-tuple-element.142.refs_0_.refs_3_.refs_4_), channel_id=1, source_target_pairs={{0,2},{1,3},{2,0},{3,1},{4,6},{5,7},{6,4},{7,5},{8,10},{9,11},{10,... | collective-permute-start | bytes 847880 | tf_op jit(solution)/shard_map/ppermute | solution.py:1028
  57.3 9.9 %collective-permute-start.22 = (bf16[192,768]{1,0:T(8,128)(2,1)S(1)}, bf16[192,768]{1,0:T(8,128)(2,1)S(1)}, u32[]{:S(2)}, u32[]{:S(2)}) collective-permute-start(bf16[192,768]{1,0:T(8,128)(2,1)S(1)} %collective-permute-done.20.refs_4_.refs_5_), channel_id=1, source_target_pairs={{0,4},{1,5},{2,6},{3,7},{4,0},{5,1},{6,2},{7,3},{8,12},{9,13},{10,... | collective-permute-start | bytes 884744 | tf_op jit(solution)/shard_map/ppermute | solution.py:1028
  59.7 6.6 %collective-permute-start.13 = (bf16[736,192]{1,0:T(8,128)(2,1)S(1)}, bf16[736,192]{1,0:T(8,128)(2,1)S(1)}, u32[]{:S(2)}, u32[]{:S(2)}) collective-permute-start(bf16[736,192]{1,0:T(8,128)(2,1)S(1)} %get-tuple-element.142.refs_0_.refs_3_.refs_4_), channel_id=1, source_target_pairs={{0,1},{1,0},{2,3},{3,2},{4,5},{5,4},{6,7},{7,6},{8,9},{9,8},{10,11... | collective-permute-start | bytes 847880 | tf_op jit(solution)/shard_map/ppermute | solution.py:1028
  59.7 12.6 %collective-permute-start.25 = (bf16[192,768]{1,0:T(8,128)(2,1)S(1)}, bf16[192,768]{1,0:T(8,128)(2,1)S(1)}, u32[]{:S(2)}, u32[]{:S(2)}) collective-permute-start(bf16[192,768]{1,0:T(8,128)(2,1)S(1)} %collective-permute-done.19.refs_3_.refs_4_), channel_id=1, source_target_pairs={{0,4},{1,5},{2,6},{3,7},{4,0},{5,1},{6,2},{7,3},{8,12},{9,13},{10,... | collective-permute-start | bytes 884744 | tf_op jit(solution)/shard_map/ppermute | solution.py:1028
  76.7 2.0 %collective-permute-start.27 = (bf16[368,768]{1,0:T(8,128)(2,1)S(1)}, bf16[368,768]{1,0:T(8,128)(2,1)S(1)}, u32[]{:S(2)}, u32[]{:S(2)}) collective-permute-start(bf16[368,768]{1,0:T(8,128)(2,1)S(1)} %get-tuple-element.167.refs_3_), channel_id=1, source_target_pairs={{0,1},{1,0},{2,3},{3,2},{4,5},{5,4},{6,7},{7,6},{8,9},{9,8},{10,11... | collective-permute-start | bytes 1695752 | tf_op jit(solution)/shard_map/ppermute | solution.py:1028
  78.0 15.8 %collective-permute-start.29 = (bf16[4,96,768]{2,1,0:T(8,128)(2,1)S(1)}, bf16[4,96,768]{2,1,0:T(8,128)(2,1)S(1)}, u32[]{:S(2)}, u32[]{:S(2)}) collective-permute-start(bf16[4,96,768]{2,1,0:T(8,128)(2,1)S(1)} %get-tuple-element.171), channel_id=1, source_target_pairs={{0,8},{1,9},{2,10},{3,11},{4,12},{5,13},{6,14},{7,15},{8,0},{9,1},... | collective-permute-start | bytes 1769480 | tf_op jit(solution)/shard_map/ppermute | solution.py:1028
  78.8 15.2 %collective-permute-start.28 = (bf16[368,768]{1,0:T(8,128)(2,1)S(1)}, bf16[368,768]{1,0:T(8,128)(2,1)S(1)}, u32[]{:S(2)}, u32[]{:S(2)}) collective-permute-start(bf16[368,768]{1,0:T(8,128)(2,1)S(1)} %add_rows.1.refs_0_.refs_2_), channel_id=1, source_target_pairs={{0,2},{1,3},{2,0},{3,1},{4,6},{5,7},{6,4},{7,5},{8,10},{9,11},{10,... | collective-permute-start | bytes 1695752 | tf_op jit(solution)/shard_map/ppermute | solution.py:1028
  81.9 24.6 %collective-permute-start.26 = (bf16[416,768]{1,0:T(8,128)(2,1)S(1)}, bf16[416,768]{1,0:T(8,128)(2,1)S(1)}, u32[]{:S(2)}, u32[]{:S(2)}) collective-permute-start(bf16[416,768]{1,0:T(8,128)(2,1)S(1)} %get-tuple-element.159), channel_id=1, source_target_pairs={{0,1},{1,0},{2,3},{3,2},{4,5},{5,4},{6,7},{7,6},{8,9},{9,8},{10,11... | collective-permute-start | bytes 1916936 | tf_op jit(solution)/shard_map/ppermute | solution.py:1028
  83.4 23.2 %collective-permute-start.41 = (bf16[4,96,768]{2,1,0:T(8,128)(2,1)S(1)}, bf16[4,96,768]{2,1,0:T(8,128)(2,1)S(1)}, u32[]{:S(2)}, u32[]{:S(2)}) collective-permute-start(bf16[4,96,768]{2,1,0:T(8,128)(2,1)S(1)} %get-tuple-element.216), channel_id=1, source_target_pairs={{0,4},{1,5},{2,6},{3,7},{4,0},{5,1},{6,2},{7,3},{8,12},{9,13},{10,... | collective-permute-start | bytes 1769480 | tf_op jit(solution)/shard_map/ppermute | solution.py:1028
  94.1 2.0 %collective-permute-start.30 = (bf16[368,768]{1,0:T(8,128)(2,1)S(1)}, bf16[368,768]{1,0:T(8,128)(2,1)S(1)}, u32[]{:S(2)}, u32[]{:S(2)}) collective-permute-start(bf16[368,768]{1,0:T(8,128)(2,1)S(1)} %add_pair.1.refs_0_.refs_3_), channel_id=1, source_target_pairs={{0,1},{1,0},{2,3},{3,2},{4,5},{5,4},{6,7},{7,6},{8,9},{9,8},{10,11... | collective-permute-start | bytes 1695752 | tf_op jit(solution)/shard_map/ppermute | solution.py:1028
  94.2 16.7 %collective-permute-start.35 = (bf16[2,96,768]{2,1,0:T(8,128)(2,1)S(1)}, bf16[2,96,768]{2,1,0:T(8,128)(2,1)S(1)}, u32[]{:S(2)}, u32[]{:S(2)}) collective-permute-start(bf16[2,96,768]{2,1,0:T(8,128)(2,1)S(1)} %get-tuple-element.201), channel_id=1, source_target_pairs={{0,16},{1,17},{2,18},{3,19},{4,20},{5,21},{6,22},{7,23},{8,24},{9,... | collective-permute-start | bytes 884744 | tf_op jit(solution)/shard_map/ppermute | solution.py:1028
  100.1 11.8 %collective-permute-start.33 = (bf16[4,112,384]{2,1,0:T(8,128)(2,1)S(1)}, bf16[4,112,384]{2,1,0:T(8,128)(2,1)S(1)}, u32[]{:S(2)}, u32[]{:S(2)}) collective-permute-start(bf16[4,112,384]{2,1,0:T(8,128)(2,1)S(1)} %get-tuple-element.196), channel_id=1, source_target_pairs={{0,4},{1,5},{2,6},{3,7},{4,0},{5,1},{6,2},{7,3},{8,12},{9,13},{10,... | collective-permute-start | bytes 1032200 | tf_op jit(solution)/shard_map/ppermute | solution.py:1028
  106.5 5.6 %collective-permute-start.31 = (bf16[416,768]{1,0:T(8,128)(2,1)S(1)}, bf16[416,768]{1,0:T(8,128)(2,1)S(1)}, u32[]{:S(2)}, u32[]{:S(2)}) collective-permute-start(bf16[416,768]{1,0:T(8,128)(2,1)S(1)} %get-tuple-element.185), channel_id=1, source_target_pairs={{0,1},{1,0},{2,3},{3,2},{4,5},{5,4},{6,7},{7,6},{8,9},{9,8},{10,11... | collective-permute-start | bytes 1916936 | tf_op jit(solution)/shard_map/ppermute | solution.py:1028
  106.7 10.5 %collective-permute-start.45 = (bf16[2,96,768]{2,1,0:T(8,128)(2,1)S(1)}, bf16[2,96,768]{2,1,0:T(8,128)(2,1)S(1)}, u32[]{:S(2)}, u32[]{:S(2)}) collective-permute-start(bf16[2,96,768]{2,1,0:T(8,128)(2,1)S(1)} %get-tuple-element.223), channel_id=1, source_target_pairs={{0,8},{1,9},{2,10},{3,11},{4,12},{5,13},{6,14},{7,15},{8,0},{9,1},... | collective-permute-start | bytes 884744 | tf_op jit(solution)/shard_map/ppermute | solution.py:1028
  111.0 8.5 %collective-permute-start.37 = (bf16[4,96,384]{2,1,0:T(8,128)(2,1)S(1)}, bf16[4,96,384]{2,1,0:T(8,128)(2,1)S(1)}, u32[]{:S(2)}, u32[]{:S(2)}) collective-permute-start(bf16[4,96,384]{2,1,0:T(8,128)(2,1)S(1)} %get-tuple-element.206), channel_id=1, source_target_pairs={{0,4},{1,5},{2,6},{3,7},{4,0},{5,1},{6,2},{7,3},{8,12},{9,13},{10,... | collective-permute-start | bytes 884744 | tf_op jit(solution)/shard_map/ppermute | solution.py:1028
  112.0 8.9 %collective-permute-start.34 = (bf16[2,112,384]{2,1,0:T(8,128)(2,1)S(1)}, bf16[2,112,384]{2,1,0:T(8,128)(2,1)S(1)}, u32[]{:S(2)}, u32[]{:S(2)}) collective-permute-start(bf16[2,112,384]{2,1,0:T(8,128)(2,1)S(1)} %get-tuple-element.198), channel_id=1, source_target_pairs={{0,8},{1,9},{2,10},{3,11},{4,12},{5,13},{6,14},{7,15},{8,0},{9,1},... | collective-permute-start | bytes 516104 | tf_op jit(solution)/shard_map/ppermute | solution.py:1028
  112.3 26.6 %collective-permute-start.32 = (bf16[416,768]{1,0:T(8,128)(2,1)S(1)}, bf16[416,768]{1,0:T(8,128)(2,1)S(1)}, u32[]{:S(2)}, u32[]{:S(2)}) collective-permute-start(bf16[416,768]{1,0:T(8,128)(2,1)S(1)} %get-tuple-element.188), channel_id=1, source_target_pairs={{0,2},{1,3},{2,0},{3,1},{4,6},{5,7},{6,4},{7,5},{8,10},{9,11},{10,... | collective-permute-start | bytes 1916936 | tf_op jit(solution)/shard_map/ppermute | solution.py:1028
  117.3 15.3 %collective-permute-start.46 = (bf16[96,768]{1,0:T(8,128)(2,1)S(1)}, bf16[96,768]{1,0:T(8,128)(2,1)S(1)}, u32[]{:S(2)}, u32[]{:S(2)}) collective-permute-start(bf16[96,768]{1,0:T(8,128)(2,1)S(1)} %get-tuple-element.225), channel_id=1, source_target_pairs={{0,16},{1,17},{2,18},{3,19},{4,20},{5,21},{6,22},{7,23},{8,24},{9,... | collective-permute-start | bytes 442376 | tf_op jit(solution)/shard_map/ppermute | solution.py:1028
  118.6 5.1 %collective-permute-start.47 = (bf16[96,768]{1,0:T(8,128)(2,1)S(1)}, bf16[96,768]{1,0:T(8,128)(2,1)S(1)}, u32[]{:S(2)}, u32[]{:S(2)}) collective-permute-start(bf16[96,768]{1,0:T(8,128)(2,1)S(1)} %get-tuple-element.227), channel_id=1, source_target_pairs={{0,4},{1,5},{2,6},{3,7},{4,0},{5,1},{6,2},{7,3},{8,12},{9,13},{10,... | collective-permute-start | bytes 442376 | tf_op jit(solution)/shard_map/ppermute | solution.py:1028
  120.9 5.8 %collective-permute-start.38 = (bf16[96,384]{1,0:T(8,128)(2,1)S(1)}, bf16[96,384]{1,0:T(8,128)(2,1)S(1)}, u32[]{:S(2)}, u32[]{:S(2)}) collective-permute-start(bf16[96,384]{1,0:T(8,128)(2,1)S(1)} %get-tuple-element.209), channel_id=1, source_target_pairs={{0,8},{1,9},{2,10},{3,11},{4,12},{5,13},{6,14},{7,15},{8,0},{9,1},... | collective-permute-start | bytes 221192 | tf_op jit(solution)/shard_map/ppermute | solution.py:1028
  121.5 13.0 %collective-permute-start.36 = (bf16[112,384]{1,0:T(8,128)(2,1)S(1)}, bf16[112,384]{1,0:T(8,128)(2,1)S(1)}, u32[]{:S(2)}, u32[]{:S(2)}) collective-permute-start(bf16[112,384]{1,0:T(8,128)(2,1)S(1)} %get-tuple-element.203), channel_id=1, source_target_pairs={{0,16},{1,17},{2,18},{3,19},{4,20},{5,21},{6,22},{7,23},{8,24},{9,... | collective-permute-start | bytes 258056 | tf_op jit(solution)/shard_map/ppermute | solution.py:1028
  124.5 10.0 %collective-permute-start.40 = (bf16[96,384]{1,0:T(8,128)(2,1)S(1)}, bf16[96,384]{1,0:T(8,128)(2,1)S(1)}, u32[]{:S(2)}, u32[]{:S(2)}) collective-permute-start(bf16[96,384]{1,0:T(8,128)(2,1)S(1)} %get-tuple-element.212), channel_id=1, source_target_pairs={{0,24},{1,25},{2,26},{3,27},{4,28},{5,29},{6,30},{7,31},{8,16},{9,... | collective-permute-start | bytes 221192 | tf_op jit(solution)/shard_map/ppermute | solution.py:1028
  126.6 10.5 %collective-permute-start.39 = (bf16[96,384]{1,0:T(8,128)(2,1)S(1)}, bf16[96,384]{1,0:T(8,128)(2,1)S(1)}, u32[]{:S(2)}, u32[]{:S(2)}) collective-permute-start(bf16[96,384]{1,0:T(8,128)(2,1)S(1)} %get-tuple-element.211), channel_id=1, source_target_pairs={{0,16},{1,17},{2,18},{3,19},{4,20},{5,21},{6,22},{7,23},{8,24},{9,... | collective-permute-start | bytes 221192 | tf_op jit(solution)/shard_map/ppermute | solution.py:1028
  133.6 5.4 %collective-permute-start.49 = (bf16[64,768]{1,0:T(8,128)(2,1)S(1)}, bf16[64,768]{1,0:T(8,128)(2,1)S(1)}, u32[]{:S(2)}, u32[]{:S(2)}) collective-permute-start(bf16[64,768]{1,0:T(8,128)(2,1)S(1)} %get-tuple-element.230), channel_id=1, source_target_pairs={{0,2},{1,3},{2,0},{3,1},{4,6},{5,7},{6,4},{7,5},{8,10},{9,11},{10,... | collective-permute-start | bytes 294920 | tf_op jit(solution)/shard_map/ppermute | solution.py:1028
  137.9 4.6 %collective-permute-start.43 = (bf16[64,768]{1,0:T(8,128)(2,1)S(1)}, bf16[64,768]{1,0:T(8,128)(2,1)S(1)}, u32[]{:S(2)}, u32[]{:S(2)}) collective-permute-start(bf16[64,768]{1,0:T(8,128)(2,1)S(1)} %get-tuple-element.221), channel_id=1, source_target_pairs={{0,2},{1,3},{2,0},{3,1},{4,6},{5,7},{6,4},{7,5},{8,10},{9,11},{10,... | collective-permute-start | bytes 294920 | tf_op jit(solution)/shard_map/ppermute | solution.py:1028
  139.0 3.6 %collective-permute-start.50 = (bf16[64,768]{1,0:T(8,128)(2,1)S(1)}, bf16[64,768]{1,0:T(8,128)(2,1)S(1)}, u32[]{:S(2)}, u32[]{:S(2)}) collective-permute-start(bf16[64,768]{1,0:T(8,128)(2,1)S(1)} %collective-permute-done.49.refs_2_), channel_id=1, source_target_pairs={{0,1},{1,0},{2,3},{3,2},{4,5},{5,4},{6,7},{7,6},{8,9},{9,8},{10,11... | collective-permute-start | bytes 294920 | tf_op jit(solution)/shard_map/ppermute | solution.py:1028
  139.0 3.5 %collective-permute-start.42 = (bf16[32,768]{1,0:T(8,128)(2,1)S(1)}, bf16[32,768]{1,0:T(8,128)(2,1)S(1)}, u32[]{:S(2)}, u32[]{:S(2)}) collective-permute-start(bf16[32,768]{1,0:T(8,128)(2,1)S(1)} %get-tuple-element.220), channel_id=1, source_target_pairs={{0,1},{1,0},{2,3},{3,2},{4,5},{5,4},{6,7},{7,6},{8,9},{9,8},{10,11... | collective-permute-start | bytes 147464 | tf_op jit(solution)/shard_map/ppermute | solution.py:1028
  139.5 3.0 %collective-permute-start.48 = (bf16[32,768]{1,0:T(8,128)(2,1)S(1)}, bf16[32,768]{1,0:T(8,128)(2,1)S(1)}, u32[]{:S(2)}, u32[]{:S(2)}) collective-permute-start(bf16[32,768]{1,0:T(8,128)(2,1)S(1)} %get-tuple-element.229), channel_id=1, source_target_pairs={{0,1},{1,0},{2,3},{3,2},{4,5},{5,4},{6,7},{7,6},{8,9},{9,8},{10,11... | collective-permute-start | bytes 147464 | tf_op jit(solution)/shard_map/ppermute | solution.py:1028
  142.5 2.5 %collective-permute-start.44 = (bf16[64,768]{1,0:T(8,128)(2,1)S(1)}, bf16[64,768]{1,0:T(8,128)(2,1)S(1)}, u32[]{:S(2)}, u32[]{:S(2)}) collective-permute-start(bf16[64,768]{1,0:T(8,128)(2,1)S(1)} %collective-permute-done.43.refs_2_), channel_id=1, source_target_pairs={{0,1},{1,0},{2,3},{3,2},{4,5},{5,4},{6,7},{7,6},{8,9},{9,8},{10,11... | collective-permute-start | bytes 294920 | tf_op jit(solution)/shard_map/ppermute | solution.py:1028
  (18 other events, 117.6 us)

commit v6 on v5

--- a/solution.py
+++ b/solution.py
@@ -377,17 +377,17 @@
 
 PAD_ID = 99
 PLAN = (
-    (9.0, ()), (0, (0,)), (0, (0,)), (0, (2,)), (7.0, (2,)), (0, ()), (0, ()), (0, ()), (0, ()), (0, (4,)),
-    (0, (1,)), (0, (3,)), (0, (8,)), (0, ()), (0, (12, 1)), (0, (5, 10)), (0, (7, 3)), (20, ()), (0, ()),
-    (0, (11, 16)), (0, ()), (3.6, (17,)), (0, ()), (4, (3, 16, 0)), (0, (23,)), (0, (19, 0, 15)),
-    (0, (10,)), (0, ()), (0, (23, 6, 9)), (1.6, ()), (0, (18,)), (0, (29, 15)), (0.001, (28, 30)),
-    (2.8, ()), (45.0, (19,)), (0, (33, 31)), (0.185, (33, 20)), (0, (36,)), (0.09, (19, 36, 13)),
-    (0, (33, 25)), (0.6, (38,)), (0, (40, 9, 38)), (1.2, ()), (0, ()), (0.7, (31,)), (0, ()),
-    (0.001, (44,)), (0, (38, 44)), (0.001, ()), (0, (48,)), (21.0, ()), (0, ()), (0.002, ()), (0, (45,)),
-    (1.4, ()), (0, ()), (0.065, (46,)), (0, (56, 43, 48)), (1.8, (23,)), (0, (58, 37)), (0.07, (35, 44)),
-    (0, (47,)), (0.001, ()), (0, ()), (0.105, (58,)), (0, (55,)), (0, (65,)), (0, ()), (2.1, (33,)),
-    (0, (60,)), (0.7, (55, 54)), (0.7, (70,)), (0, ()), (0, ()), (0, (55,)), (3, ()), (0.9, (50,)), (0, ()),
-    (0, (59,)), (0, (78, 77)), (0.001, ()), (3, (80,)),
+    (9.0, ()), (0, (0,)), (0, (0,)), (0, (2,)), (7.0, (2,)), (0, ()), (0, ()), (0, (0,)), (0, (0,)),
+    (0, (4, 0)), (0, (2,)), (0, (3,)), (0, (8,)), (0, ()), (0, (12, 1)), (0, (5, 10)), (0, (7, 3)),
+    (60, ()), (0, ()), (0, (11, 16)), (0, ()), (36.0, (17,)), (0, ()), (1.2, (3, 16, 0)), (0, (23,)),
+    (0, (19, 0, 15)), (0, (5,)), (0, ()), (0, (23, 6, 9)), (48.0, ()), (0, (18,)), (0, (29, 15, 27)),
+    (0.002, (28, 30, 23)), (5.6, ()), (0.37, (22,)), (0, (34,)), (0.001, (19, 34, 13)), (0, (33, 25)),
+    (0.002, (19, 30)), (0, ()), (0.6, (36,)), (0, (9, 36)), (1.2, ()), (0, ()), (0.07, ()), (0, ()),
+    (0.27, ()), (0, (36, 44, 46)), (0.001, ()), (0, ()), (21.0, ()), (0, ()), (7.0, (34,)), (0, (47,)),
+    (0.002, ()), (0, (45, 47)), (2.1, ()), (0, ()), (0.0325, ()), (0, (43, 48)), (0.36, (23, 59)),
+    (0, (58,)), (0.105, (60,)), (0, (57,)), (0, (63,)), (0, (49,)), (2.1, (33,)), (0, (52,)), (2.1, ()),
+    (0, ()), (2.1, ()), (0.7, (61,)), (0, ()), (0, ()), (0, (57, 67)), (3, (66,)), (9.0, (70,)), (0, (70,)),
+    (0, (61,)), (0, (78, 77, 13)), (0.002, ()), (0.1, ()),
 )
 STEPS = []
 
@@ -1168,8 +1168,6 @@
             [pltpu.VMEM((768, 768), F32)],
         )
 
-    down_away, down_kept = make_down(active)
-    down_came = send(down_away, "z", 1)
     sum_away, sum_kept, grad_hidden = call(
         lower_rows,
         [sds(368, 768), *keep(sds(368, 768, dtype=F32), sds(736, 768))],
@@ -1179,6 +1177,8 @@
     sum_came = send(sum_away, "core", 1)
     chip_sum = call(add_rows, [sds(368, 768)], [Keep(sum_kept), sum_came])[0]
     chip_came = send(chip_sum, "x", 1)
+    down_away, down_kept = make_down(active)
+    down_came = send(down_away, "z", 1)
     up_away, up_kept = call(
         up_grads,
         half,
@@ -1217,6 +1217,7 @@
     )
     a_came = send(a_away, "y", 1)
     up_steps = halve_y(up_kept, up_came)
+    down_last = side_y(down_two, down_came)
     grad_qk, b_away, b_kept = call(
         score_back,
         [Keep(sds(736, 384)), sds(4, 96, 384), Keep(sds(4, 96, 384, dtype=F32))],
@@ -1238,10 +1239,9 @@
         [Keep(m_kept), m_came, Keep(h_kept), h_came],
     )
     far_rows = send(go, "x", 1)
-    down_last = side_y(down_two, down_came)
-    up_last = halve_z(up_steps)
     b_steps = add_y(b_kept, b_came)
     a_last = halve_z(a_pair)
+    up_last = halve_z(up_steps)
     grad_down = add_last(down_last)
     pieces = [Keep(sds(32, 768, dtype=F32)), sds(32, 768), sds(64, 768)]
     held = pltpu.VMEM((4, 32, 768), F32)

time: 147 us -> 143 us (0.973)
  waiting for transfers between devices: 62.1 us -> 58.2 us
  local copies, waits for them, and re-layouts: 3.31 us -> 0.79 us
  starting transfers between devices: 46.3 us -> 48.4 us
    ppermute x51, waiting for transfers between devices: 62.1 us -> 58.2 us  [send(): STEPS.append(lax.ppermute(rows, ('dp', 'blk'), pairs))]
    unnamed x30 -> x24, local copies, waits for them, and re-layouts: 3.24 us -> 0.71 us
    ppermute x51, starting transfers between devices: 46.3 us -> 48.4 us  [send(): STEPS.append(lax.ppermute(rows, ('dp', 'blk'), pairs))]
  transfers between devices with their start and end apart: 51 -> 51, of which waited for: 28 -> 25; matrix products, arithmetic and copies ran while one was open for 0% -> 0% of each run, Pallas kernels for 19% -> 19%
where the time goes in v6:
time: 143 us; the launch traced here: 142 us
  waiting for transfers between devices  58.2 us (41%)
  starting transfers between devices  48.4 us (34%)
  Pallas kernels  34 us (24%)
    ppermute x51, waiting for transfers between devices, send(): STEPS.append(lax.ppermute(rows, ('dp', 'blk'), pairs))  58.2 us
    ppermute x51, starting transfers between devices, send(): STEPS.append(lax.ppermute(rows, ('dp', 'blk'), pairs))  48.4 us
    pallas_call x31, Pallas kernels, call(): pl.pallas_call(body, out_shape=tuple((pltpu.VMEM(v.value.shape, v.value.d...  34 us
  transfers between devices with their start and end apart: 51, of which 25 were waited for; matrix products, arithmetic and copies ran while one was open for 0% of the time, Pallas kernels for 19%

profile of v6, /device:TPU:0, one launch (start us, length us, event | category | flops | bytes accessed | tf_op | source)
XLA Modules:
  0.0 142.5 jit_solution(15589118873198107384)
XLA Ops:
  0.7 1.3 pick_pieces.1
  2.0 3.0 %collective-permute-start.1 = (bf16[96,768]{1,0:T(8,128)(2,1)S(1)}, bf16[96,768]{1,0:T(8,128)(2,1)S(1)}, u32[]{:S(2)}, u32[]{:S(2)}) collective-permute-start(bf16[96,768]{1,0:T(8,128)(2,1)S(1)} %get-tuple-element.130), channel_id=1, source_target_pairs={{0,2},{1,3},{2,0},{3,1},{4,6},{5,7},{6,4},{7,5},{8,10},{9,11},{10,... | collective-permute-start | bytes 442376 | tf_op jit(solution)/shard_map/ppermute | solution.py:1028
  6.2 2.6 %collective-permute-done.1.refs_2_ = bf16[96,768]{1,0:T(8,128)(2,1)S(1)} collective-permute-done((bf16[96,768]{1,0:T(8,128)(2,1)S(1)}, bf16[96,768]{1,0:T(8,128)(2,1)S(1)}, u32[]{:S(2)}, u32[]{:S(2)}) %collective-permute-start.1) | collective-permute-done | bytes 147488 | tf_op jit(solution)/shard_map/ppermute | solution.py:1028
  8.8 1.8 %collective-permute-start.7 = (bf16[352,768]{1,0:T(8,128)(2,1)S(1)}, bf16[352,768]{1,0:T(8,128)(2,1)S(1)}, u32[]{:S(2)}, u32[]{:S(2)}) collective-permute-start(bf16[352,768]{1,0:T(8,128)(2,1)S(1)} %get-tuple-element.135.refs_0_), channel_id=1, source_target_pairs={{0,2},{1,3},{2,0},{3,1},{4,6},{5,7},{6,4},{7,5},{8,10},{9,11},{10,... | collective-permute-start | bytes 1622024 | tf_op jit(solution)/shard_map/ppermute | solution.py:1028
  10.8 1.6 %collective-permute-start.4 = (bf16[112,768]{1,0:T(8,128)(2,1)S(1)}, bf16[112,768]{1,0:T(8,128)(2,1)S(1)}, u32[]{:S(2)}, u32[]{:S(2)}) collective-permute-start(bf16[112,768]{1,0:T(8,128)(2,1)S(1)} %get-tuple-element.136.refs_0_), channel_id=1, source_target_pairs={{0,8},{1,9},{2,10},{3,11},{4,12},{5,13},{6,14},{7,15},{8,0},{9,1},... | collective-permute-start | bytes 516104 | tf_op jit(solution)/shard_map/ppermute | solution.py:1028
  12.4 1.5 %collective-permute-start.8 = (bf16[112,768]{1,0:T(8,128)(2,1)S(1)}, bf16[112,768]{1,0:T(8,128)(2,1)S(1)}, u32[]{:S(2)}, u32[]{:S(2)}) collective-permute-start(bf16[112,768]{1,0:T(8,128)(2,1)S(1)} %get-tuple-element.136.refs_0_), channel_id=1, source_target_pairs={{0,4},{1,5},{2,6},{3,7},{4,0},{5,1},{6,2},{7,3},{8,12},{9,13},{10,... | collective-permute-start | bytes 516104 | tf_op jit(solution)/shard_map/ppermute | solution.py:1028
  13.9 2.6 %collective-permute-start.3 = (bf16[112,768]{1,0:T(8,128)(2,1)S(1)}, bf16[112,768]{1,0:T(8,128)(2,1)S(1)}, u32[]{:S(2)}, u32[]{:S(2)}) collective-permute-start(bf16[112,768]{1,0:T(8,128)(2,1)S(1)} %get-tuple-element.136.refs_0_), channel_id=1, source_target_pairs={{0,16},{1,17},{2,18},{3,19},{4,20},{5,21},{6,22},{7,23},{8,24},{9,... | collective-permute-start | bytes 516104 | tf_op jit(solution)/shard_map/ppermute | solution.py:1028
  16.5 2.4 %collective-permute-done.4.refs_1_ = bf16[112,768]{1,0:T(8,128)(2,1)S(1)} collective-permute-done((bf16[112,768]{1,0:T(8,128)(2,1)S(1)}, bf16[112,768]{1,0:T(8,128)(2,1)S(1)}, u32[]{:S(2)}, u32[]{:S(2)}) %collective-permute-start.4) | collective-permute-done | bytes 172064 | tf_op jit(solution)/shard_map/ppermute | solution.py:1028
  18.9 3.2 %collective-permute-start.5 = (bf16[112,768]{1,0:T(8,128)(2,1)S(1)}, bf16[112,768]{1,0:T(8,128)(2,1)S(1)}, u32[]{:S(2)}, u32[]{:S(2)}) collective-permute-start(bf16[112,768]{1,0:T(8,128)(2,1)S(1)} %collective-permute-done.4.refs_1_), channel_id=1, source_target_pairs={{0,4},{1,5},{2,6},{3,7},{4,0},{5,1},{6,2},{7,3},{8,12},{9,13},{10,... | collective-permute-start | bytes 516104 | tf_op jit(solution)/shard_map/ppermute | solution.py:1028
  22.1 1.4 collective-permute-done.7.refs_2_
  26.5 1.7 %collective-permute-start.11 = (bf16[112,768]{1,0:T(8,128)(2,1)S(1)}, bf16[112,768]{1,0:T(8,128)(2,1)}, u32[]{:S(2)}, u32[]{:S(2)}) collective-permute-start(bf16[112,768]{1,0:T(8,128)(2,1)S(1)} %collective-permute-done.3.refs_2_), channel_id=1, source_target_pairs={{0,4},{1,5},{2,6},{3,7},{4,0},{5,1},{6,2},{7,3},{8,12},{9,13},{10,... | collective-permute-start | bytes 516104 | tf_op jit(solution)/shard_map/ppermute | solution.py:1028
  28.3 3.3 %collective-permute-start.19 = (bf16[192,768]{1,0:T(8,128)(2,1)S(1)}, bf16[192,768]{1,0:T(8,128)(2,1)S(1)}, u32[]{:S(2)}, u32[]{:S(2)}) collective-permute-start(bf16[192,768]{1,0:T(8,128)(2,1)S(1)} %get-tuple-element.157.refs_1_), channel_id=1, source_target_pairs={{0,16},{1,17},{2,18},{3,19},{4,20},{5,21},{6,22},{7,23},{8,24},{9,... | collective-permute-start | bytes 884744 | tf_op jit(solution)/shard_map/ppermute | solution.py:1028
  31.6 3.4 %collective-permute-done.10.refs_3_ = bf16[112,768]{1,0:T(8,128)(2,1)} collective-permute-done((bf16[112,768]{1,0:T(8,128)(2,1)S(1)}, bf16[112,768]{1,0:T(8,128)(2,1)}, u32[]{:S(2)}, u32[]{:S(2)}) %collective-permute-start.10) | collective-permute-done | bytes 172064 | tf_op jit(solution)/shard_map/ppermute | solution.py:1028
  35.0 3.5 %collective-permute-start.12 = (bf16[112,768]{1,0:T(8,128)(2,1)}, bf16[112,768]{1,0:T(8,128)(2,1)S(1)}, u32[]{:S(2)}, u32[]{:S(2)}) collective-permute-start(bf16[112,768]{1,0:T(8,128)(2,1)} %collective-permute-done.10.refs_3_), channel_id=1, source_target_pairs={{0,4},{1,5},{2,6},{3,7},{4,0},{5,1},{6,2},{7,3},{8,12},{9,13},{10,... | collective-permute-start | bytes 516104 | tf_op jit(solution)/shard_map/ppermute | solution.py:1028
  38.5 2.1 %norm_rows_in.1 = (f32[736,768]{1,0:T(8,128)S(1)}, f32[2,368,368]{2,1,0:T(8,128)S(1)}, bf16[736,768]{1,0:T(8,128)(2,1)S(1)}, bf16[736,768]{1,0:T(8,128)(2,1)S(1)}, bf16[736,768]{1,0:T(8,128)(2,1)S(1)}) custom-call(bf16[352,768]{1,0:T(8,128)(2,1)S(1)} %get-tuple-element.135.refs_0_, bf16[352,768]{1,0:T(8,128)(2,1)S(1)} %collective-permute-done.6.refs_1_, ...), custom_call_target="tpu_custom_call" | custom-call | flops 60000002048 | tf_op jit(solution)/shard_map/norm_rows_in/pallas_call | solution.py:475
  40.6 2.3 %collective-permute-done.12.refs_7_ = bf16[112,768]{1,0:T(8,128)(2,1)S(1)} collective-permute-done((bf16[112,768]{1,0:T(8,128)(2,1)}, bf16[112,768]{1,0:T(8,128)(2,1)S(1)}, u32[]{:S(2)}, u32[]{:S(2)}) %collective-permute-start.12) | collective-permute-done | bytes 172064 | tf_op jit(solution)/shard_map/ppermute | solution.py:1028
  42.9 1.3 open_pack.1
  44.2 1.3 collective-permute-start.16
  45.5 1.7 %collective-permute-start.21 = (bf16[192,768]{1,0:T(8,128)(2,1)S(1)}, bf16[192,768]{1,0:T(8,128)(2,1)S(1)}, u32[]{:S(2)}, u32[]{:S(2)}) collective-permute-start(bf16[192,768]{1,0:T(8,128)(2,1)S(1)} %get-tuple-element.157.refs_1_), channel_id=1, source_target_pairs={{0,4},{1,5},{2,6},{3,7},{4,0},{5,1},{6,2},{7,3},{8,12},{9,13},{10,... | collective-permute-start | bytes 884744 | tf_op jit(solution)/shard_map/ppermute | solution.py:1028
  47.3 4.2 %collective-permute-done.23.refs_2_ = bf16[192,768]{1,0:T(8,128)(2,1)S(1)} collective-permute-done((bf16[192,768]{1,0:T(8,128)(2,1)S(1)}, bf16[192,768]{1,0:T(8,128)(2,1)S(1)}, u32[]{:S(2)}, u32[]{:S(2)}) %collective-permute-start.23) | collective-permute-done | bytes 294944 | tf_op jit(solution)/shard_map/ppermute | solution.py:1028
  52.3 3.2 %attend.1 = (bf16[736,192]{1,0:T(8,128)(2,1)S(1)}, bf16[736,576]{1,0:T(8,128)(2,1)S(1)}, bf16[6,368,368]{2,1,0:T(8,128)(2,1)S(1)}) custom-call(f32[736,768]{1,0:T(8,128)S(1)} %get-tuple-element.138.refs_8_.refs_0_, f32[2,368,368]{2,1,0:T(8,128)S(1)} %get-tuple-element.139.refs_1_, bf16[768,576]{1,0:T(8,128)(2,1)S(1)} %get-tuple-element.142.refs_2_, ...), custom_call_target="tpu_custom_call" | custom-call | flops 1200000000 | tf_op jit(solution)/shard_map/attend/pallas_call | solution.py:475
  55.5 2.1 %collective-permute-done.20.refs_4_ = bf16[192,768]{1,0:T(8,128)(2,1)S(1)} collective-permute-done((bf16[192,768]{1,0:T(8,128)(2,1)S(1)}, bf16[192,768]{1,0:T(8,128)(2,1)S(1)}, u32[]{:S(2)}, u32[]{:S(2)}) %collective-permute-start.20) | collective-permute-done | bytes 294944 | tf_op jit(solution)/shard_map/ppermute | solution.py:1028
  57.6 2.5 %collective-permute-done.24.refs_6_.refs_2_ = bf16[192,768]{1,0:T(8,128)(2,1)S(1)} collective-permute-done((bf16[192,768]{1,0:T(8,128)(2,1)S(1)}, bf16[192,768]{1,0:T(8,128)(2,1)S(1)}, u32[]{:S(2)}, u32[]{:S(2)}) %collective-permute-start.24) | collective-permute-done | bytes 294944 | tf_op jit(solution)/shard_map/ppermute | solution.py:1028
  62.5 6.9 %collective-permute-done.14.refs_2_.refs_5_ = bf16[736,192]{1,0:T(8,128)(2,1)S(1)} collective-permute-done((bf16[736,192]{1,0:T(8,128)(2,1)S(1)}, bf16[736,192]{1,0:T(8,128)(2,1)S(1)}, u32[]{:S(2)}, u32[]{:S(2)}) %collective-permute-start.14) | collective-permute-done | bytes 282656 | tf_op jit(solution)/shard_map/ppermute | solution.py:1028
  69.5 1.7 %collective-permute-done.18.refs_3_.refs_6_ = bf16[736,192]{1,0:T(8,128)(2,1)S(1)} collective-permute-done((bf16[736,192]{1,0:T(8,128)(2,1)S(1)}, bf16[736,192]{1,0:T(8,128)(2,1)S(1)}, u32[]{:S(2)}, u32[]{:S(2)}) %collective-permute-start.18) | collective-permute-done | bytes 282656 | tf_op jit(solution)/shard_map/ppermute | solution.py:1028
  71.2 2.1 %branch_rows.1 = (bf16[736,768]{1,0:T(8,128)(2,1)S(1)}, bf16[736,768]{1,0:T(8,128)(2,1)S(1)}, f32[208,768]{1,0:T(8,128)S(1)}) custom-call(bf16[736,192]{1,0:T(8,128)(2,1)S(1)} %get-tuple-element.146.refs_0_.refs_9_.refs_3_.refs_4_, bf16[736,192]{1,0:T(8,128)(2,1)S(1)} %collective-permute-done.13.refs_1_.refs_8_.refs_4_.refs_3_, ...), custom_call_target="tpu_custom_call" | custom-call | flops 2000000 | tf_op jit(solution)/shard_map/branch_rows/pallas_call | solution.py:475
  73.3 1.7 %raise_rows.1 = (bf16[736,768]{1,0:T(8,128)(2,1)S(1)}, f32[736,768]{1,0:T(8,128)S(1)}, bf16[768,768]{1,0:T(8,128)(2,1)S(1)}, bf16[768,768]{1,0:T(8,128)(2,1)S(1)}) custom-call(bf16[736,768]{1,0:T(8,128)(2,1)S(1)} %get-tuple-element.156.refs_0_, bf16[192,768]{1,0:T(8,128)(2,1)S(1)} %get-tuple-element.157.refs_1_, ...), custom_call_target="tpu_custom_call" | custom-call | flops 5600000000 | tf_op jit(solution)/shard_map/raise_rows/pallas_call | solution.py:475
  75.0 2.6 %lower_rows.1 = (bf16[368,768]{1,0:T(8,128)(2,1)S(1)}, f32[368,768]{1,0:T(8,128)S(1)}, bf16[736,768]{1,0:T(8,128)(2,1)S(1)}) custom-call(f32[736,768]{1,0:T(8,128)S(1)} %get-tuple-element.166.refs_0_, bf16[736,768]{1,0:T(8,128)(2,1)S(1)} %get-tuple-element.167.refs_1_, bf16[768,768]{1,0:T(8,128)(2,1)S(1)} %get-tuple-element.168.refs_2_, ...), custom_call_target="tpu_custom_call" | custom-call | flops 370000000 | tf_op jit(solution)/shard_map/lower_rows/pallas_call | solution.py:475
  81.0 1.4 up_grads.1
  82.4 1.5 %collective-permute-start.45 = (bf16[4,96,768]{2,1,0:T(8,128)(2,1)S(1)}, bf16[4,96,768]{2,1,0:T(8,128)(2,1)S(1)}, u32[]{:S(2)}, u32[]{:S(2)}) collective-permute-start(bf16[4,96,768]{2,1,0:T(8,128)(2,1)S(1)} %get-tuple-element.227), channel_id=1, source_target_pairs={{0,4},{1,5},{2,6},{3,7},{4,0},{5,1},{6,2},{7,3},{8,12},{9,13},{10,... | collective-permute-start | bytes 1769480 | tf_op jit(solution)/shard_map/ppermute | solution.py:1028
  83.9 1.7 %mlp_rows.1 = (bf16[416,768]{1,0:T(8,128)(2,1)S(1)}, f32[416,768]{1,0:T(8,128)S(1)}, f32[8,768]{1,0:T(8,128)S(1)}, bf16[736,192]{1,0:T(8,128)(2,1)S(1)}) custom-call(bf16[736,768]{1,0:T(8,128)(2,1)S(1)} %get-tuple-element.160.refs_0_.refs_2_, bf16[768,768]{1,0:T(8,128)(2,1)S(1)} %get-tuple-element.161.refs_1_.refs_3_, ...), custom_call_target="tpu_custom_call" | custom-call | flops 1200000000 | tf_op jit(solution)/shard_map/mlp_rows/pallas_call | solution.py:475
  85.7 9.1 %collective-permute-done.29.refs_1_ = bf16[4,96,768]{2,1,0:T(8,128)(2,1)S(1)} collective-permute-done((bf16[4,96,768]{2,1,0:T(8,128)(2,1)S(1)}, bf16[4,96,768]{2,1,0:T(8,128)(2,1)S(1)}, u32[]{:S(2)}, u32[]{:S(2)}) %collective-permute-start.29) | collective-permute-done | bytes 589856 | tf_op jit(solution)/shard_map/ppermute | solution.py:1028
  95.4 2.1 %collective-permute-done.45.refs_1_ = bf16[4,96,768]{2,1,0:T(8,128)(2,1)S(1)} collective-permute-done((bf16[4,96,768]{2,1,0:T(8,128)(2,1)S(1)}, bf16[4,96,768]{2,1,0:T(8,128)(2,1)S(1)}, u32[]{:S(2)}, u32[]{:S(2)}) %collective-permute-start.45) | collective-permute-done | bytes 589856 | tf_op jit(solution)/shard_map/ppermute | solution.py:1028
  97.7 1.6 %collective-permute-start.46 = (bf16[2,96,768]{2,1,0:T(8,128)(2,1)S(1)}, bf16[2,96,768]{2,1,0:T(8,128)(2,1)S(1)}, u32[]{:S(2)}, u32[]{:S(2)}) collective-permute-start(bf16[2,96,768]{2,1,0:T(8,128)(2,1)S(1)} %get-tuple-element.229), channel_id=1, source_target_pairs={{0,8},{1,9},{2,10},{3,11},{4,12},{5,13},{6,14},{7,15},{8,0},{9,1},... | collective-permute-start | bytes 884744 | tf_op jit(solution)/shard_map/ppermute | solution.py:1028
  99.2 3.9 %branch_back.1 = (f32[208,768]{1,0:T(8,128)S(1)}, bf16[736,192]{1,0:T(8,128)(2,1)S(1)}, bf16[736,192]{1,0:T(8,128)(2,1)S(1)}, bf16[4,112,384]{2,1,0:T(8,128)(2,1)S(1)}, f32[4,112,384]{2,1,0:T(8,128)S(1)}) custom-call(bf16[368,768]{1,0:T(8,128)(2,1)S(1)} %add_pair.1.refs_0_, bf16[368,768]{1,0:T(8,128)(2,1)S(1)} %collective-permute-done.30.refs_1_, ...), custom_call_target="tpu_custom_call" | custom-call | flops 1000000 | tf_op jit(solution)/shard_map/branch_back/pallas_call | solution.py:475
  103.2 1.5 %collective-permute-start.33 = (bf16[4,112,384]{2,1,0:T(8,128)(2,1)S(1)}, bf16[4,112,384]{2,1,0:T(8,128)(2,1)S(1)}, u32[]{:S(2)}, u32[]{:S(2)}) collective-permute-start(bf16[4,112,384]{2,1,0:T(8,128)(2,1)S(1)} %get-tuple-element.198), channel_id=1, source_target_pairs={{0,4},{1,5},{2,6},{3,7},{4,0},{5,1},{6,2},{7,3},{8,12},{9,13},{10,... | collective-permute-start | bytes 1032200 | tf_op jit(solution)/shard_map/ppermute | solution.py:1028
  104.6 3.8 %score_back.1 = (bf16[736,384]{1,0:T(8,128)(2,1)S(1)}, bf16[4,96,384]{2,1,0:T(8,128)(2,1)S(1)}, f32[4,96,384]{2,1,0:T(8,128)S(1)}) custom-call(bf16[6,368,368]{2,1,0:T(8,128)(2,1)S(1)} %get-tuple-element.164.refs_7_.refs_0_, bf16[736,576]{1,0:T(8,128)(2,1)S(1)} %get-tuple-element.165.refs_1_, bf16[736,192]{1,0:T(8,128)(2,1)S(1)} %get-tuple-element.182.refs_2_, ...), custom_call_target="tpu_custom_call" | custom-call | flops 2000000 | tf_op jit(solution)/shard_map/score_back/pallas_call | solution.py:475
  110.8 1.8 %collective-permute-start.37 = (bf16[4,96,384]{2,1,0:T(8,128)(2,1)S(1)}, bf16[4,96,384]{2,1,0:T(8,128)(2,1)S(1)}, u32[]{:S(2)}, u32[]{:S(2)}) collective-permute-start(bf16[4,96,384]{2,1,0:T(8,128)(2,1)S(1)} %get-tuple-element.208), channel_id=1, source_target_pairs={{0,4},{1,5},{2,6},{3,7},{4,0},{5,1},{6,2},{7,3},{8,12},{9,13},{10,... | collective-permute-start | bytes 884744 | tf_op jit(solution)/shard_map/ppermute | solution.py:1028
  114.1 2.6 %collective-permute-start.47 = (bf16[96,768]{1,0:T(8,128)(2,1)S(1)}, bf16[96,768]{1,0:T(8,128)(2,1)S(1)}, u32[]{:S(2)}, u32[]{:S(2)}) collective-permute-start(bf16[96,768]{1,0:T(8,128)(2,1)S(1)} %get-tuple-element.231), channel_id=1, source_target_pairs={{0,16},{1,17},{2,18},{3,19},{4,20},{5,21},{6,22},{7,23},{8,24},{9,... | collective-permute-start | bytes 442376 | tf_op jit(solution)/shard_map/ppermute | solution.py:1028
  117.0 3.8 %collective-permute-done.37.refs_1_ = bf16[4,96,384]{2,1,0:T(8,128)(2,1)S(1)} collective-permute-done((bf16[4,96,384]{2,1,0:T(8,128)(2,1)S(1)}, bf16[4,96,384]{2,1,0:T(8,128)(2,1)S(1)}, u32[]{:S(2)}, u32[]{:S(2)}) %collective-permute-start.37) | collective-permute-done | bytes 294944 | tf_op jit(solution)/shard_map/ppermute | solution.py:1028
  120.8 1.6 %collective-permute-done.34.refs_1_ = bf16[2,112,384]{2,1,0:T(8,128)(2,1)S(1)} collective-permute-done((bf16[2,112,384]{2,1,0:T(8,128)(2,1)S(1)}, bf16[2,112,384]{2,1,0:T(8,128)(2,1)S(1)}, u32[]{:S(2)}, u32[]{:S(2)}) %collective-permute-start.34) | collective-permute-done | bytes 172064 | tf_op jit(solution)/shard_map/ppermute | solution.py:1028
  122.4 2.9 %collective-permute-start.36 = (bf16[112,384]{1,0:T(8,128)(2,1)S(1)}, bf16[112,384]{1,0:T(8,128)(2,1)S(1)}, u32[]{:S(2)}, u32[]{:S(2)}) collective-permute-start(bf16[112,384]{1,0:T(8,128)(2,1)S(1)} %get-tuple-element.205), channel_id=1, source_target_pairs={{0,16},{1,17},{2,18},{3,19},{4,20},{5,21},{6,22},{7,23},{8,24},{9,... | collective-permute-start | bytes 258056 | tf_op jit(solution)/shard_map/ppermute | solution.py:1028
  125.3 1.6 %collective-permute-done.38.refs_3_ = bf16[96,384]{1,0:T(8,128)(2,1)S(1)} collective-permute-done((bf16[96,384]{1,0:T(8,128)(2,1)S(1)}, bf16[96,384]{1,0:T(8,128)(2,1)S(1)}, u32[]{:S(2)}, u32[]{:S(2)}) %collective-permute-start.38) | collective-permute-done | bytes 73760 | tf_op jit(solution)/shard_map/ppermute | solution.py:1028
  126.9 2.0 %collective-permute-start.40 = (bf16[96,384]{1,0:T(8,128)(2,1)S(1)}, bf16[96,384]{1,0:T(8,128)(2,1)S(1)}, u32[]{:S(2)}, u32[]{:S(2)}) collective-permute-start(bf16[96,384]{1,0:T(8,128)(2,1)S(1)} %get-tuple-element.215), channel_id=1, source_target_pairs={{0,24},{1,25},{2,26},{3,27},{4,28},{5,29},{6,30},{7,31},{8,16},{9,... | collective-permute-start | bytes 221192 | tf_op jit(solution)/shard_map/ppermute | solution.py:1028
  131.0 2.2 %collective-permute-done.40.refs_5_ = bf16[96,384]{1,0:T(8,128)(2,1)S(1)} collective-permute-done((bf16[96,384]{1,0:T(8,128)(2,1)S(1)}, bf16[96,384]{1,0:T(8,128)(2,1)S(1)}, u32[]{:S(2)}, u32[]{:S(2)}) %collective-permute-start.40) | collective-permute-done | bytes 73760 | tf_op jit(solution)/shard_map/ppermute | solution.py:1028
  133.2 1.7 %collective-permute-done.39.refs_4_ = bf16[96,384]{1,0:T(8,128)(2,1)S(1)} collective-permute-done((bf16[96,384]{1,0:T(8,128)(2,1)S(1)}, bf16[96,384]{1,0:T(8,128)(2,1)S(1)}, u32[]{:S(2)}, u32[]{:S(2)}) %collective-permute-start.39) | collective-permute-done | bytes 73760 | tf_op jit(solution)/shard_map/ppermute | solution.py:1028
  135.6 1.8 %collective-permute-start.43 = (bf16[64,768]{1,0:T(8,128)(2,1)S(1)}, bf16[64,768]{1,0:T(8,128)(2,1)S(1)}, u32[]{:S(2)}, u32[]{:S(2)}) collective-permute-start(bf16[64,768]{1,0:T(8,128)(2,1)S(1)} %get-tuple-element.222), channel_id=1, source_target_pairs={{0,2},{1,3},{2,0},{3,1},{4,6},{5,7},{6,4},{7,5},{8,10},{9,11},{10,... | collective-permute-start | bytes 294920 | tf_op jit(solution)/shard_map/ppermute | solution.py:1028
  138.0 1.5 %finish_rows.1 = (bf16[176,768]{1,0:T(8,128)(2,1)}, bf16[20,768]{1,0:T(8,128)(2,1)}, f32[176,768]{1,0:T(8,128)}, f32[20,768]{1,0:T(8,128)}) custom-call(f32[416,768]{1,0:T(8,128)S(1)} %get-tuple-element.189.refs_0_.refs_2_, bf16[416,768]{1,0:T(8,128)(2,1)S(1)} %collective-permute-done.32.refs_1_.refs_2_, f32[208,768]{1,0:T(8,128)S(1)} %get-tuple-element.192.refs_2_, ...), custom_call_target="tpu_custom_call" | custom-call | flops 2000000 | tf_op jit(solution)/shard_map/finish_rows/pallas_call | solution.py:475
  (110 shorter events, 22.5 us)
Async XLA Ops:
  2.0 6.9 %collective-permute-start.1 = (bf16[96,768]{1,0:T(8,128)(2,1)S(1)}, bf16[96,768]{1,0:T(8,128)(2,1)S(1)}, u32[]{:S(2)}, u32[]{:S(2)}) collective-permute-start(bf16[96,768]{1,0:T(8,128)(2,1)S(1)} %get-tuple-element.130), channel_id=1, source_target_pairs={{0,2},{1,3},{2,0},{3,1},{4,6},{5,7},{6,4},{7,5},{8,10},{9,11},{10,... | collective-permute-start | bytes 442376 | tf_op jit(solution)/shard_map/ppermute | solution.py:1028
  8.8 1.8 %collective-permute-start.2 = (bf16[96,768]{1,0:T(8,128)(2,1)S(1)}, bf16[96,768]{1,0:T(8,128)(2,1)S(1)}, u32[]{:S(2)}, u32[]{:S(2)}) collective-permute-start(bf16[96,768]{1,0:T(8,128)(2,1)S(1)} %collective-permute-done.1.refs_2_), channel_id=1, source_target_pairs={{0,1},{1,0},{2,3},{3,2},{4,5},{5,4},{6,7},{7,6},{8,9},{9,8},{10,11... | collective-permute-start | bytes 442376 | tf_op jit(solution)/shard_map/ppermute | solution.py:1028
  8.8 14.7 %collective-permute-start.7 = (bf16[352,768]{1,0:T(8,128)(2,1)S(1)}, bf16[352,768]{1,0:T(8,128)(2,1)S(1)}, u32[]{:S(2)}, u32[]{:S(2)}) collective-permute-start(bf16[352,768]{1,0:T(8,128)(2,1)S(1)} %get-tuple-element.135.refs_0_), channel_id=1, source_target_pairs={{0,2},{1,3},{2,0},{3,1},{4,6},{5,7},{6,4},{7,5},{8,10},{9,11},{10,... | collective-permute-start | bytes 1622024 | tf_op jit(solution)/shard_map/ppermute | solution.py:1028
  10.8 8.1 %collective-permute-start.4 = (bf16[112,768]{1,0:T(8,128)(2,1)S(1)}, bf16[112,768]{1,0:T(8,128)(2,1)S(1)}, u32[]{:S(2)}, u32[]{:S(2)}) collective-permute-start(bf16[112,768]{1,0:T(8,128)(2,1)S(1)} %get-tuple-element.136.refs_0_), channel_id=1, source_target_pairs={{0,8},{1,9},{2,10},{3,11},{4,12},{5,13},{6,14},{7,15},{8,0},{9,1},... | collective-permute-start | bytes 516104 | tf_op jit(solution)/shard_map/ppermute | solution.py:1028
  12.4 9.7 %collective-permute-start.8 = (bf16[112,768]{1,0:T(8,128)(2,1)S(1)}, bf16[112,768]{1,0:T(8,128)(2,1)S(1)}, u32[]{:S(2)}, u32[]{:S(2)}) collective-permute-start(bf16[112,768]{1,0:T(8,128)(2,1)S(1)} %get-tuple-element.136.refs_0_), channel_id=1, source_target_pairs={{0,4},{1,5},{2,6},{3,7},{4,0},{5,1},{6,2},{7,3},{8,12},{9,13},{10,... | collective-permute-start | bytes 516104 | tf_op jit(solution)/shard_map/ppermute | solution.py:1028
  13.9 10.5 %collective-permute-start.3 = (bf16[112,768]{1,0:T(8,128)(2,1)S(1)}, bf16[112,768]{1,0:T(8,128)(2,1)S(1)}, u32[]{:S(2)}, u32[]{:S(2)}) collective-permute-start(bf16[112,768]{1,0:T(8,128)(2,1)S(1)} %get-tuple-element.136.refs_0_), channel_id=1, source_target_pairs={{0,16},{1,17},{2,18},{3,19},{4,20},{5,21},{6,22},{7,23},{8,24},{9,... | collective-permute-start | bytes 516104 | tf_op jit(solution)/shard_map/ppermute | solution.py:1028
  18.9 6.6 %collective-permute-start.5 = (bf16[112,768]{1,0:T(8,128)(2,1)S(1)}, bf16[112,768]{1,0:T(8,128)(2,1)S(1)}, u32[]{:S(2)}, u32[]{:S(2)}) collective-permute-start(bf16[112,768]{1,0:T(8,128)(2,1)S(1)} %collective-permute-done.4.refs_1_), channel_id=1, source_target_pairs={{0,4},{1,5},{2,6},{3,7},{4,0},{5,1},{6,2},{7,3},{8,12},{9,13},{10,... | collective-permute-start | bytes 516104 | tf_op jit(solution)/shard_map/ppermute | solution.py:1028
  23.5 14.9 %collective-permute-start.9 = (bf16[352,768]{1,0:T(8,128)(2,1)S(1)}, bf16[352,768]{1,0:T(8,128)(2,1)S(1)}, u32[]{:S(2)}, u32[]{:S(2)}) collective-permute-start(bf16[352,768]{1,0:T(8,128)(2,1)S(1)} %collective-permute-done.7.refs_2_), channel_id=1, source_target_pairs={{0,1},{1,0},{2,3},{3,2},{4,5},{5,4},{6,7},{7,6},{8,9},{9,8},{10,11... | collective-permute-start | bytes 1622024 | tf_op jit(solution)/shard_map/ppermute | solution.py:1028
  26.2 12.2 %collective-permute-start.6 = (bf16[352,768]{1,0:T(8,128)(2,1)S(1)}, bf16[352,768]{1,0:T(8,128)(2,1)S(1)}, u32[]{:S(2)}, u32[]{:S(2)}) collective-permute-start(bf16[352,768]{1,0:T(8,128)(2,1)S(1)} %get-tuple-element.135.refs_0_), channel_id=1, source_target_pairs={{0,1},{1,0},{2,3},{3,2},{4,5},{5,4},{6,7},{7,6},{8,9},{9,8},{10,11... | collective-permute-start | bytes 1622024 | tf_op jit(solution)/shard_map/ppermute | solution.py:1028
  26.2 8.7 %collective-permute-start.10 = (bf16[112,768]{1,0:T(8,128)(2,1)S(1)}, bf16[112,768]{1,0:T(8,128)(2,1)}, u32[]{:S(2)}, u32[]{:S(2)}) collective-permute-start(bf16[112,768]{1,0:T(8,128)(2,1)S(1)} %collective-permute-done.3.refs_2_), channel_id=1, source_target_pairs={{0,8},{1,9},{2,10},{3,11},{4,12},{5,13},{6,14},{7,15},{8,0},{9,1},... | collective-permute-start | bytes 516104 | tf_op jit(solution)/shard_map/ppermute | solution.py:1028
  26.5 11.9 %collective-permute-start.11 = (bf16[112,768]{1,0:T(8,128)(2,1)S(1)}, bf16[112,768]{1,0:T(8,128)(2,1)}, u32[]{:S(2)}, u32[]{:S(2)}) collective-permute-start(bf16[112,768]{1,0:T(8,128)(2,1)S(1)} %collective-permute-done.3.refs_2_), channel_id=1, source_target_pairs={{0,4},{1,5},{2,6},{3,7},{4,0},{5,1},{6,2},{7,3},{8,12},{9,13},{10,... | collective-permute-start | bytes 516104 | tf_op jit(solution)/shard_map/ppermute | solution.py:1028
  28.3 19.0 %collective-permute-start.19 = (bf16[192,768]{1,0:T(8,128)(2,1)S(1)}, bf16[192,768]{1,0:T(8,128)(2,1)S(1)}, u32[]{:S(2)}, u32[]{:S(2)}) collective-permute-start(bf16[192,768]{1,0:T(8,128)(2,1)S(1)} %get-tuple-element.157.refs_1_), channel_id=1, source_target_pairs={{0,16},{1,17},{2,18},{3,19},{4,20},{5,21},{6,22},{7,23},{8,24},{9,... | collective-permute-start | bytes 884744 | tf_op jit(solution)/shard_map/ppermute | solution.py:1028
  35.0 7.9 %collective-permute-start.12 = (bf16[112,768]{1,0:T(8,128)(2,1)}, bf16[112,768]{1,0:T(8,128)(2,1)S(1)}, u32[]{:S(2)}, u32[]{:S(2)}) collective-permute-start(bf16[112,768]{1,0:T(8,128)(2,1)} %collective-permute-done.10.refs_3_), channel_id=1, source_target_pairs={{0,4},{1,5},{2,6},{3,7},{4,0},{5,1},{6,2},{7,3},{8,12},{9,13},{10,... | collective-permute-start | bytes 516104 | tf_op jit(solution)/shard_map/ppermute | solution.py:1028
  38.4 13.1 %collective-permute-start.23 = (bf16[192,768]{1,0:T(8,128)(2,1)S(1)}, bf16[192,768]{1,0:T(8,128)(2,1)S(1)}, u32[]{:S(2)}, u32[]{:S(2)}) collective-permute-start(bf16[192,768]{1,0:T(8,128)(2,1)S(1)} %get-tuple-element.157.refs_1_), channel_id=1, source_target_pairs={{0,8},{1,9},{2,10},{3,11},{4,12},{5,13},{6,14},{7,15},{8,0},{9,1},... | collective-permute-start | bytes 884744 | tf_op jit(solution)/shard_map/ppermute | solution.py:1028
  44.2 8.1 %collective-permute-start.16 = (bf16[192,768]{1,0:T(8,128)(2,1)S(1)}, bf16[192,768]{1,0:T(8,128)(2,1)S(1)}, u32[]{:S(2)}, u32[]{:S(2)}) collective-permute-start(bf16[192,768]{1,0:T(8,128)(2,1)S(1)} %get-tuple-element.148.refs_0_), channel_id=1, source_target_pairs={{0,2},{1,3},{2,0},{3,1},{4,6},{5,7},{6,4},{7,5},{8,10},{9,11},{10,... | collective-permute-start | bytes 884744 | tf_op jit(solution)/shard_map/ppermute | solution.py:1028
  45.5 10.0 %collective-permute-start.21 = (bf16[192,768]{1,0:T(8,128)(2,1)S(1)}, bf16[192,768]{1,0:T(8,128)(2,1)S(1)}, u32[]{:S(2)}, u32[]{:S(2)}) collective-permute-start(bf16[192,768]{1,0:T(8,128)(2,1)S(1)} %get-tuple-element.157.refs_1_), channel_id=1, source_target_pairs={{0,4},{1,5},{2,6},{3,7},{4,0},{5,1},{6,2},{7,3},{8,12},{9,13},{10,... | collective-permute-start | bytes 884744 | tf_op jit(solution)/shard_map/ppermute | solution.py:1028
  47.3 10.3 %collective-permute-start.20 = (bf16[192,768]{1,0:T(8,128)(2,1)S(1)}, bf16[192,768]{1,0:T(8,128)(2,1)S(1)}, u32[]{:S(2)}, u32[]{:S(2)}) collective-permute-start(bf16[192,768]{1,0:T(8,128)(2,1)S(1)} %collective-permute-done.19.refs_3_.refs_4_), channel_id=1, source_target_pairs={{0,8},{1,9},{2,10},{3,11},{4,12},{5,13},{6,14},{7,15},{8,0},{9,1},... | collective-permute-start | bytes 884744 | tf_op jit(solution)/shard_map/ppermute | solution.py:1028
  51.5 8.6 %collective-permute-start.24 = (bf16[192,768]{1,0:T(8,128)(2,1)S(1)}, bf16[192,768]{1,0:T(8,128)(2,1)S(1)}, u32[]{:S(2)}, u32[]{:S(2)}) collective-permute-start(bf16[192,768]{1,0:T(8,128)(2,1)S(1)} %collective-permute-done.23.refs_2_), channel_id=1, source_target_pairs={{0,4},{1,5},{2,6},{3,7},{4,0},{5,1},{6,2},{7,3},{8,12},{9,13},{10,... | collective-permute-start | bytes 884744 | tf_op jit(solution)/shard_map/ppermute | solution.py:1028
  51.5 9.8 %collective-permute-start.15 = (bf16[192,768]{1,0:T(8,128)(2,1)S(1)}, bf16[192,768]{1,0:T(8,128)(2,1)S(1)}, u32[]{:S(2)}, u32[]{:S(2)}) collective-permute-start(bf16[192,768]{1,0:T(8,128)(2,1)S(1)} %get-tuple-element.148.refs_0_), channel_id=1, source_target_pairs={{0,1},{1,0},{2,3},{3,2},{4,5},{5,4},{6,7},{7,6},{8,9},{9,8},{10,11... | collective-permute-start | bytes 884744 | tf_op jit(solution)/shard_map/ppermute | solution.py:1028
  52.3 9.7 %collective-permute-start.17 = (bf16[192,768]{1,0:T(8,128)(2,1)S(1)}, bf16[192,768]{1,0:T(8,128)(2,1)S(1)}, u32[]{:S(2)}, u32[]{:S(2)}) collective-permute-start(bf16[192,768]{1,0:T(8,128)(2,1)S(1)} %collective-permute-done.16.refs_2_.refs_4_), channel_id=1, source_target_pairs={{0,1},{1,0},{2,3},{3,2},{4,5},{5,4},{6,7},{7,6},{8,9},{9,8},{10,11... | collective-permute-start | bytes 884744 | tf_op jit(solution)/shard_map/ppermute | solution.py:1028
  57.6 11.9 %collective-permute-start.22 = (bf16[192,768]{1,0:T(8,128)(2,1)S(1)}, bf16[192,768]{1,0:T(8,128)(2,1)S(1)}, u32[]{:S(2)}, u32[]{:S(2)}) collective-permute-start(bf16[192,768]{1,0:T(8,128)(2,1)S(1)} %collective-permute-done.20.refs_4_), channel_id=1, source_target_pairs={{0,4},{1,5},{2,6},{3,7},{4,0},{5,1},{6,2},{7,3},{8,12},{9,13},{10,... | collective-permute-start | bytes 884744 | tf_op jit(solution)/shard_map/ppermute | solution.py:1028
  57.6 11.9 %collective-permute-start.13 = (bf16[736,192]{1,0:T(8,128)(2,1)S(1)}, bf16[736,192]{1,0:T(8,128)(2,1)S(1)}, u32[]{:S(2)}, u32[]{:S(2)}) collective-permute-start(bf16[736,192]{1,0:T(8,128)(2,1)S(1)} %get-tuple-element.146.refs_0_.refs_9_.refs_3_.refs_4_), channel_id=1, source_target_pairs={{0,1},{1,0},{2,3},{3,2},{4,5},{5,4},{6,7},{7,6},{8,9},{9,8},{10,11... | collective-permute-start | bytes 847880 | tf_op jit(solution)/shard_map/ppermute | solution.py:1028
  60.1 9.4 %collective-permute-start.14 = (bf16[736,192]{1,0:T(8,128)(2,1)S(1)}, bf16[736,192]{1,0:T(8,128)(2,1)S(1)}, u32[]{:S(2)}, u32[]{:S(2)}) collective-permute-start(bf16[736,192]{1,0:T(8,128)(2,1)S(1)} %get-tuple-element.146.refs_0_.refs_9_.refs_3_.refs_4_), channel_id=1, source_target_pairs={{0,2},{1,3},{2,0},{3,1},{4,6},{5,7},{6,4},{7,5},{8,10},{9,11},{10,... | collective-permute-start | bytes 847880 | tf_op jit(solution)/shard_map/ppermute | solution.py:1028
  61.3 12.0 %collective-permute-start.25 = (bf16[192,768]{1,0:T(8,128)(2,1)S(1)}, bf16[192,768]{1,0:T(8,128)(2,1)S(1)}, u32[]{:S(2)}, u32[]{:S(2)}) collective-permute-start(bf16[192,768]{1,0:T(8,128)(2,1)S(1)} %collective-permute-done.19.refs_3_.refs_4_), channel_id=1, source_target_pairs={{0,4},{1,5},{2,6},{3,7},{4,0},{5,1},{6,2},{7,3},{8,12},{9,13},{10,... | collective-permute-start | bytes 884744 | tf_op jit(solution)/shard_map/ppermute | solution.py:1028
  77.6 2.0 %collective-permute-start.27 = (bf16[368,768]{1,0:T(8,128)(2,1)S(1)}, bf16[368,768]{1,0:T(8,128)(2,1)S(1)}, u32[]{:S(2)}, u32[]{:S(2)}) collective-permute-start(bf16[368,768]{1,0:T(8,128)(2,1)S(1)} %get-tuple-element.171.refs_3_.refs_2_), channel_id=1, source_target_pairs={{0,1},{1,0},{2,3},{3,2},{4,5},{5,4},{6,7},{7,6},{8,9},{9,8},{10,11... | collective-permute-start | bytes 1695752 | tf_op jit(solution)/shard_map/ppermute | solution.py:1028
  79.1 15.7 %collective-permute-start.29 = (bf16[4,96,768]{2,1,0:T(8,128)(2,1)S(1)}, bf16[4,96,768]{2,1,0:T(8,128)(2,1)S(1)}, u32[]{:S(2)}, u32[]{:S(2)}) collective-permute-start(bf16[4,96,768]{2,1,0:T(8,128)(2,1)S(1)} %get-tuple-element.174), channel_id=1, source_target_pairs={{0,8},{1,9},{2,10},{3,11},{4,12},{5,13},{6,14},{7,15},{8,0},{9,1},... | collective-permute-start | bytes 1769480 | tf_op jit(solution)/shard_map/ppermute | solution.py:1028
  79.8 15.4 %collective-permute-start.28 = (bf16[368,768]{1,0:T(8,128)(2,1)S(1)}, bf16[368,768]{1,0:T(8,128)(2,1)S(1)}, u32[]{:S(2)}, u32[]{:S(2)}) collective-permute-start(bf16[368,768]{1,0:T(8,128)(2,1)S(1)} %add_rows.1.refs_0_.refs_2_), channel_id=1, source_target_pairs={{0,2},{1,3},{2,0},{3,1},{4,6},{5,7},{6,4},{7,5},{8,10},{9,11},{10,... | collective-permute-start | bytes 1695752 | tf_op jit(solution)/shard_map/ppermute | solution.py:1028
  82.4 15.2 %collective-permute-start.45 = (bf16[4,96,768]{2,1,0:T(8,128)(2,1)S(1)}, bf16[4,96,768]{2,1,0:T(8,128)(2,1)S(1)}, u32[]{:S(2)}, u32[]{:S(2)}) collective-permute-start(bf16[4,96,768]{2,1,0:T(8,128)(2,1)S(1)} %get-tuple-element.227), channel_id=1, source_target_pairs={{0,4},{1,5},{2,6},{3,7},{4,0},{5,1},{6,2},{7,3},{8,12},{9,13},{10,... | collective-permute-start | bytes 1769480 | tf_op jit(solution)/shard_map/ppermute | solution.py:1028
  85.6 24.1 %collective-permute-start.26 = (bf16[416,768]{1,0:T(8,128)(2,1)S(1)}, bf16[416,768]{1,0:T(8,128)(2,1)S(1)}, u32[]{:S(2)}, u32[]{:S(2)}) collective-permute-start(bf16[416,768]{1,0:T(8,128)(2,1)S(1)} %get-tuple-element.163), channel_id=1, source_target_pairs={{0,1},{1,0},{2,3},{3,2},{4,5},{5,4},{6,7},{7,6},{8,9},{9,8},{10,11... | collective-permute-start | bytes 1916936 | tf_op jit(solution)/shard_map/ppermute | solution.py:1028
  94.9 15.8 %collective-permute-start.35 = (bf16[2,96,768]{2,1,0:T(8,128)(2,1)S(1)}, bf16[2,96,768]{2,1,0:T(8,128)(2,1)S(1)}, u32[]{:S(2)}, u32[]{:S(2)}) collective-permute-start(bf16[2,96,768]{2,1,0:T(8,128)(2,1)S(1)} %get-tuple-element.203), channel_id=1, source_target_pairs={{0,16},{1,17},{2,18},{3,19},{4,20},{5,21},{6,22},{7,23},{8,24},{9,... | collective-permute-start | bytes 884744 | tf_op jit(solution)/shard_map/ppermute | solution.py:1028
  95.4 3.9 %collective-permute-start.30 = (bf16[368,768]{1,0:T(8,128)(2,1)S(1)}, bf16[368,768]{1,0:T(8,128)(2,1)S(1)}, u32[]{:S(2)}, u32[]{:S(2)}) collective-permute-start(bf16[368,768]{1,0:T(8,128)(2,1)S(1)} %add_pair.1.refs_0_), channel_id=1, source_target_pairs={{0,1},{1,0},{2,3},{3,2},{4,5},{5,4},{6,7},{7,6},{8,9},{9,8},{10,11... | collective-permute-start | bytes 1695752 | tf_op jit(solution)/shard_map/ppermute | solution.py:1028
  97.7 16.3 %collective-permute-start.46 = (bf16[2,96,768]{2,1,0:T(8,128)(2,1)S(1)}, bf16[2,96,768]{2,1,0:T(8,128)(2,1)S(1)}, u32[]{:S(2)}, u32[]{:S(2)}) collective-permute-start(bf16[2,96,768]{2,1,0:T(8,128)(2,1)S(1)} %get-tuple-element.229), channel_id=1, source_target_pairs={{0,8},{1,9},{2,10},{3,11},{4,12},{5,13},{6,14},{7,15},{8,0},{9,1},... | collective-permute-start | bytes 884744 | tf_op jit(solution)/shard_map/ppermute | solution.py:1028
  103.2 10.6 %collective-permute-start.33 = (bf16[4,112,384]{2,1,0:T(8,128)(2,1)S(1)}, bf16[4,112,384]{2,1,0:T(8,128)(2,1)S(1)}, u32[]{:S(2)}, u32[]{:S(2)}) collective-permute-start(bf16[4,112,384]{2,1,0:T(8,128)(2,1)S(1)} %get-tuple-element.198), channel_id=1, source_target_pairs={{0,4},{1,5},{2,6},{3,7},{4,0},{5,1},{6,2},{7,3},{8,12},{9,13},{10,... | collective-permute-start | bytes 1032200 | tf_op jit(solution)/shard_map/ppermute | solution.py:1028
  109.7 2.9 %collective-permute-start.31 = (bf16[416,768]{1,0:T(8,128)(2,1)S(1)}, bf16[416,768]{1,0:T(8,128)(2,1)S(1)}, u32[]{:S(2)}, u32[]{:S(2)}) collective-permute-start(bf16[416,768]{1,0:T(8,128)(2,1)S(1)} %get-tuple-element.188), channel_id=1, source_target_pairs={{0,1},{1,0},{2,3},{3,2},{4,5},{5,4},{6,7},{7,6},{8,9},{9,8},{10,11... | collective-permute-start | bytes 1916936 | tf_op jit(solution)/shard_map/ppermute | solution.py:1028
  110.8 9.9 %collective-permute-start.37 = (bf16[4,96,384]{2,1,0:T(8,128)(2,1)S(1)}, bf16[4,96,384]{2,1,0:T(8,128)(2,1)S(1)}, u32[]{:S(2)}, u32[]{:S(2)}) collective-permute-start(bf16[4,96,384]{2,1,0:T(8,128)(2,1)S(1)} %get-tuple-element.208), channel_id=1, source_target_pairs={{0,4},{1,5},{2,6},{3,7},{4,0},{5,1},{6,2},{7,3},{8,12},{9,13},{10,... | collective-permute-start | bytes 884744 | tf_op jit(solution)/shard_map/ppermute | solution.py:1028
  112.8 16.9 %collective-permute-start.32 = (bf16[416,768]{1,0:T(8,128)(2,1)S(1)}, bf16[416,768]{1,0:T(8,128)(2,1)S(1)}, u32[]{:S(2)}, u32[]{:S(2)}) collective-permute-start(bf16[416,768]{1,0:T(8,128)(2,1)S(1)} %get-tuple-element.191), channel_id=1, source_target_pairs={{0,2},{1,3},{2,0},{3,1},{4,6},{5,7},{6,4},{7,5},{8,10},{9,11},{10,... | collective-permute-start | bytes 1916936 | tf_op jit(solution)/shard_map/ppermute | solution.py:1028
  113.8 8.6 %collective-permute-start.34 = (bf16[2,112,384]{2,1,0:T(8,128)(2,1)S(1)}, bf16[2,112,384]{2,1,0:T(8,128)(2,1)S(1)}, u32[]{:S(2)}, u32[]{:S(2)}) collective-permute-start(bf16[2,112,384]{2,1,0:T(8,128)(2,1)S(1)} %get-tuple-element.200), channel_id=1, source_target_pairs={{0,8},{1,9},{2,10},{3,11},{4,12},{5,13},{6,14},{7,15},{8,0},{9,1},... | collective-permute-start | bytes 516104 | tf_op jit(solution)/shard_map/ppermute | solution.py:1028
  114.1 15.7 %collective-permute-start.47 = (bf16[96,768]{1,0:T(8,128)(2,1)S(1)}, bf16[96,768]{1,0:T(8,128)(2,1)S(1)}, u32[]{:S(2)}, u32[]{:S(2)}) collective-permute-start(bf16[96,768]{1,0:T(8,128)(2,1)S(1)} %get-tuple-element.231), channel_id=1, source_target_pairs={{0,16},{1,17},{2,18},{3,19},{4,20},{5,21},{6,22},{7,23},{8,24},{9,... | collective-permute-start | bytes 442376 | tf_op jit(solution)/shard_map/ppermute | solution.py:1028
  116.6 12.3 %collective-permute-start.41 = (bf16[96,768]{1,0:T(8,128)(2,1)S(1)}, bf16[96,768]{1,0:T(8,128)(2,1)S(1)}, u32[]{:S(2)}, u32[]{:S(2)}) collective-permute-start(bf16[96,768]{1,0:T(8,128)(2,1)S(1)} %get-tuple-element.217), channel_id=1, source_target_pairs={{0,4},{1,5},{2,6},{3,7},{4,0},{5,1},{6,2},{7,3},{8,12},{9,13},{10,... | collective-permute-start | bytes 442376 | tf_op jit(solution)/shard_map/ppermute | solution.py:1028
  122.4 4.6 %collective-permute-start.38 = (bf16[96,384]{1,0:T(8,128)(2,1)S(1)}, bf16[96,384]{1,0:T(8,128)(2,1)S(1)}, u32[]{:S(2)}, u32[]{:S(2)}) collective-permute-start(bf16[96,384]{1,0:T(8,128)(2,1)S(1)} %get-tuple-element.211), channel_id=1, source_target_pairs={{0,8},{1,9},{2,10},{3,11},{4,12},{5,13},{6,14},{7,15},{8,0},{9,1},... | collective-permute-start | bytes 221192 | tf_op jit(solution)/shard_map/ppermute | solution.py:1028
  122.4 8.6 %collective-permute-start.36 = (bf16[112,384]{1,0:T(8,128)(2,1)S(1)}, bf16[112,384]{1,0:T(8,128)(2,1)S(1)}, u32[]{:S(2)}, u32[]{:S(2)}) collective-permute-start(bf16[112,384]{1,0:T(8,128)(2,1)S(1)} %get-tuple-element.205), channel_id=1, source_target_pairs={{0,16},{1,17},{2,18},{3,19},{4,20},{5,21},{6,22},{7,23},{8,24},{9,... | collective-permute-start | bytes 258056 | tf_op jit(solution)/shard_map/ppermute | solution.py:1028
  126.9 6.3 %collective-permute-start.40 = (bf16[96,384]{1,0:T(8,128)(2,1)S(1)}, bf16[96,384]{1,0:T(8,128)(2,1)S(1)}, u32[]{:S(2)}, u32[]{:S(2)}) collective-permute-start(bf16[96,384]{1,0:T(8,128)(2,1)S(1)} %get-tuple-element.215), channel_id=1, source_target_pairs={{0,24},{1,25},{2,26},{3,27},{4,28},{5,29},{6,30},{7,31},{8,16},{9,... | collective-permute-start | bytes 221192 | tf_op jit(solution)/shard_map/ppermute | solution.py:1028
  129.0 5.9 %collective-permute-start.39 = (bf16[96,384]{1,0:T(8,128)(2,1)S(1)}, bf16[96,384]{1,0:T(8,128)(2,1)S(1)}, u32[]{:S(2)}, u32[]{:S(2)}) collective-permute-start(bf16[96,384]{1,0:T(8,128)(2,1)S(1)} %get-tuple-element.213), channel_id=1, source_target_pairs={{0,16},{1,17},{2,18},{3,19},{4,20},{5,21},{6,22},{7,23},{8,24},{9,... | collective-permute-start | bytes 221192 | tf_op jit(solution)/shard_map/ppermute | solution.py:1028
  129.8 7.6 %collective-permute-start.49 = (bf16[64,768]{1,0:T(8,128)(2,1)S(1)}, bf16[64,768]{1,0:T(8,128)(2,1)S(1)}, u32[]{:S(2)}, u32[]{:S(2)}) collective-permute-start(bf16[64,768]{1,0:T(8,128)(2,1)S(1)} %get-tuple-element.234), channel_id=1, source_target_pairs={{0,2},{1,3},{2,0},{3,1},{4,6},{5,7},{6,4},{7,5},{8,10},{9,11},{10,... | collective-permute-start | bytes 294920 | tf_op jit(solution)/shard_map/ppermute | solution.py:1028
  135.6 4.6 %collective-permute-start.43 = (bf16[64,768]{1,0:T(8,128)(2,1)S(1)}, bf16[64,768]{1,0:T(8,128)(2,1)S(1)}, u32[]{:S(2)}, u32[]{:S(2)}) collective-permute-start(bf16[64,768]{1,0:T(8,128)(2,1)S(1)} %get-tuple-element.222), channel_id=1, source_target_pairs={{0,2},{1,3},{2,0},{3,1},{4,6},{5,7},{6,4},{7,5},{8,10},{9,11},{10,... | collective-permute-start | bytes 294920 | tf_op jit(solution)/shard_map/ppermute | solution.py:1028
  137.4 2.8 %collective-permute-start.50 = (bf16[64,768]{1,0:T(8,128)(2,1)S(1)}, bf16[64,768]{1,0:T(8,128)(2,1)S(1)}, u32[]{:S(2)}, u32[]{:S(2)}) collective-permute-start(bf16[64,768]{1,0:T(8,128)(2,1)S(1)} %collective-permute-done.49.refs_2_), channel_id=1, source_target_pairs={{0,1},{1,0},{2,3},{3,2},{4,5},{5,4},{6,7},{7,6},{8,9},{9,8},{10,11... | collective-permute-start | bytes 294920 | tf_op jit(solution)/shard_map/ppermute | solution.py:1028
  137.4 2.8 %collective-permute-start.42 = (bf16[32,768]{1,0:T(8,128)(2,1)S(1)}, bf16[32,768]{1,0:T(8,128)(2,1)S(1)}, u32[]{:S(2)}, u32[]{:S(2)}) collective-permute-start(bf16[32,768]{1,0:T(8,128)(2,1)S(1)} %get-tuple-element.220), channel_id=1, source_target_pairs={{0,1},{1,0},{2,3},{3,2},{4,5},{5,4},{6,7},{7,6},{8,9},{9,8},{10,11... | collective-permute-start | bytes 147464 | tf_op jit(solution)/shard_map/ppermute | solution.py:1028
  137.9 2.3 %collective-permute-start.48 = (bf16[32,768]{1,0:T(8,128)(2,1)S(1)}, bf16[32,768]{1,0:T(8,128)(2,1)S(1)}, u32[]{:S(2)}, u32[]{:S(2)}) collective-permute-start(bf16[32,768]{1,0:T(8,128)(2,1)S(1)} %get-tuple-element.233), channel_id=1, source_target_pairs={{0,1},{1,0},{2,3},{3,2},{4,5},{5,4},{6,7},{7,6},{8,9},{9,8},{10,11... | collective-permute-start | bytes 147464 | tf_op jit(solution)/shard_map/ppermute | solution.py:1028
  (15 other events, 132.3 us)

commit v7 on v6

--- a/solution.py
+++ b/solution.py
@@ -377,17 +377,16 @@
 
 PAD_ID = 99
 PLAN = (
-    (9.0, ()), (0, (0,)), (0, (0,)), (0, (2,)), (7.0, (2,)), (0, ()), (0, ()), (0, (0,)), (0, (0,)),
-    (0, (4, 0)), (0, (2,)), (0, (3,)), (0, (8,)), (0, ()), (0, (12, 1)), (0, (5, 10)), (0, (7, 3)),
-    (60, ()), (0, ()), (0, (11, 16)), (0, ()), (36.0, (17,)), (0, ()), (1.2, (3, 16, 0)), (0, (23,)),
-    (0, (19, 0, 15)), (0, (5,)), (0, ()), (0, (23, 6, 9)), (48.0, ()), (0, (18,)), (0, (29, 15, 27)),
-    (0.002, (28, 30, 23)), (5.6, ()), (0.37, (22,)), (0, (34,)), (0.001, (19, 34, 13)), (0, (33, 25)),
-    (0.002, (19, 30)), (0, ()), (0.6, (36,)), (0, (9, 36)), (1.2, ()), (0, ()), (0.07, ()), (0, ()),
-    (0.27, ()), (0, (36, 44, 46)), (0.001, ()), (0, ()), (21.0, ()), (0, ()), (7.0, (34,)), (0, (47,)),
-    (0.002, ()), (0, (45, 47)), (2.1, ()), (0, ()), (0.0325, ()), (0, (43, 48)), (0.36, (23, 59)),
-    (0, (58,)), (0.105, (60,)), (0, (57,)), (0, (63,)), (0, (49,)), (2.1, (33,)), (0, (52,)), (2.1, ()),
-    (0, ()), (2.1, ()), (0.7, (61,)), (0, ()), (0, ()), (0, (57, 67)), (3, (66,)), (9.0, (70,)), (0, (70,)),
-    (0, (61,)), (0, (78, 77, 13)), (0.002, ()), (0.1, ()),
+    (9.0, ()), (0, (0,)), (0, ()), (0, (2, 0)), (21.0, ()), (0, ()), (0, ()), (0, ()), (0, (0,)), (0, ()),
+    (0, ()), (0, (8,)), (0, ()), (0, (1,)), (0, (5, 9, 11)), (0, (7, 3)), (0, ()), (0, (10, 15, 16)),
+    (0, ()), (36.0, (12,)), (0, ()), (2.4, (13,)), (0, (9,)), (0, (17,)), (0, (21,)), (0, (21,)), (0, ()),
+    (4.8, (11,)), (0, (27,)), (0, (27,)), (0.001, ()), (0.001, ()), (1.11, (20,)), (0, ()), (2.7, ()),
+    (0, ()), (0.002, (17, 28)), (0, ()), (0.6, ()), (0, (34,)), (0.6, ()), (0, ()), (0.07, ()), (0, ()),
+    (0.27, ()), (0, ()), (0.4, (44,)), (0, ()), (21.0, ()), (0, ()), (7.0, (32,)), (0, (45,)), (0.42, ()),
+    (0, (43, 45)), (1.05, ()), (0, ()), (0.0325, ()), (0, ()), (0.18, ()), (0, (56,)), (0.105, (58,)),
+    (0, ()), (0, ()), (0, (47,)), (2.1, ()), (0, ()), (2.1, ()), (0, ()), (2.1, ()), (0.35, (59,)), (0, ()),
+    (0, ()), (0, (55, 65)), (1.5, (64, 72)), (9.0, (68,)), (0, ()), (0, ()), (0, (70,)), (0.001, ()),
+    (30, ()),
 )
 STEPS = []
 
@@ -519,7 +518,7 @@
     rows[176:352, :] = cots.ready()[...]
 
 
-def join_pieces(own, near, far, near_far, w_out, w_down, pack, both, pack_f, up_f):
+def join_pieces(own, near, far, near_far, w_out, w_down, pack, both, wide, pack_f, up_f):
     place = here()[0]
     pack_f[96:112, :] = jnp.zeros((16, 768), F32)
     pieces = (
@@ -541,6 +540,8 @@
     pack[...] = pack_f[...].astype(BF16)
     both[0:96, :] = up_f[...].astype(BF16)
     both[96:192, :] = w_down[...]
+    wide[0:112, :] = pack[...]
+    wide[112:304, :] = both[...]
 
 
 def open_pack(*refs):
@@ -590,34 +591,27 @@
     return jnp.sum(jnp.where(down == across, line, 0.0), line.shape.index(count), keepdims=True)
 
 
-def norm_rows_in(
-    rows_0, rows_1, rows_2, rows_3, tail, cot_tail, ids,
-    unit, bias, tokens, cots, unit_low, rows_f,
+def attend(
+    rows_0, rows_1, rows_2, rows_3, tail, ids, w_qkv, gain_rows,
+    attended, projected, probs, tokens, unit_low, rows_f,
 ):
+    place_rows(rows_f, (rows_0, rows_1, rows_2, rows_3), tail, 0)
+    gain = gain_rows[0:1, :]
     slot = lax.broadcasted_iota(jnp.int32, (1, 16), 1)
     tail_ids = jnp.where(slot < 2 * SPECIAL, (slot >= SPECIAL).astype(jnp.int32), PAD_ID)
     for m in range(MICRO):
+        at = slice(m * 368, m * 368 + 368)
         row = jnp.concatenate([ids[b * 2 + m : b * 2 + m + 1, :] for b in range(4)] + [tail_ids], 1)
         row = row.astype(F32)
-        bias[m] = jnp.where(turned(row) == row, 0.0, MASKED)
-    blocks = (rows_0, rows_1, rows_2, rows_3)
-    place_rows(rows_f, blocks, cot_tail, 176)
-    for at in row_blocks(32):
-        cots[at, :] = rows_f[at, :].astype(BF16)
-    place_rows(rows_f, blocks, tail, 0)
-    for at in row_blocks(32):
-        rows = rows_f[at, :]
-        tokens[at, :] = rows.astype(BF16)
-        even = normalise(rows)[0]
-        unit[at, :] = even
-        unit_low[at, :] = even.astype(BF16)
-
-
-def attend(unit, bias, w_qkv, gain_rows, attended, projected, probs):
-    gain = gain_rows[0:1, :]
-    for m in range(MICRO):
-        at = slice(m * 368, m * 368 + 368)
-        qkv = mm((unit[at, :] * gain).astype(BF16), w_qkv[...])
+        bias = jnp.where(turned(row) == row, 0.0, MASKED)
+        normed = []
+        for block in row_blocks(16, at):
+            rows = rows_f[block, :]
+            tokens[block, :] = rows.astype(BF16)
+            unit = normalise(rows)[0]
+            unit_low[block, :] = unit.astype(BF16)
+            normed.append((unit * gain).astype(BF16))
+        qkv = mm(jnp.concatenate(normed, 0), w_qkv[...])
         qkv = jnp.concatenate([qkv[:, 0:192] * SCORE_SCALE, qkv[:, 192:576]], -1).astype(BF16)
         projected[at, :] = qkv
         heads = []
@@ -625,7 +619,7 @@
             q = qkv[:, h * 64 : h * 64 + 64]
             k = qkv[:, 192 + h * 64 : 192 + h * 64 + 64]
             v = qkv[:, 384 + h * 64 : 384 + h * 64 + 64]
-            scores = mm_nt(q, k) + bias[m]
+            scores = mm_nt(q, k) + bias
             weights = jnp.exp(scores - jnp.max(scores, -1, keepdims=True))
             weights = weights * (1.0 / jnp.sum(weights, -1, keepdims=True))
             weights = weights.astype(BF16)
@@ -635,7 +629,8 @@
 
 
 def order_out(
-    out_0, out_1, out_2, out_3, cots, gain_rows, ordered, mine, grad_mlp, out_f
+    out_0, out_1, out_2, out_3, rows_0, rows_1, rows_2, rows_3, cot_tail, gain_rows,
+    ordered, mine, grad_mlp, cots, out_f,
 ):
     place = here()[0]
     for k, part in enumerate((out_0, out_1, out_2, out_3)):
@@ -646,9 +641,12 @@
             out_f[pl.ds(at, 24), :] = rows[d * 24 : d * 24 + 24]
     ordered[...] = out_f[...].astype(BF16)
     mine[...] = out_f[pl.ds(pl.multiple_of(place * 192, 8), 192), :].astype(BF16)
+    place_rows(out_f, (rows_0, rows_1, rows_2, rows_3), cot_tail, 176)
     gain = gain_rows[3:4, :]
     for at in row_blocks(32):
-        grad_mlp[at, :] = (gain * cots[at, :].astype(F32)).astype(BF16)
+        rows = out_f[at, :]
+        cots[at, :] = rows.astype(BF16)
+        grad_mlp[at, :] = (gain * rows).astype(BF16)
 
 
 def branch_rows(
@@ -683,8 +681,9 @@
     _, _, _, z, y = here()
     for slot, chunk in enumerate(chunks):
         d = chunk_index(slot, z, y)
-        w_up[pl.ds(pl.multiple_of(d * 96, 96), 96), :] = chunk[0:96, :]
-        w_down[pl.ds(pl.multiple_of(d * 96, 96), 96), :] = chunk[96:192, :]
+        skip = chunk.shape[0] - 192
+        w_up[pl.ds(pl.multiple_of(d * 96, 96), 96), :] = chunk[skip : skip + 96, :]
+        w_down[pl.ds(pl.multiple_of(d * 96, 96), 96), :] = chunk[skip + 96 : skip + 192, :]
     for m in range(MICRO):
         at = slice(m * 368, m * 368 + 368)
         rows_f[at, :] = mm(normed[at, :], w_up[...])
@@ -1088,17 +1087,16 @@
     )
     came_far = send(far, "x", 1)
     came_near, came_near_far = send(near, "core", 1), send(came_far, "core", 1)
-    pack, both = call(
+    pack, both, wide = call(
         join_pieces,
-        [sds(112, 768), sds(192, 768)],
+        [sds(112, 768), sds(192, 768), sds(304, 768)],
         [own, came_near, came_far, came_near_far, w_out, w_down],
         [pltpu.VMEM((112, 768), F32), pltpu.VMEM((96, 768), F32)],
     )
     pack_2 = send(pack, "z", 2)
     pack_1 = send(pack, "z", 1)
-    pack_y0 = send(pack, "y", 1)
+    wide_y0 = send(wide, "y", 1)
     far_rows = send(rows, "x", 1)
-    both_y0 = send(both, "y", 1)
     pack_y1 = send(pack_1, "y", 1)
     pack_3 = send(pack_2, "z", 1)
     pack_y2 = send(pack_2, "y", 1)
@@ -1106,26 +1104,21 @@
     both_1 = send(both, "z", 1)
     near_rows = send(rows, "core", 1)
     row_parts = [rows, near_rows, far_rows, send(far_rows, "core", 1)]
-    unit, bias, tokens, cots, unit_low = call(
-        norm_rows_in,
-        keep(sds(736, 768, dtype=F32), sds(2, 368, 368, dtype=F32), *[sds(736, 768)] * 3),
-        [*row_parts, special, cot_special, image_ids.reshape(8, 88)],
-        [pltpu.VMEM((736, 768), F32)],
-    )
     pack_y3 = send(pack_3, "y", 1)
     both_y1 = send(both_1, "y", 1)
     both_3 = send(both_2, "z", 1)
     qkv_full, out_part, gain_rows = call(
         open_pack,
         [Keep(sds(768, 576)), sds(192, 768), Keep(sds(8, 768, dtype=F32))],
-        [pack, pack_1, pack_2, pack_3, pack_y0, pack_y1, pack_y2, pack_y3],
+        [pack, pack_1, pack_2, pack_3, wide_y0, pack_y1, pack_y2, pack_y3],
         [pltpu.VMEM((192, 768), F32), pltpu.VMEM((8, 16, 768), F32)],
     )
     far_out = send(out_part, "x", 1)
-    attended, projected, probs = call(
+    attended, projected, probs, tokens, unit_low = call(
         attend,
-        [sds(736, 192), *keep(sds(736, 576), sds(6, 368, 368))],
-        keep(unit, bias, qkv_full, gain_rows),
+        [sds(736, 192), *keep(sds(736, 576), sds(6, 368, 368), sds(736, 768), sds(736, 768))],
+        [*row_parts, special, image_ids.reshape(8, 88), *keep(qkv_full, gain_rows)],
+        [pltpu.VMEM((736, 768), F32)],
     )
     far_heads = send(attended, "x", 1)
     both_y2 = send(both_2, "y", 1)
@@ -1134,17 +1127,17 @@
         far_out, send(far_out, "core", 1),
     ]
     both_y3 = send(both_3, "y", 1)
-    out_full, out_mine, grad_mlp = call(
+    out_full, out_mine, grad_mlp, cots = call(
         order_out,
-        keep(sds(768, 768), sds(192, 768), sds(736, 768)),
-        [*out_parts, *keep(cots, gain_rows)],
+        keep(sds(768, 768), sds(192, 768), sds(736, 768), sds(736, 768)),
+        [*out_parts, *row_parts, cot_special, Keep(gain_rows)],
         [pltpu.VMEM((768, 768), F32)],
     )
     heads = [
         attended, send(attended, "core", 1),
         far_heads, send(far_heads, "core", 1),
     ]
-    both_chunks = [both, both_1, both_2, both_3, both_y0, both_y1, both_y2, both_y3]
+    both_chunks = [both, both_1, both_2, both_3, wide_y0, both_y1, both_y2, both_y3]
     normed_mlp, branch, own_rows = call(
         branch_rows,
         keep(sds(736, 768), sds(736, 768), sds(208, 768, dtype=F32)),

time: 143 us -> 137 us (0.958)
  waiting for transfers between devices: 58.2 us -> 47.3 us
  starting transfers between devices: 48.4 us -> 53.7 us
    ppermute x51 -> x50, waiting for transfers between devices: 58.2 us -> 47.3 us  [send(): STEPS.append(lax.ppermute(rows, ('dp', 'blk'), pairs))]
    ppermute x51 -> x50, starting transfers between devices: 48.4 us -> 53.7 us  [send(): STEPS.append(lax.ppermute(rows, ('dp', 'blk'), pairs))]
    pallas_call x31 -> x30, Pallas kernels: 34 us -> 34.7 us  [call(): pl.pallas_call(body, out_shape=tuple((pltpu.VMEM(v.value.shape, v.value.d...]
  transfers between devices with their start and end apart: 51 -> 50, of which waited for: 25 -> 20; matrix products, arithmetic and copies ran while one was open for 0% -> 0% of each run, Pallas kernels for 19% -> 21%
where the time goes in v7:
time: 137 us
  starting transfers between devices  53.7 us (39%)
  waiting for transfers between devices  47.3 us (35%)
  Pallas kernels  34.7 us (25%)
    ppermute x50, starting transfers between devices, send(): STEPS.append(lax.ppermute(rows, ('dp', 'blk'), pairs))  53.7 us
    ppermute x50, waiting for transfers between devices, send(): STEPS.append(lax.ppermute(rows, ('dp', 'blk'), pairs))  47.3 us
    pallas_call x30, Pallas kernels, call(): pl.pallas_call(body, out_shape=tuple((pltpu.VMEM(v.value.shape, v.value.d...  34.7 us
  transfers between devices with their start and end apart: 50, of which 20 were waited for; matrix products, arithmetic and copies ran while one was open for 0% of the time, Pallas kernels for 21%

profile of v7, /device:TPU:0, one launch (start us, length us, event | category | flops | bytes accessed | tf_op | source)
XLA Modules:
  0.0 136.9 jit_solution(2219171443850231153)
XLA Ops:
  0.7 1.3 pick_pieces.1
  2.0 3.0 %collective-permute-start.1 = (bf16[96,768]{1,0:T(8,128)(2,1)S(1)}, bf16[96,768]{1,0:T(8,128)(2,1)S(1)}, u32[]{:S(2)}, u32[]{:S(2)}) collective-permute-start(bf16[96,768]{1,0:T(8,128)(2,1)S(1)} %get-tuple-element.114), channel_id=1, source_target_pairs={{0,2},{1,3},{2,0},{3,1},{4,6},{5,7},{6,4},{7,5},{8,10},{9,11},{10,... | collective-permute-start | bytes 442376 | tf_op jit(solution)/shard_map/ppermute | solution.py:1027
  5.0 1.3 collective-permute-done.refs_1_
  6.2 2.6 %collective-permute-done.1.refs_2_ = bf16[96,768]{1,0:T(8,128)(2,1)S(1)} collective-permute-done((bf16[96,768]{1,0:T(8,128)(2,1)S(1)}, bf16[96,768]{1,0:T(8,128)(2,1)S(1)}, u32[]{:S(2)}, u32[]{:S(2)}) %collective-permute-start.1) | collective-permute-done | bytes 147488 | tf_op jit(solution)/shard_map/ppermute | solution.py:1027
  8.8 1.7 %collective-permute-start.6 = (bf16[352,768]{1,0:T(8,128)(2,1)S(1)}, bf16[352,768]{1,0:T(8,128)(2,1)}, u32[]{:S(2)}, u32[]{:S(2)}) collective-permute-start(bf16[352,768]{1,0:T(8,128)(2,1)S(1)} %get-tuple-element.119.refs_0_.refs_4_), channel_id=1, source_target_pairs={{0,2},{1,3},{2,0},{3,1},{4,6},{5,7},{6,4},{7,5},{8,10},{9,11},{10,... | collective-permute-start | bytes 1622024 | tf_op jit(solution)/shard_map/ppermute | solution.py:1027
  10.7 2.7 %collective-permute-start.3 = (bf16[112,768]{1,0:T(8,128)(2,1)S(1)}, bf16[112,768]{1,0:T(8,128)(2,1)S(1)}, u32[]{:S(2)}, u32[]{:S(2)}) collective-permute-start(bf16[112,768]{1,0:T(8,128)(2,1)S(1)} %get-tuple-element.116.refs_0_), channel_id=1, source_target_pairs={{0,16},{1,17},{2,18},{3,19},{4,20},{5,21},{6,22},{7,23},{8,24},{9,... | collective-permute-start | bytes 516104 | tf_op jit(solution)/shard_map/ppermute | solution.py:1027
  13.4 1.5 %collective-permute-start.9 = (bf16[304,768]{1,0:T(8,128)(2,1)S(1)}, bf16[304,768]{1,0:T(8,128)(2,1)S(1)}, u32[]{:S(2)}, u32[]{:S(2)}) collective-permute-start(bf16[304,768]{1,0:T(8,128)(2,1)S(1)} %get-tuple-element.120), channel_id=1, source_target_pairs={{0,4},{1,5},{2,6},{3,7},{4,0},{5,1},{6,2},{7,3},{8,12},{9,13},{10,... | collective-permute-start | bytes 1400840 | tf_op jit(solution)/shard_map/ppermute | solution.py:1027
  14.9 1.6 %collective-permute-start.4 = (bf16[112,768]{1,0:T(8,128)(2,1)S(1)}, bf16[112,768]{1,0:T(8,128)(2,1)S(1)}, u32[]{:S(2)}, u32[]{:S(2)}) collective-permute-start(bf16[112,768]{1,0:T(8,128)(2,1)S(1)} %get-tuple-element.116.refs_0_), channel_id=1, source_target_pairs={{0,8},{1,9},{2,10},{3,11},{4,12},{5,13},{6,14},{7,15},{8,0},{9,1},... | collective-permute-start | bytes 516104 | tf_op jit(solution)/shard_map/ppermute | solution.py:1027
  16.5 5.5 %collective-permute-done.3.refs_2_ = bf16[112,768]{1,0:T(8,128)(2,1)S(1)} collective-permute-done((bf16[112,768]{1,0:T(8,128)(2,1)S(1)}, bf16[112,768]{1,0:T(8,128)(2,1)S(1)}, u32[]{:S(2)}, u32[]{:S(2)}) %collective-permute-start.3) | collective-permute-done | bytes 172064 | tf_op jit(solution)/shard_map/ppermute | solution.py:1027
  22.6 3.4 %collective-permute-start.13 = (bf16[192,768]{1,0:T(8,128)(2,1)S(1)}, bf16[192,768]{1,0:T(8,128)(2,1)S(1)}, u32[]{:S(2)}, u32[]{:S(2)}) collective-permute-start(bf16[192,768]{1,0:T(8,128)(2,1)S(1)} %get-tuple-element.125.refs_1_), channel_id=1, source_target_pairs={{0,16},{1,17},{2,18},{3,19},{4,20},{5,21},{6,22},{7,23},{8,24},{9,... | collective-permute-start | bytes 884744 | tf_op jit(solution)/shard_map/ppermute | solution.py:1027
  26.0 1.4 %collective-permute-start.5 = (bf16[112,768]{1,0:T(8,128)(2,1)S(1)}, bf16[112,768]{1,0:T(8,128)(2,1)S(1)}, u32[]{:S(2)}, u32[]{:S(2)}) collective-permute-start(bf16[112,768]{1,0:T(8,128)(2,1)S(1)} %collective-permute-done.4.refs_1_), channel_id=1, source_target_pairs={{0,4},{1,5},{2,6},{3,7},{4,0},{5,1},{6,2},{7,3},{8,12},{9,13},{10,... | collective-permute-start | bytes 516104 | tf_op jit(solution)/shard_map/ppermute | solution.py:1027
  28.1 3.0 %collective-permute-done.11.refs_3_ = bf16[112,768]{1,0:T(8,128)(2,1)S(1)} collective-permute-done((bf16[112,768]{1,0:T(8,128)(2,1)S(1)}, bf16[112,768]{1,0:T(8,128)(2,1)S(1)}, u32[]{:S(2)}, u32[]{:S(2)}) %collective-permute-start.11) | collective-permute-done | bytes 172064 | tf_op jit(solution)/shard_map/ppermute | solution.py:1027
  31.1 1.5 %collective-permute-start.12 = (bf16[112,768]{1,0:T(8,128)(2,1)S(1)}, bf16[112,768]{1,0:T(8,128)(2,1)S(1)}, u32[]{:S(2)}, u32[]{:S(2)}) collective-permute-start(bf16[112,768]{1,0:T(8,128)(2,1)S(1)} %collective-permute-done.11.refs_3_), channel_id=1, source_target_pairs={{0,4},{1,5},{2,6},{3,7},{4,0},{5,1},{6,2},{7,3},{8,12},{9,13},{10,... | collective-permute-start | bytes 516104 | tf_op jit(solution)/shard_map/ppermute | solution.py:1027
  33.4 3.7 %collective-permute-done.7.refs_6_.refs_10_ = bf16[112,768]{1,0:T(8,128)(2,1)S(1)} collective-permute-done((bf16[112,768]{1,0:T(8,128)(2,1)S(1)}, bf16[112,768]{1,0:T(8,128)(2,1)S(1)}, u32[]{:S(2)}, u32[]{:S(2)}) %collective-permute-start.7) | collective-permute-done | bytes 172064 | tf_op jit(solution)/shard_map/ppermute | solution.py:1027
  37.6 1.8 %collective-permute-done.13.refs_8_.refs_3_ = bf16[192,768]{1,0:T(8,128)(2,1)S(1)} collective-permute-done((bf16[192,768]{1,0:T(8,128)(2,1)S(1)}, bf16[192,768]{1,0:T(8,128)(2,1)S(1)}, u32[]{:S(2)}, u32[]{:S(2)}) %collective-permute-start.13) | collective-permute-done | bytes 294944 | tf_op jit(solution)/shard_map/ppermute | solution.py:1027
  39.7 1.3 collective-permute-start.16
  42.4 1.5 %collective-permute-start.22 = (bf16[192,768]{1,0:T(8,128)(2,1)S(1)}, bf16[192,768]{1,0:T(8,128)(2,1)S(1)}, u32[]{:S(2)}, u32[]{:S(2)}) collective-permute-start(bf16[192,768]{1,0:T(8,128)(2,1)S(1)} %collective-permute-done.14.refs_8_.refs_2_), channel_id=1, source_target_pairs={{0,4},{1,5},{2,6},{3,7},{4,0},{5,1},{6,2},{7,3},{8,12},{9,13},{10,... | collective-permute-start | bytes 884744 | tf_op jit(solution)/shard_map/ppermute | solution.py:1027
  43.9 5.3 %attend.1 = (bf16[736,192]{1,0:T(8,128)(2,1)S(1)}, bf16[736,576]{1,0:T(8,128)(2,1)S(1)}, bf16[6,368,368]{2,1,0:T(8,128)(2,1)S(1)}, bf16[736,768]{1,0:T(8,128)(2,1)S(1)}, bf16[736,768]{1,0:T(8,128)(2,1)S(1)}) custom-call(bf16[352,768]{1,0:T(8,128)(2,1)S(1)} %get-tuple-element.119.refs_0_.refs_4_, bf16[352,768]{1,0:T(8,128)(2,1)} %collective-permute-done.8.refs_1_.refs_5_, ...), custom_call_target="tpu_custom_call" | custom-call | flops 2400000000 | tf_op jit(solution)/shard_map/attend/pallas_call | solution.py:474
  50.4 1.6 %collective-permute-start.19 = (bf16[736,192]{1,0:T(8,128)(2,1)S(1)}, bf16[736,192]{1,0:T(8,128)(2,1)S(1)}, u32[]{:S(2)}, u32[]{:S(2)}) collective-permute-start(bf16[736,192]{1,0:T(8,128)(2,1)S(1)} %get-tuple-element.132.refs_0_.refs_3_), channel_id=1, source_target_pairs={{0,2},{1,3},{2,0},{3,1},{4,6},{5,7},{6,4},{7,5},{8,10},{9,11},{10,... | collective-permute-start | bytes 847880 | tf_op jit(solution)/shard_map/ppermute | solution.py:1027
  51.9 1.4 %collective-permute-start.23 = (bf16[192,768]{1,0:T(8,128)(2,1)S(1)}, bf16[192,768]{1,0:T(8,128)(2,1)S(1)}, u32[]{:S(2)}, u32[]{:S(2)}) collective-permute-start(bf16[192,768]{1,0:T(8,128)(2,1)S(1)} %collective-permute-done.13.refs_8_.refs_3_), channel_id=1, source_target_pairs={{0,4},{1,5},{2,6},{3,7},{4,0},{5,1},{6,2},{7,3},{8,12},{9,13},{10,... | collective-permute-start | bytes 884744 | tf_op jit(solution)/shard_map/ppermute | solution.py:1027
  53.4 2.0 %order_out.1 = (bf16[768,768]{1,0:T(8,128)(2,1)S(1)}, bf16[192,768]{1,0:T(8,128)(2,1)S(1)}, bf16[736,768]{1,0:T(8,128)(2,1)S(1)}, bf16[736,768]{1,0:T(8,128)(2,1)S(1)}) custom-call(bf16[192,768]{1,0:T(8,128)(2,1)S(1)} %get-tuple-element.128.refs_0_, bf16[192,768]{1,0:T(8,128)(2,1)S(1)} %collective-permute-done.15.refs_1_, ...), custom_call_target="tpu_custom_call" | custom-call | flops 4800000000 | tf_op jit(solution)/shard_map/order_out/pallas_call | solution.py:474
  55.4 5.4 %collective-permute-done.19.refs_2_.refs_5_ = bf16[736,192]{1,0:T(8,128)(2,1)S(1)} collective-permute-done((bf16[736,192]{1,0:T(8,128)(2,1)S(1)}, bf16[736,192]{1,0:T(8,128)(2,1)S(1)}, u32[]{:S(2)}, u32[]{:S(2)}) %collective-permute-start.19) | collective-permute-done | bytes 282656 | tf_op jit(solution)/shard_map/ppermute | solution.py:1027
  61.3 1.2 collective-permute-done.18.refs_1_.refs_4_.refs_3_
  63.0 2.1 %branch_rows.1 = (bf16[736,768]{1,0:T(8,128)(2,1)S(1)}, bf16[736,768]{1,0:T(8,128)(2,1)S(1)}, f32[208,768]{1,0:T(8,128)S(1)}) custom-call(bf16[736,192]{1,0:T(8,128)(2,1)S(1)} %get-tuple-element.132.refs_0_.refs_3_, bf16[736,192]{1,0:T(8,128)(2,1)S(1)} %collective-permute-done.18.refs_1_.refs_4_.refs_3_, ...), custom_call_target="tpu_custom_call" | custom-call | flops 1000000 | tf_op jit(solution)/shard_map/branch_rows/pallas_call | solution.py:474
  65.2 1.7 %raise_rows.1 = (bf16[736,768]{1,0:T(8,128)(2,1)S(1)}, f32[736,768]{1,0:T(8,128)S(1)}, bf16[768,768]{1,0:T(8,128)(2,1)S(1)}, bf16[768,768]{1,0:T(8,128)(2,1)S(1)}) custom-call(bf16[736,768]{1,0:T(8,128)(2,1)S(1)} %get-tuple-element.135.refs_0_, bf16[192,768]{1,0:T(8,128)(2,1)S(1)} %get-tuple-element.125.refs_1_, ...), custom_call_target="tpu_custom_call" | custom-call | flops 1000000 | tf_op jit(solution)/shard_map/raise_rows/pallas_call | solution.py:474
  66.9 2.6 %lower_rows.1 = (bf16[368,768]{1,0:T(8,128)(2,1)S(1)}, f32[368,768]{1,0:T(8,128)S(1)}, bf16[736,768]{1,0:T(8,128)(2,1)S(1)}) custom-call(f32[736,768]{1,0:T(8,128)S(1)} %get-tuple-element.145.refs_0_, bf16[736,768]{1,0:T(8,128)(2,1)S(1)} %get-tuple-element.146.refs_1_, bf16[768,768]{1,0:T(8,128)(2,1)S(1)} %get-tuple-element.147.refs_2_, ...), custom_call_target="tpu_custom_call" | custom-call | flops 1110000000 | tf_op jit(solution)/shard_map/lower_rows/pallas_call | solution.py:474
  69.7 1.3 down_grads.1
  71.9 1.4 %collective-permute-start.27 = (bf16[368,768]{1,0:T(8,128)(2,1)S(1)}, bf16[368,768]{1,0:T(8,128)(2,1)S(1)}, u32[]{:S(2)}, u32[]{:S(2)}) collective-permute-start(bf16[368,768]{1,0:T(8,128)(2,1)S(1)} %add_rows.1.refs_0_), channel_id=1, source_target_pairs={{0,2},{1,3},{2,0},{3,1},{4,6},{5,7},{6,4},{7,5},{8,10},{9,11},{10,... | collective-permute-start | bytes 1695752 | tf_op jit(solution)/shard_map/ppermute | solution.py:1027
  73.3 1.4 %up_grads.1 = (bf16[4,96,768]{2,1,0:T(8,128)(2,1)S(1)}, f32[4,96,768]{2,1,0:T(8,128)S(1)}) custom-call(bf16[736,768]{1,0:T(8,128)(2,1)S(1)} %get-tuple-element.135.refs_0_, bf16[736,768]{1,0:T(8,128)(2,1)S(1)} %get-tuple-element.193.refs_1_), custom_call_target="tpu_custom_call" | custom-call | flops 600000000 | tf_op jit(solution)/shard_map/up_grads/pallas_call | solution.py:474
  74.7 1.5 %collective-permute-start.43 = (bf16[4,96,768]{2,1,0:T(8,128)(2,1)S(1)}, bf16[4,96,768]{2,1,0:T(8,128)(2,1)S(1)}, u32[]{:S(2)}, u32[]{:S(2)}) collective-permute-start(bf16[4,96,768]{2,1,0:T(8,128)(2,1)S(1)} %get-tuple-element.196), channel_id=1, source_target_pairs={{0,4},{1,5},{2,6},{3,7},{4,0},{5,1},{6,2},{7,3},{8,12},{9,13},{10,... | collective-permute-start | bytes 1769480 | tf_op jit(solution)/shard_map/ppermute | solution.py:1027
  76.2 1.7 %mlp_rows.1 = (bf16[416,768]{1,0:T(8,128)(2,1)S(1)}, f32[416,768]{1,0:T(8,128)S(1)}, f32[8,768]{1,0:T(8,128)S(1)}, bf16[736,192]{1,0:T(8,128)(2,1)S(1)}) custom-call(bf16[736,768]{1,0:T(8,128)(2,1)S(1)} %get-tuple-element.138.refs_0_, bf16[768,768]{1,0:T(8,128)(2,1)S(1)} %get-tuple-element.139.refs_1_.refs_3_, ...), custom_call_target="tpu_custom_call" | custom-call | flops 600000000 | tf_op jit(solution)/shard_map/mlp_rows/pallas_call | solution.py:474
  78.0 8.7 %collective-permute-done.34.refs_1_ = bf16[4,96,768]{2,1,0:T(8,128)(2,1)S(1)} collective-permute-done((bf16[4,96,768]{2,1,0:T(8,128)(2,1)S(1)}, bf16[4,96,768]{2,1,0:T(8,128)(2,1)S(1)}, u32[]{:S(2)}, u32[]{:S(2)}) %collective-permute-start.34) | collective-permute-done | bytes 589856 | tf_op jit(solution)/shard_map/ppermute | solution.py:1027
  86.8 4.7 %collective-permute-start.35 = (bf16[2,96,768]{2,1,0:T(8,128)(2,1)S(1)}, bf16[2,96,768]{2,1,0:T(8,128)(2,1)S(1)}, u32[]{:S(2)}, u32[]{:S(2)}) collective-permute-start(bf16[2,96,768]{2,1,0:T(8,128)(2,1)S(1)} %get-tuple-element.179), channel_id=1, source_target_pairs={{0,16},{1,17},{2,18},{3,19},{4,20},{5,21},{6,22},{7,23},{8,24},{9,... | collective-permute-start | bytes 884744 | tf_op jit(solution)/shard_map/ppermute | solution.py:1027
  91.8 1.8 %collective-permute-start.44 = (bf16[2,96,768]{2,1,0:T(8,128)(2,1)S(1)}, bf16[2,96,768]{2,1,0:T(8,128)(2,1)S(1)}, u32[]{:S(2)}, u32[]{:S(2)}) collective-permute-start(bf16[2,96,768]{2,1,0:T(8,128)(2,1)S(1)} %get-tuple-element.198), channel_id=1, source_target_pairs={{0,8},{1,9},{2,10},{3,11},{4,12},{5,13},{6,14},{7,15},{8,0},{9,1},... | collective-permute-start | bytes 884744 | tf_op jit(solution)/shard_map/ppermute | solution.py:1027
  93.6 3.9 %branch_back.1 = (f32[208,768]{1,0:T(8,128)S(1)}, bf16[736,192]{1,0:T(8,128)(2,1)S(1)}, bf16[736,192]{1,0:T(8,128)(2,1)S(1)}, bf16[4,112,384]{2,1,0:T(8,128)(2,1)S(1)}, f32[4,112,384]{2,1,0:T(8,128)S(1)}) custom-call(bf16[368,768]{1,0:T(8,128)(2,1)S(1)} %add_pair.1.refs_0_.refs_11_, bf16[368,768]{1,0:T(8,128)(2,1)S(1)} %collective-permute-done.28.refs_1_, ...), custom_call_target="tpu_custom_call" | custom-call | flops 400000000 | tf_op jit(solution)/shard_map/branch_back/pallas_call | solution.py:474
  98.6 3.8 %score_back.1 = (bf16[736,384]{1,0:T(8,128)(2,1)S(1)}, bf16[4,96,384]{2,1,0:T(8,128)(2,1)S(1)}, f32[4,96,384]{2,1,0:T(8,128)S(1)}) custom-call(bf16[6,368,368]{2,1,0:T(8,128)(2,1)S(1)} %get-tuple-element.143.refs_7_.refs_0_, bf16[736,576]{1,0:T(8,128)(2,1)S(1)} %get-tuple-element.144.refs_1_, bf16[736,192]{1,0:T(8,128)(2,1)S(1)} %get-tuple-element.155.refs_2_, ...), custom_call_target="tpu_custom_call" | custom-call | flops 420000000 | tf_op jit(solution)/shard_map/score_back/pallas_call | solution.py:474
  102.5 1.3 project_back.1
  106.2 1.7 %collective-permute-start.30 = (bf16[416,768]{1,0:T(8,128)(2,1)S(1)}, bf16[416,768]{1,0:T(8,128)(2,1)S(1)}, u32[]{:S(2)}, u32[]{:S(2)}) collective-permute-start(bf16[416,768]{1,0:T(8,128)(2,1)S(1)} %get-tuple-element.162), channel_id=1, source_target_pairs={{0,2},{1,3},{2,0},{3,1},{4,6},{5,7},{6,4},{7,5},{8,10},{9,11},{10,... | collective-permute-start | bytes 1916936 | tf_op jit(solution)/shard_map/ppermute | solution.py:1027
  108.5 1.7 %collective-permute-start.32 = (bf16[2,112,384]{2,1,0:T(8,128)(2,1)S(1)}, bf16[2,112,384]{2,1,0:T(8,128)(2,1)S(1)}, u32[]{:S(2)}, u32[]{:S(2)}) collective-permute-start(bf16[2,112,384]{2,1,0:T(8,128)(2,1)S(1)} %get-tuple-element.172), channel_id=1, source_target_pairs={{0,8},{1,9},{2,10},{3,11},{4,12},{5,13},{6,14},{7,15},{8,0},{9,1},... | collective-permute-start | bytes 516104 | tf_op jit(solution)/shard_map/ppermute | solution.py:1027
  110.3 2.0 %collective-permute-start.45 = (bf16[96,768]{1,0:T(8,128)(2,1)S(1)}, bf16[96,768]{1,0:T(8,128)(2,1)S(1)}, u32[]{:S(2)}, u32[]{:S(2)}) collective-permute-start(bf16[96,768]{1,0:T(8,128)(2,1)S(1)} %get-tuple-element.200), channel_id=1, source_target_pairs={{0,16},{1,17},{2,18},{3,19},{4,20},{5,21},{6,22},{7,23},{8,24},{9,... | collective-permute-start | bytes 442376 | tf_op jit(solution)/shard_map/ppermute | solution.py:1027
  113.0 3.5 %collective-permute-done.32.refs_1_ = bf16[2,112,384]{2,1,0:T(8,128)(2,1)S(1)} collective-permute-done((bf16[2,112,384]{2,1,0:T(8,128)(2,1)S(1)}, bf16[2,112,384]{2,1,0:T(8,128)(2,1)S(1)}, u32[]{:S(2)}, u32[]{:S(2)}) %collective-permute-start.32) | collective-permute-done | bytes 172064 | tf_op jit(solution)/shard_map/ppermute | solution.py:1027
  116.5 2.0 %collective-permute-start.33 = (bf16[112,384]{1,0:T(8,128)(2,1)S(1)}, bf16[112,384]{1,0:T(8,128)(2,1)S(1)}, u32[]{:S(2)}, u32[]{:S(2)}) collective-permute-start(bf16[112,384]{1,0:T(8,128)(2,1)S(1)} %get-tuple-element.174), channel_id=1, source_target_pairs={{0,16},{1,17},{2,18},{3,19},{4,20},{5,21},{6,22},{7,23},{8,24},{9,... | collective-permute-start | bytes 258056 | tf_op jit(solution)/shard_map/ppermute | solution.py:1027
  118.5 2.0 %collective-permute-start.39 = (bf16[96,384]{1,0:T(8,128)(2,1)S(1)}, bf16[96,384]{1,0:T(8,128)(2,1)S(1)}, u32[]{:S(2)}, u32[]{:S(2)}) collective-permute-start(bf16[96,384]{1,0:T(8,128)(2,1)S(1)} %get-tuple-element.185), channel_id=1, source_target_pairs={{0,24},{1,25},{2,26},{3,27},{4,28},{5,29},{6,30},{7,31},{8,16},{9,... | collective-permute-start | bytes 221192 | tf_op jit(solution)/shard_map/ppermute | solution.py:1027
  121.2 1.8 %collective-permute-start.38 = (bf16[96,384]{1,0:T(8,128)(2,1)S(1)}, bf16[96,384]{1,0:T(8,128)(2,1)S(1)}, u32[]{:S(2)}, u32[]{:S(2)}) collective-permute-start(bf16[96,384]{1,0:T(8,128)(2,1)S(1)} %get-tuple-element.183), channel_id=1, source_target_pairs={{0,16},{1,17},{2,18},{3,19},{4,20},{5,21},{6,22},{7,23},{8,24},{9,... | collective-permute-start | bytes 221192 | tf_op jit(solution)/shard_map/ppermute | solution.py:1027
  124.4 1.4 %collective-permute-done.33.refs_1_ = bf16[112,384]{1,0:T(8,128)(2,1)S(1)} collective-permute-done((bf16[112,384]{1,0:T(8,128)(2,1)S(1)}, bf16[112,384]{1,0:T(8,128)(2,1)S(1)}, u32[]{:S(2)}, u32[]{:S(2)}) %collective-permute-start.33) | collective-permute-done | bytes 86048 | tf_op jit(solution)/shard_map/ppermute | solution.py:1027
  126.0 3.3 %collective-permute-done.38.refs_4_ = bf16[96,384]{1,0:T(8,128)(2,1)S(1)} collective-permute-done((bf16[96,384]{1,0:T(8,128)(2,1)S(1)}, bf16[96,384]{1,0:T(8,128)(2,1)S(1)}, u32[]{:S(2)}, u32[]{:S(2)}) %collective-permute-start.38) | collective-permute-done | bytes 73760 | tf_op jit(solution)/shard_map/ppermute | solution.py:1027
  131.7 1.4 %finish_rows.1 = (bf16[176,768]{1,0:T(8,128)(2,1)}, bf16[20,768]{1,0:T(8,128)(2,1)}, f32[176,768]{1,0:T(8,128)}, f32[20,768]{1,0:T(8,128)}) custom-call(f32[416,768]{1,0:T(8,128)S(1)} %get-tuple-element.160.refs_0_.refs_2_, bf16[416,768]{1,0:T(8,128)(2,1)S(1)} %collective-permute-done.30.refs_1_.refs_2_, f32[208,768]{1,0:T(8,128)S(1)} %get-tuple-element.163.refs_2_, ...), custom_call_target="tpu_custom_call" | custom-call | flops 1000000 | tf_op jit(solution)/shard_map/finish_rows/pallas_call | solution.py:474
  133.1 1.5 %collective-permute-done.42.refs_2_ = bf16[64,768]{1,0:T(8,128)(2,1)S(1)} collective-permute-done((bf16[64,768]{1,0:T(8,128)(2,1)S(1)}, bf16[64,768]{1,0:T(8,128)(2,1)S(1)}, u32[]{:S(2)}, u32[]{:S(2)}) %collective-permute-start.42) | collective-permute-done | bytes 98336 | tf_op jit(solution)/shard_map/ppermute | solution.py:1027
  (107 shorter events, 20.0 us)
Async XLA Ops:
  2.0 6.9 %collective-permute-start.1 = (bf16[96,768]{1,0:T(8,128)(2,1)S(1)}, bf16[96,768]{1,0:T(8,128)(2,1)S(1)}, u32[]{:S(2)}, u32[]{:S(2)}) collective-permute-start(bf16[96,768]{1,0:T(8,128)(2,1)S(1)} %get-tuple-element.114), channel_id=1, source_target_pairs={{0,2},{1,3},{2,0},{3,1},{4,6},{5,7},{6,4},{7,5},{8,10},{9,11},{10,... | collective-permute-start | bytes 442376 | tf_op jit(solution)/shard_map/ppermute | solution.py:1027
  8.8 1.7 %collective-permute-start.2 = (bf16[96,768]{1,0:T(8,128)(2,1)S(1)}, bf16[96,768]{1,0:T(8,128)(2,1)S(1)}, u32[]{:S(2)}, u32[]{:S(2)}) collective-permute-start(bf16[96,768]{1,0:T(8,128)(2,1)S(1)} %collective-permute-done.1.refs_2_), channel_id=1, source_target_pairs={{0,1},{1,0},{2,3},{3,2},{4,5},{5,4},{6,7},{7,6},{8,9},{9,8},{10,11... | collective-permute-start | bytes 442376 | tf_op jit(solution)/shard_map/ppermute | solution.py:1027
  8.8 18.6 %collective-permute-start.6 = (bf16[352,768]{1,0:T(8,128)(2,1)S(1)}, bf16[352,768]{1,0:T(8,128)(2,1)}, u32[]{:S(2)}, u32[]{:S(2)}) collective-permute-start(bf16[352,768]{1,0:T(8,128)(2,1)S(1)} %get-tuple-element.119.refs_0_.refs_4_), channel_id=1, source_target_pairs={{0,2},{1,3},{2,0},{3,1},{4,6},{5,7},{6,4},{7,5},{8,10},{9,11},{10,... | collective-permute-start | bytes 1622024 | tf_op jit(solution)/shard_map/ppermute | solution.py:1027
  10.7 11.3 %collective-permute-start.3 = (bf16[112,768]{1,0:T(8,128)(2,1)S(1)}, bf16[112,768]{1,0:T(8,128)(2,1)S(1)}, u32[]{:S(2)}, u32[]{:S(2)}) collective-permute-start(bf16[112,768]{1,0:T(8,128)(2,1)S(1)} %get-tuple-element.116.refs_0_), channel_id=1, source_target_pairs={{0,16},{1,17},{2,18},{3,19},{4,20},{5,21},{6,22},{7,23},{8,24},{9,... | collective-permute-start | bytes 516104 | tf_op jit(solution)/shard_map/ppermute | solution.py:1027
  13.4 23.7 %collective-permute-start.9 = (bf16[304,768]{1,0:T(8,128)(2,1)S(1)}, bf16[304,768]{1,0:T(8,128)(2,1)S(1)}, u32[]{:S(2)}, u32[]{:S(2)}) collective-permute-start(bf16[304,768]{1,0:T(8,128)(2,1)S(1)} %get-tuple-element.120), channel_id=1, source_target_pairs={{0,4},{1,5},{2,6},{3,7},{4,0},{5,1},{6,2},{7,3},{8,12},{9,13},{10,... | collective-permute-start | bytes 1400840 | tf_op jit(solution)/shard_map/ppermute | solution.py:1027
  14.9 11.1 %collective-permute-start.4 = (bf16[112,768]{1,0:T(8,128)(2,1)S(1)}, bf16[112,768]{1,0:T(8,128)(2,1)S(1)}, u32[]{:S(2)}, u32[]{:S(2)}) collective-permute-start(bf16[112,768]{1,0:T(8,128)(2,1)S(1)} %get-tuple-element.116.refs_0_), channel_id=1, source_target_pairs={{0,8},{1,9},{2,10},{3,11},{4,12},{5,13},{6,14},{7,15},{8,0},{9,1},... | collective-permute-start | bytes 516104 | tf_op jit(solution)/shard_map/ppermute | solution.py:1027
  22.0 9.1 %collective-permute-start.11 = (bf16[112,768]{1,0:T(8,128)(2,1)S(1)}, bf16[112,768]{1,0:T(8,128)(2,1)S(1)}, u32[]{:S(2)}, u32[]{:S(2)}) collective-permute-start(bf16[112,768]{1,0:T(8,128)(2,1)S(1)} %collective-permute-done.3.refs_2_), channel_id=1, source_target_pairs={{0,8},{1,9},{2,10},{3,11},{4,12},{5,13},{6,14},{7,15},{8,0},{9,1},... | collective-permute-start | bytes 516104 | tf_op jit(solution)/shard_map/ppermute | solution.py:1027
  22.6 16.8 %collective-permute-start.13 = (bf16[192,768]{1,0:T(8,128)(2,1)S(1)}, bf16[192,768]{1,0:T(8,128)(2,1)S(1)}, u32[]{:S(2)}, u32[]{:S(2)}) collective-permute-start(bf16[192,768]{1,0:T(8,128)(2,1)S(1)} %get-tuple-element.125.refs_1_), channel_id=1, source_target_pairs={{0,16},{1,17},{2,18},{3,19},{4,20},{5,21},{6,22},{7,23},{8,24},{9,... | collective-permute-start | bytes 884744 | tf_op jit(solution)/shard_map/ppermute | solution.py:1027
  26.0 7.3 %collective-permute-start.5 = (bf16[112,768]{1,0:T(8,128)(2,1)S(1)}, bf16[112,768]{1,0:T(8,128)(2,1)S(1)}, u32[]{:S(2)}, u32[]{:S(2)}) collective-permute-start(bf16[112,768]{1,0:T(8,128)(2,1)S(1)} %collective-permute-done.4.refs_1_), channel_id=1, source_target_pairs={{0,4},{1,5},{2,6},{3,7},{4,0},{5,1},{6,2},{7,3},{8,12},{9,13},{10,... | collective-permute-start | bytes 516104 | tf_op jit(solution)/shard_map/ppermute | solution.py:1027
  27.5 9.6 %collective-permute-start.7 = (bf16[112,768]{1,0:T(8,128)(2,1)S(1)}, bf16[112,768]{1,0:T(8,128)(2,1)S(1)}, u32[]{:S(2)}, u32[]{:S(2)}) collective-permute-start(bf16[112,768]{1,0:T(8,128)(2,1)S(1)} %collective-permute-done.3.refs_2_), channel_id=1, source_target_pairs={{0,4},{1,5},{2,6},{3,7},{4,0},{5,1},{6,2},{7,3},{8,12},{9,13},{10,... | collective-permute-start | bytes 516104 | tf_op jit(solution)/shard_map/ppermute | solution.py:1027
  31.1 8.3 %collective-permute-start.12 = (bf16[112,768]{1,0:T(8,128)(2,1)S(1)}, bf16[112,768]{1,0:T(8,128)(2,1)S(1)}, u32[]{:S(2)}, u32[]{:S(2)}) collective-permute-start(bf16[112,768]{1,0:T(8,128)(2,1)S(1)} %collective-permute-done.11.refs_3_), channel_id=1, source_target_pairs={{0,4},{1,5},{2,6},{3,7},{4,0},{5,1},{6,2},{7,3},{8,12},{9,13},{10,... | collective-permute-start | bytes 516104 | tf_op jit(solution)/shard_map/ppermute | solution.py:1027
  33.3 9.0 %collective-permute-start.14 = (bf16[192,768]{1,0:T(8,128)(2,1)S(1)}, bf16[192,768]{1,0:T(8,128)(2,1)S(1)}, u32[]{:S(2)}, u32[]{:S(2)}) collective-permute-start(bf16[192,768]{1,0:T(8,128)(2,1)S(1)} %get-tuple-element.125.refs_1_), channel_id=1, source_target_pairs={{0,8},{1,9},{2,10},{3,11},{4,12},{5,13},{6,14},{7,15},{8,0},{9,1},... | collective-permute-start | bytes 884744 | tf_op jit(solution)/shard_map/ppermute | solution.py:1027
  37.0 6.8 %collective-permute-start.8 = (bf16[352,768]{1,0:T(8,128)(2,1)S(1)}, bf16[352,768]{1,0:T(8,128)(2,1)}, u32[]{:S(2)}, u32[]{:S(2)}) collective-permute-start(bf16[352,768]{1,0:T(8,128)(2,1)S(1)} %get-tuple-element.119.refs_0_.refs_4_), channel_id=1, source_target_pairs={{0,1},{1,0},{2,3},{3,2},{4,5},{5,4},{6,7},{7,6},{8,9},{9,8},{10,11... | collective-permute-start | bytes 1622024 | tf_op jit(solution)/shard_map/ppermute | solution.py:1027
  37.0 5.3 %collective-permute-start.10 = (bf16[352,768]{1,0:T(8,128)(2,1)}, bf16[352,768]{1,0:T(8,128)(2,1)}, u32[]{:S(2)}, u32[]{:S(2)}) collective-permute-start(bf16[352,768]{1,0:T(8,128)(2,1)} %collective-permute-done.6.refs_2_.refs_6_), channel_id=1, source_target_pairs={{0,1},{1,0},{2,3},{3,2},{4,5},{5,4},{6,7},{7,6},{8,9},{9,8},{10,11... | collective-permute-start | bytes 1622024 | tf_op jit(solution)/shard_map/ppermute | solution.py:1027
  39.7 9.5 %collective-permute-start.16 = (bf16[192,768]{1,0:T(8,128)(2,1)S(1)}, bf16[192,768]{1,0:T(8,128)(2,1)S(1)}, u32[]{:S(2)}, u32[]{:S(2)}) collective-permute-start(bf16[192,768]{1,0:T(8,128)(2,1)S(1)} %get-tuple-element.128.refs_0_), channel_id=1, source_target_pairs={{0,2},{1,3},{2,0},{3,1},{4,6},{5,7},{6,4},{7,5},{8,10},{9,11},{10,... | collective-permute-start | bytes 884744 | tf_op jit(solution)/shard_map/ppermute | solution.py:1027
  41.1 8.7 %collective-permute-start.21 = (bf16[192,768]{1,0:T(8,128)(2,1)S(1)}, bf16[192,768]{1,0:T(8,128)(2,1)S(1)}, u32[]{:S(2)}, u32[]{:S(2)}) collective-permute-start(bf16[192,768]{1,0:T(8,128)(2,1)S(1)} %collective-permute-done.13.refs_8_.refs_3_), channel_id=1, source_target_pairs={{0,8},{1,9},{2,10},{3,11},{4,12},{5,13},{6,14},{7,15},{8,0},{9,1},... | collective-permute-start | bytes 884744 | tf_op jit(solution)/shard_map/ppermute | solution.py:1027
  42.4 9.5 %collective-permute-start.22 = (bf16[192,768]{1,0:T(8,128)(2,1)S(1)}, bf16[192,768]{1,0:T(8,128)(2,1)S(1)}, u32[]{:S(2)}, u32[]{:S(2)}) collective-permute-start(bf16[192,768]{1,0:T(8,128)(2,1)S(1)} %collective-permute-done.14.refs_8_.refs_2_), channel_id=1, source_target_pairs={{0,4},{1,5},{2,6},{3,7},{4,0},{5,1},{6,2},{7,3},{8,12},{9,13},{10,... | collective-permute-start | bytes 884744 | tf_op jit(solution)/shard_map/ppermute | solution.py:1027
  49.2 4.1 %collective-permute-start.15 = (bf16[192,768]{1,0:T(8,128)(2,1)S(1)}, bf16[192,768]{1,0:T(8,128)(2,1)S(1)}, u32[]{:S(2)}, u32[]{:S(2)}) collective-permute-start(bf16[192,768]{1,0:T(8,128)(2,1)S(1)} %get-tuple-element.128.refs_0_), channel_id=1, source_target_pairs={{0,1},{1,0},{2,3},{3,2},{4,5},{5,4},{6,7},{7,6},{8,9},{9,8},{10,11... | collective-permute-start | bytes 884744 | tf_op jit(solution)/shard_map/ppermute | solution.py:1027
  49.3 4.1 %collective-permute-start.17 = (bf16[192,768]{1,0:T(8,128)(2,1)S(1)}, bf16[192,768]{1,0:T(8,128)(2,1)S(1)}, u32[]{:S(2)}, u32[]{:S(2)}) collective-permute-start(bf16[192,768]{1,0:T(8,128)(2,1)S(1)} %collective-permute-done.16.refs_2_.refs_4_), channel_id=1, source_target_pairs={{0,1},{1,0},{2,3},{3,2},{4,5},{5,4},{6,7},{7,6},{8,9},{9,8},{10,11... | collective-permute-start | bytes 884744 | tf_op jit(solution)/shard_map/ppermute | solution.py:1027
  49.8 15.4 %collective-permute-start.24 = (bf16[192,768]{1,0:T(8,128)(2,1)S(1)}, bf16[192,768]{1,0:T(8,128)(2,1)S(1)}, u32[]{:S(2)}, u32[]{:S(2)}) collective-permute-start(bf16[192,768]{1,0:T(8,128)(2,1)S(1)} %collective-permute-done.21.refs_4_), channel_id=1, source_target_pairs={{0,4},{1,5},{2,6},{3,7},{4,0},{5,1},{6,2},{7,3},{8,12},{9,13},{10,... | collective-permute-start | bytes 884744 | tf_op jit(solution)/shard_map/ppermute | solution.py:1027
  50.4 10.4 %collective-permute-start.19 = (bf16[736,192]{1,0:T(8,128)(2,1)S(1)}, bf16[736,192]{1,0:T(8,128)(2,1)S(1)}, u32[]{:S(2)}, u32[]{:S(2)}) collective-permute-start(bf16[736,192]{1,0:T(8,128)(2,1)S(1)} %get-tuple-element.132.refs_0_.refs_3_), channel_id=1, source_target_pairs={{0,2},{1,3},{2,0},{3,1},{4,6},{5,7},{6,4},{7,5},{8,10},{9,11},{10,... | collective-permute-start | bytes 847880 | tf_op jit(solution)/shard_map/ppermute | solution.py:1027
  51.9 13.3 %collective-permute-start.23 = (bf16[192,768]{1,0:T(8,128)(2,1)S(1)}, bf16[192,768]{1,0:T(8,128)(2,1)S(1)}, u32[]{:S(2)}, u32[]{:S(2)}) collective-permute-start(bf16[192,768]{1,0:T(8,128)(2,1)S(1)} %collective-permute-done.13.refs_8_.refs_3_), channel_id=1, source_target_pairs={{0,4},{1,5},{2,6},{3,7},{4,0},{5,1},{6,2},{7,3},{8,12},{9,13},{10,... | collective-permute-start | bytes 884744 | tf_op jit(solution)/shard_map/ppermute | solution.py:1027
  60.8 1.7 %collective-permute-start.18 = (bf16[736,192]{1,0:T(8,128)(2,1)S(1)}, bf16[736,192]{1,0:T(8,128)(2,1)S(1)}, u32[]{:S(2)}, u32[]{:S(2)}) collective-permute-start(bf16[736,192]{1,0:T(8,128)(2,1)S(1)} %get-tuple-element.132.refs_0_.refs_3_), channel_id=1, source_target_pairs={{0,1},{1,0},{2,3},{3,2},{4,5},{5,4},{6,7},{7,6},{8,9},{9,8},{10,11... | collective-permute-start | bytes 847880 | tf_op jit(solution)/shard_map/ppermute | solution.py:1027
  60.8 2.2 %collective-permute-start.20 = (bf16[736,192]{1,0:T(8,128)(2,1)S(1)}, bf16[736,192]{1,0:T(8,128)(2,1)S(1)}, u32[]{:S(2)}, u32[]{:S(2)}) collective-permute-start(bf16[736,192]{1,0:T(8,128)(2,1)S(1)} %collective-permute-done.19.refs_2_.refs_5_), channel_id=1, source_target_pairs={{0,1},{1,0},{2,3},{3,2},{4,5},{5,4},{6,7},{7,6},{8,9},{9,8},{10,11... | collective-permute-start | bytes 847880 | tf_op jit(solution)/shard_map/ppermute | solution.py:1027
  69.5 2.3 %collective-permute-start.26 = (bf16[368,768]{1,0:T(8,128)(2,1)S(1)}, bf16[368,768]{1,0:T(8,128)(2,1)S(1)}, u32[]{:S(2)}, u32[]{:S(2)}) collective-permute-start(bf16[368,768]{1,0:T(8,128)(2,1)S(1)} %get-tuple-element.149.refs_2_), channel_id=1, source_target_pairs={{0,1},{1,0},{2,3},{3,2},{4,5},{5,4},{6,7},{7,6},{8,9},{9,8},{10,11... | collective-permute-start | bytes 1695752 | tf_op jit(solution)/shard_map/ppermute | solution.py:1027
  71.0 15.7 %collective-permute-start.34 = (bf16[4,96,768]{2,1,0:T(8,128)(2,1)S(1)}, bf16[4,96,768]{2,1,0:T(8,128)(2,1)S(1)}, u32[]{:S(2)}, u32[]{:S(2)}) collective-permute-start(bf16[4,96,768]{2,1,0:T(8,128)(2,1)S(1)} %get-tuple-element.178), channel_id=1, source_target_pairs={{0,8},{1,9},{2,10},{3,11},{4,12},{5,13},{6,14},{7,15},{8,0},{9,1},... | collective-permute-start | bytes 1769480 | tf_op jit(solution)/shard_map/ppermute | solution.py:1027
  71.9 19.5 %collective-permute-start.27 = (bf16[368,768]{1,0:T(8,128)(2,1)S(1)}, bf16[368,768]{1,0:T(8,128)(2,1)S(1)}, u32[]{:S(2)}, u32[]{:S(2)}) collective-permute-start(bf16[368,768]{1,0:T(8,128)(2,1)S(1)} %add_rows.1.refs_0_), channel_id=1, source_target_pairs={{0,2},{1,3},{2,0},{3,1},{4,6},{5,7},{6,4},{7,5},{8,10},{9,11},{10,... | collective-permute-start | bytes 1695752 | tf_op jit(solution)/shard_map/ppermute | solution.py:1027
  74.7 17.0 %collective-permute-start.43 = (bf16[4,96,768]{2,1,0:T(8,128)(2,1)S(1)}, bf16[4,96,768]{2,1,0:T(8,128)(2,1)S(1)}, u32[]{:S(2)}, u32[]{:S(2)}) collective-permute-start(bf16[4,96,768]{2,1,0:T(8,128)(2,1)S(1)} %get-tuple-element.196), channel_id=1, source_target_pairs={{0,4},{1,5},{2,6},{3,7},{4,0},{5,1},{6,2},{7,3},{8,12},{9,13},{10,... | collective-permute-start | bytes 1769480 | tf_op jit(solution)/shard_map/ppermute | solution.py:1027
  77.9 28.1 %collective-permute-start.25 = (bf16[416,768]{1,0:T(8,128)(2,1)S(1)}, bf16[416,768]{1,0:T(8,128)(2,1)S(1)}, u32[]{:S(2)}, u32[]{:S(2)}) collective-permute-start(bf16[416,768]{1,0:T(8,128)(2,1)S(1)} %get-tuple-element.142), channel_id=1, source_target_pairs={{0,1},{1,0},{2,3},{3,2},{4,5},{5,4},{6,7},{7,6},{8,9},{9,8},{10,11... | collective-permute-start | bytes 1916936 | tf_op jit(solution)/shard_map/ppermute | solution.py:1027
  86.8 18.1 %collective-permute-start.35 = (bf16[2,96,768]{2,1,0:T(8,128)(2,1)S(1)}, bf16[2,96,768]{2,1,0:T(8,128)(2,1)S(1)}, u32[]{:S(2)}, u32[]{:S(2)}) collective-permute-start(bf16[2,96,768]{2,1,0:T(8,128)(2,1)S(1)} %get-tuple-element.179), channel_id=1, source_target_pairs={{0,16},{1,17},{2,18},{3,19},{4,20},{5,21},{6,22},{7,23},{8,24},{9,... | collective-permute-start | bytes 884744 | tf_op jit(solution)/shard_map/ppermute | solution.py:1027
  91.6 2.0 %collective-permute-start.28 = (bf16[368,768]{1,0:T(8,128)(2,1)S(1)}, bf16[368,768]{1,0:T(8,128)(2,1)S(1)}, u32[]{:S(2)}, u32[]{:S(2)}) collective-permute-start(bf16[368,768]{1,0:T(8,128)(2,1)S(1)} %add_pair.1.refs_0_.refs_11_), channel_id=1, source_target_pairs={{0,1},{1,0},{2,3},{3,2},{4,5},{5,4},{6,7},{7,6},{8,9},{9,8},{10,11... | collective-permute-start | bytes 1695752 | tf_op jit(solution)/shard_map/ppermute | solution.py:1027
  91.8 18.4 %collective-permute-start.44 = (bf16[2,96,768]{2,1,0:T(8,128)(2,1)S(1)}, bf16[2,96,768]{2,1,0:T(8,128)(2,1)S(1)}, u32[]{:S(2)}, u32[]{:S(2)}) collective-permute-start(bf16[2,96,768]{2,1,0:T(8,128)(2,1)S(1)} %get-tuple-element.198), channel_id=1, source_target_pairs={{0,8},{1,9},{2,10},{3,11},{4,12},{5,13},{6,14},{7,15},{8,0},{9,1},... | collective-permute-start | bytes 884744 | tf_op jit(solution)/shard_map/ppermute | solution.py:1027
  97.5 10.8 %collective-permute-start.31 = (bf16[4,112,384]{2,1,0:T(8,128)(2,1)S(1)}, bf16[4,112,384]{2,1,0:T(8,128)(2,1)S(1)}, u32[]{:S(2)}, u32[]{:S(2)}) collective-permute-start(bf16[4,112,384]{2,1,0:T(8,128)(2,1)S(1)} %get-tuple-element.170), channel_id=1, source_target_pairs={{0,4},{1,5},{2,6},{3,7},{4,0},{5,1},{6,2},{7,3},{8,12},{9,13},{10,... | collective-permute-start | bytes 1032200 | tf_op jit(solution)/shard_map/ppermute | solution.py:1027
  103.7 2.3 %collective-permute-start.29 = (bf16[416,768]{1,0:T(8,128)(2,1)S(1)}, bf16[416,768]{1,0:T(8,128)(2,1)S(1)}, u32[]{:S(2)}, u32[]{:S(2)}) collective-permute-start(bf16[416,768]{1,0:T(8,128)(2,1)S(1)} %get-tuple-element.159), channel_id=1, source_target_pairs={{0,1},{1,0},{2,3},{3,2},{4,5},{5,4},{6,7},{7,6},{8,9},{9,8},{10,11... | collective-permute-start | bytes 1916936 | tf_op jit(solution)/shard_map/ppermute | solution.py:1027
  105.0 13.5 %collective-permute-start.36 = (bf16[4,96,384]{2,1,0:T(8,128)(2,1)S(1)}, bf16[4,96,384]{2,1,0:T(8,128)(2,1)S(1)}, u32[]{:S(2)}, u32[]{:S(2)}) collective-permute-start(bf16[4,96,384]{2,1,0:T(8,128)(2,1)S(1)} %get-tuple-element.180), channel_id=1, source_target_pairs={{0,4},{1,5},{2,6},{3,7},{4,0},{5,1},{6,2},{7,3},{8,12},{9,13},{10,... | collective-permute-start | bytes 884744 | tf_op jit(solution)/shard_map/ppermute | solution.py:1027
  106.2 17.5 %collective-permute-start.30 = (bf16[416,768]{1,0:T(8,128)(2,1)S(1)}, bf16[416,768]{1,0:T(8,128)(2,1)S(1)}, u32[]{:S(2)}, u32[]{:S(2)}) collective-permute-start(bf16[416,768]{1,0:T(8,128)(2,1)S(1)} %get-tuple-element.162), channel_id=1, source_target_pairs={{0,2},{1,3},{2,0},{3,1},{4,6},{5,7},{6,4},{7,5},{8,10},{9,11},{10,... | collective-permute-start | bytes 1916936 | tf_op jit(solution)/shard_map/ppermute | solution.py:1027
  108.5 8.0 %collective-permute-start.32 = (bf16[2,112,384]{2,1,0:T(8,128)(2,1)S(1)}, bf16[2,112,384]{2,1,0:T(8,128)(2,1)S(1)}, u32[]{:S(2)}, u32[]{:S(2)}) collective-permute-start(bf16[2,112,384]{2,1,0:T(8,128)(2,1)S(1)} %get-tuple-element.172), channel_id=1, source_target_pairs={{0,8},{1,9},{2,10},{3,11},{4,12},{5,13},{6,14},{7,15},{8,0},{9,1},... | collective-permute-start | bytes 516104 | tf_op jit(solution)/shard_map/ppermute | solution.py:1027
  110.3 10.3 %collective-permute-start.45 = (bf16[96,768]{1,0:T(8,128)(2,1)S(1)}, bf16[96,768]{1,0:T(8,128)(2,1)S(1)}, u32[]{:S(2)}, u32[]{:S(2)}) collective-permute-start(bf16[96,768]{1,0:T(8,128)(2,1)S(1)} %get-tuple-element.200), channel_id=1, source_target_pairs={{0,16},{1,17},{2,18},{3,19},{4,20},{5,21},{6,22},{7,23},{8,24},{9,... | collective-permute-start | bytes 442376 | tf_op jit(solution)/shard_map/ppermute | solution.py:1027
  112.3 8.9 %collective-permute-start.40 = (bf16[96,768]{1,0:T(8,128)(2,1)S(1)}, bf16[96,768]{1,0:T(8,128)(2,1)S(1)}, u32[]{:S(2)}, u32[]{:S(2)}) collective-permute-start(bf16[96,768]{1,0:T(8,128)(2,1)S(1)} %get-tuple-element.189), channel_id=1, source_target_pairs={{0,4},{1,5},{2,6},{3,7},{4,0},{5,1},{6,2},{7,3},{8,12},{9,13},{10,... | collective-permute-start | bytes 442376 | tf_op jit(solution)/shard_map/ppermute | solution.py:1027
  116.5 9.4 %collective-permute-start.33 = (bf16[112,384]{1,0:T(8,128)(2,1)S(1)}, bf16[112,384]{1,0:T(8,128)(2,1)S(1)}, u32[]{:S(2)}, u32[]{:S(2)}) collective-permute-start(bf16[112,384]{1,0:T(8,128)(2,1)S(1)} %get-tuple-element.174), channel_id=1, source_target_pairs={{0,16},{1,17},{2,18},{3,19},{4,20},{5,21},{6,22},{7,23},{8,24},{9,... | collective-permute-start | bytes 258056 | tf_op jit(solution)/shard_map/ppermute | solution.py:1027
  118.5 7.3 %collective-permute-start.39 = (bf16[96,384]{1,0:T(8,128)(2,1)S(1)}, bf16[96,384]{1,0:T(8,128)(2,1)S(1)}, u32[]{:S(2)}, u32[]{:S(2)}) collective-permute-start(bf16[96,384]{1,0:T(8,128)(2,1)S(1)} %get-tuple-element.185), channel_id=1, source_target_pairs={{0,24},{1,25},{2,26},{3,27},{4,28},{5,29},{6,30},{7,31},{8,16},{9,... | collective-permute-start | bytes 221192 | tf_op jit(solution)/shard_map/ppermute | solution.py:1027
  120.6 5.4 %collective-permute-start.37 = (bf16[96,384]{1,0:T(8,128)(2,1)S(1)}, bf16[96,384]{1,0:T(8,128)(2,1)S(1)}, u32[]{:S(2)}, u32[]{:S(2)}) collective-permute-start(bf16[96,384]{1,0:T(8,128)(2,1)S(1)} %get-tuple-element.182), channel_id=1, source_target_pairs={{0,8},{1,9},{2,10},{3,11},{4,12},{5,13},{6,14},{7,15},{8,0},{9,1},... | collective-permute-start | bytes 221192 | tf_op jit(solution)/shard_map/ppermute | solution.py:1027
  121.2 8.1 %collective-permute-start.38 = (bf16[96,384]{1,0:T(8,128)(2,1)S(1)}, bf16[96,384]{1,0:T(8,128)(2,1)S(1)}, u32[]{:S(2)}, u32[]{:S(2)}) collective-permute-start(bf16[96,384]{1,0:T(8,128)(2,1)S(1)} %get-tuple-element.183), channel_id=1, source_target_pairs={{0,16},{1,17},{2,18},{3,19},{4,20},{5,21},{6,22},{7,23},{8,24},{9,... | collective-permute-start | bytes 221192 | tf_op jit(solution)/shard_map/ppermute | solution.py:1027
  123.8 7.3 %collective-permute-start.46 = (bf16[64,768]{1,0:T(8,128)(2,1)S(1)}, bf16[64,768]{1,0:T(8,128)(2,1)S(1)}, u32[]{:S(2)}, u32[]{:S(2)}) collective-permute-start(bf16[64,768]{1,0:T(8,128)(2,1)S(1)} %get-tuple-element.201), channel_id=1, source_target_pairs={{0,2},{1,3},{2,0},{3,1},{4,6},{5,7},{6,4},{7,5},{8,10},{9,11},{10,... | collective-permute-start | bytes 294920 | tf_op jit(solution)/shard_map/ppermute | solution.py:1027
  130.0 4.6 %collective-permute-start.42 = (bf16[64,768]{1,0:T(8,128)(2,1)S(1)}, bf16[64,768]{1,0:T(8,128)(2,1)S(1)}, u32[]{:S(2)}, u32[]{:S(2)}) collective-permute-start(bf16[64,768]{1,0:T(8,128)(2,1)S(1)} %get-tuple-element.192), channel_id=1, source_target_pairs={{0,2},{1,3},{2,0},{3,1},{4,6},{5,7},{6,4},{7,5},{8,10},{9,11},{10,... | collective-permute-start | bytes 294920 | tf_op jit(solution)/shard_map/ppermute | solution.py:1027
  131.1 3.5 %collective-permute-start.49 = (bf16[64,768]{1,0:T(8,128)(2,1)S(1)}, bf16[64,768]{1,0:T(8,128)(2,1)S(1)}, u32[]{:S(2)}, u32[]{:S(2)}) collective-permute-start(bf16[64,768]{1,0:T(8,128)(2,1)S(1)} %collective-permute-done.46.refs_2_), channel_id=1, source_target_pairs={{0,1},{1,0},{2,3},{3,2},{4,5},{5,4},{6,7},{7,6},{8,9},{9,8},{10,11... | collective-permute-start | bytes 294920 | tf_op jit(solution)/shard_map/ppermute | solution.py:1027
  131.1 3.5 %collective-permute-start.48 = (bf16[32,768]{1,0:T(8,128)(2,1)S(1)}, bf16[32,768]{1,0:T(8,128)(2,1)S(1)}, u32[]{:S(2)}, u32[]{:S(2)}) collective-permute-start(bf16[32,768]{1,0:T(8,128)(2,1)S(1)} %get-tuple-element.204), channel_id=1, source_target_pairs={{0,1},{1,0},{2,3},{3,2},{4,5},{5,4},{6,7},{7,6},{8,9},{9,8},{10,11... | collective-permute-start | bytes 147464 | tf_op jit(solution)/shard_map/ppermute | solution.py:1027
  131.7 3.9 %collective-permute-start.41 = (bf16[32,768]{1,0:T(8,128)(2,1)S(1)}, bf16[32,768]{1,0:T(8,128)(2,1)S(1)}, u32[]{:S(2)}, u32[]{:S(2)}) collective-permute-start(bf16[32,768]{1,0:T(8,128)(2,1)S(1)} %get-tuple-element.191), channel_id=1, source_target_pairs={{0,1},{1,0},{2,3},{3,2},{4,5},{5,4},{6,7},{7,6},{8,9},{9,8},{10,11... | collective-permute-start | bytes 147464 | tf_op jit(solution)/shard_map/ppermute | solution.py:1027
  (14 other events, 98.9 us)

commit v8 on v7

--- a/solution.py
+++ b/solution.py
@@ -377,16 +377,16 @@
 
 PAD_ID = 99
 PLAN = (
-    (9.0, ()), (0, (0,)), (0, ()), (0, (2, 0)), (21.0, ()), (0, ()), (0, ()), (0, ()), (0, (0,)), (0, ()),
-    (0, ()), (0, (8,)), (0, ()), (0, (1,)), (0, (5, 9, 11)), (0, (7, 3)), (0, ()), (0, (10, 15, 16)),
-    (0, ()), (36.0, (12,)), (0, ()), (2.4, (13,)), (0, (9,)), (0, (17,)), (0, (21,)), (0, (21,)), (0, ()),
-    (4.8, (11,)), (0, (27,)), (0, (27,)), (0.001, ()), (0.001, ()), (1.11, (20,)), (0, ()), (2.7, ()),
-    (0, ()), (0.002, (17, 28)), (0, ()), (0.6, ()), (0, (34,)), (0.6, ()), (0, ()), (0.07, ()), (0, ()),
-    (0.27, ()), (0, ()), (0.4, (44,)), (0, ()), (21.0, ()), (0, ()), (7.0, (32,)), (0, (45,)), (0.42, ()),
-    (0, (43, 45)), (1.05, ()), (0, ()), (0.0325, ()), (0, ()), (0.18, ()), (0, (56,)), (0.105, (58,)),
-    (0, ()), (0, ()), (0, (47,)), (2.1, ()), (0, ()), (2.1, ()), (0, ()), (2.1, ()), (0.35, (59,)), (0, ()),
-    (0, ()), (0, (55, 65)), (1.5, (64, 72)), (9.0, (68,)), (0, ()), (0, ()), (0, (70,)), (0.001, ()),
-    (30, ()),
+    (9.0, ()), (0, (0,)), (0, (0,)), (0, (2,)), (21.0, (2,)), (0, ()), (0, ()), (0, ()), (0, (0,)),
+    (0, (2, 4, 5)), (0, ()), (0, (8,)), (0, ()), (0, ()), (0, (9, 11)), (0, (7,)), (0, ()),
+    (0, (10, 15, 16)), (0, ()), (36.0, (12,)), (0, ()), (2.4, ()), (0, (9,)), (0, (17,)), (0, (21,)),
+    (0, (21,)), (0, (21, 6, 18)), (4.8, ()), (0, (27,)), (0, (27,)), (0.001, (26, 28, 21)), (0.001, ()),
+    (1.11, ()), (0, ()), (2.7, ()), (0, ()), (0.002, ()), (0, (30,)), (0.6, (29,)), (0, (34,)), (0.6, ()),
+    (0, ()), (0.07, ()), (0, ()), (0.27, ()), (0, ()), (0.4, ()), (0, ()), (21.0, ()), (0, ()),
+    (7.0, (32,)), (0, (45,)), (0.42, ()), (0, ()), (1.05, ()), (0, ()), (0.0325, ()), (0, ()), (0.18, ()),
+    (0, (56,)), (0.105, (58,)), (0, ()), (0, ()), (0, ()), (2.1, ()), (0, (47,)), (2.1, ()), (0, ()),
+    (2.1, ()), (0.35, (59,)), (0, ()), (0, (69,)), (0, (55, 65)), (1.5, ()), (9.0, (68,)), (0, (68,)),
+    (0, ()), (0, (70,)), (0.001, ()), (30, ()),
 )
 STEPS = []
 
@@ -1117,7 +1117,7 @@
     attended, projected, probs, tokens, unit_low = call(
         attend,
         [sds(736, 192), *keep(sds(736, 576), sds(6, 368, 368), sds(736, 768), sds(736, 768))],
-        [*row_parts, special, image_ids.reshape(8, 88), *keep(qkv_full, gain_rows)],
+        [*keep(*row_parts), special, image_ids.reshape(8, 88), *keep(qkv_full, gain_rows)],
         [pltpu.VMEM((736, 768), F32)],
     )
     far_heads = send(attended, "x", 1)
@@ -1130,7 +1130,7 @@
     out_full, out_mine, grad_mlp, cots = call(
         order_out,
         keep(sds(768, 768), sds(192, 768), sds(736, 768), sds(736, 768)),
-        [*out_parts, *row_parts, cot_special, Keep(gain_rows)],
+        [*out_parts, *keep(*row_parts), cot_special, Keep(gain_rows)],
         [pltpu.VMEM((768, 768), F32)],
     )
     heads = [

time: 137 us -> 137 us (level)
  waiting for transfers between devices: 47.3 us -> 45.7 us
    ppermute x50, waiting for transfers between devices: 47.3 us -> 45.7 us  [send(): STEPS.append(lax.ppermute(rows, ('dp', 'blk'), pairs))]
  transfers between devices with their start and end apart: 50 -> 50, of which waited for: 20 -> 19; matrix products, arithmetic and copies ran while one was open for 0% -> 0% of each run, Pallas kernels for 21% -> 21%
where the time goes in v8:
time: 137 us; the launch traced here: 136 us
  starting transfers between devices  54.3 us (40%)
  waiting for transfers between devices  45.7 us (33%)
  Pallas kernels  35.2 us (26%)
    ppermute x50, starting transfers between devices, send(): STEPS.append(lax.ppermute(rows, ('dp', 'blk'), pairs))  54.3 us
    ppermute x50, waiting for transfers between devices, send(): STEPS.append(lax.ppermute(rows, ('dp', 'blk'), pairs))  45.7 us
    pallas_call x30, Pallas kernels, call(): pl.pallas_call(body, out_shape=tuple((pltpu.VMEM(v.value.shape, v.value.d...  35.2 us
  transfers between devices with their start and end apart: 50, of which 19 were waited for; matrix products, arithmetic and copies ran while one was open for 0% of the time, Pallas kernels for 21%

profile of v8, /device:TPU:0, one launch (start us, length us, event | category | flops | bytes accessed | tf_op | source)
XLA Modules:
  0.0 136.3 jit_solution(4650744923860819613)
XLA Ops:
  0.7 1.3 pick_pieces.1
  2.0 3.0 %collective-permute-start.1 = (bf16[96,768]{1,0:T(8,128)(2,1)S(1)}, bf16[96,768]{1,0:T(8,128)(2,1)S(1)}, u32[]{:S(2)}, u32[]{:S(2)}) collective-permute-start(bf16[96,768]{1,0:T(8,128)(2,1)S(1)} %get-tuple-element.119), channel_id=1, source_target_pairs={{0,2},{1,3},{2,0},{3,1},{4,6},{5,7},{6,4},{7,5},{8,10},{9,11},{10,... | collective-permute-start | bytes 442376 | tf_op jit(solution)/shard_map/ppermute | solution.py:1027
  5.0 1.3 collective-permute-done.refs_1_.refs_6_
  6.2 2.6 %collective-permute-done.1.refs_2_ = bf16[96,768]{1,0:T(8,128)(2,1)S(1)} collective-permute-done((bf16[96,768]{1,0:T(8,128)(2,1)S(1)}, bf16[96,768]{1,0:T(8,128)(2,1)S(1)}, u32[]{:S(2)}, u32[]{:S(2)}) %collective-permute-start.1) | collective-permute-done | bytes 147488 | tf_op jit(solution)/shard_map/ppermute | solution.py:1027
  8.8 1.7 %collective-permute-start.6 = (bf16[352,768]{1,0:T(8,128)(2,1)S(1)}, bf16[352,768]{1,0:T(8,128)(2,1)S(1)}, u32[]{:S(2)}, u32[]{:S(2)}) collective-permute-start(bf16[352,768]{1,0:T(8,128)(2,1)S(1)} %get-tuple-element.125.refs_0_.refs_4_), channel_id=1, source_target_pairs={{0,2},{1,3},{2,0},{3,1},{4,6},{5,7},{6,4},{7,5},{8,10},{9,11},{10,... | collective-permute-start | bytes 1622024 | tf_op jit(solution)/shard_map/ppermute | solution.py:1027
  10.7 2.7 %collective-permute-start.4 = (bf16[112,768]{1,0:T(8,128)(2,1)S(1)}, bf16[112,768]{1,0:T(8,128)(2,1)S(1)}, u32[]{:S(2)}, u32[]{:S(2)}) collective-permute-start(bf16[112,768]{1,0:T(8,128)(2,1)S(1)} %get-tuple-element.121.refs_0_), channel_id=1, source_target_pairs={{0,16},{1,17},{2,18},{3,19},{4,20},{5,21},{6,22},{7,23},{8,24},{9,... | collective-permute-start | bytes 516104 | tf_op jit(solution)/shard_map/ppermute | solution.py:1027
  13.4 1.5 %collective-permute-start.9 = (bf16[304,768]{1,0:T(8,128)(2,1)S(1)}, bf16[304,768]{1,0:T(8,128)(2,1)S(1)}, u32[]{:S(2)}, u32[]{:S(2)}) collective-permute-start(bf16[304,768]{1,0:T(8,128)(2,1)S(1)} %get-tuple-element.126), channel_id=1, source_target_pairs={{0,4},{1,5},{2,6},{3,7},{4,0},{5,1},{6,2},{7,3},{8,12},{9,13},{10,... | collective-permute-start | bytes 1400840 | tf_op jit(solution)/shard_map/ppermute | solution.py:1027
  14.9 1.6 %collective-permute-start.3 = (bf16[112,768]{1,0:T(8,128)(2,1)S(1)}, bf16[112,768]{1,0:T(8,128)(2,1)S(1)}, u32[]{:S(2)}, u32[]{:S(2)}) collective-permute-start(bf16[112,768]{1,0:T(8,128)(2,1)S(1)} %get-tuple-element.121.refs_0_), channel_id=1, source_target_pairs={{0,8},{1,9},{2,10},{3,11},{4,12},{5,13},{6,14},{7,15},{8,0},{9,1},... | collective-permute-start | bytes 516104 | tf_op jit(solution)/shard_map/ppermute | solution.py:1027
  16.5 5.5 %collective-permute-done.4.refs_2_ = bf16[112,768]{1,0:T(8,128)(2,1)S(1)} collective-permute-done((bf16[112,768]{1,0:T(8,128)(2,1)S(1)}, bf16[112,768]{1,0:T(8,128)(2,1)S(1)}, u32[]{:S(2)}, u32[]{:S(2)}) %collective-permute-start.4) | collective-permute-done | bytes 172064 | tf_op jit(solution)/shard_map/ppermute | solution.py:1027
  22.6 3.4 %collective-permute-start.13 = (bf16[192,768]{1,0:T(8,128)(2,1)S(1)}, bf16[192,768]{1,0:T(8,128)(2,1)S(1)}, u32[]{:S(2)}, u32[]{:S(2)}) collective-permute-start(bf16[192,768]{1,0:T(8,128)(2,1)S(1)} %get-tuple-element.128.refs_1_), channel_id=1, source_target_pairs={{0,16},{1,17},{2,18},{3,19},{4,20},{5,21},{6,22},{7,23},{8,24},{9,... | collective-permute-start | bytes 884744 | tf_op jit(solution)/shard_map/ppermute | solution.py:1027
  26.0 1.4 %collective-permute-start.5 = (bf16[112,768]{1,0:T(8,128)(2,1)S(1)}, bf16[112,768]{1,0:T(8,128)(2,1)S(1)}, u32[]{:S(2)}, u32[]{:S(2)}) collective-permute-start(bf16[112,768]{1,0:T(8,128)(2,1)S(1)} %collective-permute-done.3.refs_1_), channel_id=1, source_target_pairs={{0,4},{1,5},{2,6},{3,7},{4,0},{5,1},{6,2},{7,3},{8,12},{9,13},{10,... | collective-permute-start | bytes 516104 | tf_op jit(solution)/shard_map/ppermute | solution.py:1027
  28.1 3.0 %collective-permute-done.11.refs_3_ = bf16[112,768]{1,0:T(8,128)(2,1)S(1)} collective-permute-done((bf16[112,768]{1,0:T(8,128)(2,1)S(1)}, bf16[112,768]{1,0:T(8,128)(2,1)S(1)}, u32[]{:S(2)}, u32[]{:S(2)}) %collective-permute-start.11) | collective-permute-done | bytes 172064 | tf_op jit(solution)/shard_map/ppermute | solution.py:1027
  31.1 1.5 %collective-permute-start.12 = (bf16[112,768]{1,0:T(8,128)(2,1)S(1)}, bf16[112,768]{1,0:T(8,128)(2,1)S(1)}, u32[]{:S(2)}, u32[]{:S(2)}) collective-permute-start(bf16[112,768]{1,0:T(8,128)(2,1)S(1)} %collective-permute-done.11.refs_3_), channel_id=1, source_target_pairs={{0,4},{1,5},{2,6},{3,7},{4,0},{5,1},{6,2},{7,3},{8,12},{9,13},{10,... | collective-permute-start | bytes 516104 | tf_op jit(solution)/shard_map/ppermute | solution.py:1027
  33.4 3.7 %collective-permute-done.7.refs_6_ = bf16[112,768]{1,0:T(8,128)(2,1)S(1)} collective-permute-done((bf16[112,768]{1,0:T(8,128)(2,1)S(1)}, bf16[112,768]{1,0:T(8,128)(2,1)S(1)}, u32[]{:S(2)}, u32[]{:S(2)}) %collective-permute-start.7) | collective-permute-done | bytes 172064 | tf_op jit(solution)/shard_map/ppermute | solution.py:1027
  37.6 1.8 %collective-permute-done.13.refs_8_.refs_3_ = bf16[192,768]{1,0:T(8,128)(2,1)S(1)} collective-permute-done((bf16[192,768]{1,0:T(8,128)(2,1)S(1)}, bf16[192,768]{1,0:T(8,128)(2,1)S(1)}, u32[]{:S(2)}, u32[]{:S(2)}) %collective-permute-start.13) | collective-permute-done | bytes 294944 | tf_op jit(solution)/shard_map/ppermute | solution.py:1027
  40.3 1.3 collective-permute-start.15
  42.4 1.5 %collective-permute-start.23 = (bf16[192,768]{1,0:T(8,128)(2,1)S(1)}, bf16[192,768]{1,0:T(8,128)(2,1)S(1)}, u32[]{:S(2)}, u32[]{:S(2)}) collective-permute-start(bf16[192,768]{1,0:T(8,128)(2,1)S(1)} %collective-permute-done.22.refs_2_), channel_id=1, source_target_pairs={{0,4},{1,5},{2,6},{3,7},{4,0},{5,1},{6,2},{7,3},{8,12},{9,13},{10,... | collective-permute-start | bytes 884744 | tf_op jit(solution)/shard_map/ppermute | solution.py:1027
  43.9 5.1 %attend.1 = (bf16[736,192]{1,0:T(8,128)(2,1)S(1)}, bf16[736,576]{1,0:T(8,128)(2,1)S(1)}, bf16[6,368,368]{2,1,0:T(8,128)(2,1)S(1)}, bf16[736,768]{1,0:T(8,128)(2,1)S(1)}, bf16[736,768]{1,0:T(8,128)(2,1)S(1)}) custom-call(bf16[352,768]{1,0:T(8,128)(2,1)S(1)} %get-tuple-element.125.refs_0_.refs_4_, bf16[352,768]{1,0:T(8,128)(2,1)} %collective-permute-done.8.refs_1_.refs_5_, ...), custom_call_target="tpu_custom_call" | custom-call | flops 2400000000 | tf_op jit(solution)/shard_map/attend/pallas_call | solution.py:474
  49.6 1.4 collective-permute-start.21
  52.9 2.0 %order_out.1 = (bf16[768,768]{1,0:T(8,128)(2,1)S(1)}, bf16[192,768]{1,0:T(8,128)(2,1)S(1)}, bf16[736,768]{1,0:T(8,128)(2,1)S(1)}, bf16[736,768]{1,0:T(8,128)(2,1)S(1)}) custom-call(bf16[192,768]{1,0:T(8,128)(2,1)} %get-tuple-element.133.refs_0_, bf16[192,768]{1,0:T(8,128)(2,1)S(1)} %collective-permute-done.14.refs_1_, ...), custom_call_target="tpu_custom_call" | custom-call | flops 4800000000 | tf_op jit(solution)/shard_map/order_out/pallas_call | solution.py:474
  54.9 6.2 %collective-permute-done.18.refs_2_.refs_5_ = bf16[736,192]{1,0:T(8,128)(2,1)S(1)} collective-permute-done((bf16[736,192]{1,0:T(8,128)(2,1)S(1)}, bf16[736,192]{1,0:T(8,128)(2,1)S(1)}, u32[]{:S(2)}, u32[]{:S(2)}) %collective-permute-start.18) | collective-permute-done | bytes 282656 | tf_op jit(solution)/shard_map/ppermute | solution.py:1027
  61.6 1.2 collective-permute-done.17.refs_1_.refs_8_.refs_4_
  63.3 2.1 %branch_rows.1 = (bf16[736,768]{1,0:T(8,128)(2,1)S(1)}, bf16[736,768]{1,0:T(8,128)(2,1)S(1)}, f32[208,768]{1,0:T(8,128)S(1)}) custom-call(bf16[736,192]{1,0:T(8,128)(2,1)S(1)} %get-tuple-element.137.refs_0_.refs_9_.refs_3_, bf16[736,192]{1,0:T(8,128)(2,1)S(1)} %collective-permute-done.17.refs_1_.refs_8_.refs_4_, ...), custom_call_target="tpu_custom_call" | custom-call | flops 1000000 | tf_op jit(solution)/shard_map/branch_rows/pallas_call | solution.py:474
  65.5 1.7 %raise_rows.1 = (bf16[736,768]{1,0:T(8,128)(2,1)S(1)}, f32[736,768]{1,0:T(8,128)S(1)}, bf16[768,768]{1,0:T(8,128)(2,1)S(1)}, bf16[768,768]{1,0:T(8,128)(2,1)S(1)}) custom-call(bf16[736,768]{1,0:T(8,128)(2,1)S(1)} %get-tuple-element.141.refs_0_, bf16[192,768]{1,0:T(8,128)(2,1)S(1)} %get-tuple-element.128.refs_1_, ...), custom_call_target="tpu_custom_call" | custom-call | flops 1000000 | tf_op jit(solution)/shard_map/raise_rows/pallas_call | solution.py:474
  67.2 2.7 %lower_rows.1 = (bf16[368,768]{1,0:T(8,128)(2,1)S(1)}, f32[368,768]{1,0:T(8,128)S(1)}, bf16[736,768]{1,0:T(8,128)(2,1)S(1)}) custom-call(f32[736,768]{1,0:T(8,128)S(1)} %get-tuple-element.151.refs_0_, bf16[736,768]{1,0:T(8,128)(2,1)S(1)} %get-tuple-element.152.refs_1_, bf16[768,768]{1,0:T(8,128)(2,1)S(1)} %get-tuple-element.153.refs_2_, ...), custom_call_target="tpu_custom_call" | custom-call | flops 1110000000 | tf_op jit(solution)/shard_map/lower_rows/pallas_call | solution.py:474
  70.0 1.3 down_grads.1
  73.3 1.4 %up_grads.1 = (bf16[4,96,768]{2,1,0:T(8,128)(2,1)S(1)}, f32[4,96,768]{2,1,0:T(8,128)S(1)}) custom-call(bf16[736,768]{1,0:T(8,128)(2,1)S(1)} %get-tuple-element.141.refs_0_, bf16[736,768]{1,0:T(8,128)(2,1)S(1)} %get-tuple-element.200.refs_1_, bf16[736,192]{1,0:T(8,128)(2,1)S(1)} %collective-permute-done.19.refs_3_.refs_6_.refs_2_), custom_call_target="tpu_custom_call" | custom-call | flops 600000000 | tf_op jit(solution)/shard_map/up_grads/pallas_call | solution.py:474
  74.7 1.4 collective-permute-start.43
  76.1 1.7 %mlp_rows.1 = (bf16[416,768]{1,0:T(8,128)(2,1)S(1)}, f32[416,768]{1,0:T(8,128)S(1)}, f32[8,768]{1,0:T(8,128)S(1)}, bf16[736,192]{1,0:T(8,128)(2,1)S(1)}) custom-call(bf16[736,768]{1,0:T(8,128)(2,1)S(1)} %get-tuple-element.144.refs_0_, bf16[768,768]{1,0:T(8,128)(2,1)S(1)} %get-tuple-element.145.refs_1_.refs_3_, ...), custom_call_target="tpu_custom_call" | custom-call | flops 600000000 | tf_op jit(solution)/shard_map/mlp_rows/pallas_call | solution.py:474
  77.9 9.1 %collective-permute-done.38.refs_1_ = bf16[4,96,768]{2,1,0:T(8,128)(2,1)S(1)} collective-permute-done((bf16[4,96,768]{2,1,0:T(8,128)(2,1)S(1)}, bf16[4,96,768]{2,1,0:T(8,128)(2,1)S(1)}, u32[]{:S(2)}, u32[]{:S(2)}) %collective-permute-start.38) | collective-permute-done | bytes 589856 | tf_op jit(solution)/shard_map/ppermute | solution.py:1027
  87.1 4.2 %collective-permute-start.39 = (bf16[2,96,768]{2,1,0:T(8,128)(2,1)S(1)}, bf16[2,96,768]{2,1,0:T(8,128)(2,1)S(1)}, u32[]{:S(2)}, u32[]{:S(2)}) collective-permute-start(bf16[2,96,768]{2,1,0:T(8,128)(2,1)S(1)} %get-tuple-element.192), channel_id=1, source_target_pairs={{0,16},{1,17},{2,18},{3,19},{4,20},{5,21},{6,22},{7,23},{8,24},{9,... | collective-permute-start | bytes 884744 | tf_op jit(solution)/shard_map/ppermute | solution.py:1027
  91.6 1.8 %collective-permute-start.44 = (bf16[2,96,768]{2,1,0:T(8,128)(2,1)S(1)}, bf16[2,96,768]{2,1,0:T(8,128)(2,1)S(1)}, u32[]{:S(2)}, u32[]{:S(2)}) collective-permute-start(bf16[2,96,768]{2,1,0:T(8,128)(2,1)S(1)} %get-tuple-element.205), channel_id=1, source_target_pairs={{0,8},{1,9},{2,10},{3,11},{4,12},{5,13},{6,14},{7,15},{8,0},{9,1},... | collective-permute-start | bytes 884744 | tf_op jit(solution)/shard_map/ppermute | solution.py:1027
  93.4 3.9 %branch_back.1 = (f32[208,768]{1,0:T(8,128)S(1)}, bf16[736,192]{1,0:T(8,128)(2,1)S(1)}, bf16[736,192]{1,0:T(8,128)(2,1)S(1)}, bf16[4,112,384]{2,1,0:T(8,128)(2,1)S(1)}, f32[4,112,384]{2,1,0:T(8,128)S(1)}) custom-call(bf16[368,768]{1,0:T(8,128)(2,1)S(1)} %add_pair.1.refs_0_, bf16[368,768]{1,0:T(8,128)(2,1)S(1)} %collective-permute-done.28.refs_1_, ...), custom_call_target="tpu_custom_call" | custom-call | flops 400000000 | tf_op jit(solution)/shard_map/branch_back/pallas_call | solution.py:474
  97.9 3.8 %score_back.1 = (bf16[736,384]{1,0:T(8,128)(2,1)S(1)}, bf16[4,96,384]{2,1,0:T(8,128)(2,1)S(1)}, f32[4,96,384]{2,1,0:T(8,128)S(1)}) custom-call(bf16[6,368,368]{2,1,0:T(8,128)(2,1)S(1)} %get-tuple-element.149.refs_7_.refs_0_, bf16[736,576]{1,0:T(8,128)(2,1)S(1)} %get-tuple-element.150.refs_1_, bf16[736,192]{1,0:T(8,128)(2,1)S(1)} %get-tuple-element.161.refs_2_, ...), custom_call_target="tpu_custom_call" | custom-call | flops 420000000 | tf_op jit(solution)/shard_map/score_back/pallas_call | solution.py:474
  101.7 1.3 project_back.1
  103.1 1.6 %collective-permute-done.39.refs_1_ = bf16[2,96,768]{2,1,0:T(8,128)(2,1)S(1)} collective-permute-done((bf16[2,96,768]{2,1,0:T(8,128)(2,1)S(1)}, bf16[2,96,768]{2,1,0:T(8,128)(2,1)S(1)}, u32[]{:S(2)}, u32[]{:S(2)}) %collective-permute-start.39) | collective-permute-done | bytes 294944 | tf_op jit(solution)/shard_map/ppermute | solution.py:1027
  105.5 1.8 %collective-permute-start.30 = (bf16[416,768]{1,0:T(8,128)(2,1)S(1)}, bf16[416,768]{1,0:T(8,128)(2,1)S(1)}, u32[]{:S(2)}, u32[]{:S(2)}) collective-permute-start(bf16[416,768]{1,0:T(8,128)(2,1)S(1)} %get-tuple-element.168), channel_id=1, source_target_pairs={{0,2},{1,3},{2,0},{3,1},{4,6},{5,7},{6,4},{7,5},{8,10},{9,11},{10,... | collective-permute-start | bytes 1916936 | tf_op jit(solution)/shard_map/ppermute | solution.py:1027
  108.4 1.8 %collective-permute-start.32 = (bf16[2,112,384]{2,1,0:T(8,128)(2,1)S(1)}, bf16[2,112,384]{2,1,0:T(8,128)(2,1)S(1)}, u32[]{:S(2)}, u32[]{:S(2)}) collective-permute-start(bf16[2,112,384]{2,1,0:T(8,128)(2,1)S(1)} %get-tuple-element.178), channel_id=1, source_target_pairs={{0,8},{1,9},{2,10},{3,11},{4,12},{5,13},{6,14},{7,15},{8,0},{9,1},... | collective-permute-start | bytes 516104 | tf_op jit(solution)/shard_map/ppermute | solution.py:1027
  110.3 1.4 %collective-permute-start.45 = (bf16[96,768]{1,0:T(8,128)(2,1)S(1)}, bf16[96,768]{1,0:T(8,128)(2,1)S(1)}, u32[]{:S(2)}, u32[]{:S(2)}) collective-permute-start(bf16[96,768]{1,0:T(8,128)(2,1)S(1)} %get-tuple-element.207), channel_id=1, source_target_pairs={{0,16},{1,17},{2,18},{3,19},{4,20},{5,21},{6,22},{7,23},{8,24},{9,... | collective-permute-start | bytes 442376 | tf_op jit(solution)/shard_map/ppermute | solution.py:1027
  111.7 1.1 collective-permute-start.40
  112.8 3.3 %collective-permute-done.32.refs_1_ = bf16[2,112,384]{2,1,0:T(8,128)(2,1)S(1)} collective-permute-done((bf16[2,112,384]{2,1,0:T(8,128)(2,1)S(1)}, bf16[2,112,384]{2,1,0:T(8,128)(2,1)S(1)}, u32[]{:S(2)}, u32[]{:S(2)}) %collective-permute-start.32) | collective-permute-done | bytes 172064 | tf_op jit(solution)/shard_map/ppermute | solution.py:1027
  116.1 1.8 %collective-permute-start.33 = (bf16[112,384]{1,0:T(8,128)(2,1)S(1)}, bf16[112,384]{1,0:T(8,128)(2,1)S(1)}, u32[]{:S(2)}, u32[]{:S(2)}) collective-permute-start(bf16[112,384]{1,0:T(8,128)(2,1)S(1)} %get-tuple-element.181), channel_id=1, source_target_pairs={{0,16},{1,17},{2,18},{3,19},{4,20},{5,21},{6,22},{7,23},{8,24},{9,... | collective-permute-start | bytes 258056 | tf_op jit(solution)/shard_map/ppermute | solution.py:1027
  118.0 2.5 %collective-permute-start.35 = (bf16[96,384]{1,0:T(8,128)(2,1)S(1)}, bf16[96,384]{1,0:T(8,128)(2,1)S(1)}, u32[]{:S(2)}, u32[]{:S(2)}) collective-permute-start(bf16[96,384]{1,0:T(8,128)(2,1)S(1)} %get-tuple-element.185), channel_id=1, source_target_pairs={{0,8},{1,9},{2,10},{3,11},{4,12},{5,13},{6,14},{7,15},{8,0},{9,1},... | collective-permute-start | bytes 221192 | tf_op jit(solution)/shard_map/ppermute | solution.py:1027
  120.7 2.3 %collective-permute-start.37 = (bf16[96,384]{1,0:T(8,128)(2,1)S(1)}, bf16[96,384]{1,0:T(8,128)(2,1)S(1)}, u32[]{:S(2)}, u32[]{:S(2)}) collective-permute-start(bf16[96,384]{1,0:T(8,128)(2,1)S(1)} %get-tuple-element.187), channel_id=1, source_target_pairs={{0,24},{1,25},{2,26},{3,27},{4,28},{5,29},{6,30},{7,31},{8,16},{9,... | collective-permute-start | bytes 221192 | tf_op jit(solution)/shard_map/ppermute | solution.py:1027
  123.8 1.6 %collective-permute-start.46 = (bf16[64,768]{1,0:T(8,128)(2,1)S(1)}, bf16[64,768]{1,0:T(8,128)(2,1)S(1)}, u32[]{:S(2)}, u32[]{:S(2)}) collective-permute-start(bf16[64,768]{1,0:T(8,128)(2,1)S(1)} %get-tuple-element.208), channel_id=1, source_target_pairs={{0,2},{1,3},{2,0},{3,1},{4,6},{5,7},{6,4},{7,5},{8,10},{9,11},{10,... | collective-permute-start | bytes 294920 | tf_op jit(solution)/shard_map/ppermute | solution.py:1027
  125.4 2.5 %collective-permute-done.36.refs_4_ = bf16[96,384]{1,0:T(8,128)(2,1)S(1)} collective-permute-done((bf16[96,384]{1,0:T(8,128)(2,1)S(1)}, bf16[96,384]{1,0:T(8,128)(2,1)S(1)}, u32[]{:S(2)}, u32[]{:S(2)}) %collective-permute-start.36) | collective-permute-done | bytes 73760 | tf_op jit(solution)/shard_map/ppermute | solution.py:1027
  128.6 2.9 %collective-permute-start.42 = (bf16[64,768]{1,0:T(8,128)(2,1)S(1)}, bf16[64,768]{1,0:T(8,128)(2,1)S(1)}, u32[]{:S(2)}, u32[]{:S(2)}) collective-permute-start(bf16[64,768]{1,0:T(8,128)(2,1)S(1)} %get-tuple-element.199), channel_id=1, source_target_pairs={{0,2},{1,3},{2,0},{3,1},{4,6},{5,7},{6,4},{7,5},{8,10},{9,11},{10,... | collective-permute-start | bytes 294920 | tf_op jit(solution)/shard_map/ppermute | solution.py:1027
  132.0 1.4 %finish_rows.1 = (bf16[176,768]{1,0:T(8,128)(2,1)}, bf16[20,768]{1,0:T(8,128)(2,1)}, f32[176,768]{1,0:T(8,128)}, f32[20,768]{1,0:T(8,128)}) custom-call(f32[416,768]{1,0:T(8,128)S(1)} %get-tuple-element.166.refs_0_.refs_2_, bf16[416,768]{1,0:T(8,128)(2,1)S(1)} %collective-permute-done.30.refs_1_.refs_2_, f32[208,768]{1,0:T(8,128)S(1)} %get-tuple-element.169.refs_2_, ...), custom_call_target="tpu_custom_call" | custom-call | flops 1000000 | tf_op jit(solution)/shard_map/finish_rows/pallas_call | solution.py:474
  (103 shorter events, 18.5 us)
Async XLA Ops:
  2.0 6.9 %collective-permute-start.1 = (bf16[96,768]{1,0:T(8,128)(2,1)S(1)}, bf16[96,768]{1,0:T(8,128)(2,1)S(1)}, u32[]{:S(2)}, u32[]{:S(2)}) collective-permute-start(bf16[96,768]{1,0:T(8,128)(2,1)S(1)} %get-tuple-element.119), channel_id=1, source_target_pairs={{0,2},{1,3},{2,0},{3,1},{4,6},{5,7},{6,4},{7,5},{8,10},{9,11},{10,... | collective-permute-start | bytes 442376 | tf_op jit(solution)/shard_map/ppermute | solution.py:1027
  8.8 1.7 %collective-permute-start.2 = (bf16[96,768]{1,0:T(8,128)(2,1)S(1)}, bf16[96,768]{1,0:T(8,128)(2,1)S(1)}, u32[]{:S(2)}, u32[]{:S(2)}) collective-permute-start(bf16[96,768]{1,0:T(8,128)(2,1)S(1)} %collective-permute-done.1.refs_2_), channel_id=1, source_target_pairs={{0,1},{1,0},{2,3},{3,2},{4,5},{5,4},{6,7},{7,6},{8,9},{9,8},{10,11... | collective-permute-start | bytes 442376 | tf_op jit(solution)/shard_map/ppermute | solution.py:1027
  8.8 18.6 %collective-permute-start.6 = (bf16[352,768]{1,0:T(8,128)(2,1)S(1)}, bf16[352,768]{1,0:T(8,128)(2,1)S(1)}, u32[]{:S(2)}, u32[]{:S(2)}) collective-permute-start(bf16[352,768]{1,0:T(8,128)(2,1)S(1)} %get-tuple-element.125.refs_0_.refs_4_), channel_id=1, source_target_pairs={{0,2},{1,3},{2,0},{3,1},{4,6},{5,7},{6,4},{7,5},{8,10},{9,11},{10,... | collective-permute-start | bytes 1622024 | tf_op jit(solution)/shard_map/ppermute | solution.py:1027
  10.7 11.3 %collective-permute-start.4 = (bf16[112,768]{1,0:T(8,128)(2,1)S(1)}, bf16[112,768]{1,0:T(8,128)(2,1)S(1)}, u32[]{:S(2)}, u32[]{:S(2)}) collective-permute-start(bf16[112,768]{1,0:T(8,128)(2,1)S(1)} %get-tuple-element.121.refs_0_), channel_id=1, source_target_pairs={{0,16},{1,17},{2,18},{3,19},{4,20},{5,21},{6,22},{7,23},{8,24},{9,... | collective-permute-start | bytes 516104 | tf_op jit(solution)/shard_map/ppermute | solution.py:1027
  13.4 23.7 %collective-permute-start.9 = (bf16[304,768]{1,0:T(8,128)(2,1)S(1)}, bf16[304,768]{1,0:T(8,128)(2,1)S(1)}, u32[]{:S(2)}, u32[]{:S(2)}) collective-permute-start(bf16[304,768]{1,0:T(8,128)(2,1)S(1)} %get-tuple-element.126), channel_id=1, source_target_pairs={{0,4},{1,5},{2,6},{3,7},{4,0},{5,1},{6,2},{7,3},{8,12},{9,13},{10,... | collective-permute-start | bytes 1400840 | tf_op jit(solution)/shard_map/ppermute | solution.py:1027
  14.9 11.1 %collective-permute-start.3 = (bf16[112,768]{1,0:T(8,128)(2,1)S(1)}, bf16[112,768]{1,0:T(8,128)(2,1)S(1)}, u32[]{:S(2)}, u32[]{:S(2)}) collective-permute-start(bf16[112,768]{1,0:T(8,128)(2,1)S(1)} %get-tuple-element.121.refs_0_), channel_id=1, source_target_pairs={{0,8},{1,9},{2,10},{3,11},{4,12},{5,13},{6,14},{7,15},{8,0},{9,1},... | collective-permute-start | bytes 516104 | tf_op jit(solution)/shard_map/ppermute | solution.py:1027
  22.0 9.1 %collective-permute-start.11 = (bf16[112,768]{1,0:T(8,128)(2,1)S(1)}, bf16[112,768]{1,0:T(8,128)(2,1)S(1)}, u32[]{:S(2)}, u32[]{:S(2)}) collective-permute-start(bf16[112,768]{1,0:T(8,128)(2,1)S(1)} %collective-permute-done.4.refs_2_), channel_id=1, source_target_pairs={{0,8},{1,9},{2,10},{3,11},{4,12},{5,13},{6,14},{7,15},{8,0},{9,1},... | collective-permute-start | bytes 516104 | tf_op jit(solution)/shard_map/ppermute | solution.py:1027
  22.6 16.8 %collective-permute-start.13 = (bf16[192,768]{1,0:T(8,128)(2,1)S(1)}, bf16[192,768]{1,0:T(8,128)(2,1)S(1)}, u32[]{:S(2)}, u32[]{:S(2)}) collective-permute-start(bf16[192,768]{1,0:T(8,128)(2,1)S(1)} %get-tuple-element.128.refs_1_), channel_id=1, source_target_pairs={{0,16},{1,17},{2,18},{3,19},{4,20},{5,21},{6,22},{7,23},{8,24},{9,... | collective-permute-start | bytes 884744 | tf_op jit(solution)/shard_map/ppermute | solution.py:1027
  26.0 7.3 %collective-permute-start.5 = (bf16[112,768]{1,0:T(8,128)(2,1)S(1)}, bf16[112,768]{1,0:T(8,128)(2,1)S(1)}, u32[]{:S(2)}, u32[]{:S(2)}) collective-permute-start(bf16[112,768]{1,0:T(8,128)(2,1)S(1)} %collective-permute-done.3.refs_1_), channel_id=1, source_target_pairs={{0,4},{1,5},{2,6},{3,7},{4,0},{5,1},{6,2},{7,3},{8,12},{9,13},{10,... | collective-permute-start | bytes 516104 | tf_op jit(solution)/shard_map/ppermute | solution.py:1027
  27.5 9.6 %collective-permute-start.7 = (bf16[112,768]{1,0:T(8,128)(2,1)S(1)}, bf16[112,768]{1,0:T(8,128)(2,1)S(1)}, u32[]{:S(2)}, u32[]{:S(2)}) collective-permute-start(bf16[112,768]{1,0:T(8,128)(2,1)S(1)} %collective-permute-done.4.refs_2_), channel_id=1, source_target_pairs={{0,4},{1,5},{2,6},{3,7},{4,0},{5,1},{6,2},{7,3},{8,12},{9,13},{10,... | collective-permute-start | bytes 516104 | tf_op jit(solution)/shard_map/ppermute | solution.py:1027
  31.1 8.3 %collective-permute-start.12 = (bf16[112,768]{1,0:T(8,128)(2,1)S(1)}, bf16[112,768]{1,0:T(8,128)(2,1)S(1)}, u32[]{:S(2)}, u32[]{:S(2)}) collective-permute-start(bf16[112,768]{1,0:T(8,128)(2,1)S(1)} %collective-permute-done.11.refs_3_), channel_id=1, source_target_pairs={{0,4},{1,5},{2,6},{3,7},{4,0},{5,1},{6,2},{7,3},{8,12},{9,13},{10,... | collective-permute-start | bytes 516104 | tf_op jit(solution)/shard_map/ppermute | solution.py:1027
  33.4 9.0 %collective-permute-start.22 = (bf16[192,768]{1,0:T(8,128)(2,1)S(1)}, bf16[192,768]{1,0:T(8,128)(2,1)S(1)}, u32[]{:S(2)}, u32[]{:S(2)}) collective-permute-start(bf16[192,768]{1,0:T(8,128)(2,1)S(1)} %get-tuple-element.128.refs_1_), channel_id=1, source_target_pairs={{0,8},{1,9},{2,10},{3,11},{4,12},{5,13},{6,14},{7,15},{8,0},{9,1},... | collective-permute-start | bytes 884744 | tf_op jit(solution)/shard_map/ppermute | solution.py:1027
  37.0 6.8 %collective-permute-start.8 = (bf16[352,768]{1,0:T(8,128)(2,1)S(1)}, bf16[352,768]{1,0:T(8,128)(2,1)}, u32[]{:S(2)}, u32[]{:S(2)}) collective-permute-start(bf16[352,768]{1,0:T(8,128)(2,1)S(1)} %get-tuple-element.125.refs_0_.refs_4_), channel_id=1, source_target_pairs={{0,1},{1,0},{2,3},{3,2},{4,5},{5,4},{6,7},{7,6},{8,9},{9,8},{10,11... | collective-permute-start | bytes 1622024 | tf_op jit(solution)/shard_map/ppermute | solution.py:1027
  37.0 5.3 %collective-permute-start.10 = (bf16[352,768]{1,0:T(8,128)(2,1)S(1)}, bf16[352,768]{1,0:T(8,128)(2,1)}, u32[]{:S(2)}, u32[]{:S(2)}) collective-permute-start(bf16[352,768]{1,0:T(8,128)(2,1)S(1)} %collective-permute-done.6.refs_2_.refs_6_), channel_id=1, source_target_pairs={{0,1},{1,0},{2,3},{3,2},{4,5},{5,4},{6,7},{7,6},{8,9},{9,8},{10,11... | collective-permute-start | bytes 1622024 | tf_op jit(solution)/shard_map/ppermute | solution.py:1027
  40.3 8.7 %collective-permute-start.15 = (bf16[192,768]{1,0:T(8,128)(2,1)}, bf16[192,768]{1,0:T(8,128)(2,1)}, u32[]{:S(2)}, u32[]{:S(2)}) collective-permute-start(bf16[192,768]{1,0:T(8,128)(2,1)} %get-tuple-element.133.refs_0_), channel_id=1, source_target_pairs={{0,2},{1,3},{2,0},{3,1},{4,6},{5,7},{6,4},{7,5},{8,10},{9,11},{10,... | collective-permute-start | bytes 884744 | tf_op jit(solution)/shard_map/ppermute | solution.py:1027
  41.7 7.9 %collective-permute-start.20 = (bf16[192,768]{1,0:T(8,128)(2,1)S(1)}, bf16[192,768]{1,0:T(8,128)(2,1)S(1)}, u32[]{:S(2)}, u32[]{:S(2)}) collective-permute-start(bf16[192,768]{1,0:T(8,128)(2,1)S(1)} %collective-permute-done.13.refs_8_.refs_3_), channel_id=1, source_target_pairs={{0,8},{1,9},{2,10},{3,11},{4,12},{5,13},{6,14},{7,15},{8,0},{9,1},... | collective-permute-start | bytes 884744 | tf_op jit(solution)/shard_map/ppermute | solution.py:1027
  42.4 9.6 %collective-permute-start.23 = (bf16[192,768]{1,0:T(8,128)(2,1)S(1)}, bf16[192,768]{1,0:T(8,128)(2,1)S(1)}, u32[]{:S(2)}, u32[]{:S(2)}) collective-permute-start(bf16[192,768]{1,0:T(8,128)(2,1)S(1)} %collective-permute-done.22.refs_2_), channel_id=1, source_target_pairs={{0,4},{1,5},{2,6},{3,7},{4,0},{5,1},{6,2},{7,3},{8,12},{9,13},{10,... | collective-permute-start | bytes 884744 | tf_op jit(solution)/shard_map/ppermute | solution.py:1027
  49.0 3.9 %collective-permute-start.14 = (bf16[192,768]{1,0:T(8,128)(2,1)}, bf16[192,768]{1,0:T(8,128)(2,1)S(1)}, u32[]{:S(2)}, u32[]{:S(2)}) collective-permute-start(bf16[192,768]{1,0:T(8,128)(2,1)} %get-tuple-element.133.refs_0_), channel_id=1, source_target_pairs={{0,1},{1,0},{2,3},{3,2},{4,5},{5,4},{6,7},{7,6},{8,9},{9,8},{10,11... | collective-permute-start | bytes 884744 | tf_op jit(solution)/shard_map/ppermute | solution.py:1027
  49.1 3.8 %collective-permute-start.16 = (bf16[192,768]{1,0:T(8,128)(2,1)}, bf16[192,768]{1,0:T(8,128)(2,1)S(1)}, u32[]{:S(2)}, u32[]{:S(2)}) collective-permute-start(bf16[192,768]{1,0:T(8,128)(2,1)} %collective-permute-done.15.refs_2_), channel_id=1, source_target_pairs={{0,1},{1,0},{2,3},{3,2},{4,5},{5,4},{6,7},{7,6},{8,9},{9,8},{10,11... | collective-permute-start | bytes 884744 | tf_op jit(solution)/shard_map/ppermute | solution.py:1027
  49.6 12.0 %collective-permute-start.21 = (bf16[192,768]{1,0:T(8,128)(2,1)S(1)}, bf16[192,768]{1,0:T(8,128)(2,1)S(1)}, u32[]{:S(2)}, u32[]{:S(2)}) collective-permute-start(bf16[192,768]{1,0:T(8,128)(2,1)S(1)} %collective-permute-done.20.refs_4_), channel_id=1, source_target_pairs={{0,4},{1,5},{2,6},{3,7},{4,0},{5,1},{6,2},{7,3},{8,12},{9,13},{10,... | collective-permute-start | bytes 884744 | tf_op jit(solution)/shard_map/ppermute | solution.py:1027
  50.9 10.1 %collective-permute-start.18 = (bf16[736,192]{1,0:T(8,128)(2,1)S(1)}, bf16[736,192]{1,0:T(8,128)(2,1)S(1)}, u32[]{:S(2)}, u32[]{:S(2)}) collective-permute-start(bf16[736,192]{1,0:T(8,128)(2,1)S(1)} %get-tuple-element.137.refs_0_.refs_9_.refs_3_), channel_id=1, source_target_pairs={{0,2},{1,3},{2,0},{3,1},{4,6},{5,7},{6,4},{7,5},{8,10},{9,11},{10,... | collective-permute-start | bytes 847880 | tf_op jit(solution)/shard_map/ppermute | solution.py:1027
  52.0 13.5 %collective-permute-start.24 = (bf16[192,768]{1,0:T(8,128)(2,1)S(1)}, bf16[192,768]{1,0:T(8,128)(2,1)S(1)}, u32[]{:S(2)}, u32[]{:S(2)}) collective-permute-start(bf16[192,768]{1,0:T(8,128)(2,1)S(1)} %collective-permute-done.13.refs_8_.refs_3_), channel_id=1, source_target_pairs={{0,4},{1,5},{2,6},{3,7},{4,0},{5,1},{6,2},{7,3},{8,12},{9,13},{10,... | collective-permute-start | bytes 884744 | tf_op jit(solution)/shard_map/ppermute | solution.py:1027
  61.1 1.7 %collective-permute-start.17 = (bf16[736,192]{1,0:T(8,128)(2,1)S(1)}, bf16[736,192]{1,0:T(8,128)(2,1)S(1)}, u32[]{:S(2)}, u32[]{:S(2)}) collective-permute-start(bf16[736,192]{1,0:T(8,128)(2,1)S(1)} %get-tuple-element.137.refs_0_.refs_9_.refs_3_), channel_id=1, source_target_pairs={{0,1},{1,0},{2,3},{3,2},{4,5},{5,4},{6,7},{7,6},{8,9},{9,8},{10,11... | collective-permute-start | bytes 847880 | tf_op jit(solution)/shard_map/ppermute | solution.py:1027
  61.1 2.2 %collective-permute-start.19 = (bf16[736,192]{1,0:T(8,128)(2,1)S(1)}, bf16[736,192]{1,0:T(8,128)(2,1)S(1)}, u32[]{:S(2)}, u32[]{:S(2)}) collective-permute-start(bf16[736,192]{1,0:T(8,128)(2,1)S(1)} %collective-permute-done.18.refs_2_.refs_5_), channel_id=1, source_target_pairs={{0,1},{1,0},{2,3},{3,2},{4,5},{5,4},{6,7},{7,6},{8,9},{9,8},{10,11... | collective-permute-start | bytes 847880 | tf_op jit(solution)/shard_map/ppermute | solution.py:1027
  69.8 2.4 %collective-permute-start.26 = (bf16[368,768]{1,0:T(8,128)(2,1)S(1)}, bf16[368,768]{1,0:T(8,128)(2,1)S(1)}, u32[]{:S(2)}, u32[]{:S(2)}) collective-permute-start(bf16[368,768]{1,0:T(8,128)(2,1)S(1)} %get-tuple-element.155.refs_2_), channel_id=1, source_target_pairs={{0,1},{1,0},{2,3},{3,2},{4,5},{5,4},{6,7},{7,6},{8,9},{9,8},{10,11... | collective-permute-start | bytes 1695752 | tf_op jit(solution)/shard_map/ppermute | solution.py:1027
  71.3 15.7 %collective-permute-start.38 = (bf16[4,96,768]{2,1,0:T(8,128)(2,1)S(1)}, bf16[4,96,768]{2,1,0:T(8,128)(2,1)S(1)}, u32[]{:S(2)}, u32[]{:S(2)}) collective-permute-start(bf16[4,96,768]{2,1,0:T(8,128)(2,1)S(1)} %get-tuple-element.190), channel_id=1, source_target_pairs={{0,8},{1,9},{2,10},{3,11},{4,12},{5,13},{6,14},{7,15},{8,0},{9,1},... | collective-permute-start | bytes 1769480 | tf_op jit(solution)/shard_map/ppermute | solution.py:1027
  72.3 18.9 %collective-permute-start.27 = (bf16[368,768]{1,0:T(8,128)(2,1)S(1)}, bf16[368,768]{1,0:T(8,128)(2,1)S(1)}, u32[]{:S(2)}, u32[]{:S(2)}) collective-permute-start(bf16[368,768]{1,0:T(8,128)(2,1)S(1)} %add_rows.1.refs_0_), channel_id=1, source_target_pairs={{0,2},{1,3},{2,0},{3,1},{4,6},{5,7},{6,4},{7,5},{8,10},{9,11},{10,... | collective-permute-start | bytes 1695752 | tf_op jit(solution)/shard_map/ppermute | solution.py:1027
  74.7 16.8 %collective-permute-start.43 = (bf16[4,96,768]{2,1,0:T(8,128)(2,1)S(1)}, bf16[4,96,768]{2,1,0:T(8,128)(2,1)S(1)}, u32[]{:S(2)}, u32[]{:S(2)}) collective-permute-start(bf16[4,96,768]{2,1,0:T(8,128)(2,1)S(1)} %get-tuple-element.203), channel_id=1, source_target_pairs={{0,4},{1,5},{2,6},{3,7},{4,0},{5,1},{6,2},{7,3},{8,12},{9,13},{10,... | collective-permute-start | bytes 1769480 | tf_op jit(solution)/shard_map/ppermute | solution.py:1027
  77.8 27.5 %collective-permute-start.25 = (bf16[416,768]{1,0:T(8,128)(2,1)S(1)}, bf16[416,768]{1,0:T(8,128)(2,1)S(1)}, u32[]{:S(2)}, u32[]{:S(2)}) collective-permute-start(bf16[416,768]{1,0:T(8,128)(2,1)S(1)} %get-tuple-element.148), channel_id=1, source_target_pairs={{0,1},{1,0},{2,3},{3,2},{4,5},{5,4},{6,7},{7,6},{8,9},{9,8},{10,11... | collective-permute-start | bytes 1916936 | tf_op jit(solution)/shard_map/ppermute | solution.py:1027
  87.1 17.6 %collective-permute-start.39 = (bf16[2,96,768]{2,1,0:T(8,128)(2,1)S(1)}, bf16[2,96,768]{2,1,0:T(8,128)(2,1)S(1)}, u32[]{:S(2)}, u32[]{:S(2)}) collective-permute-start(bf16[2,96,768]{2,1,0:T(8,128)(2,1)S(1)} %get-tuple-element.192), channel_id=1, source_target_pairs={{0,16},{1,17},{2,18},{3,19},{4,20},{5,21},{6,22},{7,23},{8,24},{9,... | collective-permute-start | bytes 884744 | tf_op jit(solution)/shard_map/ppermute | solution.py:1027
  91.4 2.0 %collective-permute-start.28 = (bf16[368,768]{1,0:T(8,128)(2,1)S(1)}, bf16[368,768]{1,0:T(8,128)(2,1)S(1)}, u32[]{:S(2)}, u32[]{:S(2)}) collective-permute-start(bf16[368,768]{1,0:T(8,128)(2,1)S(1)} %add_pair.1.refs_0_), channel_id=1, source_target_pairs={{0,1},{1,0},{2,3},{3,2},{4,5},{5,4},{6,7},{7,6},{8,9},{9,8},{10,11... | collective-permute-start | bytes 1695752 | tf_op jit(solution)/shard_map/ppermute | solution.py:1027
  91.6 18.6 %collective-permute-start.44 = (bf16[2,96,768]{2,1,0:T(8,128)(2,1)S(1)}, bf16[2,96,768]{2,1,0:T(8,128)(2,1)S(1)}, u32[]{:S(2)}, u32[]{:S(2)}) collective-permute-start(bf16[2,96,768]{2,1,0:T(8,128)(2,1)S(1)} %get-tuple-element.205), channel_id=1, source_target_pairs={{0,8},{1,9},{2,10},{3,11},{4,12},{5,13},{6,14},{7,15},{8,0},{9,1},... | collective-permute-start | bytes 884744 | tf_op jit(solution)/shard_map/ppermute | solution.py:1027
  97.3 11.0 %collective-permute-start.31 = (bf16[4,112,384]{2,1,0:T(8,128)(2,1)S(1)}, bf16[4,112,384]{2,1,0:T(8,128)(2,1)S(1)}, u32[]{:S(2)}, u32[]{:S(2)}) collective-permute-start(bf16[4,112,384]{2,1,0:T(8,128)(2,1)S(1)} %get-tuple-element.176), channel_id=1, source_target_pairs={{0,4},{1,5},{2,6},{3,7},{4,0},{5,1},{6,2},{7,3},{8,12},{9,13},{10,... | collective-permute-start | bytes 1032200 | tf_op jit(solution)/shard_map/ppermute | solution.py:1027
  103.0 2.3 %collective-permute-start.29 = (bf16[416,768]{1,0:T(8,128)(2,1)S(1)}, bf16[416,768]{1,0:T(8,128)(2,1)S(1)}, u32[]{:S(2)}, u32[]{:S(2)}) collective-permute-start(bf16[416,768]{1,0:T(8,128)(2,1)S(1)} %get-tuple-element.165), channel_id=1, source_target_pairs={{0,1},{1,0},{2,3},{3,2},{4,5},{5,4},{6,7},{7,6},{8,9},{9,8},{10,11... | collective-permute-start | bytes 1916936 | tf_op jit(solution)/shard_map/ppermute | solution.py:1027
  104.8 13.2 %collective-permute-start.34 = (bf16[4,96,384]{2,1,0:T(8,128)(2,1)S(1)}, bf16[4,96,384]{2,1,0:T(8,128)(2,1)S(1)}, u32[]{:S(2)}, u32[]{:S(2)}) collective-permute-start(bf16[4,96,384]{2,1,0:T(8,128)(2,1)S(1)} %get-tuple-element.183), channel_id=1, source_target_pairs={{0,4},{1,5},{2,6},{3,7},{4,0},{5,1},{6,2},{7,3},{8,12},{9,13},{10,... | collective-permute-start | bytes 884744 | tf_op jit(solution)/shard_map/ppermute | solution.py:1027
  105.5 18.2 %collective-permute-start.30 = (bf16[416,768]{1,0:T(8,128)(2,1)S(1)}, bf16[416,768]{1,0:T(8,128)(2,1)S(1)}, u32[]{:S(2)}, u32[]{:S(2)}) collective-permute-start(bf16[416,768]{1,0:T(8,128)(2,1)S(1)} %get-tuple-element.168), channel_id=1, source_target_pairs={{0,2},{1,3},{2,0},{3,1},{4,6},{5,7},{6,4},{7,5},{8,10},{9,11},{10,... | collective-permute-start | bytes 1916936 | tf_op jit(solution)/shard_map/ppermute | solution.py:1027
  108.4 7.7 %collective-permute-start.32 = (bf16[2,112,384]{2,1,0:T(8,128)(2,1)S(1)}, bf16[2,112,384]{2,1,0:T(8,128)(2,1)S(1)}, u32[]{:S(2)}, u32[]{:S(2)}) collective-permute-start(bf16[2,112,384]{2,1,0:T(8,128)(2,1)S(1)} %get-tuple-element.178), channel_id=1, source_target_pairs={{0,8},{1,9},{2,10},{3,11},{4,12},{5,13},{6,14},{7,15},{8,0},{9,1},... | collective-permute-start | bytes 516104 | tf_op jit(solution)/shard_map/ppermute | solution.py:1027
  110.3 10.4 %collective-permute-start.45 = (bf16[96,768]{1,0:T(8,128)(2,1)S(1)}, bf16[96,768]{1,0:T(8,128)(2,1)S(1)}, u32[]{:S(2)}, u32[]{:S(2)}) collective-permute-start(bf16[96,768]{1,0:T(8,128)(2,1)S(1)} %get-tuple-element.207), channel_id=1, source_target_pairs={{0,16},{1,17},{2,18},{3,19},{4,20},{5,21},{6,22},{7,23},{8,24},{9,... | collective-permute-start | bytes 442376 | tf_op jit(solution)/shard_map/ppermute | solution.py:1027
  111.7 9.0 %collective-permute-start.40 = (bf16[96,768]{1,0:T(8,128)(2,1)S(1)}, bf16[96,768]{1,0:T(8,128)(2,1)S(1)}, u32[]{:S(2)}, u32[]{:S(2)}) collective-permute-start(bf16[96,768]{1,0:T(8,128)(2,1)S(1)} %get-tuple-element.195), channel_id=1, source_target_pairs={{0,4},{1,5},{2,6},{3,7},{4,0},{5,1},{6,2},{7,3},{8,12},{9,13},{10,... | collective-permute-start | bytes 442376 | tf_op jit(solution)/shard_map/ppermute | solution.py:1027
  116.1 9.3 %collective-permute-start.33 = (bf16[112,384]{1,0:T(8,128)(2,1)S(1)}, bf16[112,384]{1,0:T(8,128)(2,1)S(1)}, u32[]{:S(2)}, u32[]{:S(2)}) collective-permute-start(bf16[112,384]{1,0:T(8,128)(2,1)S(1)} %get-tuple-element.181), channel_id=1, source_target_pairs={{0,16},{1,17},{2,18},{3,19},{4,20},{5,21},{6,22},{7,23},{8,24},{9,... | collective-permute-start | bytes 258056 | tf_op jit(solution)/shard_map/ppermute | solution.py:1027
  118.0 7.4 %collective-permute-start.35 = (bf16[96,384]{1,0:T(8,128)(2,1)S(1)}, bf16[96,384]{1,0:T(8,128)(2,1)S(1)}, u32[]{:S(2)}, u32[]{:S(2)}) collective-permute-start(bf16[96,384]{1,0:T(8,128)(2,1)S(1)} %get-tuple-element.185), channel_id=1, source_target_pairs={{0,8},{1,9},{2,10},{3,11},{4,12},{5,13},{6,14},{7,15},{8,0},{9,1},... | collective-permute-start | bytes 221192 | tf_op jit(solution)/shard_map/ppermute | solution.py:1027
  120.7 7.1 %collective-permute-start.36 = (bf16[96,384]{1,0:T(8,128)(2,1)S(1)}, bf16[96,384]{1,0:T(8,128)(2,1)S(1)}, u32[]{:S(2)}, u32[]{:S(2)}) collective-permute-start(bf16[96,384]{1,0:T(8,128)(2,1)S(1)} %get-tuple-element.186), channel_id=1, source_target_pairs={{0,16},{1,17},{2,18},{3,19},{4,20},{5,21},{6,22},{7,23},{8,24},{9,... | collective-permute-start | bytes 221192 | tf_op jit(solution)/shard_map/ppermute | solution.py:1027
  120.7 7.1 %collective-permute-start.37 = (bf16[96,384]{1,0:T(8,128)(2,1)S(1)}, bf16[96,384]{1,0:T(8,128)(2,1)S(1)}, u32[]{:S(2)}, u32[]{:S(2)}) collective-permute-start(bf16[96,384]{1,0:T(8,128)(2,1)S(1)} %get-tuple-element.187), channel_id=1, source_target_pairs={{0,24},{1,25},{2,26},{3,27},{4,28},{5,29},{6,30},{7,31},{8,16},{9,... | collective-permute-start | bytes 221192 | tf_op jit(solution)/shard_map/ppermute | solution.py:1027
  123.8 7.7 %collective-permute-start.46 = (bf16[64,768]{1,0:T(8,128)(2,1)S(1)}, bf16[64,768]{1,0:T(8,128)(2,1)S(1)}, u32[]{:S(2)}, u32[]{:S(2)}) collective-permute-start(bf16[64,768]{1,0:T(8,128)(2,1)S(1)} %get-tuple-element.208), channel_id=1, source_target_pairs={{0,2},{1,3},{2,0},{3,1},{4,6},{5,7},{6,4},{7,5},{8,10},{9,11},{10,... | collective-permute-start | bytes 294920 | tf_op jit(solution)/shard_map/ppermute | solution.py:1027
  128.6 5.5 %collective-permute-start.42 = (bf16[64,768]{1,0:T(8,128)(2,1)S(1)}, bf16[64,768]{1,0:T(8,128)(2,1)S(1)}, u32[]{:S(2)}, u32[]{:S(2)}) collective-permute-start(bf16[64,768]{1,0:T(8,128)(2,1)S(1)} %get-tuple-element.199), channel_id=1, source_target_pairs={{0,2},{1,3},{2,0},{3,1},{4,6},{5,7},{6,4},{7,5},{8,10},{9,11},{10,... | collective-permute-start | bytes 294920 | tf_op jit(solution)/shard_map/ppermute | solution.py:1027
  131.5 2.6 %collective-permute-start.49 = (bf16[64,768]{1,0:T(8,128)(2,1)S(1)}, bf16[64,768]{1,0:T(8,128)(2,1)S(1)}, u32[]{:S(2)}, u32[]{:S(2)}) collective-permute-start(bf16[64,768]{1,0:T(8,128)(2,1)S(1)} %collective-permute-done.46.refs_2_), channel_id=1, source_target_pairs={{0,1},{1,0},{2,3},{3,2},{4,5},{5,4},{6,7},{7,6},{8,9},{9,8},{10,11... | collective-permute-start | bytes 294920 | tf_op jit(solution)/shard_map/ppermute | solution.py:1027
  131.5 2.6 %collective-permute-start.48 = (bf16[32,768]{1,0:T(8,128)(2,1)S(1)}, bf16[32,768]{1,0:T(8,128)(2,1)S(1)}, u32[]{:S(2)}, u32[]{:S(2)}) collective-permute-start(bf16[32,768]{1,0:T(8,128)(2,1)S(1)} %get-tuple-element.212), channel_id=1, source_target_pairs={{0,1},{1,0},{2,3},{3,2},{4,5},{5,4},{6,7},{7,6},{8,9},{9,8},{10,11... | collective-permute-start | bytes 147464 | tf_op jit(solution)/shard_map/ppermute | solution.py:1027
  132.0 3.1 %collective-permute-start.41 = (bf16[32,768]{1,0:T(8,128)(2,1)S(1)}, bf16[32,768]{1,0:T(8,128)(2,1)S(1)}, u32[]{:S(2)}, u32[]{:S(2)}) collective-permute-start(bf16[32,768]{1,0:T(8,128)(2,1)S(1)} %get-tuple-element.197), channel_id=1, source_target_pairs={{0,1},{1,0},{2,3},{3,2},{4,5},{5,4},{6,7},{7,6},{8,9},{9,8},{10,11... | collective-permute-start | bytes 147464 | tf_op jit(solution)/shard_map/ppermute | solution.py:1027
  (12 other events, 86.1 us)

commit v9 on v8

--- a/solution.py
+++ b/solution.py
@@ -593,7 +593,7 @@
 
 def attend(
     rows_0, rows_1, rows_2, rows_3, tail, ids, w_qkv, gain_rows,
-    attended, projected, probs, tokens, unit_low, rows_f,
+    attended, projected, probs, tokens, unit_low, rows_f, normed,
 ):
     place_rows(rows_f, (rows_0, rows_1, rows_2, rows_3), tail, 0)
     gain = gain_rows[0:1, :]
@@ -604,14 +604,13 @@
         row = jnp.concatenate([ids[b * 2 + m : b * 2 + m + 1, :] for b in range(4)] + [tail_ids], 1)
         row = row.astype(F32)
         bias = jnp.where(turned(row) == row, 0.0, MASKED)
-        normed = []
         for block in row_blocks(16, at):
             rows = rows_f[block, :]
             tokens[block, :] = rows.astype(BF16)
             unit = normalise(rows)[0]
             unit_low[block, :] = unit.astype(BF16)
-            normed.append((unit * gain).astype(BF16))
-        qkv = mm(jnp.concatenate(normed, 0), w_qkv[...])
+            normed[block, :] = (unit * gain).astype(BF16)
+        qkv = mm(normed[at, :], w_qkv[...])
         qkv = jnp.concatenate([qkv[:, 0:192] * SCORE_SCALE, qkv[:, 192:576]], -1).astype(BF16)
         projected[at, :] = qkv
         heads = []
@@ -808,7 +807,7 @@
 
     gain_s, gain_n = gain_rows[1:2, :], gain_rows[2:3, :]
     scale_sum = jnp.zeros((8, 768), F32)
-    for at in row_blocks(32):
+    for at in row_blocks(16):
         grown = branch[at, :].astype(F32)
         unit, scale = normalise(tokens[at, :].astype(F32) + gain_s * grown)
         pulled = work[at, :] * gain_n
@@ -1118,7 +1117,7 @@
         attend,
         [sds(736, 192), *keep(sds(736, 576), sds(6, 368, 368), sds(736, 768), sds(736, 768))],
         [*keep(*row_parts), special, image_ids.reshape(8, 88), *keep(qkv_full, gain_rows)],
-        [pltpu.VMEM((736, 768), F32)],
+        [pltpu.VMEM((736, 768), F32), pltpu.VMEM((736, 768), BF16)],
     )
     far_heads = send(attended, "x", 1)
     both_y2 = send(both_2, "y", 1)

time: 137 us -> 137 us (level)
  no operation moved by 1% of the time
where the time goes in v9:
time: 137 us; the launch traced here: 136 us
  starting transfers between devices  54.3 us (40%)
  waiting for transfers between devices  45.7 us (33%)
  Pallas kernels  35.2 us (26%)
    ppermute x50, starting transfers between devices, send(): STEPS.append(lax.ppermute(rows, ('dp', 'blk'), pairs))  54.3 us
    ppermute x50, waiting for transfers between devices, send(): STEPS.append(lax.ppermute(rows, ('dp', 'blk'), pairs))  45.7 us
    pallas_call x30, Pallas kernels, call(): pl.pallas_call(body, out_shape=tuple((pltpu.VMEM(v.value.shape, v.value.d...  35.2 us
  transfers between devices with their start and end apart: 50, of which 19 were waited for; matrix products, arithmetic and copies ran while one was open for 0% of the time, Pallas kernels for 21%

profile of v9, /device:TPU:0, one launch (start us, length us, event | category | flops | bytes accessed | tf_op | source)
XLA Modules:
  0.0 136.3 jit_solution(3516959480664086085)
XLA Ops:
  0.7 1.3 pick_pieces.1
  2.0 3.0 %collective-permute-start.1 = (bf16[96,768]{1,0:T(8,128)(2,1)S(1)}, bf16[96,768]{1,0:T(8,128)(2,1)S(1)}, u32[]{:S(2)}, u32[]{:S(2)}) collective-permute-start(bf16[96,768]{1,0:T(8,128)(2,1)S(1)} %get-tuple-element.119), channel_id=1, source_target_pairs={{0,2},{1,3},{2,0},{3,1},{4,6},{5,7},{6,4},{7,5},{8,10},{9,11},{10,... | collective-permute-start | bytes 442376 | tf_op jit(solution)/shard_map/ppermute | solution.py:1026
  5.0 1.3 collective-permute-done.refs_1_.refs_6_
  6.2 2.6 %collective-permute-done.1.refs_2_ = bf16[96,768]{1,0:T(8,128)(2,1)S(1)} collective-permute-done((bf16[96,768]{1,0:T(8,128)(2,1)S(1)}, bf16[96,768]{1,0:T(8,128)(2,1)S(1)}, u32[]{:S(2)}, u32[]{:S(2)}) %collective-permute-start.1) | collective-permute-done | bytes 147488 | tf_op jit(solution)/shard_map/ppermute | solution.py:1026
  8.8 1.7 %collective-permute-start.6 = (bf16[352,768]{1,0:T(8,128)(2,1)S(1)}, bf16[352,768]{1,0:T(8,128)(2,1)S(1)}, u32[]{:S(2)}, u32[]{:S(2)}) collective-permute-start(bf16[352,768]{1,0:T(8,128)(2,1)S(1)} %get-tuple-element.125.refs_0_.refs_4_), channel_id=1, source_target_pairs={{0,2},{1,3},{2,0},{3,1},{4,6},{5,7},{6,4},{7,5},{8,10},{9,11},{10,... | collective-permute-start | bytes 1622024 | tf_op jit(solution)/shard_map/ppermute | solution.py:1026
  10.7 2.7 %collective-permute-start.4 = (bf16[112,768]{1,0:T(8,128)(2,1)S(1)}, bf16[112,768]{1,0:T(8,128)(2,1)S(1)}, u32[]{:S(2)}, u32[]{:S(2)}) collective-permute-start(bf16[112,768]{1,0:T(8,128)(2,1)S(1)} %get-tuple-element.121.refs_0_), channel_id=1, source_target_pairs={{0,16},{1,17},{2,18},{3,19},{4,20},{5,21},{6,22},{7,23},{8,24},{9,... | collective-permute-start | bytes 516104 | tf_op jit(solution)/shard_map/ppermute | solution.py:1026
  13.4 1.5 %collective-permute-start.9 = (bf16[304,768]{1,0:T(8,128)(2,1)S(1)}, bf16[304,768]{1,0:T(8,128)(2,1)S(1)}, u32[]{:S(2)}, u32[]{:S(2)}) collective-permute-start(bf16[304,768]{1,0:T(8,128)(2,1)S(1)} %get-tuple-element.126), channel_id=1, source_target_pairs={{0,4},{1,5},{2,6},{3,7},{4,0},{5,1},{6,2},{7,3},{8,12},{9,13},{10,... | collective-permute-start | bytes 1400840 | tf_op jit(solution)/shard_map/ppermute | solution.py:1026
  14.9 1.6 %collective-permute-start.3 = (bf16[112,768]{1,0:T(8,128)(2,1)S(1)}, bf16[112,768]{1,0:T(8,128)(2,1)S(1)}, u32[]{:S(2)}, u32[]{:S(2)}) collective-permute-start(bf16[112,768]{1,0:T(8,128)(2,1)S(1)} %get-tuple-element.121.refs_0_), channel_id=1, source_target_pairs={{0,8},{1,9},{2,10},{3,11},{4,12},{5,13},{6,14},{7,15},{8,0},{9,1},... | collective-permute-start | bytes 516104 | tf_op jit(solution)/shard_map/ppermute | solution.py:1026
  16.5 5.5 %collective-permute-done.4.refs_2_ = bf16[112,768]{1,0:T(8,128)(2,1)S(1)} collective-permute-done((bf16[112,768]{1,0:T(8,128)(2,1)S(1)}, bf16[112,768]{1,0:T(8,128)(2,1)S(1)}, u32[]{:S(2)}, u32[]{:S(2)}) %collective-permute-start.4) | collective-permute-done | bytes 172064 | tf_op jit(solution)/shard_map/ppermute | solution.py:1026
  22.6 3.4 %collective-permute-start.13 = (bf16[192,768]{1,0:T(8,128)(2,1)S(1)}, bf16[192,768]{1,0:T(8,128)(2,1)S(1)}, u32[]{:S(2)}, u32[]{:S(2)}) collective-permute-start(bf16[192,768]{1,0:T(8,128)(2,1)S(1)} %get-tuple-element.128.refs_1_), channel_id=1, source_target_pairs={{0,16},{1,17},{2,18},{3,19},{4,20},{5,21},{6,22},{7,23},{8,24},{9,... | collective-permute-start | bytes 884744 | tf_op jit(solution)/shard_map/ppermute | solution.py:1026
  26.0 1.4 %collective-permute-start.5 = (bf16[112,768]{1,0:T(8,128)(2,1)S(1)}, bf16[112,768]{1,0:T(8,128)(2,1)S(1)}, u32[]{:S(2)}, u32[]{:S(2)}) collective-permute-start(bf16[112,768]{1,0:T(8,128)(2,1)S(1)} %collective-permute-done.3.refs_1_), channel_id=1, source_target_pairs={{0,4},{1,5},{2,6},{3,7},{4,0},{5,1},{6,2},{7,3},{8,12},{9,13},{10,... | collective-permute-start | bytes 516104 | tf_op jit(solution)/shard_map/ppermute | solution.py:1026
  28.1 3.0 %collective-permute-done.11.refs_3_ = bf16[112,768]{1,0:T(8,128)(2,1)S(1)} collective-permute-done((bf16[112,768]{1,0:T(8,128)(2,1)S(1)}, bf16[112,768]{1,0:T(8,128)(2,1)S(1)}, u32[]{:S(2)}, u32[]{:S(2)}) %collective-permute-start.11) | collective-permute-done | bytes 172064 | tf_op jit(solution)/shard_map/ppermute | solution.py:1026
  31.1 1.5 %collective-permute-start.12 = (bf16[112,768]{1,0:T(8,128)(2,1)S(1)}, bf16[112,768]{1,0:T(8,128)(2,1)S(1)}, u32[]{:S(2)}, u32[]{:S(2)}) collective-permute-start(bf16[112,768]{1,0:T(8,128)(2,1)S(1)} %collective-permute-done.11.refs_3_), channel_id=1, source_target_pairs={{0,4},{1,5},{2,6},{3,7},{4,0},{5,1},{6,2},{7,3},{8,12},{9,13},{10,... | collective-permute-start | bytes 516104 | tf_op jit(solution)/shard_map/ppermute | solution.py:1026
  33.4 3.7 %collective-permute-done.7.refs_6_ = bf16[112,768]{1,0:T(8,128)(2,1)S(1)} collective-permute-done((bf16[112,768]{1,0:T(8,128)(2,1)S(1)}, bf16[112,768]{1,0:T(8,128)(2,1)S(1)}, u32[]{:S(2)}, u32[]{:S(2)}) %collective-permute-start.7) | collective-permute-done | bytes 172064 | tf_op jit(solution)/shard_map/ppermute | solution.py:1026
  37.6 1.8 %collective-permute-done.13.refs_8_.refs_3_ = bf16[192,768]{1,0:T(8,128)(2,1)S(1)} collective-permute-done((bf16[192,768]{1,0:T(8,128)(2,1)S(1)}, bf16[192,768]{1,0:T(8,128)(2,1)S(1)}, u32[]{:S(2)}, u32[]{:S(2)}) %collective-permute-start.13) | collective-permute-done | bytes 294944 | tf_op jit(solution)/shard_map/ppermute | solution.py:1026
  40.3 1.3 collective-permute-start.15
  42.4 1.5 %collective-permute-start.23 = (bf16[192,768]{1,0:T(8,128)(2,1)S(1)}, bf16[192,768]{1,0:T(8,128)(2,1)S(1)}, u32[]{:S(2)}, u32[]{:S(2)}) collective-permute-start(bf16[192,768]{1,0:T(8,128)(2,1)S(1)} %collective-permute-done.22.refs_2_), channel_id=1, source_target_pairs={{0,4},{1,5},{2,6},{3,7},{4,0},{5,1},{6,2},{7,3},{8,12},{9,13},{10,... | collective-permute-start | bytes 884744 | tf_op jit(solution)/shard_map/ppermute | solution.py:1026
  43.9 5.1 %attend.1 = (bf16[736,192]{1,0:T(8,128)(2,1)S(1)}, bf16[736,576]{1,0:T(8,128)(2,1)S(1)}, bf16[6,368,368]{2,1,0:T(8,128)(2,1)S(1)}, bf16[736,768]{1,0:T(8,128)(2,1)S(1)}, bf16[736,768]{1,0:T(8,128)(2,1)S(1)}) custom-call(bf16[352,768]{1,0:T(8,128)(2,1)S(1)} %get-tuple-element.125.refs_0_.refs_4_, bf16[352,768]{1,0:T(8,128)(2,1)} %collective-permute-done.8.refs_1_.refs_5_, ...), custom_call_target="tpu_custom_call" | custom-call | flops 2400000000 | tf_op jit(solution)/shard_map/attend/pallas_call | solution.py:474
  49.6 1.4 collective-permute-start.21
  52.9 2.0 %order_out.1 = (bf16[768,768]{1,0:T(8,128)(2,1)S(1)}, bf16[192,768]{1,0:T(8,128)(2,1)S(1)}, bf16[736,768]{1,0:T(8,128)(2,1)S(1)}, bf16[736,768]{1,0:T(8,128)(2,1)S(1)}) custom-call(bf16[192,768]{1,0:T(8,128)(2,1)} %get-tuple-element.133.refs_0_, bf16[192,768]{1,0:T(8,128)(2,1)S(1)} %collective-permute-done.14.refs_1_, ...), custom_call_target="tpu_custom_call" | custom-call | flops 4800000000 | tf_op jit(solution)/shard_map/order_out/pallas_call | solution.py:474
  54.9 6.2 %collective-permute-done.18.refs_2_.refs_5_ = bf16[736,192]{1,0:T(8,128)(2,1)S(1)} collective-permute-done((bf16[736,192]{1,0:T(8,128)(2,1)S(1)}, bf16[736,192]{1,0:T(8,128)(2,1)S(1)}, u32[]{:S(2)}, u32[]{:S(2)}) %collective-permute-start.18) | collective-permute-done | bytes 282656 | tf_op jit(solution)/shard_map/ppermute | solution.py:1026
  61.6 1.2 collective-permute-done.17.refs_1_.refs_8_.refs_4_
  63.3 2.1 %branch_rows.1 = (bf16[736,768]{1,0:T(8,128)(2,1)S(1)}, bf16[736,768]{1,0:T(8,128)(2,1)S(1)}, f32[208,768]{1,0:T(8,128)S(1)}) custom-call(bf16[736,192]{1,0:T(8,128)(2,1)S(1)} %get-tuple-element.137.refs_0_.refs_9_.refs_3_, bf16[736,192]{1,0:T(8,128)(2,1)S(1)} %collective-permute-done.17.refs_1_.refs_8_.refs_4_, ...), custom_call_target="tpu_custom_call" | custom-call | flops 1000000 | tf_op jit(solution)/shard_map/branch_rows/pallas_call | solution.py:474
  65.5 1.7 %raise_rows.1 = (bf16[736,768]{1,0:T(8,128)(2,1)S(1)}, f32[736,768]{1,0:T(8,128)S(1)}, bf16[768,768]{1,0:T(8,128)(2,1)S(1)}, bf16[768,768]{1,0:T(8,128)(2,1)S(1)}) custom-call(bf16[736,768]{1,0:T(8,128)(2,1)S(1)} %get-tuple-element.141.refs_0_, bf16[192,768]{1,0:T(8,128)(2,1)S(1)} %get-tuple-element.128.refs_1_, ...), custom_call_target="tpu_custom_call" | custom-call | flops 1000000 | tf_op jit(solution)/shard_map/raise_rows/pallas_call | solution.py:474
  67.2 2.7 %lower_rows.1 = (bf16[368,768]{1,0:T(8,128)(2,1)S(1)}, f32[368,768]{1,0:T(8,128)S(1)}, bf16[736,768]{1,0:T(8,128)(2,1)S(1)}) custom-call(f32[736,768]{1,0:T(8,128)S(1)} %get-tuple-element.151.refs_0_, bf16[736,768]{1,0:T(8,128)(2,1)S(1)} %get-tuple-element.152.refs_1_, bf16[768,768]{1,0:T(8,128)(2,1)S(1)} %get-tuple-element.153.refs_2_, ...), custom_call_target="tpu_custom_call" | custom-call | flops 1110000000 | tf_op jit(solution)/shard_map/lower_rows/pallas_call | solution.py:474
  70.0 1.3 down_grads.1
  73.3 1.4 %up_grads.1 = (bf16[4,96,768]{2,1,0:T(8,128)(2,1)S(1)}, f32[4,96,768]{2,1,0:T(8,128)S(1)}) custom-call(bf16[736,768]{1,0:T(8,128)(2,1)S(1)} %get-tuple-element.141.refs_0_, bf16[736,768]{1,0:T(8,128)(2,1)S(1)} %get-tuple-element.200.refs_1_, bf16[736,192]{1,0:T(8,128)(2,1)S(1)} %collective-permute-done.19.refs_3_.refs_6_.refs_2_), custom_call_target="tpu_custom_call" | custom-call | flops 600000000 | tf_op jit(solution)/shard_map/up_grads/pallas_call | solution.py:474
  74.7 1.4 collective-permute-start.43
  76.1 1.7 %mlp_rows.1 = (bf16[416,768]{1,0:T(8,128)(2,1)S(1)}, f32[416,768]{1,0:T(8,128)S(1)}, f32[8,768]{1,0:T(8,128)S(1)}, bf16[736,192]{1,0:T(8,128)(2,1)S(1)}) custom-call(bf16[736,768]{1,0:T(8,128)(2,1)S(1)} %get-tuple-element.144.refs_0_, bf16[768,768]{1,0:T(8,128)(2,1)S(1)} %get-tuple-element.145.refs_1_.refs_3_, ...), custom_call_target="tpu_custom_call" | custom-call | flops 600000000 | tf_op jit(solution)/shard_map/mlp_rows/pallas_call | solution.py:474
  77.9 9.1 %collective-permute-done.38.refs_1_ = bf16[4,96,768]{2,1,0:T(8,128)(2,1)S(1)} collective-permute-done((bf16[4,96,768]{2,1,0:T(8,128)(2,1)S(1)}, bf16[4,96,768]{2,1,0:T(8,128)(2,1)S(1)}, u32[]{:S(2)}, u32[]{:S(2)}) %collective-permute-start.38) | collective-permute-done | bytes 589856 | tf_op jit(solution)/shard_map/ppermute | solution.py:1026
  87.1 4.2 %collective-permute-start.39 = (bf16[2,96,768]{2,1,0:T(8,128)(2,1)S(1)}, bf16[2,96,768]{2,1,0:T(8,128)(2,1)S(1)}, u32[]{:S(2)}, u32[]{:S(2)}) collective-permute-start(bf16[2,96,768]{2,1,0:T(8,128)(2,1)S(1)} %get-tuple-element.192), channel_id=1, source_target_pairs={{0,16},{1,17},{2,18},{3,19},{4,20},{5,21},{6,22},{7,23},{8,24},{9,... | collective-permute-start | bytes 884744 | tf_op jit(solution)/shard_map/ppermute | solution.py:1026
  91.6 1.8 %collective-permute-start.44 = (bf16[2,96,768]{2,1,0:T(8,128)(2,1)S(1)}, bf16[2,96,768]{2,1,0:T(8,128)(2,1)S(1)}, u32[]{:S(2)}, u32[]{:S(2)}) collective-permute-start(bf16[2,96,768]{2,1,0:T(8,128)(2,1)S(1)} %get-tuple-element.205), channel_id=1, source_target_pairs={{0,8},{1,9},{2,10},{3,11},{4,12},{5,13},{6,14},{7,15},{8,0},{9,1},... | collective-permute-start | bytes 884744 | tf_op jit(solution)/shard_map/ppermute | solution.py:1026
  93.4 3.9 %branch_back.1 = (f32[208,768]{1,0:T(8,128)S(1)}, bf16[736,192]{1,0:T(8,128)(2,1)S(1)}, bf16[736,192]{1,0:T(8,128)(2,1)S(1)}, bf16[4,112,384]{2,1,0:T(8,128)(2,1)S(1)}, f32[4,112,384]{2,1,0:T(8,128)S(1)}) custom-call(bf16[368,768]{1,0:T(8,128)(2,1)S(1)} %add_pair.1.refs_0_, bf16[368,768]{1,0:T(8,128)(2,1)S(1)} %collective-permute-done.28.refs_1_, ...), custom_call_target="tpu_custom_call" | custom-call | flops 400000000 | tf_op jit(solution)/shard_map/branch_back/pallas_call | solution.py:474
  97.9 3.8 %score_back.1 = (bf16[736,384]{1,0:T(8,128)(2,1)S(1)}, bf16[4,96,384]{2,1,0:T(8,128)(2,1)S(1)}, f32[4,96,384]{2,1,0:T(8,128)S(1)}) custom-call(bf16[6,368,368]{2,1,0:T(8,128)(2,1)S(1)} %get-tuple-element.149.refs_7_.refs_0_, bf16[736,576]{1,0:T(8,128)(2,1)S(1)} %get-tuple-element.150.refs_1_, bf16[736,192]{1,0:T(8,128)(2,1)S(1)} %get-tuple-element.161.refs_2_, ...), custom_call_target="tpu_custom_call" | custom-call | flops 420000000 | tf_op jit(solution)/shard_map/score_back/pallas_call | solution.py:474
  101.7 1.3 project_back.1
  103.1 1.6 %collective-permute-done.39.refs_1_ = bf16[2,96,768]{2,1,0:T(8,128)(2,1)S(1)} collective-permute-done((bf16[2,96,768]{2,1,0:T(8,128)(2,1)S(1)}, bf16[2,96,768]{2,1,0:T(8,128)(2,1)S(1)}, u32[]{:S(2)}, u32[]{:S(2)}) %collective-permute-start.39) | collective-permute-done | bytes 294944 | tf_op jit(solution)/shard_map/ppermute | solution.py:1026
  105.5 1.8 %collective-permute-start.30 = (bf16[416,768]{1,0:T(8,128)(2,1)S(1)}, bf16[416,768]{1,0:T(8,128)(2,1)S(1)}, u32[]{:S(2)}, u32[]{:S(2)}) collective-permute-start(bf16[416,768]{1,0:T(8,128)(2,1)S(1)} %get-tuple-element.168), channel_id=1, source_target_pairs={{0,2},{1,3},{2,0},{3,1},{4,6},{5,7},{6,4},{7,5},{8,10},{9,11},{10,... | collective-permute-start | bytes 1916936 | tf_op jit(solution)/shard_map/ppermute | solution.py:1026
  108.4 1.8 %collective-permute-start.32 = (bf16[2,112,384]{2,1,0:T(8,128)(2,1)S(1)}, bf16[2,112,384]{2,1,0:T(8,128)(2,1)S(1)}, u32[]{:S(2)}, u32[]{:S(2)}) collective-permute-start(bf16[2,112,384]{2,1,0:T(8,128)(2,1)S(1)} %get-tuple-element.178), channel_id=1, source_target_pairs={{0,8},{1,9},{2,10},{3,11},{4,12},{5,13},{6,14},{7,15},{8,0},{9,1},... | collective-permute-start | bytes 516104 | tf_op jit(solution)/shard_map/ppermute | solution.py:1026
  110.3 1.4 %collective-permute-start.45 = (bf16[96,768]{1,0:T(8,128)(2,1)S(1)}, bf16[96,768]{1,0:T(8,128)(2,1)S(1)}, u32[]{:S(2)}, u32[]{:S(2)}) collective-permute-start(bf16[96,768]{1,0:T(8,128)(2,1)S(1)} %get-tuple-element.207), channel_id=1, source_target_pairs={{0,16},{1,17},{2,18},{3,19},{4,20},{5,21},{6,22},{7,23},{8,24},{9,... | collective-permute-start | bytes 442376 | tf_op jit(solution)/shard_map/ppermute | solution.py:1026
  111.7 1.1 collective-permute-start.40
  112.8 3.3 %collective-permute-done.32.refs_1_ = bf16[2,112,384]{2,1,0:T(8,128)(2,1)S(1)} collective-permute-done((bf16[2,112,384]{2,1,0:T(8,128)(2,1)S(1)}, bf16[2,112,384]{2,1,0:T(8,128)(2,1)S(1)}, u32[]{:S(2)}, u32[]{:S(2)}) %collective-permute-start.32) | collective-permute-done | bytes 172064 | tf_op jit(solution)/shard_map/ppermute | solution.py:1026
  116.1 1.8 %collective-permute-start.33 = (bf16[112,384]{1,0:T(8,128)(2,1)S(1)}, bf16[112,384]{1,0:T(8,128)(2,1)S(1)}, u32[]{:S(2)}, u32[]{:S(2)}) collective-permute-start(bf16[112,384]{1,0:T(8,128)(2,1)S(1)} %get-tuple-element.181), channel_id=1, source_target_pairs={{0,16},{1,17},{2,18},{3,19},{4,20},{5,21},{6,22},{7,23},{8,24},{9,... | collective-permute-start | bytes 258056 | tf_op jit(solution)/shard_map/ppermute | solution.py:1026
  118.0 2.5 %collective-permute-start.35 = (bf16[96,384]{1,0:T(8,128)(2,1)S(1)}, bf16[96,384]{1,0:T(8,128)(2,1)S(1)}, u32[]{:S(2)}, u32[]{:S(2)}) collective-permute-start(bf16[96,384]{1,0:T(8,128)(2,1)S(1)} %get-tuple-element.185), channel_id=1, source_target_pairs={{0,8},{1,9},{2,10},{3,11},{4,12},{5,13},{6,14},{7,15},{8,0},{9,1},... | collective-permute-start | bytes 221192 | tf_op jit(solution)/shard_map/ppermute | solution.py:1026
  120.7 2.3 %collective-permute-start.37 = (bf16[96,384]{1,0:T(8,128)(2,1)S(1)}, bf16[96,384]{1,0:T(8,128)(2,1)S(1)}, u32[]{:S(2)}, u32[]{:S(2)}) collective-permute-start(bf16[96,384]{1,0:T(8,128)(2,1)S(1)} %get-tuple-element.187), channel_id=1, source_target_pairs={{0,24},{1,25},{2,26},{3,27},{4,28},{5,29},{6,30},{7,31},{8,16},{9,... | collective-permute-start | bytes 221192 | tf_op jit(solution)/shard_map/ppermute | solution.py:1026
  123.8 1.6 %collective-permute-start.46 = (bf16[64,768]{1,0:T(8,128)(2,1)S(1)}, bf16[64,768]{1,0:T(8,128)(2,1)S(1)}, u32[]{:S(2)}, u32[]{:S(2)}) collective-permute-start(bf16[64,768]{1,0:T(8,128)(2,1)S(1)} %get-tuple-element.208), channel_id=1, source_target_pairs={{0,2},{1,3},{2,0},{3,1},{4,6},{5,7},{6,4},{7,5},{8,10},{9,11},{10,... | collective-permute-start | bytes 294920 | tf_op jit(solution)/shard_map/ppermute | solution.py:1026
  125.4 2.5 %collective-permute-done.36.refs_4_ = bf16[96,384]{1,0:T(8,128)(2,1)S(1)} collective-permute-done((bf16[96,384]{1,0:T(8,128)(2,1)S(1)}, bf16[96,384]{1,0:T(8,128)(2,1)S(1)}, u32[]{:S(2)}, u32[]{:S(2)}) %collective-permute-start.36) | collective-permute-done | bytes 73760 | tf_op jit(solution)/shard_map/ppermute | solution.py:1026
  128.6 2.9 %collective-permute-start.42 = (bf16[64,768]{1,0:T(8,128)(2,1)S(1)}, bf16[64,768]{1,0:T(8,128)(2,1)S(1)}, u32[]{:S(2)}, u32[]{:S(2)}) collective-permute-start(bf16[64,768]{1,0:T(8,128)(2,1)S(1)} %get-tuple-element.199), channel_id=1, source_target_pairs={{0,2},{1,3},{2,0},{3,1},{4,6},{5,7},{6,4},{7,5},{8,10},{9,11},{10,... | collective-permute-start | bytes 294920 | tf_op jit(solution)/shard_map/ppermute | solution.py:1026
  132.0 1.4 %finish_rows.1 = (bf16[176,768]{1,0:T(8,128)(2,1)}, bf16[20,768]{1,0:T(8,128)(2,1)}, f32[176,768]{1,0:T(8,128)}, f32[20,768]{1,0:T(8,128)}) custom-call(f32[416,768]{1,0:T(8,128)S(1)} %get-tuple-element.166.refs_0_.refs_2_, bf16[416,768]{1,0:T(8,128)(2,1)S(1)} %collective-permute-done.30.refs_1_.refs_2_, f32[208,768]{1,0:T(8,128)S(1)} %get-tuple-element.169.refs_2_, ...), custom_call_target="tpu_custom_call" | custom-call | flops 1000000 | tf_op jit(solution)/shard_map/finish_rows/pallas_call | solution.py:474
  (103 shorter events, 18.5 us)
Async XLA Ops:
  2.0 6.9 %collective-permute-start.1 = (bf16[96,768]{1,0:T(8,128)(2,1)S(1)}, bf16[96,768]{1,0:T(8,128)(2,1)S(1)}, u32[]{:S(2)}, u32[]{:S(2)}) collective-permute-start(bf16[96,768]{1,0:T(8,128)(2,1)S(1)} %get-tuple-element.119), channel_id=1, source_target_pairs={{0,2},{1,3},{2,0},{3,1},{4,6},{5,7},{6,4},{7,5},{8,10},{9,11},{10,... | collective-permute-start | bytes 442376 | tf_op jit(solution)/shard_map/ppermute | solution.py:1026
  8.8 1.7 %collective-permute-start.2 = (bf16[96,768]{1,0:T(8,128)(2,1)S(1)}, bf16[96,768]{1,0:T(8,128)(2,1)S(1)}, u32[]{:S(2)}, u32[]{:S(2)}) collective-permute-start(bf16[96,768]{1,0:T(8,128)(2,1)S(1)} %collective-permute-done.1.refs_2_), channel_id=1, source_target_pairs={{0,1},{1,0},{2,3},{3,2},{4,5},{5,4},{6,7},{7,6},{8,9},{9,8},{10,11... | collective-permute-start | bytes 442376 | tf_op jit(solution)/shard_map/ppermute | solution.py:1026
  8.8 18.6 %collective-permute-start.6 = (bf16[352,768]{1,0:T(8,128)(2,1)S(1)}, bf16[352,768]{1,0:T(8,128)(2,1)S(1)}, u32[]{:S(2)}, u32[]{:S(2)}) collective-permute-start(bf16[352,768]{1,0:T(8,128)(2,1)S(1)} %get-tuple-element.125.refs_0_.refs_4_), channel_id=1, source_target_pairs={{0,2},{1,3},{2,0},{3,1},{4,6},{5,7},{6,4},{7,5},{8,10},{9,11},{10,... | collective-permute-start | bytes 1622024 | tf_op jit(solution)/shard_map/ppermute | solution.py:1026
  10.7 11.3 %collective-permute-start.4 = (bf16[112,768]{1,0:T(8,128)(2,1)S(1)}, bf16[112,768]{1,0:T(8,128)(2,1)S(1)}, u32[]{:S(2)}, u32[]{:S(2)}) collective-permute-start(bf16[112,768]{1,0:T(8,128)(2,1)S(1)} %get-tuple-element.121.refs_0_), channel_id=1, source_target_pairs={{0,16},{1,17},{2,18},{3,19},{4,20},{5,21},{6,22},{7,23},{8,24},{9,... | collective-permute-start | bytes 516104 | tf_op jit(solution)/shard_map/ppermute | solution.py:1026
  13.4 23.7 %collective-permute-start.9 = (bf16[304,768]{1,0:T(8,128)(2,1)S(1)}, bf16[304,768]{1,0:T(8,128)(2,1)S(1)}, u32[]{:S(2)}, u32[]{:S(2)}) collective-permute-start(bf16[304,768]{1,0:T(8,128)(2,1)S(1)} %get-tuple-element.126), channel_id=1, source_target_pairs={{0,4},{1,5},{2,6},{3,7},{4,0},{5,1},{6,2},{7,3},{8,12},{9,13},{10,... | collective-permute-start | bytes 1400840 | tf_op jit(solution)/shard_map/ppermute | solution.py:1026
  14.9 11.1 %collective-permute-start.3 = (bf16[112,768]{1,0:T(8,128)(2,1)S(1)}, bf16[112,768]{1,0:T(8,128)(2,1)S(1)}, u32[]{:S(2)}, u32[]{:S(2)}) collective-permute-start(bf16[112,768]{1,0:T(8,128)(2,1)S(1)} %get-tuple-element.121.refs_0_), channel_id=1, source_target_pairs={{0,8},{1,9},{2,10},{3,11},{4,12},{5,13},{6,14},{7,15},{8,0},{9,1},... | collective-permute-start | bytes 516104 | tf_op jit(solution)/shard_map/ppermute | solution.py:1026
  22.0 9.1 %collective-permute-start.11 = (bf16[112,768]{1,0:T(8,128)(2,1)S(1)}, bf16[112,768]{1,0:T(8,128)(2,1)S(1)}, u32[]{:S(2)}, u32[]{:S(2)}) collective-permute-start(bf16[112,768]{1,0:T(8,128)(2,1)S(1)} %collective-permute-done.4.refs_2_), channel_id=1, source_target_pairs={{0,8},{1,9},{2,10},{3,11},{4,12},{5,13},{6,14},{7,15},{8,0},{9,1},... | collective-permute-start | bytes 516104 | tf_op jit(solution)/shard_map/ppermute | solution.py:1026
  22.6 16.8 %collective-permute-start.13 = (bf16[192,768]{1,0:T(8,128)(2,1)S(1)}, bf16[192,768]{1,0:T(8,128)(2,1)S(1)}, u32[]{:S(2)}, u32[]{:S(2)}) collective-permute-start(bf16[192,768]{1,0:T(8,128)(2,1)S(1)} %get-tuple-element.128.refs_1_), channel_id=1, source_target_pairs={{0,16},{1,17},{2,18},{3,19},{4,20},{5,21},{6,22},{7,23},{8,24},{9,... | collective-permute-start | bytes 884744 | tf_op jit(solution)/shard_map/ppermute | solution.py:1026
  26.0 7.3 %collective-permute-start.5 = (bf16[112,768]{1,0:T(8,128)(2,1)S(1)}, bf16[112,768]{1,0:T(8,128)(2,1)S(1)}, u32[]{:S(2)}, u32[]{:S(2)}) collective-permute-start(bf16[112,768]{1,0:T(8,128)(2,1)S(1)} %collective-permute-done.3.refs_1_), channel_id=1, source_target_pairs={{0,4},{1,5},{2,6},{3,7},{4,0},{5,1},{6,2},{7,3},{8,12},{9,13},{10,... | collective-permute-start | bytes 516104 | tf_op jit(solution)/shard_map/ppermute | solution.py:1026
  27.5 9.6 %collective-permute-start.7 = (bf16[112,768]{1,0:T(8,128)(2,1)S(1)}, bf16[112,768]{1,0:T(8,128)(2,1)S(1)}, u32[]{:S(2)}, u32[]{:S(2)}) collective-permute-start(bf16[112,768]{1,0:T(8,128)(2,1)S(1)} %collective-permute-done.4.refs_2_), channel_id=1, source_target_pairs={{0,4},{1,5},{2,6},{3,7},{4,0},{5,1},{6,2},{7,3},{8,12},{9,13},{10,... | collective-permute-start | bytes 516104 | tf_op jit(solution)/shard_map/ppermute | solution.py:1026
  31.1 8.3 %collective-permute-start.12 = (bf16[112,768]{1,0:T(8,128)(2,1)S(1)}, bf16[112,768]{1,0:T(8,128)(2,1)S(1)}, u32[]{:S(2)}, u32[]{:S(2)}) collective-permute-start(bf16[112,768]{1,0:T(8,128)(2,1)S(1)} %collective-permute-done.11.refs_3_), channel_id=1, source_target_pairs={{0,4},{1,5},{2,6},{3,7},{4,0},{5,1},{6,2},{7,3},{8,12},{9,13},{10,... | collective-permute-start | bytes 516104 | tf_op jit(solution)/shard_map/ppermute | solution.py:1026
  33.4 9.0 %collective-permute-start.22 = (bf16[192,768]{1,0:T(8,128)(2,1)S(1)}, bf16[192,768]{1,0:T(8,128)(2,1)S(1)}, u32[]{:S(2)}, u32[]{:S(2)}) collective-permute-start(bf16[192,768]{1,0:T(8,128)(2,1)S(1)} %get-tuple-element.128.refs_1_), channel_id=1, source_target_pairs={{0,8},{1,9},{2,10},{3,11},{4,12},{5,13},{6,14},{7,15},{8,0},{9,1},... | collective-permute-start | bytes 884744 | tf_op jit(solution)/shard_map/ppermute | solution.py:1026
  37.0 6.8 %collective-permute-start.8 = (bf16[352,768]{1,0:T(8,128)(2,1)S(1)}, bf16[352,768]{1,0:T(8,128)(2,1)}, u32[]{:S(2)}, u32[]{:S(2)}) collective-permute-start(bf16[352,768]{1,0:T(8,128)(2,1)S(1)} %get-tuple-element.125.refs_0_.refs_4_), channel_id=1, source_target_pairs={{0,1},{1,0},{2,3},{3,2},{4,5},{5,4},{6,7},{7,6},{8,9},{9,8},{10,11... | collective-permute-start | bytes 1622024 | tf_op jit(solution)/shard_map/ppermute | solution.py:1026
  37.0 5.3 %collective-permute-start.10 = (bf16[352,768]{1,0:T(8,128)(2,1)S(1)}, bf16[352,768]{1,0:T(8,128)(2,1)}, u32[]{:S(2)}, u32[]{:S(2)}) collective-permute-start(bf16[352,768]{1,0:T(8,128)(2,1)S(1)} %collective-permute-done.6.refs_2_.refs_6_), channel_id=1, source_target_pairs={{0,1},{1,0},{2,3},{3,2},{4,5},{5,4},{6,7},{7,6},{8,9},{9,8},{10,11... | collective-permute-start | bytes 1622024 | tf_op jit(solution)/shard_map/ppermute | solution.py:1026
  40.3 8.7 %collective-permute-start.15 = (bf16[192,768]{1,0:T(8,128)(2,1)}, bf16[192,768]{1,0:T(8,128)(2,1)}, u32[]{:S(2)}, u32[]{:S(2)}) collective-permute-start(bf16[192,768]{1,0:T(8,128)(2,1)} %get-tuple-element.133.refs_0_), channel_id=1, source_target_pairs={{0,2},{1,3},{2,0},{3,1},{4,6},{5,7},{6,4},{7,5},{8,10},{9,11},{10,... | collective-permute-start | bytes 884744 | tf_op jit(solution)/shard_map/ppermute | solution.py:1026
  41.7 7.9 %collective-permute-start.20 = (bf16[192,768]{1,0:T(8,128)(2,1)S(1)}, bf16[192,768]{1,0:T(8,128)(2,1)S(1)}, u32[]{:S(2)}, u32[]{:S(2)}) collective-permute-start(bf16[192,768]{1,0:T(8,128)(2,1)S(1)} %collective-permute-done.13.refs_8_.refs_3_), channel_id=1, source_target_pairs={{0,8},{1,9},{2,10},{3,11},{4,12},{5,13},{6,14},{7,15},{8,0},{9,1},... | collective-permute-start | bytes 884744 | tf_op jit(solution)/shard_map/ppermute | solution.py:1026
  42.4 9.6 %collective-permute-start.23 = (bf16[192,768]{1,0:T(8,128)(2,1)S(1)}, bf16[192,768]{1,0:T(8,128)(2,1)S(1)}, u32[]{:S(2)}, u32[]{:S(2)}) collective-permute-start(bf16[192,768]{1,0:T(8,128)(2,1)S(1)} %collective-permute-done.22.refs_2_), channel_id=1, source_target_pairs={{0,4},{1,5},{2,6},{3,7},{4,0},{5,1},{6,2},{7,3},{8,12},{9,13},{10,... | collective-permute-start | bytes 884744 | tf_op jit(solution)/shard_map/ppermute | solution.py:1026
  49.0 3.9 %collective-permute-start.14 = (bf16[192,768]{1,0:T(8,128)(2,1)}, bf16[192,768]{1,0:T(8,128)(2,1)S(1)}, u32[]{:S(2)}, u32[]{:S(2)}) collective-permute-start(bf16[192,768]{1,0:T(8,128)(2,1)} %get-tuple-element.133.refs_0_), channel_id=1, source_target_pairs={{0,1},{1,0},{2,3},{3,2},{4,5},{5,4},{6,7},{7,6},{8,9},{9,8},{10,11... | collective-permute-start | bytes 884744 | tf_op jit(solution)/shard_map/ppermute | solution.py:1026
  49.1 3.8 %collective-permute-start.16 = (bf16[192,768]{1,0:T(8,128)(2,1)}, bf16[192,768]{1,0:T(8,128)(2,1)S(1)}, u32[]{:S(2)}, u32[]{:S(2)}) collective-permute-start(bf16[192,768]{1,0:T(8,128)(2,1)} %collective-permute-done.15.refs_2_), channel_id=1, source_target_pairs={{0,1},{1,0},{2,3},{3,2},{4,5},{5,4},{6,7},{7,6},{8,9},{9,8},{10,11... | collective-permute-start | bytes 884744 | tf_op jit(solution)/shard_map/ppermute | solution.py:1026
  49.6 12.0 %collective-permute-start.21 = (bf16[192,768]{1,0:T(8,128)(2,1)S(1)}, bf16[192,768]{1,0:T(8,128)(2,1)S(1)}, u32[]{:S(2)}, u32[]{:S(2)}) collective-permute-start(bf16[192,768]{1,0:T(8,128)(2,1)S(1)} %collective-permute-done.20.refs_4_), channel_id=1, source_target_pairs={{0,4},{1,5},{2,6},{3,7},{4,0},{5,1},{6,2},{7,3},{8,12},{9,13},{10,... | collective-permute-start | bytes 884744 | tf_op jit(solution)/shard_map/ppermute | solution.py:1026
  50.9 10.1 %collective-permute-start.18 = (bf16[736,192]{1,0:T(8,128)(2,1)S(1)}, bf16[736,192]{1,0:T(8,128)(2,1)S(1)}, u32[]{:S(2)}, u32[]{:S(2)}) collective-permute-start(bf16[736,192]{1,0:T(8,128)(2,1)S(1)} %get-tuple-element.137.refs_0_.refs_9_.refs_3_), channel_id=1, source_target_pairs={{0,2},{1,3},{2,0},{3,1},{4,6},{5,7},{6,4},{7,5},{8,10},{9,11},{10,... | collective-permute-start | bytes 847880 | tf_op jit(solution)/shard_map/ppermute | solution.py:1026
  52.0 13.5 %collective-permute-start.24 = (bf16[192,768]{1,0:T(8,128)(2,1)S(1)}, bf16[192,768]{1,0:T(8,128)(2,1)S(1)}, u32[]{:S(2)}, u32[]{:S(2)}) collective-permute-start(bf16[192,768]{1,0:T(8,128)(2,1)S(1)} %collective-permute-done.13.refs_8_.refs_3_), channel_id=1, source_target_pairs={{0,4},{1,5},{2,6},{3,7},{4,0},{5,1},{6,2},{7,3},{8,12},{9,13},{10,... | collective-permute-start | bytes 884744 | tf_op jit(solution)/shard_map/ppermute | solution.py:1026
  61.1 1.7 %collective-permute-start.17 = (bf16[736,192]{1,0:T(8,128)(2,1)S(1)}, bf16[736,192]{1,0:T(8,128)(2,1)S(1)}, u32[]{:S(2)}, u32[]{:S(2)}) collective-permute-start(bf16[736,192]{1,0:T(8,128)(2,1)S(1)} %get-tuple-element.137.refs_0_.refs_9_.refs_3_), channel_id=1, source_target_pairs={{0,1},{1,0},{2,3},{3,2},{4,5},{5,4},{6,7},{7,6},{8,9},{9,8},{10,11... | collective-permute-start | bytes 847880 | tf_op jit(solution)/shard_map/ppermute | solution.py:1026
  61.1 2.2 %collective-permute-start.19 = (bf16[736,192]{1,0:T(8,128)(2,1)S(1)}, bf16[736,192]{1,0:T(8,128)(2,1)S(1)}, u32[]{:S(2)}, u32[]{:S(2)}) collective-permute-start(bf16[736,192]{1,0:T(8,128)(2,1)S(1)} %collective-permute-done.18.refs_2_.refs_5_), channel_id=1, source_target_pairs={{0,1},{1,0},{2,3},{3,2},{4,5},{5,4},{6,7},{7,6},{8,9},{9,8},{10,11... | collective-permute-start | bytes 847880 | tf_op jit(solution)/shard_map/ppermute | solution.py:1026
  69.8 2.4 %collective-permute-start.26 = (bf16[368,768]{1,0:T(8,128)(2,1)S(1)}, bf16[368,768]{1,0:T(8,128)(2,1)S(1)}, u32[]{:S(2)}, u32[]{:S(2)}) collective-permute-start(bf16[368,768]{1,0:T(8,128)(2,1)S(1)} %get-tuple-element.155.refs_2_), channel_id=1, source_target_pairs={{0,1},{1,0},{2,3},{3,2},{4,5},{5,4},{6,7},{7,6},{8,9},{9,8},{10,11... | collective-permute-start | bytes 1695752 | tf_op jit(solution)/shard_map/ppermute | solution.py:1026
  71.3 15.7 %collective-permute-start.38 = (bf16[4,96,768]{2,1,0:T(8,128)(2,1)S(1)}, bf16[4,96,768]{2,1,0:T(8,128)(2,1)S(1)}, u32[]{:S(2)}, u32[]{:S(2)}) collective-permute-start(bf16[4,96,768]{2,1,0:T(8,128)(2,1)S(1)} %get-tuple-element.190), channel_id=1, source_target_pairs={{0,8},{1,9},{2,10},{3,11},{4,12},{5,13},{6,14},{7,15},{8,0},{9,1},... | collective-permute-start | bytes 1769480 | tf_op jit(solution)/shard_map/ppermute | solution.py:1026
  72.3 18.9 %collective-permute-start.27 = (bf16[368,768]{1,0:T(8,128)(2,1)S(1)}, bf16[368,768]{1,0:T(8,128)(2,1)S(1)}, u32[]{:S(2)}, u32[]{:S(2)}) collective-permute-start(bf16[368,768]{1,0:T(8,128)(2,1)S(1)} %add_rows.1.refs_0_), channel_id=1, source_target_pairs={{0,2},{1,3},{2,0},{3,1},{4,6},{5,7},{6,4},{7,5},{8,10},{9,11},{10,... | collective-permute-start | bytes 1695752 | tf_op jit(solution)/shard_map/ppermute | solution.py:1026
  74.7 16.8 %collective-permute-start.43 = (bf16[4,96,768]{2,1,0:T(8,128)(2,1)S(1)}, bf16[4,96,768]{2,1,0:T(8,128)(2,1)S(1)}, u32[]{:S(2)}, u32[]{:S(2)}) collective-permute-start(bf16[4,96,768]{2,1,0:T(8,128)(2,1)S(1)} %get-tuple-element.203), channel_id=1, source_target_pairs={{0,4},{1,5},{2,6},{3,7},{4,0},{5,1},{6,2},{7,3},{8,12},{9,13},{10,... | collective-permute-start | bytes 1769480 | tf_op jit(solution)/shard_map/ppermute | solution.py:1026
  77.8 27.5 %collective-permute-start.25 = (bf16[416,768]{1,0:T(8,128)(2,1)S(1)}, bf16[416,768]{1,0:T(8,128)(2,1)S(1)}, u32[]{:S(2)}, u32[]{:S(2)}) collective-permute-start(bf16[416,768]{1,0:T(8,128)(2,1)S(1)} %get-tuple-element.148), channel_id=1, source_target_pairs={{0,1},{1,0},{2,3},{3,2},{4,5},{5,4},{6,7},{7,6},{8,9},{9,8},{10,11... | collective-permute-start | bytes 1916936 | tf_op jit(solution)/shard_map/ppermute | solution.py:1026
  87.1 17.6 %collective-permute-start.39 = (bf16[2,96,768]{2,1,0:T(8,128)(2,1)S(1)}, bf16[2,96,768]{2,1,0:T(8,128)(2,1)S(1)}, u32[]{:S(2)}, u32[]{:S(2)}) collective-permute-start(bf16[2,96,768]{2,1,0:T(8,128)(2,1)S(1)} %get-tuple-element.192), channel_id=1, source_target_pairs={{0,16},{1,17},{2,18},{3,19},{4,20},{5,21},{6,22},{7,23},{8,24},{9,... | collective-permute-start | bytes 884744 | tf_op jit(solution)/shard_map/ppermute | solution.py:1026
  91.4 2.0 %collective-permute-start.28 = (bf16[368,768]{1,0:T(8,128)(2,1)S(1)}, bf16[368,768]{1,0:T(8,128)(2,1)S(1)}, u32[]{:S(2)}, u32[]{:S(2)}) collective-permute-start(bf16[368,768]{1,0:T(8,128)(2,1)S(1)} %add_pair.1.refs_0_), channel_id=1, source_target_pairs={{0,1},{1,0},{2,3},{3,2},{4,5},{5,4},{6,7},{7,6},{8,9},{9,8},{10,11... | collective-permute-start | bytes 1695752 | tf_op jit(solution)/shard_map/ppermute | solution.py:1026
  91.6 18.6 %collective-permute-start.44 = (bf16[2,96,768]{2,1,0:T(8,128)(2,1)S(1)}, bf16[2,96,768]{2,1,0:T(8,128)(2,1)S(1)}, u32[]{:S(2)}, u32[]{:S(2)}) collective-permute-start(bf16[2,96,768]{2,1,0:T(8,128)(2,1)S(1)} %get-tuple-element.205), channel_id=1, source_target_pairs={{0,8},{1,9},{2,10},{3,11},{4,12},{5,13},{6,14},{7,15},{8,0},{9,1},... | collective-permute-start | bytes 884744 | tf_op jit(solution)/shard_map/ppermute | solution.py:1026
  97.3 11.0 %collective-permute-start.31 = (bf16[4,112,384]{2,1,0:T(8,128)(2,1)S(1)}, bf16[4,112,384]{2,1,0:T(8,128)(2,1)S(1)}, u32[]{:S(2)}, u32[]{:S(2)}) collective-permute-start(bf16[4,112,384]{2,1,0:T(8,128)(2,1)S(1)} %get-tuple-element.176), channel_id=1, source_target_pairs={{0,4},{1,5},{2,6},{3,7},{4,0},{5,1},{6,2},{7,3},{8,12},{9,13},{10,... | collective-permute-start | bytes 1032200 | tf_op jit(solution)/shard_map/ppermute | solution.py:1026
  103.0 2.3 %collective-permute-start.29 = (bf16[416,768]{1,0:T(8,128)(2,1)S(1)}, bf16[416,768]{1,0:T(8,128)(2,1)S(1)}, u32[]{:S(2)}, u32[]{:S(2)}) collective-permute-start(bf16[416,768]{1,0:T(8,128)(2,1)S(1)} %get-tuple-element.165), channel_id=1, source_target_pairs={{0,1},{1,0},{2,3},{3,2},{4,5},{5,4},{6,7},{7,6},{8,9},{9,8},{10,11... | collective-permute-start | bytes 1916936 | tf_op jit(solution)/shard_map/ppermute | solution.py:1026
  104.8 13.2 %collective-permute-start.34 = (bf16[4,96,384]{2,1,0:T(8,128)(2,1)S(1)}, bf16[4,96,384]{2,1,0:T(8,128)(2,1)S(1)}, u32[]{:S(2)}, u32[]{:S(2)}) collective-permute-start(bf16[4,96,384]{2,1,0:T(8,128)(2,1)S(1)} %get-tuple-element.183), channel_id=1, source_target_pairs={{0,4},{1,5},{2,6},{3,7},{4,0},{5,1},{6,2},{7,3},{8,12},{9,13},{10,... | collective-permute-start | bytes 884744 | tf_op jit(solution)/shard_map/ppermute | solution.py:1026
  105.5 18.2 %collective-permute-start.30 = (bf16[416,768]{1,0:T(8,128)(2,1)S(1)}, bf16[416,768]{1,0:T(8,128)(2,1)S(1)}, u32[]{:S(2)}, u32[]{:S(2)}) collective-permute-start(bf16[416,768]{1,0:T(8,128)(2,1)S(1)} %get-tuple-element.168), channel_id=1, source_target_pairs={{0,2},{1,3},{2,0},{3,1},{4,6},{5,7},{6,4},{7,5},{8,10},{9,11},{10,... | collective-permute-start | bytes 1916936 | tf_op jit(solution)/shard_map/ppermute | solution.py:1026
  108.4 7.7 %collective-permute-start.32 = (bf16[2,112,384]{2,1,0:T(8,128)(2,1)S(1)}, bf16[2,112,384]{2,1,0:T(8,128)(2,1)S(1)}, u32[]{:S(2)}, u32[]{:S(2)}) collective-permute-start(bf16[2,112,384]{2,1,0:T(8,128)(2,1)S(1)} %get-tuple-element.178), channel_id=1, source_target_pairs={{0,8},{1,9},{2,10},{3,11},{4,12},{5,13},{6,14},{7,15},{8,0},{9,1},... | collective-permute-start | bytes 516104 | tf_op jit(solution)/shard_map/ppermute | solution.py:1026
  110.3 10.4 %collective-permute-start.45 = (bf16[96,768]{1,0:T(8,128)(2,1)S(1)}, bf16[96,768]{1,0:T(8,128)(2,1)S(1)}, u32[]{:S(2)}, u32[]{:S(2)}) collective-permute-start(bf16[96,768]{1,0:T(8,128)(2,1)S(1)} %get-tuple-element.207), channel_id=1, source_target_pairs={{0,16},{1,17},{2,18},{3,19},{4,20},{5,21},{6,22},{7,23},{8,24},{9,... | collective-permute-start | bytes 442376 | tf_op jit(solution)/shard_map/ppermute | solution.py:1026
  111.7 9.0 %collective-permute-start.40 = (bf16[96,768]{1,0:T(8,128)(2,1)S(1)}, bf16[96,768]{1,0:T(8,128)(2,1)S(1)}, u32[]{:S(2)}, u32[]{:S(2)}) collective-permute-start(bf16[96,768]{1,0:T(8,128)(2,1)S(1)} %get-tuple-element.195), channel_id=1, source_target_pairs={{0,4},{1,5},{2,6},{3,7},{4,0},{5,1},{6,2},{7,3},{8,12},{9,13},{10,... | collective-permute-start | bytes 442376 | tf_op jit(solution)/shard_map/ppermute | solution.py:1026
  116.1 9.2 %collective-permute-start.33 = (bf16[112,384]{1,0:T(8,128)(2,1)S(1)}, bf16[112,384]{1,0:T(8,128)(2,1)S(1)}, u32[]{:S(2)}, u32[]{:S(2)}) collective-permute-start(bf16[112,384]{1,0:T(8,128)(2,1)S(1)} %get-tuple-element.181), channel_id=1, source_target_pairs={{0,16},{1,17},{2,18},{3,19},{4,20},{5,21},{6,22},{7,23},{8,24},{9,... | collective-permute-start | bytes 258056 | tf_op jit(solution)/shard_map/ppermute | solution.py:1026
  118.0 7.4 %collective-permute-start.35 = (bf16[96,384]{1,0:T(8,128)(2,1)S(1)}, bf16[96,384]{1,0:T(8,128)(2,1)S(1)}, u32[]{:S(2)}, u32[]{:S(2)}) collective-permute-start(bf16[96,384]{1,0:T(8,128)(2,1)S(1)} %get-tuple-element.185), channel_id=1, source_target_pairs={{0,8},{1,9},{2,10},{3,11},{4,12},{5,13},{6,14},{7,15},{8,0},{9,1},... | collective-permute-start | bytes 221192 | tf_op jit(solution)/shard_map/ppermute | solution.py:1026
  120.7 7.2 %collective-permute-start.36 = (bf16[96,384]{1,0:T(8,128)(2,1)S(1)}, bf16[96,384]{1,0:T(8,128)(2,1)S(1)}, u32[]{:S(2)}, u32[]{:S(2)}) collective-permute-start(bf16[96,384]{1,0:T(8,128)(2,1)S(1)} %get-tuple-element.186), channel_id=1, source_target_pairs={{0,16},{1,17},{2,18},{3,19},{4,20},{5,21},{6,22},{7,23},{8,24},{9,... | collective-permute-start | bytes 221192 | tf_op jit(solution)/shard_map/ppermute | solution.py:1026
  120.7 7.2 %collective-permute-start.37 = (bf16[96,384]{1,0:T(8,128)(2,1)S(1)}, bf16[96,384]{1,0:T(8,128)(2,1)S(1)}, u32[]{:S(2)}, u32[]{:S(2)}) collective-permute-start(bf16[96,384]{1,0:T(8,128)(2,1)S(1)} %get-tuple-element.187), channel_id=1, source_target_pairs={{0,24},{1,25},{2,26},{3,27},{4,28},{5,29},{6,30},{7,31},{8,16},{9,... | collective-permute-start | bytes 221192 | tf_op jit(solution)/shard_map/ppermute | solution.py:1026
  123.8 7.7 %collective-permute-start.46 = (bf16[64,768]{1,0:T(8,128)(2,1)S(1)}, bf16[64,768]{1,0:T(8,128)(2,1)S(1)}, u32[]{:S(2)}, u32[]{:S(2)}) collective-permute-start(bf16[64,768]{1,0:T(8,128)(2,1)S(1)} %get-tuple-element.208), channel_id=1, source_target_pairs={{0,2},{1,3},{2,0},{3,1},{4,6},{5,7},{6,4},{7,5},{8,10},{9,11},{10,... | collective-permute-start | bytes 294920 | tf_op jit(solution)/shard_map/ppermute | solution.py:1026
  128.6 5.5 %collective-permute-start.42 = (bf16[64,768]{1,0:T(8,128)(2,1)S(1)}, bf16[64,768]{1,0:T(8,128)(2,1)S(1)}, u32[]{:S(2)}, u32[]{:S(2)}) collective-permute-start(bf16[64,768]{1,0:T(8,128)(2,1)S(1)} %get-tuple-element.199), channel_id=1, source_target_pairs={{0,2},{1,3},{2,0},{3,1},{4,6},{5,7},{6,4},{7,5},{8,10},{9,11},{10,... | collective-permute-start | bytes 294920 | tf_op jit(solution)/shard_map/ppermute | solution.py:1026
  131.5 2.6 %collective-permute-start.49 = (bf16[64,768]{1,0:T(8,128)(2,1)S(1)}, bf16[64,768]{1,0:T(8,128)(2,1)S(1)}, u32[]{:S(2)}, u32[]{:S(2)}) collective-permute-start(bf16[64,768]{1,0:T(8,128)(2,1)S(1)} %collective-permute-done.46.refs_2_), channel_id=1, source_target_pairs={{0,1},{1,0},{2,3},{3,2},{4,5},{5,4},{6,7},{7,6},{8,9},{9,8},{10,11... | collective-permute-start | bytes 294920 | tf_op jit(solution)/shard_map/ppermute | solution.py:1026
  131.5 2.6 %collective-permute-start.48 = (bf16[32,768]{1,0:T(8,128)(2,1)S(1)}, bf16[32,768]{1,0:T(8,128)(2,1)S(1)}, u32[]{:S(2)}, u32[]{:S(2)}) collective-permute-start(bf16[32,768]{1,0:T(8,128)(2,1)S(1)} %get-tuple-element.212), channel_id=1, source_target_pairs={{0,1},{1,0},{2,3},{3,2},{4,5},{5,4},{6,7},{7,6},{8,9},{9,8},{10,11... | collective-permute-start | bytes 147464 | tf_op jit(solution)/shard_map/ppermute | solution.py:1026
  132.0 3.1 %collective-permute-start.41 = (bf16[32,768]{1,0:T(8,128)(2,1)S(1)}, bf16[32,768]{1,0:T(8,128)(2,1)S(1)}, u32[]{:S(2)}, u32[]{:S(2)}) collective-permute-start(bf16[32,768]{1,0:T(8,128)(2,1)S(1)} %get-tuple-element.197), channel_id=1, source_target_pairs={{0,1},{1,0},{2,3},{3,2},{4,5},{5,4},{6,7},{7,6},{8,9},{9,8},{10,11... | collective-permute-start | bytes 147464 | tf_op jit(solution)/shard_map/ppermute | solution.py:1026
  (12 other events, 86.1 us)
